TPU v7x, 32 devices: a whole 2x2x4 slice. The times are simulated.
32 devices in a mesh: blk: 16 (over z, x, core), red: 2 (over y).
Axes of the slice: x: 2, y: 2, z: 4, core: 2. Of those that a mesh axis runs over, the one named last changes fastest.
Arguments:
- amplitudes: float32 [4096, 1536], P('blk', 'red'), may hold values from -6 to 6
- integrals: float32 [4096, 1536], P('blk', 'red'), may hold values from -0.4375 to 0.4375
- cd_irrep: int32 [2, 768], P('red'), may hold values from 0 to 7, never falling along the last dimension, each value on 1 to 192 neighbouring positions
- ab_irrep: int32 [16, 256], P('blk'), may hold values from 0 to 7, never falling along the last dimension, each value on 1 to 64 neighbouring positions
- ij_irrep: int32 [16, 256], P('blk'), may hold values from 0 to 7, never falling along the last dimension, each value on 1 to 64 neighbouring positions
Outputs:
- ladder: float32 [4, 4096, 256], P(None, ('blk', 'red'))
Inputs may be any that keep to these rules, and one draw needn't show every extreme that they name: `cd_irrep`: each row's labels never fall, every irrep 0 to 7 occurs in every row, and each irrep holds at most 192 positions of a row, exactly that many for some irrep. `ab_irrep`: each row's labels never fall, every irrep 0 to 7 occurs in every row, and each irrep holds at most 64 positions of a row, exactly that many for some irrep. `ij_irrep`: each row's labels never fall, every irrep 0 to 7 occurs in every row, and each irrep holds at most 64 positions of a row, exactly that many for some irrep.
All inputs are finite; a program needn't handle non-finite values.
Results may differ from a plain program's by a relative error of at most 0.0003.
Values sent between devices are 32-bit elements; how exact they have to be, the bound alone decides.
No kernel may reach another device: no remote copies, remote signals or barrier semaphores. Data moves between devices by JAX's collectives and lax.ppermute only.
A program may use at most 64 MiB of HBM per device.

v0:
```python
import jax
import jax.numpy as jnp
from jax import lax
from jax.sharding import PartitionSpec as P

SHIFTS = 4


def shifted(shard, axis, by):
    count = lax.axis_size(axis)
    return lax.ppermute(shard, axis, [(i, (i + by) % count) for i in range(count)])


def screen_slab(amp_slab, slab_labels, cd_labels):
    return jnp.where(slab_labels[0][:, None] == cd_labels[0][None, :], amp_slab, jnp.float32(0.0))


def make_term(row_block, block_labels, screened, slab_labels):

    def term(start, count):
        row_labels = block_labels[0]
        product = lax.dot_general(
            row_block,
            screened,
            (((1,), (1,)), ((), ())),
            precision=lax.Precision.HIGHEST,
            preferred_element_type=jnp.float32,
        )
        return jnp.where(row_labels[:, None] == slab_labels[0][None, :], product, jnp.float32(0.0))

    return term


def reduce_terms(term_list, row_count):
    local_rows = row_count // lax.axis_size("red")
    summed = [
        lax.psum_scatter(
            term(jnp.int32(0), local_rows * lax.axis_size("red")),
            "red",
            scatter_dimension=0,
            tiled=True,
        )
        for term in term_list
    ]
    return summed


def body(amplitudes, integrals, cd_irrep, ab_irrep, ij_irrep):
    term_list = []
    slab_now, labels_now = (amplitudes, ij_irrep)
    for shift in range(SHIFTS):
        if shift > 0:
            slab_now, labels_now = shifted((slab_now, labels_now), "blk", 1)
        screened = screen_slab(slab_now, labels_now, cd_irrep)
        term_list.append(make_term(integrals, ab_irrep, screened, labels_now))
    results = reduce_terms(term_list, integrals.shape[0])
    return jnp.stack(results, 0)


def solution(mesh):
    in_specs = (P("blk", "red"), P("blk", "red"), P("red", None), P("blk", None), P("blk", None))
    out_specs = P(None, ("blk", "red"), None)
    return jax.shard_map(body, mesh=mesh, in_specs=in_specs, out_specs=out_specs, check_vma=False)
```

profile of v0, /device:TPU:0, one launch (start us, length us, event | category | flops | bytes accessed | tf_op | source)
XLA Modules:
  0.0 89.9 jit_solution(3670297467132296362)
XLA Ops:
  6.5 0.5 collective-permute-start.1
  7.0 14.8 %collective-permute-done.1 = f32[256,768]{1,0:T(8,128)S(1)} collective-permute-done((f32[256,768]{1,0:T(8,128)}, f32[256,768]{1,0:T(8,128)S(1)}, u32[]{:S(2)}, u32[]{:S(2)}) %collective-permute-start.1) | collective-permute-done | bytes 786464 | tf_op jit(solution)/shard_map/ppermute | solution.py:11
  21.8 0.7 reduce
  22.6 0.6 copy-done.2
  23.2 2.7 %fusion = f32[256,256]{0,1:T(8,128)} fusion(f32[256,768]{1,0:T(8,128)S(1)} %copy-done, f32[256,768]{1,0:T(8,128)} %param.5, s32[768]{0:T(1024)S(1)} %reduce, s32[256]{0:T(256)S(1)} %bitcast.37, s32[256]{0:T(256)S(1)} %bitcast.33), kind=kOutput, calls=%fused_computation.4 | convolution fusion | flops 604504064 | bytes 1840128 | tf_op jit(solution)/shard_map/dot_general | solution.py:22
  26.0 0.0 reduce-scatter.7.cloned.1.call-start
  26.0 0.1 collective-permute-start
  26.1 9.9 %collective-permute-done.3 = f32[256,768]{1,0:T(8,128)S(1)} collective-permute-done((f32[256,768]{1,0:T(8,128)S(1)}, f32[256,768]{1,0:T(8,128)S(1)}, u32[]{:S(2)}, u32[]{:S(2)}) %collective-permute-start.3) | collective-permute-done | bytes 786464 | tf_op jit(solution)/shard_map/ppermute | solution.py:11
  36.0 0.0 collective-permute-done
  36.0 1.6 %compare_select_fusion.2 = f32[256,256]{0,1:T(8,128)} fusion(s32[256]{0:T(256)S(1)} %bitcast.34, s32[256]{0:T(256)S(1)} %bitcast.38, f32[256,768]{1,0:T(8,128)S(1)} %copy-done, f32[256,768]{1,0:T(8,128)S(1)} %collective-permute-done.1, s32[768]{0:T(1024)S(1)} %reduce), kind=kOutput, calls=%fused_computation.28 | convolution fusion | flops 604504064 | bytes 1840128 | tf_op jit(solution)/shard_map/dot_general | solution.py:22
  37.6 0.0 reduce-scatter.9.cloned.1.call-start
  37.6 0.1 collective-permute-start.2
  37.7 12.4 %collective-permute-done.2 = s32[1,256]{1,0:T(1,128)S(1)} collective-permute-done((s32[1,256]{1,0:T(1,128)S(1)}, s32[1,256]{1,0:T(1,128)S(1)}, u32[]{:S(2)}, u32[]{:S(2)}) %collective-permute-start.2) | collective-permute-done | bytes 1056 | tf_op jit(solution)/shard_map/ppermute | solution.py:11
  50.1 1.6 %compare_select_fusion.1 = f32[256,256]{0,1:T(8,128)} fusion(s32[256]{0:T(256)S(1)} %bitcast.35, s32[256]{0:T(256)S(1)} %bitcast.39, f32[256,768]{1,0:T(8,128)S(1)} %copy-done, f32[256,768]{1,0:T(8,128)S(1)} %collective-permute-done.3, s32[768]{0:T(1024)S(1)} %reduce), kind=kOutput, calls=%fused_computation.27 | convolution fusion | flops 604504064 | bytes 1840128 | tf_op jit(solution)/shard_map/dot_general | solution.py:22
  51.7 0.0 reduce-scatter.11.cloned.1.call-start
  51.7 0.1 collective-permute-start.4
  51.8 5.7 %collective-permute-done.4 = s32[1,256]{1,0:T(1,128)S(1)} collective-permute-done((s32[1,256]{1,0:T(1,128)S(1)}, s32[1,256]{1,0:T(1,128)S(1)}, u32[]{:S(2)}, u32[]{:S(2)}) %collective-permute-start.4) | collective-permute-done | bytes 1056 | tf_op jit(solution)/shard_map/ppermute | solution.py:11
  57.5 1.6 %compare_select_fusion = f32[256,256]{0,1:T(8,128)} fusion(s32[256]{0:T(256)S(1)} %bitcast.36, s32[256]{0:T(256)S(1)} %bitcast.40, f32[256,768]{1,0:T(8,128)S(1)} %copy-done, f32[256,768]{1,0:T(8,128)S(1)} %collective-permute-done.5, s32[768]{0:T(1024)S(1)} %reduce), kind=kOutput, calls=%fused_computation.26 | convolution fusion | flops 604504064 | bytes 1840128 | tf_op jit(solution)/shard_map/dot_general | solution.py:22
  59.1 0.0 reduce-scatter.5.cloned.1.call-done
  59.1 0.0 reduce-scatter.7.cloned.1.call-done
  59.1 8.3 %reduce-scatter.9.cloned.1.call-done = f32[128,256]{0,1:T(8,128)} async-done(((f32[256,256]{0,1:T(8,128)}), f32[128,256]{0,1:T(8,128)}) %reduce-scatter.9.cloned.1.call-update) | async-done | bytes 131088 | tf_op jit(solution)/shard_map/reduce_scatter | solution.py:37
  67.4 13.9 %reduce-scatter.11.cloned.1.call-done = f32[128,256]{0,1:T(8,128)} async-done(((f32[256,256]{0,1:T(8,128)}), f32[128,256]{0,1:T(8,128)}) %reduce-scatter.11.cloned.1.call-update) | async-done | bytes 131088 | tf_op jit(solution)/shard_map/reduce_scatter | solution.py:37
  81.3 1.1 %pad_maximum_fusion = f32[4,128,256]{1,2,0:T(8,128)S(1)} fusion(f32[1,128,256]{1,2,0:T(8,128)} %bitcast.32, f32[1,128,256]{1,2,0:T(8,128)} %bitcast.31, f32[1,128,256]{1,2,0:T(8,128)} %bitcast.30, f32[1,128,256]{1,2,0:T(8,128)} %bitcast.29), kind=kLoop, calls=%fused_computation.13 | loop fusion | flops 393216 | bytes 1048576 | tf_op jit(solution)/shard_map/stack | solution.py:57
  82.4 1.0 %copy.6 = f32[4,128,256]{2,1,0:T(8,128)} copy(f32[4,128,256]{1,2,0:T(8,128)S(1)} %pad_maximum_fusion) | data formatting | bytes 1048576 | tf_op jit(solution)/shard_map/stack | solution.py:57
  (13 shorter events, 0.1 us)
Async XLA Ops:
  6.5 16.0 %copy-start = (f32[256,768]{1,0:T(8,128)S(1)}, f32[256,768]{1,0:T(8,128)}, u32[]{:S(2)}) copy-start(f32[256,768]{1,0:T(8,128)} %param.6) | copy-start | bytes 2359300
  6.5 52.6 %reduce-scatter.5.cloned.1.call-start = ((), (), s32[]{:S(2)}) async-start(), calls=%async_computation.4 | async-start | bytes 393216 | tf_op jit(solution)/shard_map/reduce_scatter | solution.py:37
  6.5 15.3 %collective-permute-start.1 = (f32[256,768]{1,0:T(8,128)}, f32[256,768]{1,0:T(8,128)S(1)}, u32[]{:S(2)}, u32[]{:S(2)}) collective-permute-start(f32[256,768]{1,0:T(8,128)} %param.5), channel_id=1, source_target_pairs={{0,2},{2,4},{4,6},{6,8},{8,10},{10,12},{12,14},{14,16},{16,18},{18... | collective-permute-start | bytes 2359304 | tf_op jit(solution)/shard_map/ppermute | solution.py:11
  21.8 14.1 %collective-permute-start.3 = (f32[256,768]{1,0:T(8,128)S(1)}, f32[256,768]{1,0:T(8,128)S(1)}, u32[]{:S(2)}, u32[]{:S(2)}) collective-permute-start(f32[256,768]{1,0:T(8,128)S(1)} %collective-permute-done.1), channel_id=1, source_target_pairs={{0,2},{2,4},{4,6},{6,8},{8,10},{10,12},{12,14},{14,16},{16,18},{18... | collective-permute-start | bytes 2359304 | tf_op jit(solution)/shard_map/ppermute | solution.py:11
  22.5 0.7 copy-start.2
  22.6 0.7 copy-start.1
  26.0 33.2 %reduce-scatter.7.cloned.1.call-start = ((), (), s32[]{:S(2)}) async-start(), calls=%async_computation.5 | async-start | bytes 393216 | tf_op jit(solution)/shard_map/reduce_scatter | solution.py:37
  26.0 10.0 %collective-permute-start = (s32[1,256]{1,0:T(1,128)S(1)}, s32[1,256]{1,0:T(1,128)S(1)}, u32[]{:S(2)}, u32[]{:S(2)}) collective-permute-start(s32[1,256]{1,0:T(1,128)S(1)} %copy-done.2), channel_id=1, source_target_pairs={{0,2},{2,4},{4,6},{6,8},{8,10},{10,12},{12,14},{14,16},{16,18},{18... | collective-permute-start | bytes 3080 | tf_op jit(solution)/shard_map/ppermute | solution.py:11
  36.0 21.5 %collective-permute-start.5 = (f32[256,768]{1,0:T(8,128)S(1)}, f32[256,768]{1,0:T(8,128)S(1)}, u32[]{:S(2)}, u32[]{:S(2)}) collective-permute-start(f32[256,768]{1,0:T(8,128)S(1)} %collective-permute-done.3), channel_id=1, source_target_pairs={{0,2},{2,4},{4,6},{6,8},{8,10},{10,12},{12,14},{14,16},{16,18},{18... | collective-permute-start | bytes 2359304 | tf_op jit(solution)/shard_map/ppermute | solution.py:11
  37.6 29.8 %reduce-scatter.9.cloned.1.call-start = ((), (), s32[]{:S(2)}) async-start(), calls=%async_computation.6 | async-start | bytes 393216 | tf_op jit(solution)/shard_map/reduce_scatter | solution.py:37
  37.6 12.5 %collective-permute-start.2 = (s32[1,256]{1,0:T(1,128)S(1)}, s32[1,256]{1,0:T(1,128)S(1)}, u32[]{:S(2)}, u32[]{:S(2)}) collective-permute-start(s32[1,256]{1,0:T(1,128)S(1)} %collective-permute-done), channel_id=1, source_target_pairs={{0,2},{2,4},{4,6},{6,8},{8,10},{10,12},{12,14},{14,16},{16,18},{18... | collective-permute-start | bytes 3080 | tf_op jit(solution)/shard_map/ppermute | solution.py:11
  51.7 29.6 %reduce-scatter.11.cloned.1.call-start = ((), (), s32[]{:S(2)}) async-start(), calls=%async_computation.7 | async-start | bytes 393216 | tf_op jit(solution)/shard_map/reduce_scatter | solution.py:37
  51.7 5.7 %collective-permute-start.4 = (s32[1,256]{1,0:T(1,128)S(1)}, s32[1,256]{1,0:T(1,128)S(1)}, u32[]{:S(2)}, u32[]{:S(2)}) collective-permute-start(s32[1,256]{1,0:T(1,128)S(1)} %collective-permute-done.2), channel_id=1, source_target_pairs={{0,2},{2,4},{4,6},{6,8},{8,10},{10,12},{12,14},{14,16},{16,18},{18... | collective-permute-start | bytes 3080 | tf_op jit(solution)/shard_map/ppermute | solution.py:11
Sparse Core Ops, SparseCore 0:
  26.1 13.3 reduce-scatter.4
  41.8 11.6 reduce-scatter.6
  55.7 11.6 reduce-scatter.8
  69.5 11.6 reduce-scatter.10
where the time goes:
time: 90.1 us; the launch traced here: 89.9 us
  waiting for transfers between devices  65.1 us (72%)
  between operations  13.2 us (15%)
  matrix products  7.37 us (8%)
  other arithmetic  1.83 us (2%)
  local copies, waits for them, and re-layouts  1.67 us (2%)
    ppermute x6, waiting for transfers between devices, shifted(): lax.ppermute(shard, axis, [(i, (i + by) % count) for i in range(count)])  42.9 us
    reduce_scatter x4, waiting for transfers between devices, reduce_terms(): lax.psum_scatter(term(jnp.int32(0), local_rows * lax.axis_size('red')), '...  22.2 us
    dot_general x4, matrix products, term(): lax.dot_general(row_block, screened, (((1,), (1,)), ((), ())), precision=...  7.37 us
  transfers between devices with their start and end apart: 10, of which 6 were waited for; matrix products, arithmetic and copies ran while one was open for 9% of the time, Pallas kernels for 0%

commit v1 on v0

v1 whole, which is shorter than its diff:
```python
import functools
import jax
import jax.numpy as jnp
from jax import lax
from jax.experimental import pallas as pl
from jax.experimental.pallas import tpu as pltpu
from jax.sharding import PartitionSpec as P

IRREPS = 8
LANES = 128
F32 = jnp.float32


def column(labels):
    return jnp.broadcast_to(labels.astype(F32), (LANES, labels.shape[1])).T


def fold(rows_ref, row_labels, cd_labels, width):
    total = None
    for start in range(0, rows_ref.shape[1], width):
        part = slice(start, start + width)
        kept = jnp.where(row_labels[:, :1] == cd_labels[:, part], rows_ref[:, part], 0.0)
        total = kept if total is None else total + kept
    return total


def pack_kernel(amp_ref, ij_ref, cd_ref, out_ref):
    width = out_ref.shape[0] - 8
    folded = fold(amp_ref, column(ij_ref[...]), cd_ref[...].astype(F32), width)
    out_ref[:width, :] = folded.T
    out_ref[width:, :] = jnp.broadcast_to(ij_ref[...].astype(F32), (8, out_ref.shape[1]))


def fold_rows_kernel(rows_ref, ab_ref, cd_ref, out_ref):
    out_ref[...] = fold(rows_ref, column(ab_ref[...]), cd_ref[...].astype(F32), out_ref.shape[1])


def product(rows, slab_ref, row_labels, narrow):
    width = rows.shape[1]
    full = jnp.dot(rows, slab_ref[:width, :], precision=lax.Precision.HIGHEST, preferred_element_type=F32)
    full = jnp.where(row_labels[:, :1] == slab_ref[width:width + 1, :], full, 0.0)
    total = None
    for start in range(0, full.shape[1], narrow):
        part = full[:, start:start + narrow]
        total = part if total is None else total + part
    return total


def terms_kernel(rows_ref, ab_ref, own_ref, two_ref, mix_ref, swap_ref, keep_ref, send_ref, labels_ref, all_ref):
    narrow = keep_ref.shape[1] // 4
    width = rows_ref.shape[1]
    odd = lax.rem(lax.axis_index("blk"), 2) == 1
    row_labels = column(ab_ref[...])
    rows = rows_ref[...]
    own, two, mix, swap = [product(rows, ref, row_labels, narrow) for ref in (own_ref, two_ref, mix_ref, swap_ref)]
    one = jnp.where(odd, mix, swap)
    three = jnp.where(odd, swap, mix)
    all_ref[...] = jnp.concatenate([own, one, two, three], axis=1)
    own, two, mix, swap = [ref[width:width + 1, :] for ref in (own_ref, two_ref, mix_ref, swap_ref)]
    labels_ref[...] = jnp.concatenate([own, jnp.where(odd, mix, swap), two, jnp.where(odd, swap, mix)] * 2, axis=0)
    parts = send_ref.shape[0] + 1
    mine = lax.axis_index("red")
    count = keep_ref.shape[0]
    keep_ref[...] = all_ref[pl.ds(pl.multiple_of(mine * count, count), count), :]
    for step in range(1, parts):
        peer = lax.rem(mine + step, parts)
        send_ref[step - 1] = all_ref[pl.ds(pl.multiple_of(peer * count, count), count), :]


def finish_kernel(parts, keep_ref, *refs):
    taken, (labels_ref, ab_ref, out_ref) = refs[:parts - 1], refs[parts - 1:]
    total = keep_ref[...]
    for ref in taken:
        total = total + ref[...]
    count = total.shape[0]
    narrow = total.shape[1] // 4
    rows = column(ab_ref[...])
    mine = lax.axis_index("red")
    own = rows[:count]
    for part in range(1, parts):
        own = jnp.where(mine == part, rows[part * count:(part + 1) * count], own)
    for m in range(4):
        wide = jnp.concatenate([total[:, m * narrow:(m + 1) * narrow]] * (out_ref.shape[2] // narrow), axis=1)
        out_ref[m] = jnp.where(own[:, :1] == labels_ref[m:m + 1, :], wide, 0.0)


def whole(shape, dtype=F32):
    return jax.ShapeDtypeStruct(shape, dtype)


def vmem(count):
    return [pl.BlockSpec(memory_space=pltpu.VMEM)] * count


def call(kernel, out_shape, args, flops, **more):
    outs = out_shape if isinstance(out_shape, list) else [out_shape]
    moved = sum(a.size * 4 for a in list(args) + outs)
    return pl.pallas_call(
        kernel,
        out_shape=out_shape,
        in_specs=vmem(len(args)),
        out_specs=vmem(len(outs)) if isinstance(out_shape, list) else vmem(1)[0],
        cost_estimate=pl.CostEstimate(flops=flops, bytes_accessed=moved, transcendentals=0),
        compiler_params=pltpu.CompilerParams(vmem_limit_bytes=32 * 1024 * 1024),
        **more,
    )(*args)


def body(amplitudes, integrals, cd_irrep, ab_irrep, ij_irrep):
    blocks, parts = lax.axis_size("blk"), lax.axis_size("red")
    pairs, depth = amplitudes.shape
    row_count = integrals.shape[0]
    width, narrow = depth // 4, pairs // 4
    count = row_count // parts

    two_on = [(i, (i + 2) % blocks) for i in range(blocks)]
    mixed = [(i, (i + 1 if i % 2 == 0 else i + 3) % blocks) for i in range(blocks)]
    cores = [(i, i ^ 1) for i in range(blocks)]

    own = call(pack_kernel, whole((width + 8, pairs)), (amplitudes, ij_irrep, cd_irrep), 4 * amplitudes.size)
    two = lax.ppermute(own, "blk", two_on)
    mix = lax.ppermute(own, "blk", mixed)
    rows = call(fold_rows_kernel, whole((row_count, width)), (integrals, ab_irrep, cd_irrep), 4 * integrals.size)
    swap = lax.ppermute(two, "blk", cores)
    keep, send, labels = call(
        terms_kernel,
        [whole((count, 4 * narrow)), whole((parts - 1, count, 4 * narrow)), whole((8, pairs))],
        (rows, ab_irrep, own, two, mix, swap),
        4 * 2 * row_count * width * pairs,
        scratch_shapes=[pltpu.VMEM((row_count, 4 * narrow), F32)],
    )
    taken = [
        lax.ppermute(send[step - 1], "red", [(i, (i + step) % parts) for i in range(parts)])
        for step in range(1, parts)
    ]
    return call(
        functools.partial(finish_kernel, parts),
        whole((4, count, pairs)),
        (keep, *taken, labels, ab_irrep),
        4 * 2 * count * pairs,
    )


def solution(mesh):
    in_specs = (P("blk", "red"), P("blk", "red"), P("red", None), P("blk", None), P("blk", None))
    out_specs = P(None, ("blk", "red"), None)
    return jax.shard_map(body, mesh=mesh, in_specs=in_specs, out_specs=out_specs, check_vma=False)
```

time: 90.1 us -> 24.3 us (0.27)
  waiting for transfers between devices: 65.1 us -> 13.8 us
  between operations: 13.2 us -> 0.03 us
  matrix products: 7.37 us -> 0 us
  starting transfers between devices: 0.76 us -> 4.8 us
  Pallas kernels: 0 us -> 3 us
  other arithmetic: 1.83 us -> 0 us
    ppermute x6 -> x4, waiting for transfers between devices: 42.9 us -> 13.8 us  [the longest x1 8.94 us: body(): two = lax.ppermute(own, 'blk', two_on)]
    reduce_scatter x4 -> x0, waiting for transfers between devices: 22.2 us -> none  [reduce_terms(): lax.psum_scatter(term(jnp.int32(0), local_rows * lax.axis_size('red')), '...]
    dot_general x4 -> x0, matrix products: 7.37 us -> none  [term(): lax.dot_general(row_block, screened, (((1,), (1,)), ((), ())), precision=...]
    ppermute x6 -> x4, starting transfers between devices: 0.63 us -> 4.8 us  [the longest x1 2.99 us: body(): two = lax.ppermute(own, 'blk', two_on)]
    pallas_call x0 -> x4, Pallas kernels: none -> 3 us  [call(): pl.pallas_call(kernel, out_shape=out_shape, in_specs=vmem(len(args)), out...]
    unnamed x6 -> x10, local copies, waits for them, and re-layouts: 0.68 us -> 2.5 us
    another operation x1 -> x0, other arithmetic: 1.13 us -> none  [body(): return jnp.stack(results, 0)]
    another operation x1 -> x0, local copies, waits for them, and re-layouts: 1 us -> none  [body(): return jnp.stack(results, 0)]
  transfers between devices with their start and end apart: 10 -> 4, of which waited for: 6 -> 3; matrix products, arithmetic and copies ran while one was open for 9% -> 0% of each run, Pallas kernels for 0% -> 1%
where the time goes in v1:
time: 24.3 us; the launch traced here: 24.2 us
  waiting for transfers between devices  13.8 us (57%)
  starting transfers between devices  4.8 us (20%)
  Pallas kernels  3 us (12%)
  local copies, waits for them, and re-layouts  2.5 us (10%)
    ppermute x1, waiting for transfers between devices, body(): two = lax.ppermute(own, 'blk', two_on)  8.94 us
    ppermute x1, waiting for transfers between devices, body(): lax.ppermute(send[step - 1], 'red', [(i, (i + step) % parts) for i in ran...  3.8 us
    pallas_call x4, Pallas kernels, call(): pl.pallas_call(kernel, out_shape=out_shape, in_specs=vmem(len(args)), out...  3 us
    ppermute x1, starting transfers between devices, body(): two = lax.ppermute(own, 'blk', two_on)  2.99 us
    unnamed x10, local copies, waits for them, and re-layouts  2.5 us
    ppermute x1, starting transfers between devices, body(): lax.ppermute(send[step - 1], 'red', [(i, (i + step) % parts) for i in ran...  1.8 us
    ppermute x1, waiting for transfers between devices, body(): swap = lax.ppermute(two, 'blk', cores)  1.08 us
  transfers between devices with their start and end apart: 4, of which 3 were waited for; matrix products, arithmetic and copies ran while one was open for 0% of the time, Pallas kernels for 1%

profile of v1, /device:TPU:0, one launch (start us, length us, event | category | flops | bytes accessed | tf_op | source)
XLA Modules:
  0.0 24.2 jit_solution(4715471370378750621)
XLA Ops:
  0.0 0.0 copy-start.1
  0.0 1.1 %copy-done.1 = f32[256,768]{1,0:T(8,128)S(1)} copy-done((f32[256,768]{1,0:T(8,128)S(1)}, f32[256,768]{1,0:T(8,128)}, u32[]{:S(2)}) %copy-start.1) | copy-done | bytes 786456
  1.1 0.0 copy-start.2
  1.1 0.7 %copy-done.2 = s32[1,768]{1,0:T(1,128)S(1)} copy-done((s32[1,768]{1,0:T(1,128)S(1)}, s32[1,768]{1,0:T(1,128)}, u32[]{:S(2)}) %copy-start.2) | copy-done | bytes 3096
  1.8 0.0 copy-start.4
  1.8 0.7 %copy-done.4 = s32[1,256]{1,0:T(1,128)S(1)} copy-done((s32[1,256]{1,0:T(1,128)S(1)}, s32[1,256]{1,0:T(1,128)}, u32[]{:S(2)}) %copy-start.4) | copy-done | bytes 1048
  2.5 0.0 copy-start
  2.5 0.0 copy-start.3
  2.5 0.4 %shard_map.56.own_ref = f32[200,256]{1,0:T(8,128)S(1)} custom-call(f32[256,768]{1,0:T(8,128)S(1)} %copy-done.1, s32[1,256]{1,0:T(1,128)S(1)} %copy-done.4, s32[1,768]{1,0:T(1,128)S(1)} %copy-done.2), custom_call_target="tpu_custom_call" | custom-call | flops 786432 | bytes 995328 | tf_op jit(solution)/shard_map/pallas_call | solution.py:98
  2.9 3.0 %collective-permute-start = (f32[200,256]{1,0:T(8,128)S(1)}, f32[200,256]{1,0:T(8,128)S(1)}, u32[]{:S(2)}, u32[]{:S(2)}) collective-permute-start(f32[200,256]{1,0:T(8,128)S(1)} %shard_map.56.own_ref), channel_id=1, source_target_pairs={{0,4},{2,6},{4,8},{6,10},{8,12},{10,14},{12,16},{14,18},{16,20},{1... | collective-permute-start | bytes 614408 | tf_op jit(solution)/shard_map/ppermute | solution.py:121
  5.9 0.0 collective-permute-start.1
  5.9 8.9 %collective-permute-done.two_ref = f32[200,256]{1,0:T(8,128)S(1)} collective-permute-done((f32[200,256]{1,0:T(8,128)S(1)}, f32[200,256]{1,0:T(8,128)S(1)}, u32[]{:S(2)}, u32[]{:S(2)}) %collective-permute-start) | collective-permute-done | bytes 204832 | tf_op jit(solution)/shard_map/ppermute | solution.py:121
  14.9 0.0 collective-permute-start.2
  14.9 0.0 copy-done
  14.9 0.0 copy-done.3
  14.9 0.3 %shard_map.55.rows_ref = f32[256,192]{1,0:T(8,128)S(1)} custom-call(f32[256,768]{1,0:T(8,128)S(1)} %copy-done, s32[1,256]{1,0:T(1,128)S(1)} %copy-done.3, s32[1,768]{1,0:T(1,128)S(1)} %copy-done.2), custom_call_target="tpu_custom_call" | custom-call | flops 786432 | bytes 987136 | tf_op jit(solution)/shard_map/pallas_call | solution.py:98
  15.2 0.0 collective-permute-done.1.mix_ref
  15.2 1.1 %collective-permute-done.2.swap_ref = f32[200,256]{1,0:T(8,128)S(1)} collective-permute-done((f32[200,256]{1,0:T(8,128)S(1)}, f32[200,256]{1,0:T(8,128)S(1)}, u32[]{:S(2)}, u32[]{:S(2)}) %collective-permute-start.2) | collective-permute-done | bytes 204832 | tf_op jit(solution)/shard_map/ppermute | solution.py:124
  16.3 1.3 %shard_map.57 = (f32[128,256]{1,0:T(8,128)S(1)}, f32[1,128,256]{2,1,0:T(8,128)S(1)}, f32[8,256]{1,0:T(8,128)S(1)}) custom-call(f32[256,192]{1,0:T(8,128)S(1)} %shard_map.55.rows_ref, s32[1,256]{1,0:T(1,128)S(1)} %copy-done.3, f32[200,256]{1,0:T(8,128)S(1)} %shard_map.56.own_ref, f32[200,256]{1,0:T(8,128)S(1)} %collective-permute-done.two_ref, ...), custom_call_target="tpu_custom_call" | custom-call | flops 100663296 | bytes 1287168 | tf_op jit(solution)/shard_map/pallas_call | solution.py:98
  17.6 1.8 %collective-permute-start.3 = (f32[128,256]{1,0:T(8,128)S(1)}, f32[128,256]{1,0:T(8,128)S(1)}, u32[]{:S(2)}, u32[]{:S(2)}) collective-permute-start(f32[128,256]{1,0:T(8,128)S(1)} %bitcast.1), channel_id=1, source_target_pairs={{0,1},{1,0},{2,3},{3,2},{4,5},{5,4},{6,7},{7,6},{8,9},{9,8},{10,11... | collective-permute-start | bytes 393224 | tf_op jit(solution)/shard_map/ppermute | solution.py:133
  19.4 3.8 %collective-permute-done.3.refs_0_ = f32[128,256]{1,0:T(8,128)S(1)} collective-permute-done((f32[128,256]{1,0:T(8,128)S(1)}, f32[128,256]{1,0:T(8,128)S(1)}, u32[]{:S(2)}, u32[]{:S(2)}) %collective-permute-start.3) | collective-permute-done | bytes 131104 | tf_op jit(solution)/shard_map/ppermute | solution.py:133
  23.2 1.0 %shard_map.58 = f32[4,128,256]{2,1,0:T(8,128)} custom-call(f32[128,256]{1,0:T(8,128)S(1)} %get-tuple-element.8.keep_ref, f32[128,256]{1,0:T(8,128)S(1)} %collective-permute-done.3.refs_0_, f32[8,256]{1,0:T(8,128)S(1)} %get-tuple-element.10.refs_1_, s32[1,256]{1,0:T(1,128)S(1)} %copy-done.3), custom_call_target="tpu_custom_call" | custom-call | flops 262144 | bytes 795648 | tf_op jit(solution)/shard_map/pallas_call | solution.py:98
Async XLA Ops:
  0.0 1.1 %copy-start.1 = (f32[256,768]{1,0:T(8,128)S(1)}, f32[256,768]{1,0:T(8,128)}, u32[]{:S(2)}) copy-start(f32[256,768]{1,0:T(8,128)} %amp_ref.1) | copy-start | bytes 2359300
  1.1 0.7 %copy-start.2 = (s32[1,768]{1,0:T(1,128)S(1)}, s32[1,768]{1,0:T(1,128)}, u32[]{:S(2)}) copy-start(s32[1,768]{1,0:T(1,128)} %cd_ref.3) | copy-start | bytes 9220
  1.8 0.7 %copy-start.4 = (s32[1,256]{1,0:T(1,128)S(1)}, s32[1,256]{1,0:T(1,128)}, u32[]{:S(2)}) copy-start(s32[1,256]{1,0:T(1,128)} %ij_ref.1) | copy-start | bytes 3076
  2.5 12.4 %copy-start = (f32[256,768]{1,0:T(8,128)S(1)}, f32[256,768]{1,0:T(8,128)}, u32[]{:S(2)}) copy-start(f32[256,768]{1,0:T(8,128)} %rows_ref.1) | copy-start | bytes 2359300
  2.5 12.4 %copy-start.3 = (s32[1,256]{1,0:T(1,128)S(1)}, s32[1,256]{1,0:T(1,128)}, u32[]{:S(2)}) copy-start(s32[1,256]{1,0:T(1,128)} %refs_2_.1) | copy-start | bytes 3076
  2.9 11.9 %collective-permute-start = (f32[200,256]{1,0:T(8,128)S(1)}, f32[200,256]{1,0:T(8,128)S(1)}, u32[]{:S(2)}, u32[]{:S(2)}) collective-permute-start(f32[200,256]{1,0:T(8,128)S(1)} %shard_map.56.own_ref), channel_id=1, source_target_pairs={{0,4},{2,6},{4,8},{6,10},{8,12},{10,14},{12,16},{14,18},{16,20},{1... | collective-permute-start | bytes 614408 | tf_op jit(solution)/shard_map/ppermute | solution.py:121
  5.9 9.3 %collective-permute-start.1 = (f32[200,256]{1,0:T(8,128)S(1)}, f32[200,256]{1,0:T(8,128)S(1)}, u32[]{:S(2)}, u32[]{:S(2)}) collective-permute-start(f32[200,256]{1,0:T(8,128)S(1)} %shard_map.56.own_ref), channel_id=1, source_target_pairs={{0,2},{2,8},{4,6},{6,12},{8,10},{10,16},{12,14},{14,20},{16,18},{1... | collective-permute-start | bytes 614408 | tf_op jit(solution)/shard_map/ppermute | solution.py:122
  14.9 1.5 %collective-permute-start.2 = (f32[200,256]{1,0:T(8,128)S(1)}, f32[200,256]{1,0:T(8,128)S(1)}, u32[]{:S(2)}, u32[]{:S(2)}) collective-permute-start(f32[200,256]{1,0:T(8,128)S(1)} %collective-permute-done.two_ref), channel_id=1, source_target_pairs={{0,2},{2,0},{4,6},{6,4},{8,10},{10,8},{12,14},{14,12},{16,18},{18,... | collective-permute-start | bytes 614408 | tf_op jit(solution)/shard_map/ppermute | solution.py:124
  17.6 5.6 %collective-permute-start.3 = (f32[128,256]{1,0:T(8,128)S(1)}, f32[128,256]{1,0:T(8,128)S(1)}, u32[]{:S(2)}, u32[]{:S(2)}) collective-permute-start(f32[128,256]{1,0:T(8,128)S(1)} %bitcast.1), channel_id=1, source_target_pairs={{0,1},{1,0},{2,3},{3,2},{4,5},{5,4},{6,7},{7,6},{8,9},{9,8},{10,11... | collective-permute-start | bytes 393224 | tf_op jit(solution)/shard_map/ppermute | solution.py:133

commit v2 on v1

v2 whole, which is shorter than its diff:
```python
import functools
import jax
import jax.numpy as jnp
from jax import lax
from jax.experimental import pallas as pl
from jax.experimental.pallas import tpu as pltpu
from jax.sharding import PartitionSpec as P

LANES = 128
F32 = jnp.float32
ONCHIP = pl.BlockSpec(memory_space=pltpu.VMEM)
OFFCHIP = pl.BlockSpec(memory_space=pltpu.HBM)


def column(labels):
    return jnp.broadcast_to(labels.astype(F32), (LANES, labels.shape[1])).T


def fold(rows, row_labels, cd_labels, width):
    total = None
    for start in range(0, rows.shape[1], width):
        part = slice(start, start + width)
        kept = jnp.where(row_labels[:, :1] == cd_labels[:, part], rows[:, part], 0.0)
        total = kept if total is None else total + kept
    return total


def fetch(pairs, sems):
    copies = [pltpu.make_async_copy(src, dst, sems.at[i]) for i, (src, dst) in enumerate(pairs)]
    for copy in copies:
        copy.start()
    return copies


def chunks(count):
    return [pl.ds(start, LANES) for start in range(0, count, LANES)]


def pack_kernel(amp_ref, ij_ref, cd_ref, out_ref, amp, ij, cd, sems):
    pairs, width = amp.shape[0], out_ref.shape[0] - 8
    parts = chunks(pairs)
    copies = fetch([(ij_ref, ij), (cd_ref, cd)] + [(amp_ref.at[c], amp.at[c]) for c in parts], sems)
    copies[0].wait()
    copies[1].wait()
    rows = column(ij[...])
    labels = cd[...].astype(F32)
    out_ref[width:, :] = jnp.broadcast_to(ij[...].astype(F32), (8, pairs))
    for copy, c in zip(copies[2:], parts):
        copy.wait()
        out_ref[:width, c] = fold(amp[c, :], rows[c.start:c.start + LANES], labels, width).T


def narrowed(rows, slab_ref, row_labels):
    width = rows.shape[1]
    full = jnp.dot(rows, slab_ref[:width, :], precision=lax.Precision.HIGHEST, preferred_element_type=F32)
    full = jnp.where(row_labels[:, :1] == slab_ref[width:width + 1, :], full, 0.0)
    narrow = full.shape[1] // 4
    return sum(full[:, k * narrow:(k + 1) * narrow] for k in range(1, 4)) + full[:, :narrow]


def first_kernel(v_ref, ab_ref, cd_ref, own_ref, rows_ref, column_ref, out_ref, v, ab, cd, sems):
    width = rows_ref.shape[1]
    parts = chunks(v.shape[0])
    copies = fetch([(ab_ref, ab), (cd_ref, cd)] + [(v_ref.at[c], v.at[c]) for c in parts], sems)
    copies[0].wait()
    copies[1].wait()
    column_ref[...] = column(ab[...])
    labels = cd[...].astype(F32)
    for copy, c in zip(copies[2:], parts):
        copy.wait()
        rows_ref[c, :] = fold(v[c, :], column_ref[c, :], labels, width)
    out_ref[...] = narrowed(rows_ref[...], own_ref, column_ref[...])


def middle_kernel(rows_ref, column_ref, two_ref, mix_ref, out_ref):
    narrow = out_ref.shape[1] // 2
    out_ref[:, :narrow] = narrowed(rows_ref[...], two_ref, column_ref[...])
    out_ref[:, narrow:] = narrowed(rows_ref[...], mix_ref, column_ref[...])


def last_kernel(rows_ref, column_ref, own_out, mid_out, own_ref, two_ref, mix_ref, late_ref, swap_ref, keep_ref, send_ref, labels_ref, all_ref):
    narrow = own_out.shape[1]
    width = rows_ref.shape[1]
    place = lax.rem(lax.axis_index("blk"), 4)
    odd = lax.rem(place, 2) == 1
    mix_term, mix_labels = mid_out[:, narrow:], mix_ref[width:width + 1, :]
    swap_term = narrowed(rows_ref[...], swap_ref, column_ref[...])
    swap_labels = swap_ref[width:width + 1, :]
    all_ref[...] = jnp.concatenate(
        [own_out[...], jnp.where(odd, mix_term, swap_term), mid_out[:, :narrow], jnp.where(odd, swap_term, mix_term)], axis=1)
    labels_ref[...] = jnp.concatenate(
        [own_ref[width:width + 1, :], jnp.where(odd, mix_labels, swap_labels), two_ref[width:width + 1, :],
         jnp.where(odd, swap_labels, mix_labels)] * 2, axis=0)

    @pl.when(place == 2)
    def _():
        all_ref[:, 3 * narrow:] = narrowed(rows_ref[...], late_ref, column_ref[...])
        labels_ref[3:4, :] = late_ref[width:width + 1, :]

    parts = send_ref.shape[0] + 1
    mine = lax.axis_index("red")
    count = keep_ref.shape[0]
    keep_ref[...] = all_ref[pl.ds(pl.multiple_of(mine * count, count), count), :]
    for step in range(1, parts):
        peer = lax.rem(mine + step, parts)
        send_ref[step - 1] = all_ref[pl.ds(pl.multiple_of(peer * count, count), count), :]


def finish_kernel(parts, keep_ref, *refs):
    taken, (labels_ref, column_ref, out_ref) = refs[:parts - 1], refs[parts - 1:]
    total = keep_ref[...]
    for ref in taken:
        total = total + ref[...]
    count = total.shape[0]
    narrow = total.shape[1] // 4
    mine = lax.axis_index("red")
    own = column_ref[pl.ds(pl.multiple_of(mine * count, count), count), :]
    for m in range(4):
        wide = jnp.concatenate([total[:, m * narrow:(m + 1) * narrow]] * (out_ref.shape[2] // narrow), axis=1)
        out_ref[m] = jnp.where(own[:, :1] == labels_ref[m:m + 1, :], wide, 0.0)


def whole(*shape):
    return jax.ShapeDtypeStruct(shape, F32)


def call(kernel, out_shape, args, flops, off=0, scratch=()):
    moved = sum(a.size * 4 for a in list(args) + out_shape)
    args = [pltpu.with_memory_space_constraint(a, pltpu.HBM) for a in args[:off]] + list(args[off:])
    return pl.pallas_call(
        kernel,
        out_shape=out_shape,
        in_specs=[OFFCHIP] * off + [ONCHIP] * (len(args) - off),
        out_specs=[ONCHIP] * len(out_shape),
        scratch_shapes=list(scratch),
        cost_estimate=pl.CostEstimate(flops=flops, bytes_accessed=moved, transcendentals=0),
        compiler_params=pltpu.CompilerParams(vmem_limit_bytes=32 * 1024 * 1024),
    )(*args)


def body(amplitudes, integrals, cd_irrep, ab_irrep, ij_irrep):
    blocks, parts = lax.axis_size("blk"), lax.axis_size("red")
    pairs, depth = amplitudes.shape
    row_count = integrals.shape[0]
    width, narrow = depth // 4, pairs // 4
    count = row_count // parts
    one_product = 12 * row_count * width * pairs

    def moved(array, steps):
        return lax.ppermute(array, "blk", [(i, (i + steps[i % 4]) % blocks) for i in range(blocks)])

    def staging(array, labels):
        return [
            pltpu.VMEM(array.shape, F32),
            pltpu.VMEM(labels.shape, jnp.int32),
            pltpu.VMEM(cd_irrep.shape, jnp.int32),
            pltpu.SemaphoreType.DMA((2 + array.shape[0] // LANES,)),
        ]

    own, = call(pack_kernel, [whole(width + 8, pairs)], (amplitudes, ij_irrep, cd_irrep),
                4 * amplitudes.size, 3, staging(amplitudes, ij_irrep))
    two = moved(own, (2, 2, 2, 2))
    mix = moved(own, (1, 3, 1, -1))
    rows, column_labels, own_term = call(
        first_kernel, [whole(row_count, width), whole(row_count, LANES), whole(row_count, narrow)],
        (integrals, ab_irrep, cd_irrep, own), 4 * integrals.size + one_product, 3, staging(integrals, ab_irrep))
    own_late, rows = lax.optimization_barrier((own, rows))
    late = moved(own_late, (1, -1, 1, 3))
    swap = moved(two, (1, -1, 1, -1))
    mid_term, = call(middle_kernel, [whole(row_count, 2 * narrow)], (rows, column_labels, two, mix), 2 * one_product)
    keep, send, labels = call(
        last_kernel,
        [whole(count, 4 * narrow), whole(parts - 1, count, 4 * narrow), whole(8, pairs)],
        (rows, column_labels, own_term, mid_term, own, two, mix, late, swap),
        2 * one_product, 0, [pltpu.VMEM((row_count, 4 * narrow), F32)])
    taken = [
        lax.ppermute(send[step - 1], "red", [(i, (i + step) % parts) for i in range(parts)])
        for step in range(1, parts)
    ]
    out, = call(functools.partial(finish_kernel, parts), [whole(4, count, pairs)],
                (keep, *taken, labels, column_labels), 4 * 2 * count * pairs)
    return out


def solution(mesh):
    in_specs = (P("blk", "red"), P("blk", "red"), P("red", None), P("blk", None), P("blk", None))
    out_specs = P(None, ("blk", "red"), None)
    return jax.shard_map(body, mesh=mesh, in_specs=in_specs, out_specs=out_specs, check_vma=False)
```

time: 24.3 us -> 21.6 us (0.89)
  waiting for transfers between devices: 13.8 us -> 9.41 us
  Pallas kernels: 3 us -> 5.71 us
  local copies, waits for them, and re-layouts: 2.5 us -> 0 us
  starting transfers between devices: 4.8 us -> 6.32 us
    ppermute x3 -> x4, waiting for transfers between devices: 10 us -> 5.39 us  [moved(): lax.ppermute(array, 'blk', [(i, (i + steps[i % 4]) % blocks) for i in ran...]
    pallas_call x4 -> x5, Pallas kernels: 3 us -> 5.71 us  [call(): pl.pallas_call(kernel, out_shape=out_shape, in_specs=[OFFCHIP] * off + [O...]
    unnamed x10 -> x0, local copies, waits for them, and re-layouts: 2.5 us -> none
    ppermute x3 -> x4, starting transfers between devices: 3 us -> 4.73 us  [moved(): lax.ppermute(array, 'blk', [(i, (i + steps[i % 4]) % blocks) for i in ran...]
  transfers between devices with their start and end apart: 4 -> 5, of which waited for: 3 -> 3; matrix products, arithmetic and copies ran while one was open for 0% -> 0% of each run, Pallas kernels for 1% -> 13%
where the time goes in v2:
time: 21.6 us; the launch traced here: 21.5 us
  waiting for transfers between devices  9.41 us (44%)
  starting transfers between devices  6.32 us (29%)
  Pallas kernels  5.71 us (26%)
    pallas_call x5, Pallas kernels, call(): pl.pallas_call(kernel, out_shape=out_shape, in_specs=[OFFCHIP] * off + [O...  5.71 us
    ppermute x4, waiting for transfers between devices, moved(): lax.ppermute(array, 'blk', [(i, (i + steps[i % 4]) % blocks) for i in ran...  5.39 us
    ppermute x4, starting transfers between devices, moved(): lax.ppermute(array, 'blk', [(i, (i + steps[i % 4]) % blocks) for i in ran...  4.73 us
    ppermute x1, waiting for transfers between devices, body(): lax.ppermute(send[step - 1], 'red', [(i, (i + step) % parts) for i in ran...  4.02 us
    ppermute x1, starting transfers between devices, body(): lax.ppermute(send[step - 1], 'red', [(i, (i + step) % parts) for i in ran...  1.58 us
  transfers between devices with their start and end apart: 5, of which 3 were waited for; matrix products, arithmetic and copies ran while one was open for 0% of the time, Pallas kernels for 13%

profile of v2, /device:TPU:0, one launch (start us, length us, event | category | flops | bytes accessed | tf_op | source)
XLA Modules:
  0.0 21.5 jit_solution(7438483156899812533)
XLA Ops:
  0.0 1.6 %shard_map.55.own_ref = f32[200,256]{1,0:T(8,128)S(1)} custom-call(f32[256,768]{1,0:T(8,128)} %amp_ref.1, s32[1,256]{1,0:T(1,128)} %ij_ref.1, s32[1,768]{1,0:T(1,128)} %cd_ref.3), custom_call_target="tpu_custom_call" | custom-call | flops 786432 | bytes 995328 | tf_op jit(solution)/shard_map/pallas_call | solution.py:130
  1.6 3.0 %collective-permute-start = (f32[200,256]{1,0:T(8,128)S(1)}, f32[200,256]{1,0:T(8,128)S(1)}, u32[]{:S(2)}, u32[]{:S(2)}) collective-permute-start(f32[200,256]{1,0:T(8,128)S(1)} %shard_map.55.own_ref), channel_id=1, source_target_pairs={{0,4},{2,6},{4,8},{6,10},{8,12},{10,14},{12,16},{14,18},{16,20},{1... | collective-permute-start | bytes 614408 | tf_op jit(solution)/shard_map/ppermute | solution.py:150
  4.6 0.0 collective-permute-start.1
  4.6 1.9 %shard_map.56 = (f32[256,192]{1,0:T(8,128)S(1)}, f32[256,128]{1,0:T(8,128)S(1)}, f32[256,64]{1,0:T(8,128)S(1)}) custom-call(f32[256,768]{1,0:T(8,128)} %v_ref.1, s32[1,256]{1,0:T(1,128)} %ab_ref.1, s32[1,768]{1,0:T(1,128)} %cd_ref.3, f32[200,256]{1,0:T(8,128)S(1)} %shard_map.55.own_ref), custom_call_target="tpu_custom_call" | custom-call | flops 151781376 | bytes 1388544 | tf_op jit(solution)/shard_map/pallas_call | solution.py:130
  6.5 1.7 %collective-permute-start.2 = (f32[200,256]{1,0:T(8,128)S(1)}, f32[200,256]{1,0:T(8,128)S(1)}, u32[]{:S(2)}, u32[]{:S(2)}) collective-permute-start(f32[200,256]{1,0:T(8,128)S(1)} %shard_map.55.own_ref), channel_id=1, source_target_pairs={{0,2},{2,0},{4,6},{6,12},{8,10},{10,8},{12,14},{14,20},{16,18},{18... | collective-permute-start | bytes 614408 | tf_op jit(solution)/shard_map/ppermute | solution.py:150
  8.3 4.8 %collective-permute-done.two_ref = f32[200,256]{1,0:T(8,128)S(1)} collective-permute-done((f32[200,256]{1,0:T(8,128)S(1)}, f32[200,256]{1,0:T(8,128)S(1)}, u32[]{:S(2)}, u32[]{:S(2)}) %collective-permute-start) | collective-permute-done | bytes 204832 | tf_op jit(solution)/shard_map/ppermute | solution.py:150
  13.0 0.0 collective-permute-start.3
  13.0 0.0 collective-permute-done.1.mix_ref
  13.0 0.8 %shard_map.57.mid_out = f32[256,128]{1,0:T(8,128)S(1)} custom-call(f32[256,192]{1,0:T(8,128)S(1)} %get-tuple-element.14.rows_ref, f32[256,128]{1,0:T(8,128)S(1)} %get-tuple-element.15.column_ref.refs_2_, f32[200,256]{1,0:T(8,128)S(1)} %collective-permute-done.two_ref, f32[200,256]{1,0:T(8,128)S(1)} %collective-permute-done.1.mix_ref), custom_call_target="tpu_custom_call" | custom-call | flops 301989888 | bytes 868352 | tf_op jit(solution)/shard_map/pallas_call | solution.py:130
  13.8 0.0 collective-permute-done.2.late_ref
  13.8 0.6 %collective-permute-done.3.swap_ref = f32[200,256]{1,0:T(8,128)S(1)} collective-permute-done((f32[200,256]{1,0:T(8,128)S(1)}, f32[200,256]{1,0:T(8,128)S(1)}, u32[]{:S(2)}, u32[]{:S(2)}) %collective-permute-start.3) | collective-permute-done | bytes 204832 | tf_op jit(solution)/shard_map/ppermute | solution.py:150
  14.5 0.5 %shard_map.58 = (f32[128,256]{1,0:T(8,128)S(1)}, f32[1,128,256]{2,1,0:T(8,128)S(1)}, f32[8,256]{1,0:T(8,128)S(1)}) custom-call(f32[256,192]{1,0:T(8,128)S(1)} %get-tuple-element.14.rows_ref, f32[256,128]{1,0:T(8,128)S(1)} %get-tuple-element.15.column_ref.refs_2_, f32[256,64]{1,0:T(8,128)S(1)} %get-tuple-element.16.own_out, ...), custom_call_target="tpu_custom_call" | custom-call | flops 301989888 | bytes 1818624 | tf_op jit(solution)/shard_map/pallas_call | solution.py:130
  14.9 1.6 %collective-permute-start.4 = (f32[128,256]{1,0:T(8,128)S(1)}, f32[128,256]{1,0:T(8,128)S(1)}, u32[]{:S(2)}, u32[]{:S(2)}) collective-permute-start(f32[128,256]{1,0:T(8,128)S(1)} %bitcast.1), channel_id=1, source_target_pairs={{0,1},{1,0},{2,3},{3,2},{4,5},{5,4},{6,7},{7,6},{8,9},{9,8},{10,11... | collective-permute-start | bytes 393224 | tf_op jit(solution)/shard_map/ppermute | solution.py:177
  16.5 4.0 %collective-permute-done.4.refs_0_ = f32[128,256]{1,0:T(8,128)S(1)} collective-permute-done((f32[128,256]{1,0:T(8,128)S(1)}, f32[128,256]{1,0:T(8,128)S(1)}, u32[]{:S(2)}, u32[]{:S(2)}) %collective-permute-start.4) | collective-permute-done | bytes 131104 | tf_op jit(solution)/shard_map/ppermute | solution.py:177
  20.6 0.9 %shard_map.59 = f32[4,128,256]{2,1,0:T(8,128)} custom-call(f32[128,256]{1,0:T(8,128)S(1)} %get-tuple-element.18.keep_ref, f32[128,256]{1,0:T(8,128)S(1)} %collective-permute-done.4.refs_0_, f32[8,256]{1,0:T(8,128)S(1)} %get-tuple-element.20.refs_1_, f32[256,128]{1,0:T(8,128)S(1)} %get-tuple-element.15.column_ref.refs_2_), custom_call_target="tpu_custom_call" | custom-call | flops 262144 | bytes 925696 | tf_op jit(solution)/shard_map/pallas_call | solution.py:130
Async XLA Ops:
  1.6 11.4 %collective-permute-start = (f32[200,256]{1,0:T(8,128)S(1)}, f32[200,256]{1,0:T(8,128)S(1)}, u32[]{:S(2)}, u32[]{:S(2)}) collective-permute-start(f32[200,256]{1,0:T(8,128)S(1)} %shard_map.55.own_ref), channel_id=1, source_target_pairs={{0,4},{2,6},{4,8},{6,10},{8,12},{10,14},{12,16},{14,18},{16,20},{1... | collective-permute-start | bytes 614408 | tf_op jit(solution)/shard_map/ppermute | solution.py:150
  4.6 8.4 %collective-permute-start.1 = (f32[200,256]{1,0:T(8,128)S(1)}, f32[200,256]{1,0:T(8,128)S(1)}, u32[]{:S(2)}, u32[]{:S(2)}) collective-permute-start(f32[200,256]{1,0:T(8,128)S(1)} %shard_map.55.own_ref), channel_id=1, source_target_pairs={{0,2},{2,8},{4,6},{6,4},{8,10},{10,16},{12,14},{14,12},{16,18},{18... | collective-permute-start | bytes 614408 | tf_op jit(solution)/shard_map/ppermute | solution.py:150
  6.5 7.3 %collective-permute-start.2 = (f32[200,256]{1,0:T(8,128)S(1)}, f32[200,256]{1,0:T(8,128)S(1)}, u32[]{:S(2)}, u32[]{:S(2)}) collective-permute-start(f32[200,256]{1,0:T(8,128)S(1)} %shard_map.55.own_ref), channel_id=1, source_target_pairs={{0,2},{2,0},{4,6},{6,12},{8,10},{10,8},{12,14},{14,20},{16,18},{18... | collective-permute-start | bytes 614408 | tf_op jit(solution)/shard_map/ppermute | solution.py:150
  13.0 1.5 %collective-permute-start.3 = (f32[200,256]{1,0:T(8,128)S(1)}, f32[200,256]{1,0:T(8,128)S(1)}, u32[]{:S(2)}, u32[]{:S(2)}) collective-permute-start(f32[200,256]{1,0:T(8,128)S(1)} %collective-permute-done.two_ref), channel_id=1, source_target_pairs={{0,2},{2,0},{4,6},{6,4},{8,10},{10,8},{12,14},{14,12},{16,18},{18,... | collective-permute-start | bytes 614408 | tf_op jit(solution)/shard_map/ppermute | solution.py:150
  14.9 5.6 %collective-permute-start.4 = (f32[128,256]{1,0:T(8,128)S(1)}, f32[128,256]{1,0:T(8,128)S(1)}, u32[]{:S(2)}, u32[]{:S(2)}) collective-permute-start(f32[128,256]{1,0:T(8,128)S(1)} %bitcast.1), channel_id=1, source_target_pairs={{0,1},{1,0},{2,3},{3,2},{4,5},{5,4},{6,7},{7,6},{8,9},{9,8},{10,11... | collective-permute-start | bytes 393224 | tf_op jit(solution)/shard_map/ppermute | solution.py:177

commit v3 on v2

v3 whole, which is shorter than its diff:
```python
import functools
import jax
import jax.numpy as jnp
from jax import lax
from jax.experimental import pallas as pl
from jax.experimental.pallas import tpu as pltpu
from jax.sharding import PartitionSpec as P

LANES = 128
F32 = jnp.float32
ONCHIP = pl.BlockSpec(memory_space=pltpu.VMEM)
OFFCHIP = pl.BlockSpec(memory_space=pltpu.HBM)


def column(labels):
    return jnp.broadcast_to(labels.astype(F32), (LANES, labels.shape[1])).T


def fold(rows, row_labels, cd_labels, width):
    total = None
    for start in range(0, rows.shape[1], width):
        part = slice(start, start + width)
        kept = jnp.where(row_labels[:, :1] == cd_labels[:, part], rows[:, part], 0.0)
        total = kept if total is None else total + kept
    return total


def fetch(pairs, sems):
    copies = [pltpu.make_async_copy(src, dst, sems.at[i]) for i, (src, dst) in enumerate(pairs)]
    for copy in copies:
        copy.start()
    return copies


def chunks(count):
    return [pl.ds(start, LANES) for start in range(0, count, LANES)]


def pack_kernel(amp_ref, ij_ref, cd_ref, out_ref, amp, ij, cd, sems):
    pairs, width = amp.shape[0], out_ref.shape[0] - 8
    parts = chunks(pairs)
    copies = fetch([(ij_ref, ij), (cd_ref, cd)] + [(amp_ref.at[c], amp.at[c]) for c in parts], sems)
    copies[0].wait()
    copies[1].wait()
    rows = column(ij[...])
    labels = cd[...].astype(F32)
    out_ref[width:, :] = jnp.broadcast_to(ij[...].astype(F32), (8, pairs))
    for copy, c in zip(copies[2:], parts):
        copy.wait()
        out_ref[:width, c] = fold(amp[c, :], rows[c.start:c.start + LANES], labels, width).T


def narrowed(rows, slab_ref, row_labels):
    width = rows.shape[1]
    full = jnp.dot(rows, slab_ref[:width, :], precision=lax.Precision.HIGHEST, preferred_element_type=F32)
    full = jnp.where(row_labels[:, :1] == slab_ref[width:width + 1, :], full, 0.0)
    narrow = full.shape[1] // 4
    return sum(full[:, k * narrow:(k + 1) * narrow] for k in range(1, 4)) + full[:, :narrow]


def halved(term):
    half = term.shape[0] // 2
    return jnp.concatenate([term[:half], term[half:]], axis=1)


def unhalved(term):
    half = term.shape[1] // 2
    return jnp.concatenate([term[:, :half], term[:, half:]], axis=0)


def first_kernel(v_ref, ab_ref, cd_ref, own_ref, rows_ref, column_ref, keep_ref, send_ref, v, ab, cd, labels, sems):
    width, count = rows_ref.shape[1], keep_ref.shape[0]
    parts = v.shape[0] // count
    mine = lax.axis_index("red")
    places = [pl.ds(pl.multiple_of(lax.rem(mine + k, parts) * count, count), count) for k in range(parts)]
    held = [pl.ds(k * count, count) for k in range(parts)]
    copies = fetch([(ab_ref, ab), (cd_ref, cd)] + [(v_ref.at[p], v.at[h]) for p, h in zip(places, held)], sems)
    copies[0].wait()
    copies[1].wait()
    labels[...] = column(ab[...])
    cd_labels = cd[...].astype(F32)
    for copy, p, h in zip(copies[2:], places, held):
        column_ref[h, :] = labels[p, :]
        copy.wait()
        rows_ref[h, :] = fold(v[h, :], column_ref[h, :], cd_labels, width)
    term = narrowed(rows_ref[...], own_ref, column_ref[...])
    keep_ref[...] = term[:count]
    for k in range(1, parts):
        send_ref[k - 1] = halved(term[k * count:(k + 1) * count])


def mix_kernel(rows_ref, column_ref, mix_ref, out_ref):
    out_ref[...] = narrowed(rows_ref[...], mix_ref, column_ref[...])


def two_kernel(rows_ref, column_ref, mix_term, two_ref, late_ref, keep_ref, send_ref, third):
    count, narrow = keep_ref.shape
    parts = send_ref.shape[0] + 1
    third[...] = mix_term[...]

    @pl.when(lax.rem(lax.axis_index("blk"), 4) == 2)
    def _():
        third[...] = narrowed(rows_ref[...], late_ref, column_ref[...])

    term = narrowed(rows_ref[count:, :], two_ref, column_ref[count:, :])
    keep_ref[...] = third[:count, :]
    for k in range(1, parts):
        send_ref[k - 1] = jnp.concatenate([term[(k - 1) * count:k * count], third[k * count:(k + 1) * count, :]], axis=1)


def swap_kernel(rows_ref, column_ref, swap_ref, send_ref):
    parts, count = send_ref.shape[0] + 1, 2 * send_ref.shape[1]
    term = narrowed(rows_ref[count:, :], swap_ref, column_ref[count:, :])
    for k in range(1, parts):
        send_ref[k - 1] = halved(term[(k - 1) * count:k * count])


def keep_kernel(rows_ref, column_ref, own_ref, two_ref, mix_ref, late_ref, swap_ref, two_out, swap_out, labels_ref):
    count = two_out.shape[0]
    width = rows_ref.shape[1]
    place = lax.rem(lax.axis_index("blk"), 4)
    two_out[...] = narrowed(rows_ref[:count, :], two_ref, column_ref[:count, :])
    swap_out[...] = narrowed(rows_ref[:count, :], swap_ref, column_ref[:count, :])
    own, two, mix, late, swap = [ref[width:width + 1, :] for ref in (own_ref, two_ref, mix_ref, late_ref, swap_ref)]
    third = jnp.where(place == 2, late, mix)
    odd = lax.rem(place, 2) == 1
    labels_ref[...] = jnp.concatenate([own, jnp.where(odd, third, swap), two, jnp.where(odd, swap, third)] * 2, axis=0)


def finish_kernel(parts, *refs):
    (own_keep, third_keep, two_keep, swap_keep), refs = refs[:4], refs[4:]
    own_in, pair_in, swap_in = [refs[i * (parts - 1):(i + 1) * (parts - 1)] for i in range(3)]
    labels_ref, column_ref, out_ref = refs[3 * (parts - 1):]
    count, narrow = own_keep.shape
    own = sum([unhalved(ref[...]) for ref in own_in], own_keep[...])
    two = sum([ref[:, :narrow] for ref in pair_in], two_keep[...])
    third = sum([ref[:, narrow:] for ref in pair_in], third_keep[...])
    swap = sum([unhalved(ref[...]) for ref in swap_in], swap_keep[...])
    odd = lax.rem(lax.axis_index("blk"), 2) == 1
    for m, term in enumerate([own, jnp.where(odd, third, swap), two, jnp.where(odd, swap, third)]):
        wide = jnp.concatenate([term] * (out_ref.shape[2] // narrow), axis=1)
        out_ref[m] = jnp.where(column_ref[:count, :1] == labels_ref[m:m + 1, :], wide, 0.0)


def whole(*shape):
    return jax.ShapeDtypeStruct(shape, F32)


def call(kernel, out_shape, args, flops, off=0, scratch=()):
    moved = sum(a.size * 4 for a in list(args) + out_shape)
    args = [pltpu.with_memory_space_constraint(a, pltpu.HBM) for a in args[:off]] + list(args[off:])
    return pl.pallas_call(
        kernel,
        out_shape=out_shape,
        in_specs=[OFFCHIP] * off + [ONCHIP] * (len(args) - off),
        out_specs=[ONCHIP] * len(out_shape),
        scratch_shapes=list(scratch),
        cost_estimate=pl.CostEstimate(flops=flops, bytes_accessed=moved, transcendentals=0),
        compiler_params=pltpu.CompilerParams(vmem_limit_bytes=32 * 1024 * 1024),
    )(*args)


def body(amplitudes, integrals, cd_irrep, ab_irrep, ij_irrep):
    blocks, parts = lax.axis_size("blk"), lax.axis_size("red")
    pairs, depth = amplitudes.shape
    row_count = integrals.shape[0]
    width, narrow = depth // 4, pairs // 4
    count = row_count // parts
    one_product = 12 * row_count * width * pairs

    def moved(array, steps):
        return lax.ppermute(array, "blk", [(i, (i + steps[i % 4]) % blocks) for i in range(blocks)])

    def exchanged(array):
        return [
            lax.ppermute(array[k - 1], "red", [(i, (i + k) % parts) for i in range(parts)])
            for k in range(1, parts)
        ]

    def after(array, *earlier):
        return lax.optimization_barrier((array, *earlier))[0]

    def staging(array, labels, copies):
        return [
            pltpu.VMEM(array.shape, F32),
            pltpu.VMEM(labels.shape, jnp.int32),
            pltpu.VMEM(cd_irrep.shape, jnp.int32),
        ], pltpu.SemaphoreType.DMA((2 + copies,))

    stage, sems = staging(amplitudes, ij_irrep, pairs // LANES)
    own, = call(pack_kernel, [whole(width + 8, pairs)], (amplitudes, ij_irrep, cd_irrep),
                4 * amplitudes.size, 3, stage + [sems])
    two = moved(own, (2, 2, 2, 2))
    mix = moved(own, (1, 3, 1, -1))
    stage, sems = staging(integrals, ab_irrep, parts)
    rows, labels, own_keep, own_send = call(
        first_kernel,
        [whole(row_count, width), whole(row_count, LANES), whole(count, narrow), whole(parts - 1, count // 2, 2 * narrow)],
        (integrals, ab_irrep, cd_irrep, own), 32 * one_product, 3,
        stage + [pltpu.VMEM((row_count, LANES), F32), sems])
    own_in = exchanged(own_send)
    mix_term, = call(mix_kernel, [whole(row_count, narrow)], (rows, labels, mix), one_product)
    late = moved(after(own, mix_term, *own_in), (1, -1, 1, 3))
    swap = moved(two, (1, -1, 1, -1))
    third_keep, pair_send = call(
        two_kernel, [whole(count, narrow), whole(parts - 1, count, 2 * narrow)],
        (rows, labels, mix_term, two, late), one_product, 0, [pltpu.VMEM((row_count, narrow), F32)])
    pair_in = exchanged(pair_send)
    swap_send, = call(swap_kernel, [whole(parts - 1, count // 2, 2 * narrow)],
                      (rows, labels, after(swap, pair_send)), one_product // 2)
    swap_in = exchanged(swap_send)
    two_keep, swap_keep, slab_labels = call(
        keep_kernel, [whole(count, narrow), whole(count, narrow), whole(8, pairs)],
        (rows, labels, own, two, mix, late, after(swap, swap_send)), one_product)
    out, = call(functools.partial(finish_kernel, parts), [whole(4, count, pairs)],
                (own_keep, third_keep, two_keep, swap_keep, *own_in, *pair_in, *swap_in, slab_labels, labels),
                4 * 2 * count * pairs)
    return out


def solution(mesh):
    in_specs = (P("blk", "red"), P("blk", "red"), P("red", None), P("blk", None), P("blk", None))
    out_specs = P(None, ("blk", "red"), None)
    return jax.shard_map(body, mesh=mesh, in_specs=in_specs, out_specs=out_specs, check_vma=False)
```

time: 21.6 us -> 24.2 us (1.12)
  the two profiles are of different devices: /device:TPU:0 before, /device:TPU:2 now
where the time goes in v3:
time: 24.2 us; the launch traced here: 24 us
  waiting for transfers between devices  10 us (41%)
  starting transfers between devices  7.03 us (29%)
  Pallas kernels  6.92 us (29%)
    pallas_call x7, Pallas kernels, call(): pl.pallas_call(kernel, out_shape=out_shape, in_specs=[OFFCHIP] * off + [O...  6.92 us
    ppermute x4, waiting for transfers between devices, moved(): lax.ppermute(array, 'blk', [(i, (i + steps[i % 4]) % blocks) for i in ran...  5.3 us
    ppermute x3, waiting for transfers between devices, exchanged(): lax.ppermute(array[k - 1], 'red', [(i, (i + k) % parts) for i in range(pa...  4.73 us
    ppermute x3, starting transfers between devices, exchanged(): lax.ppermute(array[k - 1], 'red', [(i, (i + k) % parts) for i in range(pa...  3.74 us
    ppermute x4, starting transfers between devices, moved(): lax.ppermute(array, 'blk', [(i, (i + steps[i % 4]) % blocks) for i in ran...  3.29 us
  transfers between devices with their start and end apart: 7, of which 3 were waited for; matrix products, arithmetic and copies ran while one was open for 0% of the time, Pallas kernels for 18%

profile of v3, /device:TPU:2, one launch (start us, length us, event | category | flops | bytes accessed | tf_op | source)
XLA Modules:
  0.0 24.0 jit_solution(13192093314134455066)
XLA Ops:
  0.0 1.6 %shard_map.55.own_ref = f32[200,256]{1,0:T(8,128)S(1)} custom-call(f32[256,768]{1,0:T(8,128)} %amp_ref.1, s32[1,256]{1,0:T(1,128)} %ij_ref.1, s32[1,768]{1,0:T(1,128)} %cd_ref.3), custom_call_target="tpu_custom_call" | custom-call | flops 786432 | bytes 995328 | tf_op jit(solution)/shard_map/pallas_call | solution.py:152
  1.6 1.6 %collective-permute-start.1 = (f32[200,256]{1,0:T(8,128)S(1)}, f32[200,256]{1,0:T(8,128)S(1)}, u32[]{:S(2)}, u32[]{:S(2)}) collective-permute-start(f32[200,256]{1,0:T(8,128)S(1)} %shard_map.55.own_ref), channel_id=1, source_target_pairs={{0,4},{2,6},{4,8},{6,10},{8,12},{10,14},{12,16},{14,18},{16,20},{1... | collective-permute-start | bytes 614408 | tf_op jit(solution)/shard_map/ppermute | solution.py:172
  3.2 0.0 collective-permute-start
  3.2 1.9 %shard_map.56 = (f32[256,192]{1,0:T(8,128)S(1)}, f32[256,128]{1,0:T(8,128)S(1)}, f32[128,64]{1,0:T(8,128)S(1)}, f32[1,64,128]{2,1,0:T(8,128)S(1)}) custom-call(f32[256,768]{1,0:T(8,128)} %v_ref.1, s32[1,256]{1,0:T(1,128)} %ab_ref.1, s32[1,768]{1,0:T(1,128)} %cd_ref.3, f32[200,256]{1,0:T(8,128)S(1)} %shard_map.55.own_ref), custom_call_target="tpu_custom_call" | custom-call | flops 4831838208 | bytes 1388544 | tf_op jit(solution)/shard_map/pallas_call | solution.py:152
  5.1 1.6 %collective-permute-start.2 = (f32[64,128]{1,0:T(8,128)S(1)}, f32[64,128]{1,0:T(8,128)S(1)}, u32[]{:S(2)}, u32[]{:S(2)}) collective-permute-start(f32[64,128]{1,0:T(8,128)S(1)} %bitcast.5), channel_id=1, source_target_pairs={{0,1},{1,0},{2,3},{3,2},{4,5},{5,4},{6,7},{7,6},{8,9},{9,8},{10,11... | collective-permute-start | bytes 98312 | tf_op jit(solution)/shard_map/ppermute | solution.py:176
  6.7 0.0 collective-permute-done.mix_ref
  6.7 0.5 %shard_map.57.mix_term = f32[256,64]{1,0:T(8,128)S(1)} custom-call(f32[256,192]{1,0:T(8,128)S(1)} %get-tuple-element.18.rows_ref, f32[256,128]{1,0:T(8,128)S(1)} %get-tuple-element.19.column_ref.refs_8_, f32[200,256]{1,0:T(8,128)S(1)} %collective-permute-done.mix_ref), custom_call_target="tpu_custom_call" | custom-call | flops 150994944 | bytes 598016 | tf_op jit(solution)/shard_map/pallas_call | solution.py:152
  7.2 1.9 %collective-permute-done.2.refs_4_ = f32[64,128]{1,0:T(8,128)S(1)} collective-permute-done((f32[64,128]{1,0:T(8,128)S(1)}, f32[64,128]{1,0:T(8,128)S(1)}, u32[]{:S(2)}, u32[]{:S(2)}) %collective-permute-start.2) | collective-permute-done | bytes 32800 | tf_op jit(solution)/shard_map/ppermute | solution.py:176
  9.1 0.0 collective-permute-start.3
  9.1 0.0 collective-permute-done.1.two_ref
  9.1 1.7 %collective-permute-start.4 = (f32[200,256]{1,0:T(8,128)S(1)}, f32[200,256]{1,0:T(8,128)S(1)}, u32[]{:S(2)}, u32[]{:S(2)}) collective-permute-start(f32[200,256]{1,0:T(8,128)S(1)} %collective-permute-done.1.two_ref), channel_id=1, source_target_pairs={{0,2},{2,0},{4,6},{6,4},{8,10},{10,8},{12,14},{14,12},{16,18},{18,... | collective-permute-start | bytes 614408 | tf_op jit(solution)/shard_map/ppermute | solution.py:172
  10.8 5.3 %collective-permute-done.3.late_ref = f32[200,256]{1,0:T(8,128)S(1)} collective-permute-done((f32[200,256]{1,0:T(8,128)S(1)}, f32[200,256]{1,0:T(8,128)S(1)}, u32[]{:S(2)}, u32[]{:S(2)}) %collective-permute-start.3) | collective-permute-done | bytes 204832 | tf_op jit(solution)/shard_map/ppermute | solution.py:172
  16.1 0.9 %shard_map.58 = (f32[128,64]{1,0:T(8,128)S(1)}, f32[1,128,128]{2,1,0:T(8,128)S(1)}) custom-call(f32[256,192]{1,0:T(8,128)S(1)} %get-tuple-element.18.rows_ref, f32[256,128]{1,0:T(8,128)S(1)} %get-tuple-element.19.column_ref.refs_8_, f32[256,64]{1,0:T(8,128)S(1)} %shard_map.57.mix_term, f32[200,256]{1,0:T(8,128)S(1)} %collective-permute-done.1.two_ref, ...), custom_call_target="tpu_custom_call" | custom-call | flops 150994944 | bytes 901120 | tf_op jit(solution)/shard_map/pallas_call | solution.py:152
  17.0 1.6 %collective-permute-start.5 = (f32[128,128]{1,0:T(8,128)S(1)}, f32[128,128]{1,0:T(8,128)S(1)}, u32[]{:S(2)}, u32[]{:S(2)}) collective-permute-start(f32[128,128]{1,0:T(8,128)S(1)} %bitcast.4), channel_id=1, source_target_pairs={{0,1},{1,0},{2,3},{3,2},{4,5},{5,4},{6,7},{7,6},{8,9},{9,8},{10,11... | collective-permute-start | bytes 196616 | tf_op jit(solution)/shard_map/ppermute | solution.py:176
  18.6 0.0 collective-permute-done.4.swap_ref
  18.6 0.4 %shard_map.59 = f32[1,64,128]{2,1,0:T(8,128)S(1)} custom-call(f32[256,192]{1,0:T(8,128)S(1)} %get-tuple-element.18.rows_ref, f32[256,128]{1,0:T(8,128)S(1)} %get-tuple-element.19.column_ref.refs_8_, f32[200,256]{1,0:T(8,128)S(1)} %collective-permute-done.4.swap_ref), custom_call_target="tpu_custom_call" | custom-call | flops 75497472 | bytes 565248 | tf_op jit(solution)/shard_map/pallas_call | solution.py:152
  19.0 0.6 %collective-permute-start.6 = (f32[64,128]{1,0:T(8,128)S(1)}, f32[64,128]{1,0:T(8,128)S(1)}, u32[]{:S(2)}, u32[]{:S(2)}) collective-permute-start(f32[64,128]{1,0:T(8,128)S(1)} %bitcast.3), channel_id=1, source_target_pairs={{0,1},{1,0},{2,3},{3,2},{4,5},{5,4},{6,7},{7,6},{8,9},{9,8},{10,11... | collective-permute-start | bytes 98312 | tf_op jit(solution)/shard_map/ppermute | solution.py:176
  19.6 0.6 %shard_map.60 = (f32[128,64]{1,0:T(8,128)S(1)}, f32[128,64]{1,0:T(8,128)S(1)}, f32[8,256]{1,0:T(8,128)S(1)}) custom-call(f32[256,192]{1,0:T(8,128)S(1)} %get-tuple-element.18.rows_ref, f32[256,128]{1,0:T(8,128)S(1)} %get-tuple-element.19.column_ref.refs_8_, f32[200,256]{1,0:T(8,128)S(1)} %shard_map.55.own_ref, ...), custom_call_target="tpu_custom_call" | custom-call | flops 150994944 | bytes 1425408 | tf_op jit(solution)/shard_map/pallas_call | solution.py:152
  20.1 2.8 %collective-permute-done.6.refs_6_ = f32[64,128]{1,0:T(8,128)S(1)} collective-permute-done((f32[64,128]{1,0:T(8,128)S(1)}, f32[64,128]{1,0:T(8,128)S(1)}, u32[]{:S(2)}, u32[]{:S(2)}) %collective-permute-start.6) | collective-permute-done | bytes 32800 | tf_op jit(solution)/shard_map/ppermute | solution.py:176
  23.0 0.0 collective-permute-done.5.refs_5_
  23.0 1.0 %shard_map.61 = f32[4,128,256]{2,1,0:T(8,128)} custom-call(f32[128,64]{1,0:T(8,128)S(1)} %get-tuple-element.17.refs_0_, f32[128,64]{1,0:T(8,128)S(1)} %get-tuple-element.22.refs_1_, f32[128,64]{1,0:T(8,128)S(1)} %get-tuple-element.26.refs_2_, f32[128,64]{1,0:T(8,128)S(1)} %get-tuple-element.27.refs_3_, f32[64,128]{1,0:T(8,128)S(1)} %collective-permute-done.2.refs_4_, ...), custom_call_target="tpu_custom_call" | custom-call | flops 262144 | bytes 925696 | tf_op jit(solution)/shard_map/pallas_call | solution.py:152
Async XLA Ops:
  1.6 7.5 %collective-permute-start.1 = (f32[200,256]{1,0:T(8,128)S(1)}, f32[200,256]{1,0:T(8,128)S(1)}, u32[]{:S(2)}, u32[]{:S(2)}) collective-permute-start(f32[200,256]{1,0:T(8,128)S(1)} %shard_map.55.own_ref), channel_id=1, source_target_pairs={{0,4},{2,6},{4,8},{6,10},{8,12},{10,14},{12,16},{14,18},{16,20},{1... | collective-permute-start | bytes 614408 | tf_op jit(solution)/shard_map/ppermute | solution.py:172
  3.2 3.5 %collective-permute-start = (f32[200,256]{1,0:T(8,128)S(1)}, f32[200,256]{1,0:T(8,128)S(1)}, u32[]{:S(2)}, u32[]{:S(2)}) collective-permute-start(f32[200,256]{1,0:T(8,128)S(1)} %shard_map.55.own_ref), channel_id=1, source_target_pairs={{0,2},{2,8},{4,6},{6,4},{8,10},{10,16},{12,14},{14,12},{16,18},{18... | collective-permute-start | bytes 614408 | tf_op jit(solution)/shard_map/ppermute | solution.py:172
  5.1 4.0 %collective-permute-start.2 = (f32[64,128]{1,0:T(8,128)S(1)}, f32[64,128]{1,0:T(8,128)S(1)}, u32[]{:S(2)}, u32[]{:S(2)}) collective-permute-start(f32[64,128]{1,0:T(8,128)S(1)} %bitcast.5), channel_id=1, source_target_pairs={{0,1},{1,0},{2,3},{3,2},{4,5},{5,4},{6,7},{7,6},{8,9},{9,8},{10,11... | collective-permute-start | bytes 98312 | tf_op jit(solution)/shard_map/ppermute | solution.py:176
  9.1 7.0 %collective-permute-start.3 = (f32[200,256]{1,0:T(8,128)S(1)}, f32[200,256]{1,0:T(8,128)S(1)}, u32[]{:S(2)}, u32[]{:S(2)}) collective-permute-start(f32[200,256]{1,0:T(8,128)S(1)} %shard_map.55.own_ref), channel_id=1, source_target_pairs={{0,2},{2,0},{4,6},{6,12},{8,10},{10,8},{12,14},{14,20},{16,18},{18... | collective-permute-start | bytes 614408 | tf_op jit(solution)/shard_map/ppermute | solution.py:172
  9.1 9.5 %collective-permute-start.4 = (f32[200,256]{1,0:T(8,128)S(1)}, f32[200,256]{1,0:T(8,128)S(1)}, u32[]{:S(2)}, u32[]{:S(2)}) collective-permute-start(f32[200,256]{1,0:T(8,128)S(1)} %collective-permute-done.1.two_ref), channel_id=1, source_target_pairs={{0,2},{2,0},{4,6},{6,4},{8,10},{10,8},{12,14},{14,12},{16,18},{18,... | collective-permute-start | bytes 614408 | tf_op jit(solution)/shard_map/ppermute | solution.py:172
  17.0 6.0 %collective-permute-start.5 = (f32[128,128]{1,0:T(8,128)S(1)}, f32[128,128]{1,0:T(8,128)S(1)}, u32[]{:S(2)}, u32[]{:S(2)}) collective-permute-start(f32[128,128]{1,0:T(8,128)S(1)} %bitcast.4), channel_id=1, source_target_pairs={{0,1},{1,0},{2,3},{3,2},{4,5},{5,4},{6,7},{7,6},{8,9},{9,8},{10,11... | collective-permute-start | bytes 196616 | tf_op jit(solution)/shard_map/ppermute | solution.py:176
  19.0 4.0 %collective-permute-start.6 = (f32[64,128]{1,0:T(8,128)S(1)}, f32[64,128]{1,0:T(8,128)S(1)}, u32[]{:S(2)}, u32[]{:S(2)}) collective-permute-start(f32[64,128]{1,0:T(8,128)S(1)} %bitcast.3), channel_id=1, source_target_pairs={{0,1},{1,0},{2,3},{3,2},{4,5},{5,4},{6,7},{7,6},{8,9},{9,8},{10,11... | collective-permute-start | bytes 98312 | tf_op jit(solution)/shard_map/ppermute | solution.py:176

commit v4 on v3

--- a/solution.py
+++ b/solution.py
@@ -89,23 +89,13 @@
         send_ref[k - 1] = halved(term[k * count:(k + 1) * count])
 
 
-def mix_kernel(rows_ref, column_ref, mix_ref, out_ref):
-    out_ref[...] = narrowed(rows_ref[...], mix_ref, column_ref[...])
-
-
-def two_kernel(rows_ref, column_ref, mix_term, two_ref, late_ref, keep_ref, send_ref, third):
-    count, narrow = keep_ref.shape
-    parts = send_ref.shape[0] + 1
-    third[...] = mix_term[...]
-
-    @pl.when(lax.rem(lax.axis_index("blk"), 4) == 2)
-    def _():
-        third[...] = narrowed(rows_ref[...], late_ref, column_ref[...])
-
-    term = narrowed(rows_ref[count:, :], two_ref, column_ref[count:, :])
-    keep_ref[...] = third[:count, :]
-    for k in range(1, parts):
-        send_ref[k - 1] = jnp.concatenate([term[(k - 1) * count:k * count], third[k * count:(k + 1) * count, :]], axis=1)
+def pair_kernel(rows_ref, column_ref, two_ref, mix_ref, send_ref):
+    parts, count = send_ref.shape[0] + 1, send_ref.shape[1]
+    narrow = send_ref.shape[2] // 2
+    for place, ref in enumerate((two_ref, mix_ref)):
+        term = narrowed(rows_ref[count:, :], ref, column_ref[count:, :])
+        for k in range(1, parts):
+            send_ref[k - 1, :, place * narrow:(place + 1) * narrow] = term[(k - 1) * count:k * count]
 
 
 def swap_kernel(rows_ref, column_ref, swap_ref, send_ref):
@@ -115,29 +105,27 @@
         send_ref[k - 1] = halved(term[(k - 1) * count:k * count])
 
 
-def keep_kernel(rows_ref, column_ref, own_ref, two_ref, mix_ref, late_ref, swap_ref, two_out, swap_out, labels_ref):
+def keep_kernel(rows_ref, column_ref, own_ref, two_ref, mix_ref, swap_ref, two_out, mix_out, swap_out, labels_ref):
     count = two_out.shape[0]
     width = rows_ref.shape[1]
-    place = lax.rem(lax.axis_index("blk"), 4)
-    two_out[...] = narrowed(rows_ref[:count, :], two_ref, column_ref[:count, :])
-    swap_out[...] = narrowed(rows_ref[:count, :], swap_ref, column_ref[:count, :])
-    own, two, mix, late, swap = [ref[width:width + 1, :] for ref in (own_ref, two_ref, mix_ref, late_ref, swap_ref)]
-    third = jnp.where(place == 2, late, mix)
-    odd = lax.rem(place, 2) == 1
-    labels_ref[...] = jnp.concatenate([own, jnp.where(odd, third, swap), two, jnp.where(odd, swap, third)] * 2, axis=0)
+    for ref, out_ref in ((two_ref, two_out), (mix_ref, mix_out), (swap_ref, swap_out)):
+        out_ref[...] = narrowed(rows_ref[:count, :], ref, column_ref[:count, :])
+    own, two, mix, swap = [ref[width:width + 1, :] for ref in (own_ref, two_ref, mix_ref, swap_ref)]
+    odd = lax.rem(lax.axis_index("blk"), 2) == 1
+    labels_ref[...] = jnp.concatenate([own, jnp.where(odd, mix, swap), two, jnp.where(odd, swap, mix)] * 2, axis=0)
 
 
 def finish_kernel(parts, *refs):
-    (own_keep, third_keep, two_keep, swap_keep), refs = refs[:4], refs[4:]
+    (own_keep, mix_keep, two_keep, swap_keep), refs = refs[:4], refs[4:]
     own_in, pair_in, swap_in = [refs[i * (parts - 1):(i + 1) * (parts - 1)] for i in range(3)]
     labels_ref, column_ref, out_ref = refs[3 * (parts - 1):]
     count, narrow = own_keep.shape
     own = sum([unhalved(ref[...]) for ref in own_in], own_keep[...])
     two = sum([ref[:, :narrow] for ref in pair_in], two_keep[...])
-    third = sum([ref[:, narrow:] for ref in pair_in], third_keep[...])
+    mix = sum([ref[:, narrow:] for ref in pair_in], mix_keep[...])
     swap = sum([unhalved(ref[...]) for ref in swap_in], swap_keep[...])
     odd = lax.rem(lax.axis_index("blk"), 2) == 1
-    for m, term in enumerate([own, jnp.where(odd, third, swap), two, jnp.where(odd, swap, third)]):
+    for m, term in enumerate([own, jnp.where(odd, mix, swap), two, jnp.where(odd, swap, mix)]):
         wide = jnp.concatenate([term] * (out_ref.shape[2] // narrow), axis=1)
         out_ref[m] = jnp.where(column_ref[:count, :1] == labels_ref[m:m + 1, :], wide, 0.0)
 
@@ -191,7 +179,6 @@
     own, = call(pack_kernel, [whole(width + 8, pairs)], (amplitudes, ij_irrep, cd_irrep),
                 4 * amplitudes.size, 3, stage + [sems])
     two = moved(own, (2, 2, 2, 2))
-    mix = moved(own, (1, 3, 1, -1))
     stage, sems = staging(integrals, ab_irrep, parts)
     rows, labels, own_keep, own_send = call(
         first_kernel,
@@ -199,21 +186,18 @@
         (integrals, ab_irrep, cd_irrep, own), 32 * one_product, 3,
         stage + [pltpu.VMEM((row_count, LANES), F32), sems])
     own_in = exchanged(own_send)
-    mix_term, = call(mix_kernel, [whole(row_count, narrow)], (rows, labels, mix), one_product)
-    late = moved(after(own, mix_term, *own_in), (1, -1, 1, 3))
-    swap = moved(two, (1, -1, 1, -1))
-    third_keep, pair_send = call(
-        two_kernel, [whole(count, narrow), whole(parts - 1, count, 2 * narrow)],
-        (rows, labels, mix_term, two, late), one_product, 0, [pltpu.VMEM((row_count, narrow), F32)])
+    mix = moved(after(own, rows), (1, 3, 1, 3))
+    swap = moved(after(two, *own_in), (1, -1, 1, -1))
+    pair_send, = call(pair_kernel, [whole(parts - 1, count, 2 * narrow)], (rows, labels, two, mix), one_product)
     pair_in = exchanged(pair_send)
     swap_send, = call(swap_kernel, [whole(parts - 1, count // 2, 2 * narrow)],
                       (rows, labels, after(swap, pair_send)), one_product // 2)
     swap_in = exchanged(swap_send)
-    two_keep, swap_keep, slab_labels = call(
-        keep_kernel, [whole(count, narrow), whole(count, narrow), whole(8, pairs)],
-        (rows, labels, own, two, mix, late, after(swap, swap_send)), one_product)
+    two_keep, mix_keep, swap_keep, slab_labels = call(
+        keep_kernel, [whole(count, narrow)] * 3 + [whole(8, pairs)],
+        (rows, labels, own, two, mix, after(swap, swap_send)), one_product)
     out, = call(functools.partial(finish_kernel, parts), [whole(4, count, pairs)],
-                (own_keep, third_keep, two_keep, swap_keep, *own_in, *pair_in, *swap_in, slab_labels, labels),
+                (own_keep, mix_keep, two_keep, swap_keep, *own_in, *pair_in, *swap_in, slab_labels, labels),
                 4 * 2 * count * pairs)
     return out
 

time: 24.2 us -> 21.3 us (0.88)
  the two profiles are of different devices: /device:TPU:2 before, /device:TPU:0 now
where the time goes in v4:
time: 21.3 us; the launch traced here: 21.1 us
  waiting for transfers between devices  8.13 us (38%)
  starting transfers between devices  6.79 us (32%)
  Pallas kernels  6.15 us (29%)
    pallas_call x6, Pallas kernels, call(): pl.pallas_call(kernel, out_shape=out_shape, in_specs=[OFFCHIP] * off + [O...  6.15 us
    ppermute x3, waiting for transfers between devices, exchanged(): lax.ppermute(array[k - 1], 'red', [(i, (i + k) % parts) for i in range(pa...  5.14 us
    ppermute x3, starting transfers between devices, exchanged(): lax.ppermute(array[k - 1], 'red', [(i, (i + k) % parts) for i in range(pa...  3.74 us
    ppermute x3, starting transfers between devices, moved(): lax.ppermute(array, 'blk', [(i, (i + steps[i % 4]) % blocks) for i in ran...  3.05 us
    ppermute x3, waiting for transfers between devices, moved(): lax.ppermute(array, 'blk', [(i, (i + steps[i % 4]) % blocks) for i in ran...  2.99 us
  transfers between devices with their start and end apart: 6, of which 5 were waited for; matrix products, arithmetic and copies ran while one was open for 0% of the time, Pallas kernels for 17%

profile of v4, /device:TPU:0, one launch (start us, length us, event | category | flops | bytes accessed | tf_op | source)
XLA Modules:
  0.0 21.1 jit_solution(3611876141462133217)
XLA Ops:
  0.0 1.6 %shard_map.55.own_ref = f32[200,256]{1,0:T(8,128)S(1)} custom-call(f32[256,768]{1,0:T(8,128)} %amp_ref.1, s32[1,256]{1,0:T(1,128)} %ij_ref.1, s32[1,768]{1,0:T(1,128)} %cd_ref.3), custom_call_target="tpu_custom_call" | custom-call | flops 786432 | bytes 995328 | tf_op jit(solution)/shard_map/pallas_call | solution.py:140
  1.6 3.0 %collective-permute-start = (f32[200,256]{1,0:T(8,128)S(1)}, f32[200,256]{1,0:T(8,128)S(1)}, u32[]{:S(2)}, u32[]{:S(2)}) collective-permute-start(f32[200,256]{1,0:T(8,128)S(1)} %shard_map.55.own_ref), channel_id=1, source_target_pairs={{0,4},{2,6},{4,8},{6,10},{8,12},{10,14},{12,16},{14,18},{16,20},{1... | collective-permute-start | bytes 614408 | tf_op jit(solution)/shard_map/ppermute | solution.py:160
  4.6 1.9 %shard_map.56 = (f32[256,192]{1,0:T(8,128)S(1)}, f32[256,128]{1,0:T(8,128)S(1)}, f32[128,64]{1,0:T(8,128)S(1)}, f32[1,64,128]{2,1,0:T(8,128)S(1)}) custom-call(f32[256,768]{1,0:T(8,128)} %v_ref.1, s32[1,256]{1,0:T(1,128)} %ab_ref.1, s32[1,768]{1,0:T(1,128)} %cd_ref.3, f32[200,256]{1,0:T(8,128)S(1)} %shard_map.55.own_ref), custom_call_target="tpu_custom_call" | custom-call | flops 4831838208 | bytes 1388544 | tf_op jit(solution)/shard_map/pallas_call | solution.py:140
  6.5 0.1 collective-permute-start.1
  6.6 1.6 %collective-permute-start.2 = (f32[64,128]{1,0:T(8,128)S(1)}, f32[64,128]{1,0:T(8,128)S(1)}, u32[]{:S(2)}, u32[]{:S(2)}) collective-permute-start(f32[64,128]{1,0:T(8,128)S(1)} %bitcast.5), channel_id=1, source_target_pairs={{0,1},{1,0},{2,3},{3,2},{4,5},{5,4},{6,7},{7,6},{8,9},{9,8},{10,11... | collective-permute-start | bytes 98312 | tf_op jit(solution)/shard_map/ppermute | solution.py:164
  8.2 2.4 %collective-permute-done.2.refs_4_ = f32[64,128]{1,0:T(8,128)S(1)} collective-permute-done((f32[64,128]{1,0:T(8,128)S(1)}, f32[64,128]{1,0:T(8,128)S(1)}, u32[]{:S(2)}, u32[]{:S(2)}) %collective-permute-start.2) | collective-permute-done | bytes 32800 | tf_op jit(solution)/shard_map/ppermute | solution.py:164
  10.6 2.5 %collective-permute-done.two_ref = f32[200,256]{1,0:T(8,128)S(1)} collective-permute-done((f32[200,256]{1,0:T(8,128)S(1)}, f32[200,256]{1,0:T(8,128)S(1)}, u32[]{:S(2)}, u32[]{:S(2)}) %collective-permute-start) | collective-permute-done | bytes 204832 | tf_op jit(solution)/shard_map/ppermute | solution.py:160
  13.0 0.0 collective-permute-start.3
  13.0 0.5 %collective-permute-done.1.mix_ref = f32[200,256]{1,0:T(8,128)S(1)} collective-permute-done((f32[200,256]{1,0:T(8,128)S(1)}, f32[200,256]{1,0:T(8,128)S(1)}, u32[]{:S(2)}, u32[]{:S(2)}) %collective-permute-start.1) | collective-permute-done | bytes 204832 | tf_op jit(solution)/shard_map/ppermute | solution.py:160
  13.6 0.6 %shard_map.57 = f32[1,128,128]{2,1,0:T(8,128)S(1)} custom-call(f32[256,192]{1,0:T(8,128)S(1)} %get-tuple-element.18.rows_ref, f32[256,128]{1,0:T(8,128)S(1)} %get-tuple-element.19.column_ref.refs_8_, f32[200,256]{1,0:T(8,128)S(1)} %collective-permute-done.two_ref, f32[200,256]{1,0:T(8,128)S(1)} %collective-permute-done.1.mix_ref), custom_call_target="tpu_custom_call" | custom-call | flops 150994944 | bytes 802816 | tf_op jit(solution)/shard_map/pallas_call | solution.py:140
  14.1 1.6 %collective-permute-start.4 = (f32[128,128]{1,0:T(8,128)S(1)}, f32[128,128]{1,0:T(8,128)S(1)}, u32[]{:S(2)}, u32[]{:S(2)}) collective-permute-start(f32[128,128]{1,0:T(8,128)S(1)} %bitcast.3), channel_id=1, source_target_pairs={{0,1},{1,0},{2,3},{3,2},{4,5},{5,4},{6,7},{7,6},{8,9},{9,8},{10,11... | collective-permute-start | bytes 196616 | tf_op jit(solution)/shard_map/ppermute | solution.py:164
  15.7 0.0 collective-permute-done.3.swap_ref
  15.7 0.4 %shard_map.58 = f32[1,64,128]{2,1,0:T(8,128)S(1)} custom-call(f32[256,192]{1,0:T(8,128)S(1)} %get-tuple-element.18.rows_ref, f32[256,128]{1,0:T(8,128)S(1)} %get-tuple-element.19.column_ref.refs_8_, f32[200,256]{1,0:T(8,128)S(1)} %collective-permute-done.3.swap_ref), custom_call_target="tpu_custom_call" | custom-call | flops 75497472 | bytes 565248 | tf_op jit(solution)/shard_map/pallas_call | solution.py:140
  16.1 0.6 %collective-permute-start.5 = (f32[64,128]{1,0:T(8,128)S(1)}, f32[64,128]{1,0:T(8,128)S(1)}, u32[]{:S(2)}, u32[]{:S(2)}) collective-permute-start(f32[64,128]{1,0:T(8,128)S(1)} %bitcast.4), channel_id=1, source_target_pairs={{0,1},{1,0},{2,3},{3,2},{4,5},{5,4},{6,7},{7,6},{8,9},{9,8},{10,11... | collective-permute-start | bytes 98312 | tf_op jit(solution)/shard_map/ppermute | solution.py:164
  16.7 0.7 %shard_map.59 = (f32[128,64]{1,0:T(8,128)S(1)}, f32[128,64]{1,0:T(8,128)S(1)}, f32[128,64]{1,0:T(8,128)S(1)}, f32[8,256]{1,0:T(8,128)S(1)}) custom-call(f32[256,192]{1,0:T(8,128)S(1)} %get-tuple-element.18.rows_ref, f32[256,128]{1,0:T(8,128)S(1)} %get-tuple-element.19.column_ref.refs_8_, f32[200,256]{1,0:T(8,128)S(1)} %shard_map.55.own_ref, ...), custom_call_target="tpu_custom_call" | custom-call | flops 150994944 | bytes 1253376 | tf_op jit(solution)/shard_map/pallas_call | solution.py:140
  17.3 1.1 %collective-permute-done.4.refs_5_ = f32[128,128]{1,0:T(8,128)S(1)} collective-permute-done((f32[128,128]{1,0:T(8,128)S(1)}, f32[128,128]{1,0:T(8,128)S(1)}, u32[]{:S(2)}, u32[]{:S(2)}) %collective-permute-start.4) | collective-permute-done | bytes 65568 | tf_op jit(solution)/shard_map/ppermute | solution.py:164
  18.4 1.6 %collective-permute-done.5.refs_6_ = f32[64,128]{1,0:T(8,128)S(1)} collective-permute-done((f32[64,128]{1,0:T(8,128)S(1)}, f32[64,128]{1,0:T(8,128)S(1)}, u32[]{:S(2)}, u32[]{:S(2)}) %collective-permute-start.5) | collective-permute-done | bytes 32800 | tf_op jit(solution)/shard_map/ppermute | solution.py:164
  20.1 1.0 %shard_map.60 = f32[4,128,256]{2,1,0:T(8,128)} custom-call(f32[128,64]{1,0:T(8,128)S(1)} %get-tuple-element.17.refs_0_, f32[128,64]{1,0:T(8,128)S(1)} %get-tuple-element.25.refs_1_, f32[128,64]{1,0:T(8,128)S(1)} %get-tuple-element.26.refs_2_, f32[128,64]{1,0:T(8,128)S(1)} %get-tuple-element.27.refs_3_, f32[64,128]{1,0:T(8,128)S(1)} %collective-permute-done.2.refs_4_, ...), custom_call_target="tpu_custom_call" | custom-call | flops 262144 | bytes 925696 | tf_op jit(solution)/shard_map/pallas_call | solution.py:140
Async XLA Ops:
  1.6 11.4 %collective-permute-start = (f32[200,256]{1,0:T(8,128)S(1)}, f32[200,256]{1,0:T(8,128)S(1)}, u32[]{:S(2)}, u32[]{:S(2)}) collective-permute-start(f32[200,256]{1,0:T(8,128)S(1)} %shard_map.55.own_ref), channel_id=1, source_target_pairs={{0,4},{2,6},{4,8},{6,10},{8,12},{10,14},{12,16},{14,18},{16,20},{1... | collective-permute-start | bytes 614408 | tf_op jit(solution)/shard_map/ppermute | solution.py:160
  6.5 7.0 %collective-permute-start.1 = (f32[200,256]{1,0:T(8,128)S(1)}, f32[200,256]{1,0:T(8,128)S(1)}, u32[]{:S(2)}, u32[]{:S(2)}) collective-permute-start(f32[200,256]{1,0:T(8,128)S(1)} %shard_map.55.own_ref), channel_id=1, source_target_pairs={{0,2},{2,8},{4,6},{6,12},{8,10},{10,16},{12,14},{14,20},{16,18},{1... | collective-permute-start | bytes 614408 | tf_op jit(solution)/shard_map/ppermute | solution.py:160
  6.6 4.0 %collective-permute-start.2 = (f32[64,128]{1,0:T(8,128)S(1)}, f32[64,128]{1,0:T(8,128)S(1)}, u32[]{:S(2)}, u32[]{:S(2)}) collective-permute-start(f32[64,128]{1,0:T(8,128)S(1)} %bitcast.5), channel_id=1, source_target_pairs={{0,1},{1,0},{2,3},{3,2},{4,5},{5,4},{6,7},{7,6},{8,9},{9,8},{10,11... | collective-permute-start | bytes 98312 | tf_op jit(solution)/shard_map/ppermute | solution.py:164
  13.0 2.7 %collective-permute-start.3 = (f32[200,256]{1,0:T(8,128)S(1)}, f32[200,256]{1,0:T(8,128)S(1)}, u32[]{:S(2)}, u32[]{:S(2)}) collective-permute-start(f32[200,256]{1,0:T(8,128)S(1)} %collective-permute-done.two_ref), channel_id=1, source_target_pairs={{0,2},{2,0},{4,6},{6,4},{8,10},{10,8},{12,14},{14,12},{16,18},{18,... | collective-permute-start | bytes 614408 | tf_op jit(solution)/shard_map/ppermute | solution.py:160
  14.1 4.3 %collective-permute-start.4 = (f32[128,128]{1,0:T(8,128)S(1)}, f32[128,128]{1,0:T(8,128)S(1)}, u32[]{:S(2)}, u32[]{:S(2)}) collective-permute-start(f32[128,128]{1,0:T(8,128)S(1)} %bitcast.3), channel_id=1, source_target_pairs={{0,1},{1,0},{2,3},{3,2},{4,5},{5,4},{6,7},{7,6},{8,9},{9,8},{10,11... | collective-permute-start | bytes 196616 | tf_op jit(solution)/shard_map/ppermute | solution.py:164
  16.1 4.0 %collective-permute-start.5 = (f32[64,128]{1,0:T(8,128)S(1)}, f32[64,128]{1,0:T(8,128)S(1)}, u32[]{:S(2)}, u32[]{:S(2)}) collective-permute-start(f32[64,128]{1,0:T(8,128)S(1)} %bitcast.4), channel_id=1, source_target_pairs={{0,1},{1,0},{2,3},{3,2},{4,5},{5,4},{6,7},{7,6},{8,9},{9,8},{10,11... | collective-permute-start | bytes 98312 | tf_op jit(solution)/shard_map/ppermute | solution.py:164

commit v5 on v4

--- a/solution.py
+++ b/solution.py
@@ -98,11 +98,12 @@
             send_ref[k - 1, :, place * narrow:(place + 1) * narrow] = term[(k - 1) * count:k * count]
 
 
-def swap_kernel(rows_ref, column_ref, swap_ref, send_ref):
-    parts, count = send_ref.shape[0] + 1, 2 * send_ref.shape[1]
+def swap_kernel(rows_ref, column_ref, swap_ref, pair_ref, send_ref):
+    parts, count = pair_ref.shape[0] + 1, pair_ref.shape[1]
     term = narrowed(rows_ref[count:, :], swap_ref, column_ref[count:, :])
     for k in range(1, parts):
-        send_ref[k - 1] = halved(term[(k - 1) * count:k * count])
+        send_ref[k - 1, :count, :] = pair_ref[k - 1]
+        send_ref[k - 1, count:, :] = halved(term[(k - 1) * count:k * count])
 
 
 def keep_kernel(rows_ref, column_ref, own_ref, two_ref, mix_ref, swap_ref, two_out, mix_out, swap_out, labels_ref):
@@ -117,13 +118,13 @@
 
 def finish_kernel(parts, *refs):
     (own_keep, mix_keep, two_keep, swap_keep), refs = refs[:4], refs[4:]
-    own_in, pair_in, swap_in = [refs[i * (parts - 1):(i + 1) * (parts - 1)] for i in range(3)]
-    labels_ref, column_ref, out_ref = refs[3 * (parts - 1):]
+    own_in, late_in = refs[:parts - 1], refs[parts - 1:2 * (parts - 1)]
+    labels_ref, column_ref, out_ref = refs[2 * (parts - 1):]
     count, narrow = own_keep.shape
     own = sum([unhalved(ref[...]) for ref in own_in], own_keep[...])
-    two = sum([ref[:, :narrow] for ref in pair_in], two_keep[...])
-    mix = sum([ref[:, narrow:] for ref in pair_in], mix_keep[...])
-    swap = sum([unhalved(ref[...]) for ref in swap_in], swap_keep[...])
+    two = sum([ref[:count, :narrow] for ref in late_in], two_keep[...])
+    mix = sum([ref[:count, narrow:] for ref in late_in], mix_keep[...])
+    swap = sum([unhalved(ref[count:, :]) for ref in late_in], swap_keep[...])
     odd = lax.rem(lax.axis_index("blk"), 2) == 1
     for m, term in enumerate([own, jnp.where(odd, mix, swap), two, jnp.where(odd, swap, mix)]):
         wide = jnp.concatenate([term] * (out_ref.shape[2] // narrow), axis=1)
@@ -189,15 +190,14 @@
     mix = moved(after(own, rows), (1, 3, 1, 3))
     swap = moved(after(two, *own_in), (1, -1, 1, -1))
     pair_send, = call(pair_kernel, [whole(parts - 1, count, 2 * narrow)], (rows, labels, two, mix), one_product)
-    pair_in = exchanged(pair_send)
-    swap_send, = call(swap_kernel, [whole(parts - 1, count // 2, 2 * narrow)],
-                      (rows, labels, after(swap, pair_send)), one_product // 2)
-    swap_in = exchanged(swap_send)
+    late_send, = call(swap_kernel, [whole(parts - 1, count + count // 2, 2 * narrow)],
+                      (rows, labels, swap, pair_send), one_product // 2)
+    late_in = exchanged(late_send)
     two_keep, mix_keep, swap_keep, slab_labels = call(
         keep_kernel, [whole(count, narrow)] * 3 + [whole(8, pairs)],
-        (rows, labels, own, two, mix, after(swap, swap_send)), one_product)
+        (rows, labels, own, two, mix, after(swap, late_send)), one_product)
     out, = call(functools.partial(finish_kernel, parts), [whole(4, count, pairs)],
-                (own_keep, mix_keep, two_keep, swap_keep, *own_in, *pair_in, *swap_in, slab_labels, labels),
+                (own_keep, mix_keep, two_keep, swap_keep, *own_in, *late_in, slab_labels, labels),
                 4 * 2 * count * pairs)
     return out
 

time: 21.3 us -> 21.9 us (1.028)
  waiting for transfers between devices: 8.13 us -> 10.4 us
  starting transfers between devices: 6.79 us -> 5.15 us
    ppermute x3, waiting for transfers between devices: 2.99 us -> 4.58 us  [moved(): lax.ppermute(array, 'blk', [(i, (i + steps[i % 4]) % blocks) for i in ran...]
    ppermute x3 -> x2, starting transfers between devices: 3.74 us -> 2.16 us  [exchanged(): lax.ppermute(array[k - 1], 'red', [(i, (i + k) % parts) for i in range(pa...]
    ppermute x3 -> x2, waiting for transfers between devices: 5.14 us -> 5.84 us  [exchanged(): lax.ppermute(array[k - 1], 'red', [(i, (i + k) % parts) for i in range(pa...]
  transfers between devices with their start and end apart: 6 -> 5, of which waited for: 5 -> 4; matrix products, arithmetic and copies ran while one was open for 0% -> 0% of each run, Pallas kernels for 17% -> 14%
where the time goes in v5:
time: 21.9 us; the launch traced here: 21.8 us
  waiting for transfers between devices  10.4 us (47%)
  Pallas kernels  6.16 us (28%)
  starting transfers between devices  5.15 us (24%)
    pallas_call x6, Pallas kernels, call(): pl.pallas_call(kernel, out_shape=out_shape, in_specs=[OFFCHIP] * off + [O...  6.16 us
    ppermute x2, waiting for transfers between devices, exchanged(): lax.ppermute(array[k - 1], 'red', [(i, (i + k) % parts) for i in range(pa...  5.84 us
    ppermute x3, waiting for transfers between devices, moved(): lax.ppermute(array, 'blk', [(i, (i + steps[i % 4]) % blocks) for i in ran...  4.58 us
    ppermute x3, starting transfers between devices, moved(): lax.ppermute(array, 'blk', [(i, (i + steps[i % 4]) % blocks) for i in ran...  3 us
    ppermute x2, starting transfers between devices, exchanged(): lax.ppermute(array[k - 1], 'red', [(i, (i + k) % parts) for i in range(pa...  2.16 us
  transfers between devices with their start and end apart: 5, of which 4 were waited for; matrix products, arithmetic and copies ran while one was open for 0% of the time, Pallas kernels for 14%

profile of v5, /device:TPU:0, one launch (start us, length us, event | category | flops | bytes accessed | tf_op | source)
XLA Modules:
  0.0 21.8 jit_solution(1533575750125109438)
XLA Ops:
  0.0 1.6 %shard_map.55.own_ref = f32[200,256]{1,0:T(8,128)S(1)} custom-call(f32[256,768]{1,0:T(8,128)} %amp_ref.1, s32[1,256]{1,0:T(1,128)} %ij_ref.1, s32[1,768]{1,0:T(1,128)} %cd_ref.3), custom_call_target="tpu_custom_call" | custom-call | flops 786432 | bytes 995328 | tf_op jit(solution)/shard_map/pallas_call | solution.py:141
  1.6 3.0 %collective-permute-start = (f32[200,256]{1,0:T(8,128)S(1)}, f32[200,256]{1,0:T(8,128)S(1)}, u32[]{:S(2)}, u32[]{:S(2)}) collective-permute-start(f32[200,256]{1,0:T(8,128)S(1)} %shard_map.55.own_ref), channel_id=1, source_target_pairs={{0,4},{2,6},{4,8},{6,10},{8,12},{10,14},{12,16},{14,18},{16,20},{1... | collective-permute-start | bytes 614408 | tf_op jit(solution)/shard_map/ppermute | solution.py:161
  4.6 1.9 %shard_map.56 = (f32[256,192]{1,0:T(8,128)S(1)}, f32[256,128]{1,0:T(8,128)S(1)}, f32[128,64]{1,0:T(8,128)S(1)}, f32[1,64,128]{2,1,0:T(8,128)S(1)}) custom-call(f32[256,768]{1,0:T(8,128)} %v_ref.1, s32[1,256]{1,0:T(1,128)} %ab_ref.1, s32[1,768]{1,0:T(1,128)} %cd_ref.3, f32[200,256]{1,0:T(8,128)S(1)} %shard_map.55.own_ref), custom_call_target="tpu_custom_call" | custom-call | flops 4831838208 | bytes 1388544 | tf_op jit(solution)/shard_map/pallas_call | solution.py:141
  6.5 1.6 %collective-permute-start.2 = (f32[64,128]{1,0:T(8,128)S(1)}, f32[64,128]{1,0:T(8,128)S(1)}, u32[]{:S(2)}, u32[]{:S(2)}) collective-permute-start(f32[64,128]{1,0:T(8,128)S(1)} %bitcast.3), channel_id=1, source_target_pairs={{0,1},{1,0},{2,3},{3,2},{4,5},{5,4},{6,7},{7,6},{8,9},{9,8},{10,11... | collective-permute-start | bytes 98312 | tf_op jit(solution)/shard_map/ppermute | solution.py:165
  8.1 0.0 collective-permute-start.1
  8.1 2.4 %collective-permute-done.2.refs_4_ = f32[64,128]{1,0:T(8,128)S(1)} collective-permute-done((f32[64,128]{1,0:T(8,128)S(1)}, f32[64,128]{1,0:T(8,128)S(1)}, u32[]{:S(2)}, u32[]{:S(2)}) %collective-permute-start.2) | collective-permute-done | bytes 32800 | tf_op jit(solution)/shard_map/ppermute | solution.py:165
  10.5 2.2 %collective-permute-done.two_ref = f32[200,256]{1,0:T(8,128)S(1)} collective-permute-done((f32[200,256]{1,0:T(8,128)S(1)}, f32[200,256]{1,0:T(8,128)S(1)}, u32[]{:S(2)}, u32[]{:S(2)}) %collective-permute-start) | collective-permute-done | bytes 204832 | tf_op jit(solution)/shard_map/ppermute | solution.py:161
  12.7 0.0 collective-permute-start.3
  12.7 2.4 %collective-permute-done.1.mix_ref = f32[200,256]{1,0:T(8,128)S(1)} collective-permute-done((f32[200,256]{1,0:T(8,128)S(1)}, f32[200,256]{1,0:T(8,128)S(1)}, u32[]{:S(2)}, u32[]{:S(2)}) %collective-permute-start.1) | collective-permute-done | bytes 204832 | tf_op jit(solution)/shard_map/ppermute | solution.py:161
  15.1 0.6 %shard_map.57.pair_ref = f32[1,128,128]{2,1,0:T(8,128)S(1)} custom-call(f32[256,192]{1,0:T(8,128)S(1)} %get-tuple-element.17.rows_ref, f32[256,128]{1,0:T(8,128)S(1)} %get-tuple-element.18.column_ref.refs_7_, f32[200,256]{1,0:T(8,128)S(1)} %collective-permute-done.two_ref, f32[200,256]{1,0:T(8,128)S(1)} %collective-permute-done.1.mix_ref), custom_call_target="tpu_custom_call" | custom-call | flops 150994944 | bytes 802816 | tf_op jit(solution)/shard_map/pallas_call | solution.py:141
  15.6 0.0 collective-permute-done.3.swap_ref
  15.6 0.4 %shard_map.58 = f32[1,192,128]{2,1,0:T(8,128)S(1)} custom-call(f32[256,192]{1,0:T(8,128)S(1)} %get-tuple-element.17.rows_ref, f32[256,128]{1,0:T(8,128)S(1)} %get-tuple-element.18.column_ref.refs_7_, f32[200,256]{1,0:T(8,128)S(1)} %collective-permute-done.3.swap_ref, f32[1,128,128]{2,1,0:T(8,128)S(1)} %shard_map.57.pair_ref), custom_call_target="tpu_custom_call" | custom-call | flops 75497472 | bytes 696320 | tf_op jit(solution)/shard_map/pallas_call | solution.py:141
  16.0 0.6 %collective-permute-start.4 = (f32[192,128]{1,0:T(8,128)S(1)}, f32[192,128]{1,0:T(8,128)S(1)}, u32[]{:S(2)}, u32[]{:S(2)}) collective-permute-start(f32[192,128]{1,0:T(8,128)S(1)} %bitcast.2), channel_id=1, source_target_pairs={{0,1},{1,0},{2,3},{3,2},{4,5},{5,4},{6,7},{7,6},{8,9},{9,8},{10,11... | collective-permute-start | bytes 294920 | tf_op jit(solution)/shard_map/ppermute | solution.py:165
  16.6 0.7 %shard_map.59 = (f32[128,64]{1,0:T(8,128)S(1)}, f32[128,64]{1,0:T(8,128)S(1)}, f32[128,64]{1,0:T(8,128)S(1)}, f32[8,256]{1,0:T(8,128)S(1)}) custom-call(f32[256,192]{1,0:T(8,128)S(1)} %get-tuple-element.17.rows_ref, f32[256,128]{1,0:T(8,128)S(1)} %get-tuple-element.18.column_ref.refs_7_, f32[200,256]{1,0:T(8,128)S(1)} %shard_map.55.own_ref, ...), custom_call_target="tpu_custom_call" | custom-call | flops 150994944 | bytes 1253376 | tf_op jit(solution)/shard_map/pallas_call | solution.py:141
  17.3 3.4 %collective-permute-done.4.refs_5_ = f32[192,128]{1,0:T(8,128)S(1)} collective-permute-done((f32[192,128]{1,0:T(8,128)S(1)}, f32[192,128]{1,0:T(8,128)S(1)}, u32[]{:S(2)}, u32[]{:S(2)}) %collective-permute-start.4) | collective-permute-done | bytes 98336 | tf_op jit(solution)/shard_map/ppermute | solution.py:165
  20.7 1.0 %shard_map.60 = f32[4,128,256]{2,1,0:T(8,128)} custom-call(f32[128,64]{1,0:T(8,128)S(1)} %get-tuple-element.16.refs_0_, f32[128,64]{1,0:T(8,128)S(1)} %get-tuple-element.23.refs_1_, f32[128,64]{1,0:T(8,128)S(1)} %get-tuple-element.24.refs_2_, f32[128,64]{1,0:T(8,128)S(1)} %get-tuple-element.25.refs_3_, f32[64,128]{1,0:T(8,128)S(1)} %collective-permute-done.2.refs_4_, ...), custom_call_target="tpu_custom_call" | custom-call | flops 262144 | bytes 925696 | tf_op jit(solution)/shard_map/pallas_call | solution.py:141
Async XLA Ops:
  1.6 11.1 %collective-permute-start = (f32[200,256]{1,0:T(8,128)S(1)}, f32[200,256]{1,0:T(8,128)S(1)}, u32[]{:S(2)}, u32[]{:S(2)}) collective-permute-start(f32[200,256]{1,0:T(8,128)S(1)} %shard_map.55.own_ref), channel_id=1, source_target_pairs={{0,4},{2,6},{4,8},{6,10},{8,12},{10,14},{12,16},{14,18},{16,20},{1... | collective-permute-start | bytes 614408 | tf_op jit(solution)/shard_map/ppermute | solution.py:161
  6.5 4.0 %collective-permute-start.2 = (f32[64,128]{1,0:T(8,128)S(1)}, f32[64,128]{1,0:T(8,128)S(1)}, u32[]{:S(2)}, u32[]{:S(2)}) collective-permute-start(f32[64,128]{1,0:T(8,128)S(1)} %bitcast.3), channel_id=1, source_target_pairs={{0,1},{1,0},{2,3},{3,2},{4,5},{5,4},{6,7},{7,6},{8,9},{9,8},{10,11... | collective-permute-start | bytes 98312 | tf_op jit(solution)/shard_map/ppermute | solution.py:165
  8.1 7.0 %collective-permute-start.1 = (f32[200,256]{1,0:T(8,128)S(1)}, f32[200,256]{1,0:T(8,128)S(1)}, u32[]{:S(2)}, u32[]{:S(2)}) collective-permute-start(f32[200,256]{1,0:T(8,128)S(1)} %shard_map.55.own_ref), channel_id=1, source_target_pairs={{0,2},{2,8},{4,6},{6,12},{8,10},{10,16},{12,14},{14,20},{16,18},{1... | collective-permute-start | bytes 614408 | tf_op jit(solution)/shard_map/ppermute | solution.py:161
  12.7 2.9 %collective-permute-start.3 = (f32[200,256]{1,0:T(8,128)S(1)}, f32[200,256]{1,0:T(8,128)S(1)}, u32[]{:S(2)}, u32[]{:S(2)}) collective-permute-start(f32[200,256]{1,0:T(8,128)S(1)} %collective-permute-done.two_ref), channel_id=1, source_target_pairs={{0,2},{2,0},{4,6},{6,4},{8,10},{10,8},{12,14},{14,12},{16,18},{18,... | collective-permute-start | bytes 614408 | tf_op jit(solution)/shard_map/ppermute | solution.py:161
  16.0 4.7 %collective-permute-start.4 = (f32[192,128]{1,0:T(8,128)S(1)}, f32[192,128]{1,0:T(8,128)S(1)}, u32[]{:S(2)}, u32[]{:S(2)}) collective-permute-start(f32[192,128]{1,0:T(8,128)S(1)} %bitcast.2), channel_id=1, source_target_pairs={{0,1},{1,0},{2,3},{3,2},{4,5},{5,4},{6,7},{7,6},{8,9},{9,8},{10,11... | collective-permute-start | bytes 294920 | tf_op jit(solution)/shard_map/ppermute | solution.py:165

commit v6 on v5

--- a/solution.py
+++ b/solution.py
@@ -68,9 +68,8 @@
     return jnp.concatenate([term[:, :half], term[:, half:]], axis=0)
 
 
-def first_kernel(v_ref, ab_ref, cd_ref, own_ref, rows_ref, column_ref, keep_ref, send_ref, v, ab, cd, labels, sems):
-    width, count = rows_ref.shape[1], keep_ref.shape[0]
-    parts = v.shape[0] // count
+def first_kernel(count, v_ref, ab_ref, cd_ref, rows_ref, column_ref, v, ab, cd, labels, sems):
+    width, parts = rows_ref.shape[1], v.shape[0] // count
     mine = lax.axis_index("red")
     places = [pl.ds(pl.multiple_of(lax.rem(mine + k, parts) * count, count), count) for k in range(parts)]
     held = [pl.ds(k * count, count) for k in range(parts)]
@@ -83,9 +82,13 @@
         column_ref[h, :] = labels[p, :]
         copy.wait()
         rows_ref[h, :] = fold(v[h, :], column_ref[h, :], cd_labels, width)
+
+
+def own_kernel(rows_ref, column_ref, own_ref, keep_ref, send_ref):
+    count = keep_ref.shape[0]
     term = narrowed(rows_ref[...], own_ref, column_ref[...])
     keep_ref[...] = term[:count]
-    for k in range(1, parts):
+    for k in range(1, send_ref.shape[0] + 1):
         send_ref[k - 1] = halved(term[k * count:(k + 1) * count])
 
 
@@ -181,15 +184,16 @@
                 4 * amplitudes.size, 3, stage + [sems])
     two = moved(own, (2, 2, 2, 2))
     stage, sems = staging(integrals, ab_irrep, parts)
-    rows, labels, own_keep, own_send = call(
-        first_kernel,
-        [whole(row_count, width), whole(row_count, LANES), whole(count, narrow), whole(parts - 1, count // 2, 2 * narrow)],
-        (integrals, ab_irrep, cd_irrep, own), 32 * one_product, 3,
-        stage + [pltpu.VMEM((row_count, LANES), F32), sems])
+    rows, labels = call(
+        functools.partial(first_kernel, count), [whole(row_count, width), whole(row_count, LANES)],
+        (integrals, ab_irrep, cd_irrep), one_product, 3, stage + [pltpu.VMEM((row_count, LANES), F32), sems])
+    own_keep, own_send = call(
+        own_kernel, [whole(count, narrow), whole(parts - 1, count // 2, 2 * narrow)],
+        (rows, labels, own), one_product)
     own_in = exchanged(own_send)
     mix = moved(after(own, rows), (1, 3, 1, 3))
     swap = moved(after(two, *own_in), (1, -1, 1, -1))
-    pair_send, = call(pair_kernel, [whole(parts - 1, count, 2 * narrow)], (rows, labels, two, mix), one_product)
+    pair_send, = call(pair_kernel, [whole(parts - 1, count, 2 * narrow)], (rows, labels, two, mix), 40 * one_product)
     late_send, = call(swap_kernel, [whole(parts - 1, count + count // 2, 2 * narrow)],
                       (rows, labels, swap, pair_send), one_product // 2)
     late_in = exchanged(late_send)

time: 21.9 us -> 21.4 us (0.977)
  waiting for transfers between devices: 10.4 us -> 8.78 us
  starting transfers between devices: 5.15 us -> 6.22 us
    ppermute x2, starting transfers between devices: 2.16 us -> 3.17 us  [exchanged(): lax.ppermute(array[k - 1], 'red', [(i, (i + k) % parts) for i in range(pa...]
    ppermute x3, waiting for transfers between devices: 4.58 us -> 3.73 us  [moved(): lax.ppermute(array, 'blk', [(i, (i + steps[i % 4]) % blocks) for i in ran...]
    ppermute x2, waiting for transfers between devices: 5.84 us -> 5.04 us  [exchanged(): lax.ppermute(array[k - 1], 'red', [(i, (i + k) % parts) for i in range(pa...]
    pallas_call x6 -> x7, Pallas kernels: 6.16 us -> 6.22 us  [call(): pl.pallas_call(kernel, out_shape=out_shape, in_specs=[OFFCHIP] * off + [O...]
  transfers between devices with their start and end apart: 5 -> 5, of which waited for: 4 -> 4; matrix products, arithmetic and copies ran while one was open for 0% -> 0% of each run, Pallas kernels for 14% -> 15%
where the time goes in v6:
time: 21.4 us; the launch traced here: 21.3 us
  waiting for transfers between devices  8.78 us (41%)
  Pallas kernels  6.22 us (29%)
  starting transfers between devices  6.22 us (29%)
    pallas_call x7, Pallas kernels, call(): pl.pallas_call(kernel, out_shape=out_shape, in_specs=[OFFCHIP] * off + [O...  6.22 us
    ppermute x2, waiting for transfers between devices, exchanged(): lax.ppermute(array[k - 1], 'red', [(i, (i + k) % parts) for i in range(pa...  5.04 us
    ppermute x3, waiting for transfers between devices, moved(): lax.ppermute(array, 'blk', [(i, (i + steps[i % 4]) % blocks) for i in ran...  3.73 us
    ppermute x2, starting transfers between devices, exchanged(): lax.ppermute(array[k - 1], 'red', [(i, (i + k) % parts) for i in range(pa...  3.17 us
    ppermute x3, starting transfers between devices, moved(): lax.ppermute(array, 'blk', [(i, (i + steps[i % 4]) % blocks) for i in ran...  3.05 us
  transfers between devices with their start and end apart: 5, of which 4 were waited for; matrix products, arithmetic and copies ran while one was open for 0% of the time, Pallas kernels for 15%

profile of v6, /device:TPU:0, one launch (start us, length us, event | category | flops | bytes accessed | tf_op | source)
XLA Modules:
  0.0 21.3 jit_solution(10138286607395979884)
XLA Ops:
  0.0 1.6 %shard_map.56.own_ref = f32[200,256]{1,0:T(8,128)S(1)} custom-call(f32[256,768]{1,0:T(8,128)} %amp_ref.1, s32[1,256]{1,0:T(1,128)} %ij_ref.1, s32[1,768]{1,0:T(1,128)} %cd_ref.3), custom_call_target="tpu_custom_call" | custom-call | flops 786432 | bytes 995328 | tf_op jit(solution)/shard_map/pallas_call | solution.py:144
  1.6 3.0 %collective-permute-start = (f32[200,256]{1,0:T(8,128)S(1)}, f32[200,256]{1,0:T(8,128)S(1)}, u32[]{:S(2)}, u32[]{:S(2)}) collective-permute-start(f32[200,256]{1,0:T(8,128)S(1)} %shard_map.56.own_ref), channel_id=1, source_target_pairs={{0,4},{2,6},{4,8},{6,10},{8,12},{10,14},{12,16},{14,18},{16,20},{1... | collective-permute-start | bytes 614408 | tf_op jit(solution)/shard_map/ppermute | solution.py:164
  4.6 1.5 %shard_map.55 = (f32[256,192]{1,0:T(8,128)S(1)}, f32[256,128]{1,0:T(8,128)S(1)}) custom-call(f32[256,768]{1,0:T(8,128)} %v_ref.1, s32[1,256]{1,0:T(1,128)} %ab_ref.1, s32[1,768]{1,0:T(1,128)} %cd_ref.3), custom_call_target="tpu_custom_call" | custom-call | flops 150994944 | bytes 1118208 | tf_op jit(solution)/shard_map/pallas_call | solution.py:144
  6.1 0.1 collective-permute-start.1
  6.2 0.5 %shard_map.57 = (f32[128,64]{1,0:T(8,128)S(1)}, f32[1,64,128]{2,1,0:T(8,128)S(1)}) custom-call(f32[256,192]{1,0:T(8,128)S(1)} %get-tuple-element.16.rows_ref, f32[256,128]{1,0:T(8,128)S(1)} %get-tuple-element.17.column_ref.refs_7_, f32[200,256]{1,0:T(8,128)S(1)} %shard_map.56.own_ref), custom_call_target="tpu_custom_call" | custom-call | flops 150994944 | bytes 598016 | tf_op jit(solution)/shard_map/pallas_call | solution.py:144
  6.7 1.6 %collective-permute-start.2 = (f32[64,128]{1,0:T(8,128)S(1)}, f32[64,128]{1,0:T(8,128)S(1)}, u32[]{:S(2)}, u32[]{:S(2)}) collective-permute-start(f32[64,128]{1,0:T(8,128)S(1)} %bitcast.3), channel_id=1, source_target_pairs={{0,1},{1,0},{2,3},{3,2},{4,5},{5,4},{6,7},{7,6},{8,9},{9,8},{10,11... | collective-permute-start | bytes 98312 | tf_op jit(solution)/shard_map/ppermute | solution.py:168
  8.2 2.4 %collective-permute-done.2.refs_4_ = f32[64,128]{1,0:T(8,128)S(1)} collective-permute-done((f32[64,128]{1,0:T(8,128)S(1)}, f32[64,128]{1,0:T(8,128)S(1)}, u32[]{:S(2)}, u32[]{:S(2)}) %collective-permute-start.2) | collective-permute-done | bytes 32800 | tf_op jit(solution)/shard_map/ppermute | solution.py:168
  10.6 2.8 %collective-permute-done.two_ref = f32[200,256]{1,0:T(8,128)S(1)} collective-permute-done((f32[200,256]{1,0:T(8,128)S(1)}, f32[200,256]{1,0:T(8,128)S(1)}, u32[]{:S(2)}, u32[]{:S(2)}) %collective-permute-start) | collective-permute-done | bytes 204832 | tf_op jit(solution)/shard_map/ppermute | solution.py:164
  13.5 0.0 collective-permute-start.3
  13.5 0.0 collective-permute-done.1.mix_ref
  13.5 0.5 %shard_map.58.pair_ref = f32[1,128,128]{2,1,0:T(8,128)S(1)} custom-call(f32[256,192]{1,0:T(8,128)S(1)} %get-tuple-element.16.rows_ref, f32[256,128]{1,0:T(8,128)S(1)} %get-tuple-element.17.column_ref.refs_7_, f32[200,256]{1,0:T(8,128)S(1)} %collective-permute-done.two_ref, f32[200,256]{1,0:T(8,128)S(1)} %collective-permute-done.1.mix_ref), custom_call_target="tpu_custom_call" | custom-call | flops 6039797760 | bytes 802816 | tf_op jit(solution)/shard_map/pallas_call | solution.py:144
  14.0 0.9 %collective-permute-done.3.swap_ref = f32[200,256]{1,0:T(8,128)S(1)} collective-permute-done((f32[200,256]{1,0:T(8,128)S(1)}, f32[200,256]{1,0:T(8,128)S(1)}, u32[]{:S(2)}, u32[]{:S(2)}) %collective-permute-start.3) | collective-permute-done | bytes 204832 | tf_op jit(solution)/shard_map/ppermute | solution.py:164
  14.9 0.4 %shard_map.59 = f32[1,192,128]{2,1,0:T(8,128)S(1)} custom-call(f32[256,192]{1,0:T(8,128)S(1)} %get-tuple-element.16.rows_ref, f32[256,128]{1,0:T(8,128)S(1)} %get-tuple-element.17.column_ref.refs_7_, f32[200,256]{1,0:T(8,128)S(1)} %collective-permute-done.3.swap_ref, f32[1,128,128]{2,1,0:T(8,128)S(1)} %shard_map.58.pair_ref), custom_call_target="tpu_custom_call" | custom-call | flops 75497472 | bytes 696320 | tf_op jit(solution)/shard_map/pallas_call | solution.py:144
  15.3 1.6 %collective-permute-start.4 = (f32[192,128]{1,0:T(8,128)S(1)}, f32[192,128]{1,0:T(8,128)S(1)}, u32[]{:S(2)}, u32[]{:S(2)}) collective-permute-start(f32[192,128]{1,0:T(8,128)S(1)} %bitcast.2), channel_id=1, source_target_pairs={{0,1},{1,0},{2,3},{3,2},{4,5},{5,4},{6,7},{7,6},{8,9},{9,8},{10,11... | collective-permute-start | bytes 294920 | tf_op jit(solution)/shard_map/ppermute | solution.py:168
  16.9 0.7 %shard_map.60 = (f32[128,64]{1,0:T(8,128)S(1)}, f32[128,64]{1,0:T(8,128)S(1)}, f32[128,64]{1,0:T(8,128)S(1)}, f32[8,256]{1,0:T(8,128)S(1)}) custom-call(f32[256,192]{1,0:T(8,128)S(1)} %get-tuple-element.16.rows_ref, f32[256,128]{1,0:T(8,128)S(1)} %get-tuple-element.17.column_ref.refs_7_, f32[200,256]{1,0:T(8,128)S(1)} %shard_map.56.own_ref, ...), custom_call_target="tpu_custom_call" | custom-call | flops 150994944 | bytes 1253376 | tf_op jit(solution)/shard_map/pallas_call | solution.py:144
  17.6 2.6 %collective-permute-done.4.refs_5_ = f32[192,128]{1,0:T(8,128)S(1)} collective-permute-done((f32[192,128]{1,0:T(8,128)S(1)}, f32[192,128]{1,0:T(8,128)S(1)}, u32[]{:S(2)}, u32[]{:S(2)}) %collective-permute-start.4) | collective-permute-done | bytes 98336 | tf_op jit(solution)/shard_map/ppermute | solution.py:168
  20.2 1.0 %shard_map.61 = f32[4,128,256]{2,1,0:T(8,128)} custom-call(f32[128,64]{1,0:T(8,128)S(1)} %get-tuple-element.18.refs_0_, f32[128,64]{1,0:T(8,128)S(1)} %get-tuple-element.23.refs_1_, f32[128,64]{1,0:T(8,128)S(1)} %get-tuple-element.24.refs_2_, f32[128,64]{1,0:T(8,128)S(1)} %get-tuple-element.25.refs_3_, f32[64,128]{1,0:T(8,128)S(1)} %collective-permute-done.2.refs_4_, ...), custom_call_target="tpu_custom_call" | custom-call | flops 262144 | bytes 925696 | tf_op jit(solution)/shard_map/pallas_call | solution.py:144
Async XLA Ops:
  1.6 11.8 %collective-permute-start = (f32[200,256]{1,0:T(8,128)S(1)}, f32[200,256]{1,0:T(8,128)S(1)}, u32[]{:S(2)}, u32[]{:S(2)}) collective-permute-start(f32[200,256]{1,0:T(8,128)S(1)} %shard_map.56.own_ref), channel_id=1, source_target_pairs={{0,4},{2,6},{4,8},{6,10},{8,12},{10,14},{12,16},{14,18},{16,20},{1... | collective-permute-start | bytes 614408 | tf_op jit(solution)/shard_map/ppermute | solution.py:164
  6.1 7.4 %collective-permute-start.1 = (f32[200,256]{1,0:T(8,128)S(1)}, f32[200,256]{1,0:T(8,128)S(1)}, u32[]{:S(2)}, u32[]{:S(2)}) collective-permute-start(f32[200,256]{1,0:T(8,128)S(1)} %shard_map.56.own_ref), channel_id=1, source_target_pairs={{0,2},{2,8},{4,6},{6,12},{8,10},{10,16},{12,14},{14,20},{16,18},{1... | collective-permute-start | bytes 614408 | tf_op jit(solution)/shard_map/ppermute | solution.py:164
  6.7 4.0 %collective-permute-start.2 = (f32[64,128]{1,0:T(8,128)S(1)}, f32[64,128]{1,0:T(8,128)S(1)}, u32[]{:S(2)}, u32[]{:S(2)}) collective-permute-start(f32[64,128]{1,0:T(8,128)S(1)} %bitcast.3), channel_id=1, source_target_pairs={{0,1},{1,0},{2,3},{3,2},{4,5},{5,4},{6,7},{7,6},{8,9},{9,8},{10,11... | collective-permute-start | bytes 98312 | tf_op jit(solution)/shard_map/ppermute | solution.py:168
  13.5 1.5 %collective-permute-start.3 = (f32[200,256]{1,0:T(8,128)S(1)}, f32[200,256]{1,0:T(8,128)S(1)}, u32[]{:S(2)}, u32[]{:S(2)}) collective-permute-start(f32[200,256]{1,0:T(8,128)S(1)} %collective-permute-done.two_ref), channel_id=1, source_target_pairs={{0,2},{2,0},{4,6},{6,4},{8,10},{10,8},{12,14},{14,12},{16,18},{18,... | collective-permute-start | bytes 614408 | tf_op jit(solution)/shard_map/ppermute | solution.py:164
  15.3 4.9 %collective-permute-start.4 = (f32[192,128]{1,0:T(8,128)S(1)}, f32[192,128]{1,0:T(8,128)S(1)}, u32[]{:S(2)}, u32[]{:S(2)}) collective-permute-start(f32[192,128]{1,0:T(8,128)S(1)} %bitcast.2), channel_id=1, source_target_pairs={{0,1},{1,0},{2,3},{3,2},{4,5},{5,4},{6,7},{7,6},{8,9},{9,8},{10,11... | collective-permute-start | bytes 294920 | tf_op jit(solution)/shard_map/ppermute | solution.py:168

commit v7 on v6

--- a/solution.py
+++ b/solution.py
@@ -191,7 +191,7 @@
         own_kernel, [whole(count, narrow), whole(parts - 1, count // 2, 2 * narrow)],
         (rows, labels, own), one_product)
     own_in = exchanged(own_send)
-    mix = moved(after(own, rows), (1, 3, 1, 3))
+    mix = moved(after(own, own_keep), (1, 3, 1, 3))
     swap = moved(after(two, *own_in), (1, -1, 1, -1))
     pair_send, = call(pair_kernel, [whole(parts - 1, count, 2 * narrow)], (rows, labels, two, mix), 40 * one_product)
     late_send, = call(swap_kernel, [whole(parts - 1, count + count // 2, 2 * narrow)],

time: 21.4 us -> 20.9 us (0.977)
  waiting for transfers between devices: 8.78 us -> 8.28 us
    ppermute x3, waiting for transfers between devices: 3.73 us -> 3.23 us  [moved(): lax.ppermute(array, 'blk', [(i, (i + steps[i % 4]) % blocks) for i in ran...]
  transfers between devices with their start and end apart: 5 -> 5, of which waited for: 4 -> 5; matrix products, arithmetic and copies ran while one was open for 0% -> 0% of each run, Pallas kernels for 15% -> 15%
where the time goes in v7:
time: 20.9 us; the launch traced here: 20.8 us
  waiting for transfers between devices  8.28 us (40%)
  Pallas kernels  6.22 us (30%)
  starting transfers between devices  6.22 us (30%)
    pallas_call x7, Pallas kernels, call(): pl.pallas_call(kernel, out_shape=out_shape, in_specs=[OFFCHIP] * off + [O...  6.22 us
    ppermute x2, waiting for transfers between devices, exchanged(): lax.ppermute(array[k - 1], 'red', [(i, (i + k) % parts) for i in range(pa...  5.04 us
    ppermute x3, waiting for transfers between devices, moved(): lax.ppermute(array, 'blk', [(i, (i + steps[i % 4]) % blocks) for i in ran...  3.23 us
    ppermute x2, starting transfers between devices, exchanged(): lax.ppermute(array[k - 1], 'red', [(i, (i + k) % parts) for i in range(pa...  3.17 us
    ppermute x3, starting transfers between devices, moved(): lax.ppermute(array, 'blk', [(i, (i + steps[i % 4]) % blocks) for i in ran...  3.05 us
  transfers between devices with their start and end apart: 5, of which 5 were waited for; matrix products, arithmetic and copies ran while one was open for 0% of the time, Pallas kernels for 15%

profile of v7, /device:TPU:0, one launch (start us, length us, event | category | flops | bytes accessed | tf_op | source)
XLA Modules:
  0.0 20.8 jit_solution(4774019213555290303)
XLA Ops:
  0.0 1.6 %shard_map.56.own_ref = f32[200,256]{1,0:T(8,128)S(1)} custom-call(f32[256,768]{1,0:T(8,128)} %amp_ref.1, s32[1,256]{1,0:T(1,128)} %ij_ref.1, s32[1,768]{1,0:T(1,128)} %cd_ref.3), custom_call_target="tpu_custom_call" | custom-call | flops 786432 | bytes 995328 | tf_op jit(solution)/shard_map/pallas_call | solution.py:144
  1.6 3.0 %collective-permute-start = (f32[200,256]{1,0:T(8,128)S(1)}, f32[200,256]{1,0:T(8,128)S(1)}, u32[]{:S(2)}, u32[]{:S(2)}) collective-permute-start(f32[200,256]{1,0:T(8,128)S(1)} %shard_map.56.own_ref), channel_id=1, source_target_pairs={{0,4},{2,6},{4,8},{6,10},{8,12},{10,14},{12,16},{14,18},{16,20},{1... | collective-permute-start | bytes 614408 | tf_op jit(solution)/shard_map/ppermute | solution.py:164
  4.6 1.5 %shard_map.55 = (f32[256,192]{1,0:T(8,128)S(1)}, f32[256,128]{1,0:T(8,128)S(1)}) custom-call(f32[256,768]{1,0:T(8,128)} %v_ref.1, s32[1,256]{1,0:T(1,128)} %ab_ref.1, s32[1,768]{1,0:T(1,128)} %cd_ref.3), custom_call_target="tpu_custom_call" | custom-call | flops 150994944 | bytes 1118208 | tf_op jit(solution)/shard_map/pallas_call | solution.py:144
  6.1 0.5 %shard_map.57 = (f32[128,64]{1,0:T(8,128)S(1)}, f32[1,64,128]{2,1,0:T(8,128)S(1)}) custom-call(f32[256,192]{1,0:T(8,128)S(1)} %get-tuple-element.16.rows_ref, f32[256,128]{1,0:T(8,128)S(1)} %get-tuple-element.17.column_ref.refs_7_, f32[200,256]{1,0:T(8,128)S(1)} %shard_map.56.own_ref), custom_call_target="tpu_custom_call" | custom-call | flops 150994944 | bytes 598016 | tf_op jit(solution)/shard_map/pallas_call | solution.py:144
  6.6 0.1 collective-permute-start.1
  6.7 1.6 %collective-permute-start.2 = (f32[64,128]{1,0:T(8,128)S(1)}, f32[64,128]{1,0:T(8,128)S(1)}, u32[]{:S(2)}, u32[]{:S(2)}) collective-permute-start(f32[64,128]{1,0:T(8,128)S(1)} %bitcast.3), channel_id=1, source_target_pairs={{0,1},{1,0},{2,3},{3,2},{4,5},{5,4},{6,7},{7,6},{8,9},{9,8},{10,11... | collective-permute-start | bytes 98312 | tf_op jit(solution)/shard_map/ppermute | solution.py:168
  8.2 2.4 %collective-permute-done.2.refs_4_ = f32[64,128]{1,0:T(8,128)S(1)} collective-permute-done((f32[64,128]{1,0:T(8,128)S(1)}, f32[64,128]{1,0:T(8,128)S(1)}, u32[]{:S(2)}, u32[]{:S(2)}) %collective-permute-start.2) | collective-permute-done | bytes 32800 | tf_op jit(solution)/shard_map/ppermute | solution.py:168
  10.6 2.3 %collective-permute-done.two_ref = f32[200,256]{1,0:T(8,128)S(1)} collective-permute-done((f32[200,256]{1,0:T(8,128)S(1)}, f32[200,256]{1,0:T(8,128)S(1)}, u32[]{:S(2)}, u32[]{:S(2)}) %collective-permute-start) | collective-permute-done | bytes 204832 | tf_op jit(solution)/shard_map/ppermute | solution.py:164
  13.0 0.0 collective-permute-start.3
  13.0 0.7 %collective-permute-done.1.mix_ref = f32[200,256]{1,0:T(8,128)S(1)} collective-permute-done((f32[200,256]{1,0:T(8,128)S(1)}, f32[200,256]{1,0:T(8,128)S(1)}, u32[]{:S(2)}, u32[]{:S(2)}) %collective-permute-start.1) | collective-permute-done | bytes 204832 | tf_op jit(solution)/shard_map/ppermute | solution.py:164
  13.6 0.5 %shard_map.58.pair_ref = f32[1,128,128]{2,1,0:T(8,128)S(1)} custom-call(f32[256,192]{1,0:T(8,128)S(1)} %get-tuple-element.16.rows_ref, f32[256,128]{1,0:T(8,128)S(1)} %get-tuple-element.17.column_ref.refs_7_, f32[200,256]{1,0:T(8,128)S(1)} %collective-permute-done.two_ref, f32[200,256]{1,0:T(8,128)S(1)} %collective-permute-done.1.mix_ref), custom_call_target="tpu_custom_call" | custom-call | flops 6039797760 | bytes 802816 | tf_op jit(solution)/shard_map/pallas_call | solution.py:144
  14.2 0.3 %collective-permute-done.3.swap_ref = f32[200,256]{1,0:T(8,128)S(1)} collective-permute-done((f32[200,256]{1,0:T(8,128)S(1)}, f32[200,256]{1,0:T(8,128)S(1)}, u32[]{:S(2)}, u32[]{:S(2)}) %collective-permute-start.3) | collective-permute-done | bytes 204832 | tf_op jit(solution)/shard_map/ppermute | solution.py:164
  14.4 0.4 %shard_map.59 = f32[1,192,128]{2,1,0:T(8,128)S(1)} custom-call(f32[256,192]{1,0:T(8,128)S(1)} %get-tuple-element.16.rows_ref, f32[256,128]{1,0:T(8,128)S(1)} %get-tuple-element.17.column_ref.refs_7_, f32[200,256]{1,0:T(8,128)S(1)} %collective-permute-done.3.swap_ref, f32[1,128,128]{2,1,0:T(8,128)S(1)} %shard_map.58.pair_ref), custom_call_target="tpu_custom_call" | custom-call | flops 75497472 | bytes 696320 | tf_op jit(solution)/shard_map/pallas_call | solution.py:144
  14.8 1.6 %collective-permute-start.4 = (f32[192,128]{1,0:T(8,128)S(1)}, f32[192,128]{1,0:T(8,128)S(1)}, u32[]{:S(2)}, u32[]{:S(2)}) collective-permute-start(f32[192,128]{1,0:T(8,128)S(1)} %bitcast.2), channel_id=1, source_target_pairs={{0,1},{1,0},{2,3},{3,2},{4,5},{5,4},{6,7},{7,6},{8,9},{9,8},{10,11... | collective-permute-start | bytes 294920 | tf_op jit(solution)/shard_map/ppermute | solution.py:168
  16.4 0.7 %shard_map.60 = (f32[128,64]{1,0:T(8,128)S(1)}, f32[128,64]{1,0:T(8,128)S(1)}, f32[128,64]{1,0:T(8,128)S(1)}, f32[8,256]{1,0:T(8,128)S(1)}) custom-call(f32[256,192]{1,0:T(8,128)S(1)} %get-tuple-element.16.rows_ref, f32[256,128]{1,0:T(8,128)S(1)} %get-tuple-element.17.column_ref.refs_7_, f32[200,256]{1,0:T(8,128)S(1)} %shard_map.56.own_ref, ...), custom_call_target="tpu_custom_call" | custom-call | flops 150994944 | bytes 1253376 | tf_op jit(solution)/shard_map/pallas_call | solution.py:144
  17.1 2.6 %collective-permute-done.4.refs_5_ = f32[192,128]{1,0:T(8,128)S(1)} collective-permute-done((f32[192,128]{1,0:T(8,128)S(1)}, f32[192,128]{1,0:T(8,128)S(1)}, u32[]{:S(2)}, u32[]{:S(2)}) %collective-permute-start.4) | collective-permute-done | bytes 98336 | tf_op jit(solution)/shard_map/ppermute | solution.py:168
  19.7 1.0 %shard_map.61 = f32[4,128,256]{2,1,0:T(8,128)} custom-call(f32[128,64]{1,0:T(8,128)S(1)} %get-tuple-element.18.refs_0_, f32[128,64]{1,0:T(8,128)S(1)} %get-tuple-element.23.refs_1_, f32[128,64]{1,0:T(8,128)S(1)} %get-tuple-element.24.refs_2_, f32[128,64]{1,0:T(8,128)S(1)} %get-tuple-element.25.refs_3_, f32[64,128]{1,0:T(8,128)S(1)} %collective-permute-done.2.refs_4_, ...), custom_call_target="tpu_custom_call" | custom-call | flops 262144 | bytes 925696 | tf_op jit(solution)/shard_map/pallas_call | solution.py:144
Async XLA Ops:
  1.6 11.3 %collective-permute-start = (f32[200,256]{1,0:T(8,128)S(1)}, f32[200,256]{1,0:T(8,128)S(1)}, u32[]{:S(2)}, u32[]{:S(2)}) collective-permute-start(f32[200,256]{1,0:T(8,128)S(1)} %shard_map.56.own_ref), channel_id=1, source_target_pairs={{0,4},{2,6},{4,8},{6,10},{8,12},{10,14},{12,16},{14,18},{16,20},{1... | collective-permute-start | bytes 614408 | tf_op jit(solution)/shard_map/ppermute | solution.py:164
  6.6 7.0 %collective-permute-start.1 = (f32[200,256]{1,0:T(8,128)S(1)}, f32[200,256]{1,0:T(8,128)S(1)}, u32[]{:S(2)}, u32[]{:S(2)}) collective-permute-start(f32[200,256]{1,0:T(8,128)S(1)} %shard_map.56.own_ref), channel_id=1, source_target_pairs={{0,2},{2,8},{4,6},{6,12},{8,10},{10,16},{12,14},{14,20},{16,18},{1... | collective-permute-start | bytes 614408 | tf_op jit(solution)/shard_map/ppermute | solution.py:164
  6.7 4.0 %collective-permute-start.2 = (f32[64,128]{1,0:T(8,128)S(1)}, f32[64,128]{1,0:T(8,128)S(1)}, u32[]{:S(2)}, u32[]{:S(2)}) collective-permute-start(f32[64,128]{1,0:T(8,128)S(1)} %bitcast.3), channel_id=1, source_target_pairs={{0,1},{1,0},{2,3},{3,2},{4,5},{5,4},{6,7},{7,6},{8,9},{9,8},{10,11... | collective-permute-start | bytes 98312 | tf_op jit(solution)/shard_map/ppermute | solution.py:168
  13.0 1.5 %collective-permute-start.3 = (f32[200,256]{1,0:T(8,128)S(1)}, f32[200,256]{1,0:T(8,128)S(1)}, u32[]{:S(2)}, u32[]{:S(2)}) collective-permute-start(f32[200,256]{1,0:T(8,128)S(1)} %collective-permute-done.two_ref), channel_id=1, source_target_pairs={{0,2},{2,0},{4,6},{6,4},{8,10},{10,8},{12,14},{14,12},{16,18},{18,... | collective-permute-start | bytes 614408 | tf_op jit(solution)/shard_map/ppermute | solution.py:164
  14.8 4.9 %collective-permute-start.4 = (f32[192,128]{1,0:T(8,128)S(1)}, f32[192,128]{1,0:T(8,128)S(1)}, u32[]{:S(2)}, u32[]{:S(2)}) collective-permute-start(f32[192,128]{1,0:T(8,128)S(1)} %bitcast.2), channel_id=1, source_target_pairs={{0,1},{1,0},{2,3},{3,2},{4,5},{5,4},{6,7},{7,6},{8,9},{9,8},{10,11... | collective-permute-start | bytes 294920 | tf_op jit(solution)/shard_map/ppermute | solution.py:168

commit v8 on v7

v8 whole, which is shorter than its diff:
```python
import functools
import jax
import jax.numpy as jnp
from jax import lax
from jax.experimental import pallas as pl
from jax.experimental.pallas import tpu as pltpu
from jax.sharding import PartitionSpec as P

LANES = 128
F32 = jnp.float32
ONCHIP = pl.BlockSpec(memory_space=pltpu.VMEM)
OFFCHIP = pl.BlockSpec(memory_space=pltpu.HBM)


def column(labels):
    return jnp.broadcast_to(labels.astype(F32), (LANES, labels.shape[1])).T


def fold(rows, row_labels, cd_labels):
    tiles = rows.shape[1] // LANES
    kept = [
        jnp.where(row_labels == cd_labels[:, k * LANES:(k + 1) * LANES], rows[:, k * LANES:(k + 1) * LANES], 0.0)
        for k in range(tiles)
    ]
    kept = [kept[k] + kept[k + tiles // 2] for k in range(tiles // 2)]
    low = lower(kept[0].shape)
    first, middle, last = kept
    middle_turned, last_turned = turned(middle), turned(last)
    return first + jnp.where(low, middle_turned, last_turned), middle + last_turned


def lower(shape):
    return lax.broadcasted_iota(jnp.int32, shape, 1) < LANES // 2


def turned(array):
    return pltpu.roll(array, LANES // 2, 1)


def fetch(pairs, sems):
    copies = [pltpu.make_async_copy(src, dst, sems.at[i]) for i, (src, dst) in enumerate(pairs)]
    for copy in copies:
        copy.start()
    return copies


def pack_kernel(amp_ref, ij_ref, cd_ref, out_ref, amp, ij, cd, sems):
    pairs, width = amp.shape[0], out_ref.shape[0] - 8
    copies = fetch([(amp_ref, amp), (ij_ref, ij), (cd_ref, cd)], sems)
    copies[1].wait()
    copies[2].wait()
    rows = column(ij[...])
    labels = cd[...].astype(F32)
    out_ref[width:, :] = jnp.broadcast_to(ij[...].astype(F32), (8, pairs))
    copies[0].wait()
    for start in range(0, pairs, LANES):
        part = slice(start, start + LANES)
        first, second = fold(amp[part, :], rows[part], labels)
        out_ref[:LANES, part] = first.T
        out_ref[LANES:width, part] = second.T[:width - LANES]


def narrowed(rows, slab_ref, row_labels):
    width = rows.shape[1]
    full = jnp.dot(rows, slab_ref[:width, :], precision=lax.Precision.HIGHEST, preferred_element_type=F32)
    labels = slab_ref[width:width + 1, :]
    total = None
    for start in range(0, full.shape[1], LANES):
        part = slice(start, start + LANES)
        kept = jnp.where(row_labels == labels[:, part], full[:, part], 0.0)
        total = kept if total is None else total + kept
    return total + turned(total)


def beside(one, other):
    return jnp.where(lower(one.shape), one, other)


def apart(array):
    low, other = lower(array.shape), turned(array)
    return jnp.where(low, array, other), jnp.where(low, other, array)


def halved(term):
    half = term.shape[0] // 2
    return beside(term[:half], term[half:])


def unhalved(term):
    return jnp.concatenate(apart(term), axis=0)


def first_kernel(count, v_ref, ab_ref, cd_ref, rows_ref, column_ref, v, ab, cd, labels, sems):
    width, parts = rows_ref.shape[1], v.shape[0] // count
    mine = lax.axis_index("red")
    places = [pl.ds(pl.multiple_of(lax.rem(mine + k, parts) * count, count), count) for k in range(parts)]
    held = [pl.ds(k * count, count) for k in range(parts)]
    copies = fetch([(ab_ref, ab), (cd_ref, cd)] + [(v_ref.at[p], v.at[h]) for p, h in zip(places, held)], sems)
    copies[0].wait()
    copies[1].wait()
    labels[...] = column(ab[...])
    cd_labels = cd[...].astype(F32)
    for copy, p, h in zip(copies[2:], places, held):
        column_ref[h, :] = labels[p, :]
        copy.wait()
        first, second = fold(v[h, :], column_ref[h, :], cd_labels)
        rows_ref[h, :LANES] = first
        rows_ref[h, LANES:] = second[:, :width - LANES]


def own_kernel(rows_ref, column_ref, own_ref, keep_ref, send_ref):
    count = keep_ref.shape[0]
    term = narrowed(rows_ref[...], own_ref, column_ref[...])
    keep_ref[...] = term[:count]
    for k in range(1, send_ref.shape[0] + 1):
        send_ref[k - 1] = halved(term[k * count:(k + 1) * count])


def pair_kernel(rows_ref, column_ref, two_ref, mix_ref, send_ref):
    parts, count = send_ref.shape[0] + 1, send_ref.shape[1]
    two, mix = [narrowed(rows_ref[count:, :], ref, column_ref[count:, :]) for ref in (two_ref, mix_ref)]
    both = beside(two, mix)
    for k in range(1, parts):
        send_ref[k - 1] = both[(k - 1) * count:k * count]


def swap_kernel(rows_ref, column_ref, swap_ref, pair_ref, send_ref):
    parts, count = pair_ref.shape[0] + 1, pair_ref.shape[1]
    term = narrowed(rows_ref[count:, :], swap_ref, column_ref[count:, :])
    for k in range(1, parts):
        send_ref[k - 1, :count, :] = pair_ref[k - 1]
        send_ref[k - 1, count:, :] = halved(term[(k - 1) * count:k * count])


def keep_kernel(rows_ref, column_ref, own_ref, two_ref, mix_ref, swap_ref, two_out, mix_out, swap_out, labels_ref):
    count = two_out.shape[0]
    width = rows_ref.shape[1]
    for ref, out_ref in ((two_ref, two_out), (mix_ref, mix_out), (swap_ref, swap_out)):
        out_ref[...] = narrowed(rows_ref[:count, :], ref, column_ref[:count, :])
    own, two, mix, swap = [ref[width:width + 1, :] for ref in (own_ref, two_ref, mix_ref, swap_ref)]
    odd = lax.rem(lax.axis_index("blk"), 2) == 1
    labels_ref[...] = jnp.concatenate([own, jnp.where(odd, mix, swap), two, jnp.where(odd, swap, mix)] * 2, axis=0)


def finish_kernel(parts, own_keep, mix_keep, two_keep, swap_keep, *refs):
    own_in, late_in = refs[:parts - 1], refs[parts - 1:2 * (parts - 1)]
    labels_ref, column_ref, out_ref, out, sems = refs[2 * (parts - 1):]
    count = own_keep.shape[0]
    rows = column_ref[:count, :]
    copies = []

    def store(m, term):
        for start in range(0, out.shape[2], LANES):
            part = slice(start, start + LANES)
            out[m, :, part] = jnp.where(rows == labels_ref[m:m + 1, part], term, 0.0)
        copies.append(pltpu.make_async_copy(out.at[m], out_ref.at[m], sems.at[m]))
        copies[-1].start()

    odd = lax.rem(lax.axis_index("blk"), 2) == 1
    store(0, sum([unhalved(ref[...]) for ref in own_in], own_keep[...]))
    pairs = [apart(ref[:count, :]) for ref in late_in]
    store(2, sum([two for two, _ in pairs], two_keep[...]))
    mix = sum([mix for _, mix in pairs], mix_keep[...])
    swap = sum([unhalved(ref[count:, :]) for ref in late_in], swap_keep[...])
    store(1, jnp.where(odd, mix, swap))
    store(3, jnp.where(odd, swap, mix))
    for copy in copies:
        copy.wait()


def whole(*shape):
    return jax.ShapeDtypeStruct(shape, F32)


def call(kernel, out_shape, args, flops, off=0, scratch=(), out_specs=ONCHIP):
    moved = sum(a.size * 4 for a in list(args) + out_shape)
    args = [pltpu.with_memory_space_constraint(a, pltpu.HBM) for a in args[:off]] + list(args[off:])
    return pl.pallas_call(
        kernel,
        out_shape=out_shape,
        in_specs=[OFFCHIP] * off + [ONCHIP] * (len(args) - off),
        out_specs=[out_specs] * len(out_shape),
        scratch_shapes=list(scratch),
        cost_estimate=pl.CostEstimate(flops=flops, bytes_accessed=moved, transcendentals=0),
        compiler_params=pltpu.CompilerParams(vmem_limit_bytes=32 * 1024 * 1024),
    )(*args)


def body(amplitudes, integrals, cd_irrep, ab_irrep, ij_irrep):
    blocks, parts = lax.axis_size("blk"), lax.axis_size("red")
    pairs, depth = amplitudes.shape
    row_count = integrals.shape[0]
    width = depth // 4
    count = row_count // parts
    one_product = 12 * row_count * width * pairs

    def moved(array, steps):
        return lax.ppermute(array, "blk", [(i, (i + steps[i % 4]) % blocks) for i in range(blocks)])

    def exchanged(array):
        return [
            lax.ppermute(array[k - 1], "red", [(i, (i + k) % parts) for i in range(parts)])
            for k in range(1, parts)
        ]

    def after(array, *earlier):
        return lax.optimization_barrier((array, *earlier))[0]

    def staging(array, labels, copies):
        return [
            pltpu.VMEM(array.shape, F32),
            pltpu.VMEM(labels.shape, jnp.int32),
            pltpu.VMEM(cd_irrep.shape, jnp.int32),
        ], pltpu.SemaphoreType.DMA((2 + copies,))

    stage, sems = staging(amplitudes, ij_irrep, 1)
    own, = call(pack_kernel, [whole(width + 8, pairs)], (amplitudes, ij_irrep, cd_irrep),
                4 * amplitudes.size, 3, stage + [sems])
    two = moved(own, (2, 2, 2, 2))
    stage, sems = staging(integrals, ab_irrep, parts)
    rows, labels = call(
        functools.partial(first_kernel, count), [whole(row_count, width), whole(row_count, LANES)],
        (integrals, ab_irrep, cd_irrep), one_product, 3, stage + [pltpu.VMEM((row_count, LANES), F32), sems])
    own_keep, own_send = call(
        own_kernel, [whole(count, LANES), whole(parts - 1, count // 2, LANES)],
        (rows, labels, own), one_product)
    own_in = exchanged(own_send)
    mix = moved(after(own, own_keep), (1, 3, 1, 3))
    swap = moved(after(two, *own_in), (1, -1, 1, -1))
    pair_send, = call(pair_kernel, [whole(parts - 1, count, LANES)], (rows, labels, two, mix), 40 * one_product)
    late_send, = call(swap_kernel, [whole(parts - 1, count + count // 2, LANES)],
                      (rows, labels, swap, pair_send), one_product // 2)
    late_in = exchanged(late_send)
    two_keep, mix_keep, swap_keep, slab_labels = call(
        keep_kernel, [whole(count, LANES)] * 3 + [whole(8, pairs)],
        (rows, labels, own, two, mix, after(swap, late_send)), one_product)
    out, = call(functools.partial(finish_kernel, parts), [whole(4, count, pairs)],
                (own_keep, mix_keep, two_keep, swap_keep, *own_in, *late_in, slab_labels, labels),
                4 * 2 * count * pairs, 0, [pltpu.VMEM((4, count, pairs), F32), pltpu.SemaphoreType.DMA((4,))], OFFCHIP)
    return out


def solution(mesh):
    in_specs = (P("blk", "red"), P("blk", "red"), P("red", None), P("blk", None), P("blk", None))
    out_specs = P(None, ("blk", "red"), None)
    return jax.shard_map(body, mesh=mesh, in_specs=in_specs, out_specs=out_specs, check_vma=False)
```

time: 20.9 us -> 20.8 us (level)
  Pallas kernels: 6.22 us -> 5.36 us
  waiting for transfers between devices: 8.28 us -> 8.93 us
    pallas_call x7, Pallas kernels: 6.22 us -> 5.36 us  [call(): pl.pallas_call(kernel, out_shape=out_shape, in_specs=[OFFCHIP] * off + [O...]
    ppermute x3, waiting for transfers between devices: 3.23 us -> 3.79 us  [moved(): lax.ppermute(array, 'blk', [(i, (i + steps[i % 4]) % blocks) for i in ran...]
  transfers between devices with their start and end apart: 5 -> 5, of which waited for: 5 -> 5; matrix products, arithmetic and copies ran while one was open for 0% -> 0% of each run, Pallas kernels for 15% -> 13%
where the time goes in v8:
time: 20.8 us; the launch traced here: 20.6 us
  waiting for transfers between devices  8.93 us (43%)
  starting transfers between devices  6.22 us (30%)
  Pallas kernels  5.36 us (26%)
    pallas_call x7, Pallas kernels, call(): pl.pallas_call(kernel, out_shape=out_shape, in_specs=[OFFCHIP] * off + [O...  5.36 us
    ppermute x2, waiting for transfers between devices, exchanged(): lax.ppermute(array[k - 1], 'red', [(i, (i + k) % parts) for i in range(pa...  5.14 us
    ppermute x3, waiting for transfers between devices, moved(): lax.ppermute(array, 'blk', [(i, (i + steps[i % 4]) % blocks) for i in ran...  3.79 us
    ppermute x2, starting transfers between devices, exchanged(): lax.ppermute(array[k - 1], 'red', [(i, (i + k) % parts) for i in range(pa...  3.17 us
    ppermute x3, starting transfers between devices, moved(): lax.ppermute(array, 'blk', [(i, (i + steps[i % 4]) % blocks) for i in ran...  3.05 us
  transfers between devices with their start and end apart: 5, of which 5 were waited for; matrix products, arithmetic and copies ran while one was open for 0% of the time, Pallas kernels for 13%

profile of v8, /device:TPU:0, one launch (start us, length us, event | category | flops | bytes accessed | tf_op | source)
XLA Modules:
  0.0 20.6 jit_solution(6626256197734938946)
XLA Ops:
  0.0 1.4 %shard_map.56.own_ref = f32[200,256]{1,0:T(8,128)S(1)} custom-call(f32[256,768]{1,0:T(8,128)} %amp_ref.1, s32[1,256]{1,0:T(1,128)} %ij_ref.1, s32[1,768]{1,0:T(1,128)} %cd_ref.3), custom_call_target="tpu_custom_call" | custom-call | flops 786432 | bytes 995328 | tf_op jit(solution)/shard_map/pallas_call | solution.py:178
  1.4 3.0 %collective-permute-start = (f32[200,256]{1,0:T(8,128)S(1)}, f32[200,256]{1,0:T(8,128)S(1)}, u32[]{:S(2)}, u32[]{:S(2)}) collective-permute-start(f32[200,256]{1,0:T(8,128)S(1)} %shard_map.56.own_ref), channel_id=1, source_target_pairs={{0,4},{2,6},{4,8},{6,10},{8,12},{10,14},{12,16},{14,18},{16,20},{1... | collective-permute-start | bytes 614408 | tf_op jit(solution)/shard_map/ppermute | solution.py:198
  4.4 1.3 %shard_map.55 = (f32[256,192]{1,0:T(8,128)S(1)}, f32[256,128]{1,0:T(8,128)S(1)}) custom-call(f32[256,768]{1,0:T(8,128)} %v_ref.1, s32[1,256]{1,0:T(1,128)} %ab_ref.1, s32[1,768]{1,0:T(1,128)} %cd_ref.3), custom_call_target="tpu_custom_call" | custom-call | flops 150994944 | bytes 1118208 | tf_op jit(solution)/shard_map/pallas_call | solution.py:178
  5.7 0.4 %shard_map.57 = (f32[128,128]{1,0:T(8,128)S(1)}, f32[1,64,128]{2,1,0:T(8,128)S(1)}) custom-call(f32[256,192]{1,0:T(8,128)S(1)} %get-tuple-element.16.rows_ref, f32[256,128]{1,0:T(8,128)S(1)} %get-tuple-element.17.column_ref.refs_3_, f32[200,256]{1,0:T(8,128)S(1)} %shard_map.56.own_ref), custom_call_target="tpu_custom_call" | custom-call | flops 150994944 | bytes 630784 | tf_op jit(solution)/shard_map/pallas_call | solution.py:178
  6.1 0.1 collective-permute-start.1
  6.2 1.6 %collective-permute-start.2 = (f32[64,128]{1,0:T(8,128)S(1)}, f32[64,128]{1,0:T(8,128)S(1)}, u32[]{:S(2)}, u32[]{:S(2)}) collective-permute-start(f32[64,128]{1,0:T(8,128)S(1)} %bitcast.3), channel_id=1, source_target_pairs={{0,1},{1,0},{2,3},{3,2},{4,5},{5,4},{6,7},{7,6},{8,9},{9,8},{10,11... | collective-permute-start | bytes 98312 | tf_op jit(solution)/shard_map/ppermute | solution.py:202
  7.8 2.4 %collective-permute-done.2.refs_0_ = f32[64,128]{1,0:T(8,128)S(1)} collective-permute-done((f32[64,128]{1,0:T(8,128)S(1)}, f32[64,128]{1,0:T(8,128)S(1)}, u32[]{:S(2)}, u32[]{:S(2)}) %collective-permute-start.2) | collective-permute-done | bytes 32800 | tf_op jit(solution)/shard_map/ppermute | solution.py:202
  10.2 2.8 %collective-permute-done.two_ref = f32[200,256]{1,0:T(8,128)S(1)} collective-permute-done((f32[200,256]{1,0:T(8,128)S(1)}, f32[200,256]{1,0:T(8,128)S(1)}, u32[]{:S(2)}, u32[]{:S(2)}) %collective-permute-start) | collective-permute-done | bytes 204832 | tf_op jit(solution)/shard_map/ppermute | solution.py:198
  13.0 0.0 collective-permute-start.3
  13.0 0.2 collective-permute-done.1.mix_ref
  13.2 0.5 %shard_map.58.pair_ref = f32[1,128,128]{2,1,0:T(8,128)S(1)} custom-call(f32[256,192]{1,0:T(8,128)S(1)} %get-tuple-element.16.rows_ref, f32[256,128]{1,0:T(8,128)S(1)} %get-tuple-element.17.column_ref.refs_3_, f32[200,256]{1,0:T(8,128)S(1)} %collective-permute-done.two_ref, f32[200,256]{1,0:T(8,128)S(1)} %collective-permute-done.1.mix_ref), custom_call_target="tpu_custom_call" | custom-call | flops 6039797760 | bytes 802816 | tf_op jit(solution)/shard_map/pallas_call | solution.py:178
  13.6 0.8 %collective-permute-done.3.swap_ref = f32[200,256]{1,0:T(8,128)S(1)} collective-permute-done((f32[200,256]{1,0:T(8,128)S(1)}, f32[200,256]{1,0:T(8,128)S(1)}, u32[]{:S(2)}, u32[]{:S(2)}) %collective-permute-start.3) | collective-permute-done | bytes 204832 | tf_op jit(solution)/shard_map/ppermute | solution.py:198
  14.4 0.3 %shard_map.59 = f32[1,192,128]{2,1,0:T(8,128)S(1)} custom-call(f32[256,192]{1,0:T(8,128)S(1)} %get-tuple-element.16.rows_ref, f32[256,128]{1,0:T(8,128)S(1)} %get-tuple-element.17.column_ref.refs_3_, f32[200,256]{1,0:T(8,128)S(1)} %collective-permute-done.3.swap_ref, f32[1,128,128]{2,1,0:T(8,128)S(1)} %shard_map.58.pair_ref), custom_call_target="tpu_custom_call" | custom-call | flops 75497472 | bytes 696320 | tf_op jit(solution)/shard_map/pallas_call | solution.py:178
  14.8 1.6 %collective-permute-start.4 = (f32[192,128]{1,0:T(8,128)S(1)}, f32[192,128]{1,0:T(8,128)S(1)}, u32[]{:S(2)}, u32[]{:S(2)}) collective-permute-start(f32[192,128]{1,0:T(8,128)S(1)} %bitcast.2), channel_id=1, source_target_pairs={{0,1},{1,0},{2,3},{3,2},{4,5},{5,4},{6,7},{7,6},{8,9},{9,8},{10,11... | collective-permute-start | bytes 294920 | tf_op jit(solution)/shard_map/ppermute | solution.py:202
  16.4 0.6 %shard_map.60 = (f32[128,128]{1,0:T(8,128)S(1)}, f32[128,128]{1,0:T(8,128)S(1)}, f32[128,128]{1,0:T(8,128)S(1)}, f32[8,256]{1,0:T(8,128)S(1)}) custom-call(f32[256,192]{1,0:T(8,128)S(1)} %get-tuple-element.16.rows_ref, f32[256,128]{1,0:T(8,128)S(1)} %get-tuple-element.17.column_ref.refs_3_, f32[200,256]{1,0:T(8,128)S(1)} %shard_map.56.own_ref, ...), custom_call_target="tpu_custom_call" | custom-call | flops 150994944 | bytes 1351680 | tf_op jit(solution)/shard_map/pallas_call | solution.py:178
  16.9 2.8 %collective-permute-done.4.refs_1_ = f32[192,128]{1,0:T(8,128)S(1)} collective-permute-done((f32[192,128]{1,0:T(8,128)S(1)}, f32[192,128]{1,0:T(8,128)S(1)}, u32[]{:S(2)}, u32[]{:S(2)}) %collective-permute-start.4) | collective-permute-done | bytes 98336 | tf_op jit(solution)/shard_map/ppermute | solution.py:202
  19.7 0.9 %shard_map.61 = f32[4,128,256]{2,1,0:T(8,128)} custom-call(f32[128,128]{1,0:T(8,128)S(1)} %get-tuple-element.18.own_keep, f32[128,128]{1,0:T(8,128)S(1)} %get-tuple-element.23.mix_keep, f32[128,128]{1,0:T(8,128)S(1)} %get-tuple-element.24.two_keep, f32[128,128]{1,0:T(8,128)S(1)} %get-tuple-element.25.swap_keep, ...), custom_call_target="tpu_custom_call" | custom-call | flops 262144 | bytes 1056768 | tf_op jit(solution)/shard_map/pallas_call | solution.py:178
Async XLA Ops:
  1.4 11.6 %collective-permute-start = (f32[200,256]{1,0:T(8,128)S(1)}, f32[200,256]{1,0:T(8,128)S(1)}, u32[]{:S(2)}, u32[]{:S(2)}) collective-permute-start(f32[200,256]{1,0:T(8,128)S(1)} %shard_map.56.own_ref), channel_id=1, source_target_pairs={{0,4},{2,6},{4,8},{6,10},{8,12},{10,14},{12,16},{14,18},{16,20},{1... | collective-permute-start | bytes 614408 | tf_op jit(solution)/shard_map/ppermute | solution.py:198
  6.1 7.0 %collective-permute-start.1 = (f32[200,256]{1,0:T(8,128)S(1)}, f32[200,256]{1,0:T(8,128)S(1)}, u32[]{:S(2)}, u32[]{:S(2)}) collective-permute-start(f32[200,256]{1,0:T(8,128)S(1)} %shard_map.56.own_ref), channel_id=1, source_target_pairs={{0,2},{2,8},{4,6},{6,12},{8,10},{10,16},{12,14},{14,20},{16,18},{1... | collective-permute-start | bytes 614408 | tf_op jit(solution)/shard_map/ppermute | solution.py:198
  6.2 4.0 %collective-permute-start.2 = (f32[64,128]{1,0:T(8,128)S(1)}, f32[64,128]{1,0:T(8,128)S(1)}, u32[]{:S(2)}, u32[]{:S(2)}) collective-permute-start(f32[64,128]{1,0:T(8,128)S(1)} %bitcast.3), channel_id=1, source_target_pairs={{0,1},{1,0},{2,3},{3,2},{4,5},{5,4},{6,7},{7,6},{8,9},{9,8},{10,11... | collective-permute-start | bytes 98312 | tf_op jit(solution)/shard_map/ppermute | solution.py:202
  13.0 1.5 %collective-permute-start.3 = (f32[200,256]{1,0:T(8,128)S(1)}, f32[200,256]{1,0:T(8,128)S(1)}, u32[]{:S(2)}, u32[]{:S(2)}) collective-permute-start(f32[200,256]{1,0:T(8,128)S(1)} %collective-permute-done.two_ref), channel_id=1, source_target_pairs={{0,2},{2,0},{4,6},{6,4},{8,10},{10,8},{12,14},{14,12},{16,18},{18,... | collective-permute-start | bytes 614408 | tf_op jit(solution)/shard_map/ppermute | solution.py:198
  14.8 4.9 %collective-permute-start.4 = (f32[192,128]{1,0:T(8,128)S(1)}, f32[192,128]{1,0:T(8,128)S(1)}, u32[]{:S(2)}, u32[]{:S(2)}) collective-permute-start(f32[192,128]{1,0:T(8,128)S(1)} %bitcast.2), channel_id=1, source_target_pairs={{0,1},{1,0},{2,3},{3,2},{4,5},{5,4},{6,7},{7,6},{8,9},{9,8},{10,11... | collective-permute-start | bytes 294920 | tf_op jit(solution)/shard_map/ppermute | solution.py:202

commit v9 on v8

--- a/solution.py
+++ b/solution.py
@@ -116,10 +116,22 @@
         send_ref[k - 1] = halved(term[k * count:(k + 1) * count])
 
 
-def pair_kernel(rows_ref, column_ref, two_ref, mix_ref, send_ref):
+def late_place():
+    return lax.rem(lax.axis_index("blk"), 4) == 2
+
+
+def third_term(part, rows_ref, column_ref, mix_ref, late_ref, out_ref):
+    for ref, here in ((mix_ref, ~late_place()), (late_ref, late_place())):
+
+        @pl.when(here)
+        def _():
+            out_ref[...] = narrowed(rows_ref[part, :], ref, column_ref[part, :])
+
+
+def pair_kernel(rows_ref, column_ref, two_ref, mix_ref, late_ref, send_ref, third):
     parts, count = send_ref.shape[0] + 1, send_ref.shape[1]
-    two, mix = [narrowed(rows_ref[count:, :], ref, column_ref[count:, :]) for ref in (two_ref, mix_ref)]
-    both = beside(two, mix)
+    third_term(slice(count, None), rows_ref, column_ref, mix_ref, late_ref, third)
+    both = beside(narrowed(rows_ref[count:, :], two_ref, column_ref[count:, :]), third[...])
     for k in range(1, parts):
         send_ref[k - 1] = both[(k - 1) * count:k * count]
 
@@ -132,12 +144,14 @@
         send_ref[k - 1, count:, :] = halved(term[(k - 1) * count:k * count])
 
 
-def keep_kernel(rows_ref, column_ref, own_ref, two_ref, mix_ref, swap_ref, two_out, mix_out, swap_out, labels_ref):
+def keep_kernel(rows_ref, column_ref, own_ref, two_ref, mix_ref, late_ref, swap_ref, two_out, mix_out, swap_out, labels_ref):
     count = two_out.shape[0]
     width = rows_ref.shape[1]
-    for ref, out_ref in ((two_ref, two_out), (mix_ref, mix_out), (swap_ref, swap_out)):
+    third_term(slice(0, count), rows_ref, column_ref, mix_ref, late_ref, mix_out)
+    for ref, out_ref in ((two_ref, two_out), (swap_ref, swap_out)):
         out_ref[...] = narrowed(rows_ref[:count, :], ref, column_ref[:count, :])
-    own, two, mix, swap = [ref[width:width + 1, :] for ref in (own_ref, two_ref, mix_ref, swap_ref)]
+    own, two, mix, late, swap = [ref[width:width + 1, :] for ref in (own_ref, two_ref, mix_ref, late_ref, swap_ref)]
+    mix = jnp.where(late_place(), late, mix)
     odd = lax.rem(lax.axis_index("blk"), 2) == 1
     labels_ref[...] = jnp.concatenate([own, jnp.where(odd, mix, swap), two, jnp.where(odd, swap, mix)] * 2, axis=0)
 
@@ -217,6 +231,7 @@
     own, = call(pack_kernel, [whole(width + 8, pairs)], (amplitudes, ij_irrep, cd_irrep),
                 4 * amplitudes.size, 3, stage + [sems])
     two = moved(own, (2, 2, 2, 2))
+    mix = moved(own, (1, 3, 1, -1))
     stage, sems = staging(integrals, ab_irrep, parts)
     rows, labels = call(
         functools.partial(first_kernel, count), [whole(row_count, width), whole(row_count, LANES)],
@@ -225,15 +240,16 @@
         own_kernel, [whole(count, LANES), whole(parts - 1, count // 2, LANES)],
         (rows, labels, own), one_product)
     own_in = exchanged(own_send)
-    mix = moved(after(own, own_keep), (1, 3, 1, 3))
+    late = moved(after(own, own_keep, mix), (1, -1, 1, 3))
     swap = moved(after(two, *own_in), (1, -1, 1, -1))
-    pair_send, = call(pair_kernel, [whole(parts - 1, count, LANES)], (rows, labels, two, mix), 40 * one_product)
+    pair_send, = call(pair_kernel, [whole(parts - 1, count, LANES)], (rows, labels, two, mix, late), one_product, 0,
+                      [pltpu.VMEM((row_count - count, LANES), F32)])
     late_send, = call(swap_kernel, [whole(parts - 1, count + count // 2, LANES)],
                       (rows, labels, swap, pair_send), one_product // 2)
     late_in = exchanged(late_send)
     two_keep, mix_keep, swap_keep, slab_labels = call(
         keep_kernel, [whole(count, LANES)] * 3 + [whole(8, pairs)],
-        (rows, labels, own, two, mix, after(swap, late_send)), one_product)
+        (rows, labels, own, two, mix, late, after(swap, late_send)), one_product)
     out, = call(functools.partial(finish_kernel, parts), [whole(4, count, pairs)],
                 (own_keep, mix_keep, two_keep, swap_keep, *own_in, *late_in, slab_labels, labels),
                 4 * 2 * count * pairs, 0, [pltpu.VMEM((4, count, pairs), F32), pltpu.SemaphoreType.DMA((4,))], OFFCHIP)

time: 20.8 us -> 20.9 us (level)
  waiting for transfers between devices: 8.93 us -> 7.78 us
  starting transfers between devices: 6.22 us -> 7.07 us
  Pallas kernels: 5.36 us -> 5.79 us
    ppermute x2, waiting for transfers between devices: 5.14 us -> 3.33 us  [exchanged(): lax.ppermute(array[k - 1], 'red', [(i, (i + k) % parts) for i in range(pa...]
    ppermute x3 -> x4, waiting for transfers between devices: 3.79 us -> 4.45 us  [moved(): lax.ppermute(array, 'blk', [(i, (i + steps[i % 4]) % blocks) for i in ran...]
    ppermute x3 -> x4, starting transfers between devices: 3.05 us -> 3.7 us  [moved(): lax.ppermute(array, 'blk', [(i, (i + steps[i % 4]) % blocks) for i in ran...]
    pallas_call x7, Pallas kernels: 5.36 us -> 5.79 us  [call(): pl.pallas_call(kernel, out_shape=out_shape, in_specs=[OFFCHIP] * off + [O...]
  transfers between devices with their start and end apart: 5 -> 6, of which waited for: 5 -> 5; matrix products, arithmetic and copies ran while one was open for 0% -> 0% of each run, Pallas kernels for 13% -> 15%
where the time goes in v9:
time: 20.9 us; the launch traced here: 20.7 us
  waiting for transfers between devices  7.78 us (37%)
  starting transfers between devices  7.07 us (34%)
  Pallas kernels  5.79 us (28%)
    pallas_call x7, Pallas kernels, call(): pl.pallas_call(kernel, out_shape=out_shape, in_specs=[OFFCHIP] * off + [O...  5.79 us
    ppermute x4, waiting for transfers between devices, moved(): lax.ppermute(array, 'blk', [(i, (i + steps[i % 4]) % blocks) for i in ran...  4.45 us
    ppermute x4, starting transfers between devices, moved(): lax.ppermute(array, 'blk', [(i, (i + steps[i % 4]) % blocks) for i in ran...  3.7 us
    ppermute x2, starting transfers between devices, exchanged(): lax.ppermute(array[k - 1], 'red', [(i, (i + k) % parts) for i in range(pa...  3.37 us
    ppermute x2, waiting for transfers between devices, exchanged(): lax.ppermute(array[k - 1], 'red', [(i, (i + k) % parts) for i in range(pa...  3.33 us
  transfers between devices with their start and end apart: 6, of which 5 were waited for; matrix products, arithmetic and copies ran while one was open for 0% of the time, Pallas kernels for 15%

profile of v9, /device:TPU:0, one launch (start us, length us, event | category | flops | bytes accessed | tf_op | source)
XLA Modules:
  0.0 20.7 jit_solution(12301007491190593641)
XLA Ops:
  0.0 1.4 %shard_map.56.own_ref = f32[200,256]{1,0:T(8,128)S(1)} custom-call(f32[256,768]{1,0:T(8,128)} %amp_ref.1, s32[1,256]{1,0:T(1,128)} %ij_ref.1, s32[1,768]{1,0:T(1,128)} %cd_ref.3), custom_call_target="tpu_custom_call" | custom-call | flops 786432 | bytes 995328 | tf_op jit(solution)/shard_map/pallas_call | solution.py:192
  1.4 0.5 %collective-permute-start.1 = (f32[200,256]{1,0:T(8,128)S(1)}, f32[200,256]{1,0:T(8,128)S(1)}, u32[]{:S(2)}, u32[]{:S(2)}) collective-permute-start(f32[200,256]{1,0:T(8,128)S(1)} %shard_map.56.own_ref), channel_id=1, source_target_pairs={{0,2},{2,8},{4,6},{6,4},{8,10},{10,16},{12,14},{14,12},{16,18},{18... | collective-permute-start | bytes 614408 | tf_op jit(solution)/shard_map/ppermute | solution.py:212
  1.9 2.6 %collective-permute-start = (f32[200,256]{1,0:T(8,128)S(1)}, f32[200,256]{1,0:T(8,128)S(1)}, u32[]{:S(2)}, u32[]{:S(2)}) collective-permute-start(f32[200,256]{1,0:T(8,128)S(1)} %shard_map.56.own_ref), channel_id=1, source_target_pairs={{0,4},{2,6},{4,8},{6,10},{8,12},{10,14},{12,16},{14,18},{16,20},{1... | collective-permute-start | bytes 614408 | tf_op jit(solution)/shard_map/ppermute | solution.py:212
  4.4 1.3 %shard_map.55 = (f32[256,192]{1,0:T(8,128)S(1)}, f32[256,128]{1,0:T(8,128)S(1)}) custom-call(f32[256,768]{1,0:T(8,128)} %v_ref.1, s32[1,256]{1,0:T(1,128)} %ab_ref.1, s32[1,768]{1,0:T(1,128)} %cd_ref.3), custom_call_target="tpu_custom_call" | custom-call | flops 150994944 | bytes 1118208 | tf_op jit(solution)/shard_map/pallas_call | solution.py:192
  5.7 0.4 %shard_map.57 = (f32[128,128]{1,0:T(8,128)S(1)}, f32[1,64,128]{2,1,0:T(8,128)S(1)}) custom-call(f32[256,192]{1,0:T(8,128)S(1)} %get-tuple-element.16.rows_ref, f32[256,128]{1,0:T(8,128)S(1)} %get-tuple-element.17.column_ref.refs_3_, f32[200,256]{1,0:T(8,128)S(1)} %shard_map.56.own_ref), custom_call_target="tpu_custom_call" | custom-call | flops 150994944 | bytes 630784 | tf_op jit(solution)/shard_map/pallas_call | solution.py:192
  6.2 1.6 %collective-permute-start.3 = (f32[64,128]{1,0:T(8,128)S(1)}, f32[64,128]{1,0:T(8,128)S(1)}, u32[]{:S(2)}, u32[]{:S(2)}) collective-permute-start(f32[64,128]{1,0:T(8,128)S(1)} %bitcast.3), channel_id=1, source_target_pairs={{0,1},{1,0},{2,3},{3,2},{4,5},{5,4},{6,7},{7,6},{8,9},{9,8},{10,11... | collective-permute-start | bytes 98312 | tf_op jit(solution)/shard_map/ppermute | solution.py:216
  7.8 1.6 %collective-permute-done.1.mix_ref = f32[200,256]{1,0:T(8,128)S(1)} collective-permute-done((f32[200,256]{1,0:T(8,128)S(1)}, f32[200,256]{1,0:T(8,128)S(1)}, u32[]{:S(2)}, u32[]{:S(2)}) %collective-permute-start.1) | collective-permute-done | bytes 204832 | tf_op jit(solution)/shard_map/ppermute | solution.py:212
  9.4 0.0 collective-permute-start.2
  9.4 0.8 %collective-permute-done.3.refs_0_ = f32[64,128]{1,0:T(8,128)S(1)} collective-permute-done((f32[64,128]{1,0:T(8,128)S(1)}, f32[64,128]{1,0:T(8,128)S(1)}, u32[]{:S(2)}, u32[]{:S(2)}) %collective-permute-start.3) | collective-permute-done | bytes 32800 | tf_op jit(solution)/shard_map/ppermute | solution.py:216
  10.2 2.4 %collective-permute-done.two_ref = f32[200,256]{1,0:T(8,128)S(1)} collective-permute-done((f32[200,256]{1,0:T(8,128)S(1)}, f32[200,256]{1,0:T(8,128)S(1)}, u32[]{:S(2)}, u32[]{:S(2)}) %collective-permute-start) | collective-permute-done | bytes 204832 | tf_op jit(solution)/shard_map/ppermute | solution.py:212
  12.6 0.6 %collective-permute-start.4 = (f32[200,256]{1,0:T(8,128)S(1)}, f32[200,256]{1,0:T(8,128)S(1)}, u32[]{:S(2)}, u32[]{:S(2)}) collective-permute-start(f32[200,256]{1,0:T(8,128)S(1)} %collective-permute-done.two_ref), channel_id=1, source_target_pairs={{0,2},{2,0},{4,6},{6,4},{8,10},{10,8},{12,14},{14,12},{16,18},{18,... | collective-permute-start | bytes 614408 | tf_op jit(solution)/shard_map/ppermute | solution.py:212
  13.2 0.0 collective-permute-done.2.late_ref
  13.2 0.7 %shard_map.58.pair_ref = f32[1,128,128]{2,1,0:T(8,128)S(1)} custom-call(f32[256,192]{1,0:T(8,128)S(1)} %get-tuple-element.16.rows_ref, f32[256,128]{1,0:T(8,128)S(1)} %get-tuple-element.17.column_ref.refs_3_, f32[200,256]{1,0:T(8,128)S(1)} %collective-permute-done.two_ref, f32[200,256]{1,0:T(8,128)S(1)} %collective-permute-done.1.mix_ref, ...), custom_call_target="tpu_custom_call" | custom-call | flops 150994944 | bytes 1007616 | tf_op jit(solution)/shard_map/pallas_call | solution.py:192
  13.9 0.4 %collective-permute-done.4.swap_ref = f32[200,256]{1,0:T(8,128)S(1)} collective-permute-done((f32[200,256]{1,0:T(8,128)S(1)}, f32[200,256]{1,0:T(8,128)S(1)}, u32[]{:S(2)}, u32[]{:S(2)}) %collective-permute-start.4) | collective-permute-done | bytes 204832 | tf_op jit(solution)/shard_map/ppermute | solution.py:212
  14.3 0.3 %shard_map.59 = f32[1,192,128]{2,1,0:T(8,128)S(1)} custom-call(f32[256,192]{1,0:T(8,128)S(1)} %get-tuple-element.16.rows_ref, f32[256,128]{1,0:T(8,128)S(1)} %get-tuple-element.17.column_ref.refs_3_, f32[200,256]{1,0:T(8,128)S(1)} %collective-permute-done.4.swap_ref, f32[1,128,128]{2,1,0:T(8,128)S(1)} %shard_map.58.pair_ref), custom_call_target="tpu_custom_call" | custom-call | flops 75497472 | bytes 696320 | tf_op jit(solution)/shard_map/pallas_call | solution.py:192
  14.7 1.8 %collective-permute-start.5 = (f32[192,128]{1,0:T(8,128)S(1)}, f32[192,128]{1,0:T(8,128)S(1)}, u32[]{:S(2)}, u32[]{:S(2)}) collective-permute-start(f32[192,128]{1,0:T(8,128)S(1)} %bitcast.2), channel_id=1, source_target_pairs={{0,1},{1,0},{2,3},{3,2},{4,5},{5,4},{6,7},{7,6},{8,9},{9,8},{10,11... | collective-permute-start | bytes 294920 | tf_op jit(solution)/shard_map/ppermute | solution.py:216
  16.4 0.8 %shard_map.60 = (f32[128,128]{1,0:T(8,128)S(1)}, f32[128,128]{1,0:T(8,128)S(1)}, f32[128,128]{1,0:T(8,128)S(1)}, f32[8,256]{1,0:T(8,128)S(1)}) custom-call(f32[256,192]{1,0:T(8,128)S(1)} %get-tuple-element.16.rows_ref, f32[256,128]{1,0:T(8,128)S(1)} %get-tuple-element.17.column_ref.refs_3_, f32[200,256]{1,0:T(8,128)S(1)} %shard_map.56.own_ref, ...), custom_call_target="tpu_custom_call" | custom-call | flops 150994944 | bytes 1556480 | tf_op jit(solution)/shard_map/pallas_call | solution.py:192
  17.2 2.5 %collective-permute-done.5.refs_1_ = f32[192,128]{1,0:T(8,128)S(1)} collective-permute-done((f32[192,128]{1,0:T(8,128)S(1)}, f32[192,128]{1,0:T(8,128)S(1)}, u32[]{:S(2)}, u32[]{:S(2)}) %collective-permute-start.5) | collective-permute-done | bytes 98336 | tf_op jit(solution)/shard_map/ppermute | solution.py:216
  19.8 0.9 %shard_map.61 = f32[4,128,256]{2,1,0:T(8,128)} custom-call(f32[128,128]{1,0:T(8,128)S(1)} %get-tuple-element.18.own_keep, f32[128,128]{1,0:T(8,128)S(1)} %get-tuple-element.23.mix_keep, f32[128,128]{1,0:T(8,128)S(1)} %get-tuple-element.24.two_keep, f32[128,128]{1,0:T(8,128)S(1)} %get-tuple-element.25.swap_keep, ...), custom_call_target="tpu_custom_call" | custom-call | flops 262144 | bytes 1056768 | tf_op jit(solution)/shard_map/pallas_call | solution.py:192
Async XLA Ops:
  1.4 8.0 %collective-permute-start.1 = (f32[200,256]{1,0:T(8,128)S(1)}, f32[200,256]{1,0:T(8,128)S(1)}, u32[]{:S(2)}, u32[]{:S(2)}) collective-permute-start(f32[200,256]{1,0:T(8,128)S(1)} %shard_map.56.own_ref), channel_id=1, source_target_pairs={{0,2},{2,8},{4,6},{6,4},{8,10},{10,16},{12,14},{14,12},{16,18},{18... | collective-permute-start | bytes 614408 | tf_op jit(solution)/shard_map/ppermute | solution.py:212
  1.9 10.7 %collective-permute-start = (f32[200,256]{1,0:T(8,128)S(1)}, f32[200,256]{1,0:T(8,128)S(1)}, u32[]{:S(2)}, u32[]{:S(2)}) collective-permute-start(f32[200,256]{1,0:T(8,128)S(1)} %shard_map.56.own_ref), channel_id=1, source_target_pairs={{0,4},{2,6},{4,8},{6,10},{8,12},{10,14},{12,16},{14,18},{16,20},{1... | collective-permute-start | bytes 614408 | tf_op jit(solution)/shard_map/ppermute | solution.py:212
  6.2 4.0 %collective-permute-start.3 = (f32[64,128]{1,0:T(8,128)S(1)}, f32[64,128]{1,0:T(8,128)S(1)}, u32[]{:S(2)}, u32[]{:S(2)}) collective-permute-start(f32[64,128]{1,0:T(8,128)S(1)} %bitcast.3), channel_id=1, source_target_pairs={{0,1},{1,0},{2,3},{3,2},{4,5},{5,4},{6,7},{7,6},{8,9},{9,8},{10,11... | collective-permute-start | bytes 98312 | tf_op jit(solution)/shard_map/ppermute | solution.py:216
  9.4 3.9 %collective-permute-start.2 = (f32[200,256]{1,0:T(8,128)S(1)}, f32[200,256]{1,0:T(8,128)S(1)}, u32[]{:S(2)}, u32[]{:S(2)}) collective-permute-start(f32[200,256]{1,0:T(8,128)S(1)} %shard_map.56.own_ref), channel_id=1, source_target_pairs={{0,2},{2,0},{4,6},{6,12},{8,10},{10,8},{12,14},{14,20},{16,18},{18... | collective-permute-start | bytes 614408 | tf_op jit(solution)/shard_map/ppermute | solution.py:212
  12.6 1.7 %collective-permute-start.4 = (f32[200,256]{1,0:T(8,128)S(1)}, f32[200,256]{1,0:T(8,128)S(1)}, u32[]{:S(2)}, u32[]{:S(2)}) collective-permute-start(f32[200,256]{1,0:T(8,128)S(1)} %collective-permute-done.two_ref), channel_id=1, source_target_pairs={{0,2},{2,0},{4,6},{6,4},{8,10},{10,8},{12,14},{14,12},{16,18},{18,... | collective-permute-start | bytes 614408 | tf_op jit(solution)/shard_map/ppermute | solution.py:212
  14.7 5.1 %collective-permute-start.5 = (f32[192,128]{1,0:T(8,128)S(1)}, f32[192,128]{1,0:T(8,128)S(1)}, u32[]{:S(2)}, u32[]{:S(2)}) collective-permute-start(f32[192,128]{1,0:T(8,128)S(1)} %bitcast.2), channel_id=1, source_target_pairs={{0,1},{1,0},{2,3},{3,2},{4,5},{5,4},{6,7},{7,6},{8,9},{9,8},{10,11... | collective-permute-start | bytes 294920 | tf_op jit(solution)/shard_map/ppermute | solution.py:216

commit v10 on v9

--- a/solution.py
+++ b/solution.py
@@ -108,6 +108,10 @@
         rows_ref[h, LANES:] = second[:, :width - LANES]
 
 
+def labels_kernel(slab_ref, out_ref):
+    out_ref[...] = slab_ref[slab_ref.shape[0] - 8:, :]
+
+
 def own_kernel(rows_ref, column_ref, own_ref, keep_ref, send_ref):
     count = keep_ref.shape[0]
     term = narrowed(rows_ref[...], own_ref, column_ref[...])
@@ -144,16 +148,16 @@
         send_ref[k - 1, count:, :] = halved(term[(k - 1) * count:k * count])
 
 
-def keep_kernel(rows_ref, column_ref, own_ref, two_ref, mix_ref, late_ref, swap_ref, two_out, mix_out, swap_out, labels_ref):
+def keep_kernel(rows_ref, column_ref, own_labels, two_ref, mix_ref, late_ref, swap_ref, two_out, mix_out, swap_out, labels_ref):
     count = two_out.shape[0]
     width = rows_ref.shape[1]
     third_term(slice(0, count), rows_ref, column_ref, mix_ref, late_ref, mix_out)
     for ref, out_ref in ((two_ref, two_out), (swap_ref, swap_out)):
         out_ref[...] = narrowed(rows_ref[:count, :], ref, column_ref[:count, :])
-    own, two, mix, late, swap = [ref[width:width + 1, :] for ref in (own_ref, two_ref, mix_ref, late_ref, swap_ref)]
+    two, mix, late, swap = [ref[width:width + 1, :] for ref in (two_ref, mix_ref, late_ref, swap_ref)]
     mix = jnp.where(late_place(), late, mix)
     odd = lax.rem(lax.axis_index("blk"), 2) == 1
-    labels_ref[...] = jnp.concatenate([own, jnp.where(odd, mix, swap), two, jnp.where(odd, swap, mix)] * 2, axis=0)
+    labels_ref[...] = jnp.concatenate([own_labels[:1, :], jnp.where(odd, mix, swap), two, jnp.where(odd, swap, mix)] * 2, axis=0)
 
 
 def finish_kernel(parts, own_keep, mix_keep, two_keep, swap_keep, *refs):
@@ -231,11 +235,12 @@
     own, = call(pack_kernel, [whole(width + 8, pairs)], (amplitudes, ij_irrep, cd_irrep),
                 4 * amplitudes.size, 3, stage + [sems])
     two = moved(own, (2, 2, 2, 2))
-    mix = moved(own, (1, 3, 1, -1))
+    own_labels, = call(labels_kernel, [whole(8, pairs)], (own,), 8 * pairs)
+    mix = moved(after(own, own_labels), (1, 3, 1, -1))
     stage, sems = staging(integrals, ab_irrep, parts)
     rows, labels = call(
         functools.partial(first_kernel, count), [whole(row_count, width), whole(row_count, LANES)],
-        (integrals, ab_irrep, cd_irrep), one_product, 3, stage + [pltpu.VMEM((row_count, LANES), F32), sems])
+        (integrals, ab_irrep, cd_irrep), 64 * one_product, 3, stage + [pltpu.VMEM((row_count, LANES), F32), sems])
     own_keep, own_send = call(
         own_kernel, [whole(count, LANES), whole(parts - 1, count // 2, LANES)],
         (rows, labels, own), one_product)
@@ -249,7 +254,7 @@
     late_in = exchanged(late_send)
     two_keep, mix_keep, swap_keep, slab_labels = call(
         keep_kernel, [whole(count, LANES)] * 3 + [whole(8, pairs)],
-        (rows, labels, own, two, mix, late, after(swap, late_send)), one_product)
+        (rows, labels, own_labels, two, mix, late, after(swap, late_send)), one_product)
     out, = call(functools.partial(finish_kernel, parts), [whole(4, count, pairs)],
                 (own_keep, mix_keep, two_keep, swap_keep, *own_in, *late_in, slab_labels, labels),
                 4 * 2 * count * pairs, 0, [pltpu.VMEM((4, count, pairs), F32), pltpu.SemaphoreType.DMA((4,))], OFFCHIP)

time: 20.9 us -> 20.3 us (0.971)
  starting transfers between devices: 7.07 us -> 6.17 us
  waiting for transfers between devices: 7.78 us -> 8.08 us
    ppermute x4, waiting for transfers between devices: 4.45 us -> 5.56 us  [moved(): lax.ppermute(array, 'blk', [(i, (i + steps[i % 4]) % blocks) for i in ran...]
    ppermute x2, waiting for transfers between devices: 3.33 us -> 2.52 us  [exchanged(): lax.ppermute(array[k - 1], 'red', [(i, (i + k) % parts) for i in range(pa...]
    ppermute x4, starting transfers between devices: 3.7 us -> 3 us  [moved(): lax.ppermute(array, 'blk', [(i, (i + steps[i % 4]) % blocks) for i in ran...]
    pallas_call x7 -> x8, Pallas kernels: 5.79 us -> 5.79 us  [call(): pl.pallas_call(kernel, out_shape=out_shape, in_specs=[OFFCHIP] * off + [O...]
  transfers between devices with their start and end apart: 6 -> 6, of which waited for: 5 -> 5; matrix products, arithmetic and copies ran while one was open for 0% -> 0% of each run, Pallas kernels for 15% -> 16%
where the time goes in v10:
time: 20.3 us; the launch traced here: 20.1 us
  waiting for transfers between devices  8.08 us (40%)
  starting transfers between devices  6.17 us (30%)
  Pallas kernels  5.79 us (29%)
    pallas_call x8, Pallas kernels, call(): pl.pallas_call(kernel, out_shape=out_shape, in_specs=[OFFCHIP] * off + [O...  5.79 us
    ppermute x4, waiting for transfers between devices, moved(): lax.ppermute(array, 'blk', [(i, (i + steps[i % 4]) % blocks) for i in ran...  5.56 us
    ppermute x2, starting transfers between devices, exchanged(): lax.ppermute(array[k - 1], 'red', [(i, (i + k) % parts) for i in range(pa...  3.17 us
    ppermute x4, starting transfers between devices, moved(): lax.ppermute(array, 'blk', [(i, (i + steps[i % 4]) % blocks) for i in ran...  3 us
    ppermute x2, waiting for transfers between devices, exchanged(): lax.ppermute(array[k - 1], 'red', [(i, (i + k) % parts) for i in range(pa...  2.52 us
  transfers between devices with their start and end apart: 6, of which 5 were waited for; matrix products, arithmetic and copies ran while one was open for 0% of the time, Pallas kernels for 16%

profile of v10, /device:TPU:0, one launch (start us, length us, event | category | flops | bytes accessed | tf_op | source)
XLA Modules:
  0.0 20.1 jit_solution(766883568474704102)
XLA Ops:
  0.0 1.4 %shard_map.56.own_ref.slab_ref = f32[200,256]{1,0:T(8,128)S(1)} custom-call(f32[256,768]{1,0:T(8,128)} %amp_ref.1, s32[1,256]{1,0:T(1,128)} %ij_ref.1, s32[1,768]{1,0:T(1,128)} %cd_ref.3), custom_call_target="tpu_custom_call" | custom-call | flops 786432 | bytes 995328 | tf_op jit(solution)/shard_map/pallas_call | solution.py:196
  1.4 3.0 %collective-permute-start = (f32[200,256]{1,0:T(8,128)S(1)}, f32[200,256]{1,0:T(8,128)S(1)}, u32[]{:S(2)}, u32[]{:S(2)}) collective-permute-start(f32[200,256]{1,0:T(8,128)S(1)} %shard_map.56.own_ref.slab_ref), channel_id=1, source_target_pairs={{0,4},{2,6},{4,8},{6,10},{8,12},{10,14},{12,16},{14,18},{16,20},{1... | collective-permute-start | bytes 614408 | tf_op jit(solution)/shard_map/ppermute | solution.py:216
  4.4 0.0 collective-permute-start.1
  4.4 1.3 %shard_map.55 = (f32[256,192]{1,0:T(8,128)S(1)}, f32[256,128]{1,0:T(8,128)S(1)}) custom-call(f32[256,768]{1,0:T(8,128)} %v_ref.1, s32[1,256]{1,0:T(1,128)} %ab_ref.1, s32[1,768]{1,0:T(1,128)} %cd_ref.3), custom_call_target="tpu_custom_call" | custom-call | flops 9663676416 | bytes 1118208 | tf_op jit(solution)/shard_map/pallas_call | solution.py:196
  5.7 0.4 %shard_map.57 = (f32[128,128]{1,0:T(8,128)S(1)}, f32[1,64,128]{2,1,0:T(8,128)S(1)}) custom-call(f32[256,192]{1,0:T(8,128)S(1)} %get-tuple-element.17.rows_ref, f32[256,128]{1,0:T(8,128)S(1)} %get-tuple-element.18.column_ref.refs_3_, f32[200,256]{1,0:T(8,128)S(1)} %shard_map.56.own_ref.slab_ref), custom_call_target="tpu_custom_call" | custom-call | flops 150994944 | bytes 630784 | tf_op jit(solution)/shard_map/pallas_call | solution.py:196
  6.1 1.6 %collective-permute-start.3 = (f32[64,128]{1,0:T(8,128)S(1)}, f32[64,128]{1,0:T(8,128)S(1)}, u32[]{:S(2)}, u32[]{:S(2)}) collective-permute-start(f32[64,128]{1,0:T(8,128)S(1)} %bitcast.3), channel_id=1, source_target_pairs={{0,1},{1,0},{2,3},{3,2},{4,5},{5,4},{6,7},{7,6},{8,9},{9,8},{10,11... | collective-permute-start | bytes 98312 | tf_op jit(solution)/shard_map/ppermute | solution.py:220
  7.7 3.7 %collective-permute-done.1.mix_ref = f32[200,256]{1,0:T(8,128)S(1)} collective-permute-done((f32[200,256]{1,0:T(8,128)S(1)}, f32[200,256]{1,0:T(8,128)S(1)}, u32[]{:S(2)}, u32[]{:S(2)}) %collective-permute-start.1) | collective-permute-done | bytes 204832 | tf_op jit(solution)/shard_map/ppermute | solution.py:216
  11.4 0.0 collective-permute-start.2
  11.4 0.0 collective-permute-done.3.refs_0_
  11.4 1.1 %collective-permute-done.two_ref = f32[200,256]{1,0:T(8,128)S(1)} collective-permute-done((f32[200,256]{1,0:T(8,128)S(1)}, f32[200,256]{1,0:T(8,128)S(1)}, u32[]{:S(2)}, u32[]{:S(2)}) %collective-permute-start) | collective-permute-done | bytes 204832 | tf_op jit(solution)/shard_map/ppermute | solution.py:216
  12.5 0.0 collective-permute-start.4
  12.5 0.3 %collective-permute-done.2.late_ref = f32[200,256]{1,0:T(8,128)S(1)} collective-permute-done((f32[200,256]{1,0:T(8,128)S(1)}, f32[200,256]{1,0:T(8,128)S(1)}, u32[]{:S(2)}, u32[]{:S(2)}) %collective-permute-start.2) | collective-permute-done | bytes 204832 | tf_op jit(solution)/shard_map/ppermute | solution.py:216
  12.8 0.7 %shard_map.59.pair_ref = f32[1,128,128]{2,1,0:T(8,128)S(1)} custom-call(f32[256,192]{1,0:T(8,128)S(1)} %get-tuple-element.17.rows_ref, f32[256,128]{1,0:T(8,128)S(1)} %get-tuple-element.18.column_ref.refs_3_, f32[200,256]{1,0:T(8,128)S(1)} %collective-permute-done.two_ref, f32[200,256]{1,0:T(8,128)S(1)} %collective-permute-done.1.mix_ref, ...), custom_call_target="tpu_custom_call" | custom-call | flops 150994944 | bytes 1007616 | tf_op jit(solution)/shard_map/pallas_call | solution.py:196
  13.5 0.5 %collective-permute-done.4.swap_ref = f32[200,256]{1,0:T(8,128)S(1)} collective-permute-done((f32[200,256]{1,0:T(8,128)S(1)}, f32[200,256]{1,0:T(8,128)S(1)}, u32[]{:S(2)}, u32[]{:S(2)}) %collective-permute-start.4) | collective-permute-done | bytes 204832 | tf_op jit(solution)/shard_map/ppermute | solution.py:216
  13.9 0.3 %shard_map.60 = f32[1,192,128]{2,1,0:T(8,128)S(1)} custom-call(f32[256,192]{1,0:T(8,128)S(1)} %get-tuple-element.17.rows_ref, f32[256,128]{1,0:T(8,128)S(1)} %get-tuple-element.18.column_ref.refs_3_, f32[200,256]{1,0:T(8,128)S(1)} %collective-permute-done.4.swap_ref, f32[1,128,128]{2,1,0:T(8,128)S(1)} %shard_map.59.pair_ref), custom_call_target="tpu_custom_call" | custom-call | flops 75497472 | bytes 696320 | tf_op jit(solution)/shard_map/pallas_call | solution.py:196
  14.3 1.6 %collective-permute-start.5 = (f32[192,128]{1,0:T(8,128)S(1)}, f32[192,128]{1,0:T(8,128)S(1)}, u32[]{:S(2)}, u32[]{:S(2)}) collective-permute-start(f32[192,128]{1,0:T(8,128)S(1)} %bitcast.2), channel_id=1, source_target_pairs={{0,1},{1,0},{2,3},{3,2},{4,5},{5,4},{6,7},{7,6},{8,9},{9,8},{10,11... | collective-permute-start | bytes 294920 | tf_op jit(solution)/shard_map/ppermute | solution.py:220
  15.9 0.8 %shard_map.61 = (f32[128,128]{1,0:T(8,128)S(1)}, f32[128,128]{1,0:T(8,128)S(1)}, f32[128,128]{1,0:T(8,128)S(1)}, f32[8,256]{1,0:T(8,128)S(1)}) custom-call(f32[256,192]{1,0:T(8,128)S(1)} %get-tuple-element.17.rows_ref, f32[256,128]{1,0:T(8,128)S(1)} %get-tuple-element.18.column_ref.refs_3_, f32[8,256]{1,0:T(8,128)S(1)} %shard_map.58.own_labels, ...), custom_call_target="tpu_custom_call" | custom-call | flops 150994944 | bytes 1359872 | tf_op jit(solution)/shard_map/pallas_call | solution.py:196
  16.7 2.5 %collective-permute-done.5.refs_1_ = f32[192,128]{1,0:T(8,128)S(1)} collective-permute-done((f32[192,128]{1,0:T(8,128)S(1)}, f32[192,128]{1,0:T(8,128)S(1)}, u32[]{:S(2)}, u32[]{:S(2)}) %collective-permute-start.5) | collective-permute-done | bytes 98336 | tf_op jit(solution)/shard_map/ppermute | solution.py:220
  19.2 0.9 %shard_map.62 = f32[4,128,256]{2,1,0:T(8,128)} custom-call(f32[128,128]{1,0:T(8,128)S(1)} %get-tuple-element.19.own_keep, f32[128,128]{1,0:T(8,128)S(1)} %get-tuple-element.25.mix_keep, f32[128,128]{1,0:T(8,128)S(1)} %get-tuple-element.26.two_keep, f32[128,128]{1,0:T(8,128)S(1)} %get-tuple-element.27.swap_keep, ...), custom_call_target="tpu_custom_call" | custom-call | flops 262144 | bytes 1056768 | tf_op jit(solution)/shard_map/pallas_call | solution.py:196
  (1 shorter events, 0.0 us)
Async XLA Ops:
  1.4 11.1 %collective-permute-start = (f32[200,256]{1,0:T(8,128)S(1)}, f32[200,256]{1,0:T(8,128)S(1)}, u32[]{:S(2)}, u32[]{:S(2)}) collective-permute-start(f32[200,256]{1,0:T(8,128)S(1)} %shard_map.56.own_ref.slab_ref), channel_id=1, source_target_pairs={{0,4},{2,6},{4,8},{6,10},{8,12},{10,14},{12,16},{14,18},{16,20},{1... | collective-permute-start | bytes 614408 | tf_op jit(solution)/shard_map/ppermute | solution.py:216
  4.4 7.0 %collective-permute-start.1 = (f32[200,256]{1,0:T(8,128)S(1)}, f32[200,256]{1,0:T(8,128)S(1)}, u32[]{:S(2)}, u32[]{:S(2)}) collective-permute-start(f32[200,256]{1,0:T(8,128)S(1)} %shard_map.56.own_ref.slab_ref), channel_id=1, source_target_pairs={{0,2},{2,8},{4,6},{6,4},{8,10},{10,16},{12,14},{14,12},{16,18},{18... | collective-permute-start | bytes 614408 | tf_op jit(solution)/shard_map/ppermute | solution.py:216
  6.1 5.2 %collective-permute-start.3 = (f32[64,128]{1,0:T(8,128)S(1)}, f32[64,128]{1,0:T(8,128)S(1)}, u32[]{:S(2)}, u32[]{:S(2)}) collective-permute-start(f32[64,128]{1,0:T(8,128)S(1)} %bitcast.3), channel_id=1, source_target_pairs={{0,1},{1,0},{2,3},{3,2},{4,5},{5,4},{6,7},{7,6},{8,9},{9,8},{10,11... | collective-permute-start | bytes 98312 | tf_op jit(solution)/shard_map/ppermute | solution.py:220
  11.4 1.5 %collective-permute-start.2 = (f32[200,256]{1,0:T(8,128)S(1)}, f32[200,256]{1,0:T(8,128)S(1)}, u32[]{:S(2)}, u32[]{:S(2)}) collective-permute-start(f32[200,256]{1,0:T(8,128)S(1)} %shard_map.56.own_ref.slab_ref), channel_id=1, source_target_pairs={{0,2},{2,0},{4,6},{6,12},{8,10},{10,8},{12,14},{14,20},{16,18},{18... | collective-permute-start | bytes 614408 | tf_op jit(solution)/shard_map/ppermute | solution.py:216
  12.5 1.5 %collective-permute-start.4 = (f32[200,256]{1,0:T(8,128)S(1)}, f32[200,256]{1,0:T(8,128)S(1)}, u32[]{:S(2)}, u32[]{:S(2)}) collective-permute-start(f32[200,256]{1,0:T(8,128)S(1)} %collective-permute-done.two_ref), channel_id=1, source_target_pairs={{0,2},{2,0},{4,6},{6,4},{8,10},{10,8},{12,14},{14,12},{16,18},{18,... | collective-permute-start | bytes 614408 | tf_op jit(solution)/shard_map/ppermute | solution.py:216
  14.3 4.9 %collective-permute-start.5 = (f32[192,128]{1,0:T(8,128)S(1)}, f32[192,128]{1,0:T(8,128)S(1)}, u32[]{:S(2)}, u32[]{:S(2)}) collective-permute-start(f32[192,128]{1,0:T(8,128)S(1)} %bitcast.2), channel_id=1, source_target_pairs={{0,1},{1,0},{2,3},{3,2},{4,5},{5,4},{6,7},{7,6},{8,9},{9,8},{10,11... | collective-permute-start | bytes 294920 | tf_op jit(solution)/shard_map/ppermute | solution.py:220

commit v11 on v10

--- a/solution.py
+++ b/solution.py
@@ -124,20 +124,20 @@
     return lax.rem(lax.axis_index("blk"), 4) == 2
 
 
-def third_term(part, rows_ref, column_ref, mix_ref, late_ref, out_ref):
+def near_kernel(rows_ref, column_ref, near_ref, out_ref):
+    count = rows_ref.shape[0] - out_ref.shape[0]
+    out_ref[...] = narrowed(rows_ref[count:, :], near_ref, column_ref[count:, :])
+
+
+def pair_kernel(rows_ref, column_ref, near_ref, mix_ref, late_ref, send_ref):
+    parts, count = send_ref.shape[0] + 1, send_ref.shape[1]
     for ref, here in ((mix_ref, ~late_place()), (late_ref, late_place())):
 
         @pl.when(here)
         def _():
-            out_ref[...] = narrowed(rows_ref[part, :], ref, column_ref[part, :])
-
-
-def pair_kernel(rows_ref, column_ref, two_ref, mix_ref, late_ref, send_ref, third):
-    parts, count = send_ref.shape[0] + 1, send_ref.shape[1]
-    third_term(slice(count, None), rows_ref, column_ref, mix_ref, late_ref, third)
-    both = beside(narrowed(rows_ref[count:, :], two_ref, column_ref[count:, :]), third[...])
-    for k in range(1, parts):
-        send_ref[k - 1] = both[(k - 1) * count:k * count]
+            both = beside(near_ref[...], narrowed(rows_ref[count:, :], ref, column_ref[count:, :]))
+            for k in range(1, parts):
+                send_ref[k - 1] = both[(k - 1) * count:k * count]
 
 
 def swap_kernel(rows_ref, column_ref, swap_ref, pair_ref, send_ref):
@@ -148,19 +148,24 @@
         send_ref[k - 1, count:, :] = halved(term[(k - 1) * count:k * count])
 
 
-def keep_kernel(rows_ref, column_ref, own_labels, two_ref, mix_ref, late_ref, swap_ref, two_out, mix_out, swap_out, labels_ref):
-    count = two_out.shape[0]
+def keep_kernel(rows_ref, column_ref, own_labels, near_ref, mix_ref, late_ref, swap_ref, near_out, mix_out, swap_out, labels_ref):
+    count = near_out.shape[0]
     width = rows_ref.shape[1]
-    third_term(slice(0, count), rows_ref, column_ref, mix_ref, late_ref, mix_out)
-    for ref, out_ref in ((two_ref, two_out), (swap_ref, swap_out)):
-        out_ref[...] = narrowed(rows_ref[:count, :], ref, column_ref[:count, :])
-    two, mix, late, swap = [ref[width:width + 1, :] for ref in (two_ref, mix_ref, late_ref, swap_ref)]
+    rows, labels = rows_ref[:count, :], column_ref[:count, :]
+    for ref, out_ref in ((near_ref, near_out), (mix_ref, mix_out), (swap_ref, swap_out)):
+        out_ref[...] = narrowed(rows, ref, labels)
+
+    @pl.when(late_place())
+    def _():
+        mix_out[...] = narrowed(rows, late_ref, labels)
+
+    near, mix, late, swap = [ref[width:width + 1, :] for ref in (near_ref, mix_ref, late_ref, swap_ref)]
     mix = jnp.where(late_place(), late, mix)
     odd = lax.rem(lax.axis_index("blk"), 2) == 1
-    labels_ref[...] = jnp.concatenate([own_labels[:1, :], jnp.where(odd, mix, swap), two, jnp.where(odd, swap, mix)] * 2, axis=0)
-
-
-def finish_kernel(parts, own_keep, mix_keep, two_keep, swap_keep, *refs):
+    labels_ref[...] = jnp.concatenate([own_labels[:1, :], jnp.where(odd, mix, near), swap, jnp.where(odd, near, mix)] * 2, axis=0)
+
+
+def finish_kernel(parts, own_keep, near_keep, mix_keep, swap_keep, *refs):
     own_in, late_in = refs[:parts - 1], refs[parts - 1:2 * (parts - 1)]
     labels_ref, column_ref, out_ref, out, sems = refs[2 * (parts - 1):]
     count = own_keep.shape[0]
@@ -176,12 +181,12 @@
 
     odd = lax.rem(lax.axis_index("blk"), 2) == 1
     store(0, sum([unhalved(ref[...]) for ref in own_in], own_keep[...]))
+    store(2, sum([unhalved(ref[count:, :]) for ref in late_in], swap_keep[...]))
     pairs = [apart(ref[:count, :]) for ref in late_in]
-    store(2, sum([two for two, _ in pairs], two_keep[...]))
+    near = sum([near for near, _ in pairs], near_keep[...])
     mix = sum([mix for _, mix in pairs], mix_keep[...])
-    swap = sum([unhalved(ref[count:, :]) for ref in late_in], swap_keep[...])
-    store(1, jnp.where(odd, mix, swap))
-    store(3, jnp.where(odd, swap, mix))
+    store(1, jnp.where(odd, mix, near))
+    store(3, jnp.where(odd, near, mix))
     for copy in copies:
         copy.wait()
 
@@ -234,7 +239,7 @@
     stage, sems = staging(amplitudes, ij_irrep, 1)
     own, = call(pack_kernel, [whole(width + 8, pairs)], (amplitudes, ij_irrep, cd_irrep),
                 4 * amplitudes.size, 3, stage + [sems])
-    two = moved(own, (2, 2, 2, 2))
+    near = moved(own, (3, 1, 3, 1))
     own_labels, = call(labels_kernel, [whole(8, pairs)], (own,), 8 * pairs)
     mix = moved(after(own, own_labels), (1, 3, 1, -1))
     stage, sems = staging(integrals, ab_irrep, parts)
@@ -246,17 +251,17 @@
         (rows, labels, own), one_product)
     own_in = exchanged(own_send)
     late = moved(after(own, own_keep, mix), (1, -1, 1, 3))
-    swap = moved(after(two, *own_in), (1, -1, 1, -1))
-    pair_send, = call(pair_kernel, [whole(parts - 1, count, LANES)], (rows, labels, two, mix, late), one_product, 0,
-                      [pltpu.VMEM((row_count - count, LANES), F32)])
+    swap = moved(after(near, *own_in), (1, -1, 1, -1))
+    near_term, = call(near_kernel, [whole(row_count - count, LANES)], (rows, labels, near), one_product)
+    pair_send, = call(pair_kernel, [whole(parts - 1, count, LANES)], (rows, labels, near_term, mix, late), one_product)
     late_send, = call(swap_kernel, [whole(parts - 1, count + count // 2, LANES)],
-                      (rows, labels, swap, pair_send), one_product // 2)
+                      (rows, labels, swap, pair_send), one_product)
     late_in = exchanged(late_send)
-    two_keep, mix_keep, swap_keep, slab_labels = call(
+    near_keep, mix_keep, swap_keep, slab_labels = call(
         keep_kernel, [whole(count, LANES)] * 3 + [whole(8, pairs)],
-        (rows, labels, own_labels, two, mix, late, after(swap, late_send)), one_product)
+        (rows, labels, own_labels, near, mix, late, after(swap, late_send)), one_product)
     out, = call(functools.partial(finish_kernel, parts), [whole(4, count, pairs)],
-                (own_keep, mix_keep, two_keep, swap_keep, *own_in, *late_in, slab_labels, labels),
+                (own_keep, near_keep, mix_keep, swap_keep, *own_in, *late_in, slab_labels, labels),
                 4 * 2 * count * pairs, 0, [pltpu.VMEM((4, count, pairs), F32), pltpu.SemaphoreType.DMA((4,))], OFFCHIP)
     return out
 

time: 20.3 us -> 20.5 us (level)
  starting transfers between devices: 6.17 us -> 7.71 us
  waiting for transfers between devices: 8.08 us -> 6.97 us
  Pallas kernels: 5.79 us -> 5.57 us
    ppermute x4, waiting for transfers between devices: 5.56 us -> 4.22 us  [moved(): lax.ppermute(array, 'blk', [(i, (i + steps[i % 4]) % blocks) for i in ran...]
    ppermute x2, starting transfers between devices: 3.17 us -> 3.95 us  [exchanged(): lax.ppermute(array[k - 1], 'red', [(i, (i + k) % parts) for i in range(pa...]
    ppermute x4, starting transfers between devices: 3 us -> 3.76 us  [moved(): lax.ppermute(array, 'blk', [(i, (i + steps[i % 4]) % blocks) for i in ran...]
    ppermute x2, waiting for transfers between devices: 2.52 us -> 2.75 us  [exchanged(): lax.ppermute(array[k - 1], 'red', [(i, (i + k) % parts) for i in range(pa...]
    pallas_call x8 -> x9, Pallas kernels: 5.79 us -> 5.57 us  [call(): pl.pallas_call(kernel, out_shape=out_shape, in_specs=[OFFCHIP] * off + [O...]
  transfers between devices with their start and end apart: 6 -> 6, of which waited for: 5 -> 4; matrix products, arithmetic and copies ran while one was open for 0% -> 0% of each run, Pallas kernels for 16% -> 15%
where the time goes in v11:
time: 20.5 us; the launch traced here: 20.3 us
  starting transfers between devices  7.71 us (38%)
  waiting for transfers between devices  6.97 us (34%)
  Pallas kernels  5.57 us (27%)
    pallas_call x9, Pallas kernels, call(): pl.pallas_call(kernel, out_shape=out_shape, in_specs=[OFFCHIP] * off + [O...  5.57 us
    ppermute x4, waiting for transfers between devices, moved(): lax.ppermute(array, 'blk', [(i, (i + steps[i % 4]) % blocks) for i in ran...  4.22 us
    ppermute x2, starting transfers between devices, exchanged(): lax.ppermute(array[k - 1], 'red', [(i, (i + k) % parts) for i in range(pa...  3.95 us
    ppermute x4, starting transfers between devices, moved(): lax.ppermute(array, 'blk', [(i, (i + steps[i % 4]) % blocks) for i in ran...  3.76 us
    ppermute x2, waiting for transfers between devices, exchanged(): lax.ppermute(array[k - 1], 'red', [(i, (i + k) % parts) for i in range(pa...  2.75 us
  transfers between devices with their start and end apart: 6, of which 4 were waited for; matrix products, arithmetic and copies ran while one was open for 0% of the time, Pallas kernels for 15%

profile of v11, /device:TPU:0, one launch (start us, length us, event | category | flops | bytes accessed | tf_op | source)
XLA Modules:
  0.0 20.3 jit_solution(3918223325040504490)
XLA Ops:
  0.0 1.4 %shard_map.56.own_ref.slab_ref = f32[200,256]{1,0:T(8,128)S(1)} custom-call(f32[256,768]{1,0:T(8,128)} %amp_ref.1, s32[1,256]{1,0:T(1,128)} %ij_ref.1, s32[1,768]{1,0:T(1,128)} %cd_ref.3), custom_call_target="tpu_custom_call" | custom-call | flops 786432 | bytes 995328 | tf_op jit(solution)/shard_map/pallas_call | solution.py:201
  1.4 2.4 %collective-permute-start = (f32[200,256]{1,0:T(8,128)S(1)}, f32[200,256]{1,0:T(8,128)S(1)}, u32[]{:S(2)}, u32[]{:S(2)}) collective-permute-start(f32[200,256]{1,0:T(8,128)S(1)} %shard_map.56.own_ref.slab_ref), channel_id=1, source_target_pairs={{0,6},{2,4},{4,10},{6,8},{8,14},{10,12},{12,18},{14,16},{16,22},{1... | collective-permute-start | bytes 614408 | tf_op jit(solution)/shard_map/ppermute | solution.py:221
  3.8 0.7 %collective-permute-start.1 = (f32[200,256]{1,0:T(8,128)S(1)}, f32[200,256]{1,0:T(8,128)S(1)}, u32[]{:S(2)}, u32[]{:S(2)}) collective-permute-start(f32[200,256]{1,0:T(8,128)S(1)} %shard_map.56.own_ref.slab_ref), channel_id=1, source_target_pairs={{0,2},{2,8},{4,6},{6,4},{8,10},{10,16},{12,14},{14,12},{16,18},{18... | collective-permute-start | bytes 614408 | tf_op jit(solution)/shard_map/ppermute | solution.py:221
  4.5 1.3 %shard_map.55 = (f32[256,192]{1,0:T(8,128)S(1)}, f32[256,128]{1,0:T(8,128)S(1)}) custom-call(f32[256,768]{1,0:T(8,128)} %v_ref.1, s32[1,256]{1,0:T(1,128)} %ab_ref.1, s32[1,768]{1,0:T(1,128)} %cd_ref.3), custom_call_target="tpu_custom_call" | custom-call | flops 9663676416 | bytes 1118208 | tf_op jit(solution)/shard_map/pallas_call | solution.py:201
  5.8 0.4 %shard_map.57 = (f32[128,128]{1,0:T(8,128)S(1)}, f32[1,64,128]{2,1,0:T(8,128)S(1)}) custom-call(f32[256,192]{1,0:T(8,128)S(1)} %get-tuple-element.17.rows_ref, f32[256,128]{1,0:T(8,128)S(1)} %get-tuple-element.18.column_ref.refs_3_, f32[200,256]{1,0:T(8,128)S(1)} %shard_map.56.own_ref.slab_ref), custom_call_target="tpu_custom_call" | custom-call | flops 150994944 | bytes 630784 | tf_op jit(solution)/shard_map/pallas_call | solution.py:201
  6.2 1.6 %collective-permute-start.3 = (f32[64,128]{1,0:T(8,128)S(1)}, f32[64,128]{1,0:T(8,128)S(1)}, u32[]{:S(2)}, u32[]{:S(2)}) collective-permute-start(f32[64,128]{1,0:T(8,128)S(1)} %bitcast.3), channel_id=1, source_target_pairs={{0,1},{1,0},{2,3},{3,2},{4,5},{5,4},{6,7},{7,6},{8,9},{9,8},{10,11... | collective-permute-start | bytes 98312 | tf_op jit(solution)/shard_map/ppermute | solution.py:225
  7.8 3.3 %collective-permute-done.1.mix_ref = f32[200,256]{1,0:T(8,128)S(1)} collective-permute-done((f32[200,256]{1,0:T(8,128)S(1)}, f32[200,256]{1,0:T(8,128)S(1)}, u32[]{:S(2)}, u32[]{:S(2)}) %collective-permute-start.1) | collective-permute-done | bytes 204832 | tf_op jit(solution)/shard_map/ppermute | solution.py:221
  11.1 0.0 collective-permute-start.2
  11.1 0.0 collective-permute-done.3.refs_0_
  11.2 0.5 %collective-permute-done.near_ref = f32[200,256]{1,0:T(8,128)S(1)} collective-permute-done((f32[200,256]{1,0:T(8,128)S(1)}, f32[200,256]{1,0:T(8,128)S(1)}, u32[]{:S(2)}, u32[]{:S(2)}) %collective-permute-start) | collective-permute-done | bytes 204832 | tf_op jit(solution)/shard_map/ppermute | solution.py:221
  11.7 0.7 %collective-permute-start.4 = (f32[200,256]{1,0:T(8,128)S(1)}, f32[200,256]{1,0:T(8,128)S(1)}, u32[]{:S(2)}, u32[]{:S(2)}) collective-permute-start(f32[200,256]{1,0:T(8,128)S(1)} %collective-permute-done.near_ref), channel_id=1, source_target_pairs={{0,2},{2,0},{4,6},{6,4},{8,10},{10,8},{12,14},{14,12},{16,18},{18,... | collective-permute-start | bytes 614408 | tf_op jit(solution)/shard_map/ppermute | solution.py:221
  12.3 0.3 %shard_map.59.near_ref = f32[128,128]{1,0:T(8,128)S(1)} custom-call(f32[256,192]{1,0:T(8,128)S(1)} %get-tuple-element.17.rows_ref, f32[256,128]{1,0:T(8,128)S(1)} %get-tuple-element.18.column_ref.refs_3_, f32[200,256]{1,0:T(8,128)S(1)} %collective-permute-done.near_ref), custom_call_target="tpu_custom_call" | custom-call | flops 150994944 | bytes 598016 | tf_op jit(solution)/shard_map/pallas_call | solution.py:201
  12.7 0.0 collective-permute-done.2.late_ref
  12.7 0.3 %shard_map.60.pair_ref = f32[1,128,128]{2,1,0:T(8,128)S(1)} custom-call(f32[256,192]{1,0:T(8,128)S(1)} %get-tuple-element.17.rows_ref, f32[256,128]{1,0:T(8,128)S(1)} %get-tuple-element.18.column_ref.refs_3_, f32[128,128]{1,0:T(8,128)S(1)} %shard_map.59.near_ref, f32[200,256]{1,0:T(8,128)S(1)} %collective-permute-done.1.mix_ref, ...), custom_call_target="tpu_custom_call" | custom-call | flops 150994944 | bytes 868352 | tf_op jit(solution)/shard_map/pallas_call | solution.py:201
  13.0 0.4 %collective-permute-done.4.swap_ref = f32[200,256]{1,0:T(8,128)S(1)} collective-permute-done((f32[200,256]{1,0:T(8,128)S(1)}, f32[200,256]{1,0:T(8,128)S(1)}, u32[]{:S(2)}, u32[]{:S(2)}) %collective-permute-start.4) | collective-permute-done | bytes 204832 | tf_op jit(solution)/shard_map/ppermute | solution.py:221
  13.4 0.3 %shard_map.61 = f32[1,192,128]{2,1,0:T(8,128)S(1)} custom-call(f32[256,192]{1,0:T(8,128)S(1)} %get-tuple-element.17.rows_ref, f32[256,128]{1,0:T(8,128)S(1)} %get-tuple-element.18.column_ref.refs_3_, f32[200,256]{1,0:T(8,128)S(1)} %collective-permute-done.4.swap_ref, f32[1,128,128]{2,1,0:T(8,128)S(1)} %shard_map.60.pair_ref), custom_call_target="tpu_custom_call" | custom-call | flops 150994944 | bytes 696320 | tf_op jit(solution)/shard_map/pallas_call | solution.py:201
  13.7 2.4 %collective-permute-start.5 = (f32[192,128]{1,0:T(8,128)S(1)}, f32[192,128]{1,0:T(8,128)S(1)}, u32[]{:S(2)}, u32[]{:S(2)}) collective-permute-start(f32[192,128]{1,0:T(8,128)S(1)} %bitcast.2), channel_id=1, source_target_pairs={{0,1},{1,0},{2,3},{3,2},{4,5},{5,4},{6,7},{7,6},{8,9},{9,8},{10,11... | collective-permute-start | bytes 294920 | tf_op jit(solution)/shard_map/ppermute | solution.py:225
  16.1 0.6 %shard_map.62 = (f32[128,128]{1,0:T(8,128)S(1)}, f32[128,128]{1,0:T(8,128)S(1)}, f32[128,128]{1,0:T(8,128)S(1)}, f32[8,256]{1,0:T(8,128)S(1)}) custom-call(f32[256,192]{1,0:T(8,128)S(1)} %get-tuple-element.17.rows_ref, f32[256,128]{1,0:T(8,128)S(1)} %get-tuple-element.18.column_ref.refs_3_, f32[8,256]{1,0:T(8,128)S(1)} %shard_map.58.own_labels, ...), custom_call_target="tpu_custom_call" | custom-call | flops 150994944 | bytes 1359872 | tf_op jit(solution)/shard_map/pallas_call | solution.py:201
  16.7 2.8 %collective-permute-done.5.refs_1_ = f32[192,128]{1,0:T(8,128)S(1)} collective-permute-done((f32[192,128]{1,0:T(8,128)S(1)}, f32[192,128]{1,0:T(8,128)S(1)}, u32[]{:S(2)}, u32[]{:S(2)}) %collective-permute-start.5) | collective-permute-done | bytes 98336 | tf_op jit(solution)/shard_map/ppermute | solution.py:225
  19.4 0.9 %shard_map.63 = f32[4,128,256]{2,1,0:T(8,128)} custom-call(f32[128,128]{1,0:T(8,128)S(1)} %get-tuple-element.19.own_keep, f32[128,128]{1,0:T(8,128)S(1)} %get-tuple-element.25.near_keep, f32[128,128]{1,0:T(8,128)S(1)} %get-tuple-element.26.mix_keep, f32[128,128]{1,0:T(8,128)S(1)} %get-tuple-element.27.swap_keep, ...), custom_call_target="tpu_custom_call" | custom-call | flops 262144 | bytes 1056768 | tf_op jit(solution)/shard_map/pallas_call | solution.py:201
  (1 shorter events, 0.0 us)
Async XLA Ops:
  1.4 10.3 %collective-permute-start = (f32[200,256]{1,0:T(8,128)S(1)}, f32[200,256]{1,0:T(8,128)S(1)}, u32[]{:S(2)}, u32[]{:S(2)}) collective-permute-start(f32[200,256]{1,0:T(8,128)S(1)} %shard_map.56.own_ref.slab_ref), channel_id=1, source_target_pairs={{0,6},{2,4},{4,10},{6,8},{8,14},{10,12},{12,18},{14,16},{16,22},{1... | collective-permute-start | bytes 614408 | tf_op jit(solution)/shard_map/ppermute | solution.py:221
  3.8 7.3 %collective-permute-start.1 = (f32[200,256]{1,0:T(8,128)S(1)}, f32[200,256]{1,0:T(8,128)S(1)}, u32[]{:S(2)}, u32[]{:S(2)}) collective-permute-start(f32[200,256]{1,0:T(8,128)S(1)} %shard_map.56.own_ref.slab_ref), channel_id=1, source_target_pairs={{0,2},{2,8},{4,6},{6,4},{8,10},{10,16},{12,14},{14,12},{16,18},{18... | collective-permute-start | bytes 614408 | tf_op jit(solution)/shard_map/ppermute | solution.py:221
  6.2 4.9 %collective-permute-start.3 = (f32[64,128]{1,0:T(8,128)S(1)}, f32[64,128]{1,0:T(8,128)S(1)}, u32[]{:S(2)}, u32[]{:S(2)}) collective-permute-start(f32[64,128]{1,0:T(8,128)S(1)} %bitcast.3), channel_id=1, source_target_pairs={{0,1},{1,0},{2,3},{3,2},{4,5},{5,4},{6,7},{7,6},{8,9},{9,8},{10,11... | collective-permute-start | bytes 98312 | tf_op jit(solution)/shard_map/ppermute | solution.py:225
  11.1 1.5 %collective-permute-start.2 = (f32[200,256]{1,0:T(8,128)S(1)}, f32[200,256]{1,0:T(8,128)S(1)}, u32[]{:S(2)}, u32[]{:S(2)}) collective-permute-start(f32[200,256]{1,0:T(8,128)S(1)} %shard_map.56.own_ref.slab_ref), channel_id=1, source_target_pairs={{0,2},{2,0},{4,6},{6,12},{8,10},{10,8},{12,14},{14,20},{16,18},{18... | collective-permute-start | bytes 614408 | tf_op jit(solution)/shard_map/ppermute | solution.py:221
  11.7 1.7 %collective-permute-start.4 = (f32[200,256]{1,0:T(8,128)S(1)}, f32[200,256]{1,0:T(8,128)S(1)}, u32[]{:S(2)}, u32[]{:S(2)}) collective-permute-start(f32[200,256]{1,0:T(8,128)S(1)} %collective-permute-done.near_ref), channel_id=1, source_target_pairs={{0,2},{2,0},{4,6},{6,4},{8,10},{10,8},{12,14},{14,12},{16,18},{18,... | collective-permute-start | bytes 614408 | tf_op jit(solution)/shard_map/ppermute | solution.py:221
  13.7 5.7 %collective-permute-start.5 = (f32[192,128]{1,0:T(8,128)S(1)}, f32[192,128]{1,0:T(8,128)S(1)}, u32[]{:S(2)}, u32[]{:S(2)}) collective-permute-start(f32[192,128]{1,0:T(8,128)S(1)} %bitcast.2), channel_id=1, source_target_pairs={{0,1},{1,0},{2,3},{3,2},{4,5},{5,4},{6,7},{7,6},{8,9},{9,8},{10,11... | collective-permute-start | bytes 294920 | tf_op jit(solution)/shard_map/ppermute | solution.py:225

commit v12 on v8

--- a/solution.py
+++ b/solution.py
@@ -46,15 +46,15 @@
 
 def pack_kernel(amp_ref, ij_ref, cd_ref, out_ref, amp, ij, cd, sems):
     pairs, width = amp.shape[0], out_ref.shape[0] - 8
-    copies = fetch([(amp_ref, amp), (ij_ref, ij), (cd_ref, cd)], sems)
+    parts = [slice(start, start + LANES) for start in range(0, pairs, LANES)]
+    copies = fetch([(ij_ref, ij), (cd_ref, cd)] + [(amp_ref.at[part], amp.at[part]) for part in parts], sems)
+    copies[0].wait()
     copies[1].wait()
-    copies[2].wait()
     rows = column(ij[...])
     labels = cd[...].astype(F32)
     out_ref[width:, :] = jnp.broadcast_to(ij[...].astype(F32), (8, pairs))
-    copies[0].wait()
-    for start in range(0, pairs, LANES):
-        part = slice(start, start + LANES)
+    for copy, part in zip(copies[2:], parts):
+        copy.wait()
         first, second = fold(amp[part, :], rows[part], labels)
         out_ref[:LANES, part] = first.T
         out_ref[LANES:width, part] = second.T[:width - LANES]
@@ -108,6 +108,10 @@
         rows_ref[h, LANES:] = second[:, :width - LANES]
 
 
+def labels_kernel(slab_ref, out_ref):
+    out_ref[...] = slab_ref[slab_ref.shape[0] - 8:, :]
+
+
 def own_kernel(rows_ref, column_ref, own_ref, keep_ref, send_ref):
     count = keep_ref.shape[0]
     term = narrowed(rows_ref[...], own_ref, column_ref[...])
@@ -116,33 +120,56 @@
         send_ref[k - 1] = halved(term[k * count:(k + 1) * count])
 
 
-def pair_kernel(rows_ref, column_ref, two_ref, mix_ref, send_ref):
+def place():
+    return lax.rem(lax.axis_index("blk"), 4)
+
+
+def chosen(second, one, other, out_ref, rows, labels):
+    for ref, here in ((one, ~second), (other, second)):
+
+        @pl.when(here)
+        def _():
+            out_ref[...] = narrowed(rows, ref, labels)
+
+
+def one_kernel(rows_ref, column_ref, one_ref, out_ref):
+    count = rows_ref.shape[0] - out_ref.shape[0]
+    out_ref[...] = narrowed(rows_ref[count:, :], one_ref, column_ref[count:, :])
+
+
+def pair_kernel(rows_ref, column_ref, one_term, three_ref, late_ref, send_ref, third):
     parts, count = send_ref.shape[0] + 1, send_ref.shape[1]
-    two, mix = [narrowed(rows_ref[count:, :], ref, column_ref[count:, :]) for ref in (two_ref, mix_ref)]
-    both = beside(two, mix)
+    chosen(place() == 2, three_ref, late_ref, third, rows_ref[count:, :], column_ref[count:, :])
+    both = beside(one_term[...], third[...])
     for k in range(1, parts):
         send_ref[k - 1] = both[(k - 1) * count:k * count]
 
 
-def swap_kernel(rows_ref, column_ref, swap_ref, pair_ref, send_ref):
+def last_kernel(rows_ref, column_ref, from_one, from_three, pair_ref, send_ref, two):
     parts, count = pair_ref.shape[0] + 1, pair_ref.shape[1]
-    term = narrowed(rows_ref[count:, :], swap_ref, column_ref[count:, :])
+    chosen(lax.rem(place(), 2) == 1, from_three, from_one, two, rows_ref[count:, :], column_ref[count:, :])
     for k in range(1, parts):
         send_ref[k - 1, :count, :] = pair_ref[k - 1]
-        send_ref[k - 1, count:, :] = halved(term[(k - 1) * count:k * count])
-
-
-def keep_kernel(rows_ref, column_ref, own_ref, two_ref, mix_ref, swap_ref, two_out, mix_out, swap_out, labels_ref):
-    count = two_out.shape[0]
+        send_ref[k - 1, count:, :] = halved(two[(k - 1) * count:k * count, :])
+
+
+def keep_kernel(rows_ref, column_ref, own_labels, one_ref, three_ref, late_ref, from_one, from_three, *out_refs):
+    one_out, two_out, three_out, labels_ref = out_refs
+    count = one_out.shape[0]
     width = rows_ref.shape[1]
-    for ref, out_ref in ((two_ref, two_out), (mix_ref, mix_out), (swap_ref, swap_out)):
-        out_ref[...] = narrowed(rows_ref[:count, :], ref, column_ref[:count, :])
-    own, two, mix, swap = [ref[width:width + 1, :] for ref in (own_ref, two_ref, mix_ref, swap_ref)]
-    odd = lax.rem(lax.axis_index("blk"), 2) == 1
-    labels_ref[...] = jnp.concatenate([own, jnp.where(odd, mix, swap), two, jnp.where(odd, swap, mix)] * 2, axis=0)
-
-
-def finish_kernel(parts, own_keep, mix_keep, two_keep, swap_keep, *refs):
+    rows, labels = rows_ref[:count, :], column_ref[:count, :]
+    odd, second = lax.rem(place(), 2) == 1, place() == 2
+    one_out[...] = narrowed(rows, one_ref, labels)
+    chosen(odd, from_three, from_one, two_out, rows, labels)
+    chosen(second, three_ref, late_ref, three_out, rows, labels)
+    one, three, late, even_two, odd_two = [
+        ref[width:width + 1, :] for ref in (one_ref, three_ref, late_ref, from_three, from_one)
+    ]
+    two, three = jnp.where(odd, odd_two, even_two), jnp.where(second, late, three)
+    labels_ref[...] = jnp.concatenate([own_labels[:1, :], one, two, three] * 2, axis=0)
+
+
+def finish_kernel(parts, own_keep, one_keep, two_keep, three_keep, *refs):
     own_in, late_in = refs[:parts - 1], refs[parts - 1:2 * (parts - 1)]
     labels_ref, column_ref, out_ref, out, sems = refs[2 * (parts - 1):]
     count = own_keep.shape[0]
@@ -156,14 +183,11 @@
         copies.append(pltpu.make_async_copy(out.at[m], out_ref.at[m], sems.at[m]))
         copies[-1].start()
 
-    odd = lax.rem(lax.axis_index("blk"), 2) == 1
     store(0, sum([unhalved(ref[...]) for ref in own_in], own_keep[...]))
+    store(2, sum([unhalved(ref[count:, :]) for ref in late_in], two_keep[...]))
     pairs = [apart(ref[:count, :]) for ref in late_in]
-    store(2, sum([two for two, _ in pairs], two_keep[...]))
-    mix = sum([mix for _, mix in pairs], mix_keep[...])
-    swap = sum([unhalved(ref[count:, :]) for ref in late_in], swap_keep[...])
-    store(1, jnp.where(odd, mix, swap))
-    store(3, jnp.where(odd, swap, mix))
+    store(1, sum([one for one, _ in pairs], one_keep[...]))
+    store(3, sum([three for _, three in pairs], three_keep[...]))
     for copy in copies:
         copy.wait()
 
@@ -213,29 +237,35 @@
             pltpu.VMEM(cd_irrep.shape, jnp.int32),
         ], pltpu.SemaphoreType.DMA((2 + copies,))
 
-    stage, sems = staging(amplitudes, ij_irrep, 1)
+    stage, sems = staging(amplitudes, ij_irrep, pairs // LANES)
     own, = call(pack_kernel, [whole(width + 8, pairs)], (amplitudes, ij_irrep, cd_irrep),
                 4 * amplitudes.size, 3, stage + [sems])
-    two = moved(own, (2, 2, 2, 2))
+    one = moved(own, (1, 1, 1, 1))
+    own_labels, = call(labels_kernel, [whole(8, pairs)], (own,), 8 * pairs)
+    three = moved(after(own, own_labels), (3, 3, 3, -1))
     stage, sems = staging(integrals, ab_irrep, parts)
     rows, labels = call(
         functools.partial(first_kernel, count), [whole(row_count, width), whole(row_count, LANES)],
-        (integrals, ab_irrep, cd_irrep), one_product, 3, stage + [pltpu.VMEM((row_count, LANES), F32), sems])
+        (integrals, ab_irrep, cd_irrep), 64 * one_product, 3, stage + [pltpu.VMEM((row_count, LANES), F32), sems])
     own_keep, own_send = call(
         own_kernel, [whole(count, LANES), whole(parts - 1, count // 2, LANES)],
         (rows, labels, own), one_product)
     own_in = exchanged(own_send)
-    mix = moved(after(own, own_keep), (1, 3, 1, 3))
-    swap = moved(after(two, *own_in), (1, -1, 1, -1))
-    pair_send, = call(pair_kernel, [whole(parts - 1, count, LANES)], (rows, labels, two, mix), 40 * one_product)
-    late_send, = call(swap_kernel, [whole(parts - 1, count + count // 2, LANES)],
-                      (rows, labels, swap, pair_send), one_product // 2)
+    late = moved(after(own, own_keep), (1, -1, 1, 3))
+    from_one = moved(one, (1, -1, 1, -1))
+    from_three = moved(after(three, *own_in), (1, -1, 1, -1))
+    rest = whole(row_count - count, LANES)
+    one_term, = call(one_kernel, [rest], (rows, labels, one), one_product)
+    pair_send, = call(pair_kernel, [whole(parts - 1, count, LANES)], (rows, labels, one_term, three, late),
+                      one_product, 0, [pltpu.VMEM(rest.shape, F32)])
+    late_send, = call(last_kernel, [whole(parts - 1, count + count // 2, LANES)],
+                      (rows, labels, from_one, from_three, pair_send), one_product, 0, [pltpu.VMEM(rest.shape, F32)])
     late_in = exchanged(late_send)
-    two_keep, mix_keep, swap_keep, slab_labels = call(
+    one_keep, two_keep, three_keep, slab_labels = call(
         keep_kernel, [whole(count, LANES)] * 3 + [whole(8, pairs)],
-        (rows, labels, own, two, mix, after(swap, late_send)), one_product)
+        (rows, labels, own_labels, one, three, late, from_one, after(from_three, late_send)), one_product)
     out, = call(functools.partial(finish_kernel, parts), [whole(4, count, pairs)],
-                (own_keep, mix_keep, two_keep, swap_keep, *own_in, *late_in, slab_labels, labels),
+                (own_keep, one_keep, two_keep, three_keep, *own_in, *late_in, slab_labels, labels),
                 4 * 2 * count * pairs, 0, [pltpu.VMEM((4, count, pairs), F32), pltpu.SemaphoreType.DMA((4,))], OFFCHIP)
     return out
 

time: 20.8 us -> 21 us (level)
  the two profiles are of different devices: /device:TPU:0 before, /device:TPU:2 now
where the time goes in v12:
time: 21 us; the launch traced here: 20.9 us
  waiting for transfers between devices  9.21 us (44%)
  Pallas kernels  6.11 us (29%)
  starting transfers between devices  5.46 us (26%)
    pallas_call x9, Pallas kernels, call(): pl.pallas_call(kernel, out_shape=out_shape, in_specs=[OFFCHIP] * off + [O...  6.11 us
    ppermute x2, waiting for transfers between devices, exchanged(): lax.ppermute(array[k - 1], 'red', [(i, (i + k) % parts) for i in range(pa...  5.46 us
    ppermute x5, waiting for transfers between devices, moved(): lax.ppermute(array, 'blk', [(i, (i + steps[i % 4]) % blocks) for i in ran...  3.74 us
    ppermute x5, starting transfers between devices, moved(): lax.ppermute(array, 'blk', [(i, (i + steps[i % 4]) % blocks) for i in ran...  3.3 us
    ppermute x2, starting transfers between devices, exchanged(): lax.ppermute(array[k - 1], 'red', [(i, (i + k) % parts) for i in range(pa...  2.16 us
  transfers between devices with their start and end apart: 7, of which 3 were waited for; matrix products, arithmetic and copies ran while one was open for 0% of the time, Pallas kernels for 16%

profile of v12, /device:TPU:2, one launch (start us, length us, event | category | flops | bytes accessed | tf_op | source)
XLA Modules:
  0.0 20.9 jit_solution(4412068609928991913)
XLA Ops:
  0.0 1.4 %shard_map.56.own_ref.slab_ref = f32[200,256]{1,0:T(8,128)S(1)} custom-call(f32[256,768]{1,0:T(8,128)} %amp_ref.1, s32[1,256]{1,0:T(1,128)} %ij_ref.1, s32[1,768]{1,0:T(1,128)} %cd_ref.3), custom_call_target="tpu_custom_call" | custom-call | flops 786432 | bytes 995328 | tf_op jit(solution)/shard_map/pallas_call | solution.py:202
  1.4 0.1 collective-permute-start
  1.5 2.7 %collective-permute-start.1 = (f32[200,256]{1,0:T(8,128)S(1)}, f32[200,256]{1,0:T(8,128)S(1)}, u32[]{:S(2)}, u32[]{:S(2)}) collective-permute-start(f32[200,256]{1,0:T(8,128)S(1)} %shard_map.56.own_ref.slab_ref), channel_id=1, source_target_pairs={{0,6},{2,8},{4,10},{6,4},{8,14},{10,16},{12,18},{14,12},{16,22},{1... | collective-permute-start | bytes 614408 | tf_op jit(solution)/shard_map/ppermute | solution.py:222
  4.2 1.3 %shard_map.55 = (f32[256,192]{1,0:T(8,128)S(1)}, f32[256,128]{1,0:T(8,128)S(1)}) custom-call(f32[256,768]{1,0:T(8,128)} %v_ref.1, s32[1,256]{1,0:T(1,128)} %ab_ref.1, s32[1,768]{1,0:T(1,128)} %cd_ref.3), custom_call_target="tpu_custom_call" | custom-call | flops 9663676416 | bytes 1118208 | tf_op jit(solution)/shard_map/pallas_call | solution.py:202
  5.5 0.4 %shard_map.57 = (f32[128,128]{1,0:T(8,128)S(1)}, f32[1,64,128]{2,1,0:T(8,128)S(1)}) custom-call(f32[256,192]{1,0:T(8,128)S(1)} %get-tuple-element.17.rows_ref, f32[256,128]{1,0:T(8,128)S(1)} %get-tuple-element.18.column_ref.refs_3_, f32[200,256]{1,0:T(8,128)S(1)} %shard_map.56.own_ref.slab_ref), custom_call_target="tpu_custom_call" | custom-call | flops 150994944 | bytes 630784 | tf_op jit(solution)/shard_map/pallas_call | solution.py:202
  6.0 1.6 %collective-permute-start.4 = (f32[64,128]{1,0:T(8,128)S(1)}, f32[64,128]{1,0:T(8,128)S(1)}, u32[]{:S(2)}, u32[]{:S(2)}) collective-permute-start(f32[64,128]{1,0:T(8,128)S(1)} %bitcast.3), channel_id=1, source_target_pairs={{0,1},{1,0},{2,3},{3,2},{4,5},{5,4},{6,7},{7,6},{8,9},{9,8},{10,11... | collective-permute-start | bytes 98312 | tf_op jit(solution)/shard_map/ppermute | solution.py:226
  7.6 0.0 collective-permute-start.2
  7.6 2.4 %collective-permute-done.4.refs_0_ = f32[64,128]{1,0:T(8,128)S(1)} collective-permute-done((f32[64,128]{1,0:T(8,128)S(1)}, f32[64,128]{1,0:T(8,128)S(1)}, u32[]{:S(2)}, u32[]{:S(2)}) %collective-permute-start.4) | collective-permute-done | bytes 32800 | tf_op jit(solution)/shard_map/ppermute | solution.py:226
  10.0 0.0 collective-permute-done.1.three_ref
  10.0 0.0 collective-permute-done.one_ref
  10.0 0.0 collective-permute-start.3
  10.0 0.5 %collective-permute-start.5 = (f32[200,256]{1,0:T(8,128)S(1)}, f32[200,256]{1,0:T(8,128)S(1)}, u32[]{:S(2)}, u32[]{:S(2)}) collective-permute-start(f32[200,256]{1,0:T(8,128)S(1)} %collective-permute-done.1.three_ref), channel_id=1, source_target_pairs={{0,2},{2,0},{4,6},{6,4},{8,10},{10,8},{12,14},{14,12},{16,18},{18,... | collective-permute-start | bytes 614408 | tf_op jit(solution)/shard_map/ppermute | solution.py:222
  10.5 0.3 %shard_map.59.one_term = f32[128,128]{1,0:T(8,128)S(1)} custom-call(f32[256,192]{1,0:T(8,128)S(1)} %get-tuple-element.17.rows_ref, f32[256,128]{1,0:T(8,128)S(1)} %get-tuple-element.18.column_ref.refs_3_, f32[200,256]{1,0:T(8,128)S(1)} %collective-permute-done.one_ref), custom_call_target="tpu_custom_call" | custom-call | flops 150994944 | bytes 598016 | tf_op jit(solution)/shard_map/pallas_call | solution.py:202
  10.8 3.7 %collective-permute-done.2.late_ref = f32[200,256]{1,0:T(8,128)S(1)} collective-permute-done((f32[200,256]{1,0:T(8,128)S(1)}, f32[200,256]{1,0:T(8,128)S(1)}, u32[]{:S(2)}, u32[]{:S(2)}) %collective-permute-start.2) | collective-permute-done | bytes 204832 | tf_op jit(solution)/shard_map/ppermute | solution.py:222
  14.5 0.4 %shard_map.60.pair_ref = f32[1,128,128]{2,1,0:T(8,128)S(1)} custom-call(f32[256,192]{1,0:T(8,128)S(1)} %get-tuple-element.17.rows_ref, f32[256,128]{1,0:T(8,128)S(1)} %get-tuple-element.18.column_ref.refs_3_, f32[128,128]{1,0:T(8,128)S(1)} %shard_map.59.one_term, f32[200,256]{1,0:T(8,128)S(1)} %collective-permute-done.1.three_ref, ...), custom_call_target="tpu_custom_call" | custom-call | flops 150994944 | bytes 868352 | tf_op jit(solution)/shard_map/pallas_call | solution.py:202
  14.9 0.0 collective-permute-done.3.from_one
  14.9 0.0 collective-permute-done.5.from_three
  14.9 0.4 %shard_map.61 = f32[1,192,128]{2,1,0:T(8,128)S(1)} custom-call(f32[256,192]{1,0:T(8,128)S(1)} %get-tuple-element.17.rows_ref, f32[256,128]{1,0:T(8,128)S(1)} %get-tuple-element.18.column_ref.refs_3_, f32[200,256]{1,0:T(8,128)S(1)} %collective-permute-done.3.from_one, f32[200,256]{1,0:T(8,128)S(1)} %collective-permute-done.5.from_three, ...), custom_call_target="tpu_custom_call" | custom-call | flops 150994944 | bytes 901120 | tf_op jit(solution)/shard_map/pallas_call | solution.py:202
  15.3 0.6 %collective-permute-start.6 = (f32[192,128]{1,0:T(8,128)S(1)}, f32[192,128]{1,0:T(8,128)S(1)}, u32[]{:S(2)}, u32[]{:S(2)}) collective-permute-start(f32[192,128]{1,0:T(8,128)S(1)} %bitcast.2), channel_id=1, source_target_pairs={{0,1},{1,0},{2,3},{3,2},{4,5},{5,4},{6,7},{7,6},{8,9},{9,8},{10,11... | collective-permute-start | bytes 294920 | tf_op jit(solution)/shard_map/ppermute | solution.py:226
  15.9 1.0 %shard_map.62 = (f32[128,128]{1,0:T(8,128)S(1)}, f32[128,128]{1,0:T(8,128)S(1)}, f32[128,128]{1,0:T(8,128)S(1)}, f32[8,256]{1,0:T(8,128)S(1)}) custom-call(f32[256,192]{1,0:T(8,128)S(1)} %get-tuple-element.17.rows_ref, f32[256,128]{1,0:T(8,128)S(1)} %get-tuple-element.18.column_ref.refs_3_, f32[8,256]{1,0:T(8,128)S(1)} %shard_map.58.own_labels, ...), custom_call_target="tpu_custom_call" | custom-call | flops 150994944 | bytes 1564672 | tf_op jit(solution)/shard_map/pallas_call | solution.py:202
  16.9 3.1 %collective-permute-done.6.refs_1_ = f32[192,128]{1,0:T(8,128)S(1)} collective-permute-done((f32[192,128]{1,0:T(8,128)S(1)}, f32[192,128]{1,0:T(8,128)S(1)}, u32[]{:S(2)}, u32[]{:S(2)}) %collective-permute-start.6) | collective-permute-done | bytes 98336 | tf_op jit(solution)/shard_map/ppermute | solution.py:226
  20.0 0.9 %shard_map.63 = f32[4,128,256]{2,1,0:T(8,128)} custom-call(f32[128,128]{1,0:T(8,128)S(1)} %get-tuple-element.19.own_keep, f32[128,128]{1,0:T(8,128)S(1)} %get-tuple-element.25.one_keep, f32[128,128]{1,0:T(8,128)S(1)} %get-tuple-element.26.two_keep, f32[128,128]{1,0:T(8,128)S(1)} %get-tuple-element.27.three_keep, ...), custom_call_target="tpu_custom_call" | custom-call | flops 262144 | bytes 1056768 | tf_op jit(solution)/shard_map/pallas_call | solution.py:202
  (1 shorter events, 0.0 us)
Async XLA Ops:
  1.4 8.5 %collective-permute-start = (f32[200,256]{1,0:T(8,128)S(1)}, f32[200,256]{1,0:T(8,128)S(1)}, u32[]{:S(2)}, u32[]{:S(2)}) collective-permute-start(f32[200,256]{1,0:T(8,128)S(1)} %shard_map.56.own_ref.slab_ref), channel_id=1, source_target_pairs={{0,2},{2,4},{4,6},{6,8},{8,10},{10,12},{12,14},{14,16},{16,18},{18... | collective-permute-start | bytes 614408 | tf_op jit(solution)/shard_map/ppermute | solution.py:222
  1.5 8.5 %collective-permute-start.1 = (f32[200,256]{1,0:T(8,128)S(1)}, f32[200,256]{1,0:T(8,128)S(1)}, u32[]{:S(2)}, u32[]{:S(2)}) collective-permute-start(f32[200,256]{1,0:T(8,128)S(1)} %shard_map.56.own_ref.slab_ref), channel_id=1, source_target_pairs={{0,6},{2,8},{4,10},{6,4},{8,14},{10,16},{12,18},{14,12},{16,22},{1... | collective-permute-start | bytes 614408 | tf_op jit(solution)/shard_map/ppermute | solution.py:222
  6.0 4.0 %collective-permute-start.4 = (f32[64,128]{1,0:T(8,128)S(1)}, f32[64,128]{1,0:T(8,128)S(1)}, u32[]{:S(2)}, u32[]{:S(2)}) collective-permute-start(f32[64,128]{1,0:T(8,128)S(1)} %bitcast.3), channel_id=1, source_target_pairs={{0,1},{1,0},{2,3},{3,2},{4,5},{5,4},{6,7},{7,6},{8,9},{9,8},{10,11... | collective-permute-start | bytes 98312 | tf_op jit(solution)/shard_map/ppermute | solution.py:226
  7.6 7.0 %collective-permute-start.2 = (f32[200,256]{1,0:T(8,128)S(1)}, f32[200,256]{1,0:T(8,128)S(1)}, u32[]{:S(2)}, u32[]{:S(2)}) collective-permute-start(f32[200,256]{1,0:T(8,128)S(1)} %shard_map.56.own_ref.slab_ref), channel_id=1, source_target_pairs={{0,2},{2,0},{4,6},{6,12},{8,10},{10,8},{12,14},{14,20},{16,18},{18... | collective-permute-start | bytes 614408 | tf_op jit(solution)/shard_map/ppermute | solution.py:222
  10.0 4.9 %collective-permute-start.3 = (f32[200,256]{1,0:T(8,128)S(1)}, f32[200,256]{1,0:T(8,128)S(1)}, u32[]{:S(2)}, u32[]{:S(2)}) collective-permute-start(f32[200,256]{1,0:T(8,128)S(1)} %collective-permute-done.one_ref), channel_id=1, source_target_pairs={{0,2},{2,0},{4,6},{6,4},{8,10},{10,8},{12,14},{14,12},{16,18},{18,... | collective-permute-start | bytes 614408 | tf_op jit(solution)/shard_map/ppermute | solution.py:222
  10.0 4.9 %collective-permute-start.5 = (f32[200,256]{1,0:T(8,128)S(1)}, f32[200,256]{1,0:T(8,128)S(1)}, u32[]{:S(2)}, u32[]{:S(2)}) collective-permute-start(f32[200,256]{1,0:T(8,128)S(1)} %collective-permute-done.1.three_ref), channel_id=1, source_target_pairs={{0,2},{2,0},{4,6},{6,4},{8,10},{10,8},{12,14},{14,12},{16,18},{18,... | collective-permute-start | bytes 614408 | tf_op jit(solution)/shard_map/ppermute | solution.py:222
  15.3 4.7 %collective-permute-start.6 = (f32[192,128]{1,0:T(8,128)S(1)}, f32[192,128]{1,0:T(8,128)S(1)}, u32[]{:S(2)}, u32[]{:S(2)}) collective-permute-start(f32[192,128]{1,0:T(8,128)S(1)} %bitcast.2), channel_id=1, source_target_pairs={{0,1},{1,0},{2,3},{3,2},{4,5},{5,4},{6,7},{7,6},{8,9},{9,8},{10,11... | collective-permute-start | bytes 294920 | tf_op jit(solution)/shard_map/ppermute | solution.py:226

commit v13 on v10

--- a/solution.py
+++ b/solution.py
@@ -120,47 +120,67 @@
         send_ref[k - 1] = halved(term[k * count:(k + 1) * count])
 
 
-def late_place():
+def second():
     return lax.rem(lax.axis_index("blk"), 4) == 2
 
 
-def third_term(part, rows_ref, column_ref, mix_ref, late_ref, out_ref):
-    for ref, here in ((mix_ref, ~late_place()), (late_ref, late_place())):
-
-        @pl.when(here)
+def either(here, one, other, out_ref, rows, labels):
+    for ref, holds in ((one, here), (other, ~here)):
+
+        @pl.when(holds)
         def _():
-            out_ref[...] = narrowed(rows_ref[part, :], ref, column_ref[part, :])
-
-
-def pair_kernel(rows_ref, column_ref, two_ref, mix_ref, late_ref, send_ref, third):
+            out_ref[...] = narrowed(rows, ref, labels)
+
+
+def mix_kernel(rows_ref, column_ref, mix_ref, out_ref):
+    count = rows_ref.shape[0] - out_ref.shape[0]
+    out_ref[...] = narrowed(rows_ref[count:, :], mix_ref, column_ref[count:, :])
+
+
+def early_kernel(rows_ref, column_ref, mix_term, two_ref, send_ref, term):
+    parts, count = send_ref.shape[0] + 1, 2 * send_ref.shape[1]
+    term[...] = mix_term[...]
+
+    @pl.when(second())
+    def _():
+        term[...] = narrowed(rows_ref[count:, :], two_ref, column_ref[count:, :])
+
+    for k in range(1, parts):
+        send_ref[k - 1] = halved(term[(k - 1) * count:k * count, :])
+
+
+def other_kernel(rows_ref, column_ref, two_ref, late_ref, out_ref):
+    count = rows_ref.shape[0] - out_ref.shape[0]
+    either(second(), late_ref, two_ref, out_ref, rows_ref[count:, :], column_ref[count:, :])
+
+
+def swap_kernel(rows_ref, column_ref, swap_ref, other_ref, send_ref):
     parts, count = send_ref.shape[0] + 1, send_ref.shape[1]
-    third_term(slice(count, None), rows_ref, column_ref, mix_ref, late_ref, third)
-    both = beside(narrowed(rows_ref[count:, :], two_ref, column_ref[count:, :]), third[...])
+    both = beside(other_ref[...], narrowed(rows_ref[count:, :], swap_ref, column_ref[count:, :]))
     for k in range(1, parts):
         send_ref[k - 1] = both[(k - 1) * count:k * count]
 
 
-def swap_kernel(rows_ref, column_ref, swap_ref, pair_ref, send_ref):
-    parts, count = pair_ref.shape[0] + 1, pair_ref.shape[1]
-    term = narrowed(rows_ref[count:, :], swap_ref, column_ref[count:, :])
-    for k in range(1, parts):
-        send_ref[k - 1, :count, :] = pair_ref[k - 1]
-        send_ref[k - 1, count:, :] = halved(term[(k - 1) * count:k * count])
-
-
-def keep_kernel(rows_ref, column_ref, own_labels, two_ref, mix_ref, late_ref, swap_ref, two_out, mix_out, swap_out, labels_ref):
+def keep_kernel(parts, *refs):
+    early_in, refs = refs[:parts - 1], refs[parts - 1:]
+    rows_ref, column_ref, own_labels, two_ref, mix_ref, late_ref, swap_ref = refs[:7]
+    two_out, three_out, swap_out, labels_ref = refs[7:]
     count = two_out.shape[0]
     width = rows_ref.shape[1]
-    third_term(slice(0, count), rows_ref, column_ref, mix_ref, late_ref, mix_out)
-    for ref, out_ref in ((two_ref, two_out), (swap_ref, swap_out)):
-        out_ref[...] = narrowed(rows_ref[:count, :], ref, column_ref[:count, :])
+    rows, labels = rows_ref[:count, :], column_ref[:count, :]
+    two_out[...] = narrowed(rows, two_ref, labels)
+    swap_out[...] = narrowed(rows, swap_ref, labels)
+    either(second(), late_ref, mix_ref, three_out, rows, labels)
+    early = sum([unhalved(ref[...]) for ref in early_in[1:]], unhalved(early_in[0][...])) if early_in else 0.0
+    two_out[...] = jnp.where(second(), two_out[...] + early, two_out[...])
+    three_out[...] = jnp.where(second(), three_out[...], three_out[...] + early)
     two, mix, late, swap = [ref[width:width + 1, :] for ref in (two_ref, mix_ref, late_ref, swap_ref)]
-    mix = jnp.where(late_place(), late, mix)
+    mix = jnp.where(second(), late, mix)
     odd = lax.rem(lax.axis_index("blk"), 2) == 1
     labels_ref[...] = jnp.concatenate([own_labels[:1, :], jnp.where(odd, mix, swap), two, jnp.where(odd, swap, mix)] * 2, axis=0)
 
 
-def finish_kernel(parts, own_keep, mix_keep, two_keep, swap_keep, *refs):
+def finish_kernel(parts, own_keep, two_keep, three_keep, swap_keep, *refs):
     own_in, late_in = refs[:parts - 1], refs[parts - 1:2 * (parts - 1)]
     labels_ref, column_ref, out_ref, out, sems = refs[2 * (parts - 1):]
     count = own_keep.shape[0]
@@ -176,10 +196,11 @@
 
     odd = lax.rem(lax.axis_index("blk"), 2) == 1
     store(0, sum([unhalved(ref[...]) for ref in own_in], own_keep[...]))
-    pairs = [apart(ref[:count, :]) for ref in late_in]
-    store(2, sum([two for two, _ in pairs], two_keep[...]))
-    mix = sum([mix for _, mix in pairs], mix_keep[...])
-    swap = sum([unhalved(ref[count:, :]) for ref in late_in], swap_keep[...])
+    pairs = [apart(ref[...]) for ref in late_in]
+    two, three = two_keep[...], three_keep[...]
+    store(2, jnp.where(second(), two, sum([other for other, _ in pairs], two)))
+    mix = jnp.where(second(), sum([other for other, _ in pairs], three), three)
+    swap = sum([swap for _, swap in pairs], swap_keep[...])
     store(1, jnp.where(odd, mix, swap))
     store(3, jnp.where(odd, swap, mix))
     for copy in copies:
@@ -246,17 +267,20 @@
         (rows, labels, own), one_product)
     own_in = exchanged(own_send)
     late = moved(after(own, own_keep, mix), (1, -1, 1, 3))
-    swap = moved(after(two, *own_in), (1, -1, 1, -1))
-    pair_send, = call(pair_kernel, [whole(parts - 1, count, LANES)], (rows, labels, two, mix, late), one_product, 0,
-                      [pltpu.VMEM((row_count - count, LANES), F32)])
-    late_send, = call(swap_kernel, [whole(parts - 1, count + count // 2, LANES)],
-                      (rows, labels, swap, pair_send), one_product // 2)
+    rest = whole(row_count - count, LANES)
+    mix_term, = call(mix_kernel, [rest], (rows, labels, mix), one_product)
+    early_send, = call(early_kernel, [whole(parts - 1, count // 2, LANES)], (rows, labels, mix_term, two),
+                       one_product, 0, [pltpu.VMEM(rest.shape, F32)])
+    early_in = exchanged(early_send)
+    swap = moved(after(two, mix_term, *own_in), (1, -1, 1, -1))
+    other_term, = call(other_kernel, [rest], (rows, labels, two, late), one_product)
+    late_send, = call(swap_kernel, [whole(parts - 1, count, LANES)], (rows, labels, swap, other_term), one_product)
     late_in = exchanged(late_send)
-    two_keep, mix_keep, swap_keep, slab_labels = call(
-        keep_kernel, [whole(count, LANES)] * 3 + [whole(8, pairs)],
-        (rows, labels, own_labels, two, mix, late, after(swap, late_send)), one_product)
+    two_keep, three_keep, swap_keep, slab_labels = call(
+        functools.partial(keep_kernel, parts), [whole(count, LANES)] * 3 + [whole(8, pairs)],
+        (*early_in, rows, labels, own_labels, two, mix, late, after(swap, late_send)), 16 * one_product)
     out, = call(functools.partial(finish_kernel, parts), [whole(4, count, pairs)],
-                (own_keep, mix_keep, two_keep, swap_keep, *own_in, *late_in, slab_labels, labels),
+                (own_keep, two_keep, three_keep, swap_keep, *own_in, *late_in, slab_labels, labels),
                 4 * 2 * count * pairs, 0, [pltpu.VMEM((4, count, pairs), F32), pltpu.SemaphoreType.DMA((4,))], OFFCHIP)
     return out
 

time: 20.3 us -> 20.2 us (level)
  waiting for transfers between devices: 8.08 us -> 6.81 us
  starting transfers between devices: 6.17 us -> 7.23 us
    ppermute x4, waiting for transfers between devices: 5.56 us -> 4.44 us  [moved(): lax.ppermute(array, 'blk', [(i, (i + steps[i % 4]) % blocks) for i in ran...]
    ppermute x2 -> x3, starting transfers between devices: 3.17 us -> 4.23 us  [exchanged(): lax.ppermute(array[k - 1], 'red', [(i, (i + k) % parts) for i in range(pa...]
    ppermute x2 -> x3, waiting for transfers between devices: 2.52 us -> 2.37 us  [exchanged(): lax.ppermute(array[k - 1], 'red', [(i, (i + k) % parts) for i in range(pa...]
    pallas_call x8 -> x10, Pallas kernels: 5.79 us -> 5.93 us  [call(): pl.pallas_call(kernel, out_shape=out_shape, in_specs=[OFFCHIP] * off + [O...]
  transfers between devices with their start and end apart: 6 -> 7, of which waited for: 5 -> 4; matrix products, arithmetic and copies ran while one was open for 0% -> 0% of each run, Pallas kernels for 16% -> 18%
where the time goes in v13:
time: 20.2 us; the launch traced here: 20 us
  starting transfers between devices  7.23 us (36%)
  waiting for transfers between devices  6.81 us (34%)
  Pallas kernels  5.93 us (29%)
    pallas_call x10, Pallas kernels, call(): pl.pallas_call(kernel, out_shape=out_shape, in_specs=[OFFCHIP] * off + [O...  5.93 us
    ppermute x4, waiting for transfers between devices, moved(): lax.ppermute(array, 'blk', [(i, (i + steps[i % 4]) % blocks) for i in ran...  4.44 us
    ppermute x3, starting transfers between devices, exchanged(): lax.ppermute(array[k - 1], 'red', [(i, (i + k) % parts) for i in range(pa...  4.23 us
    ppermute x4, starting transfers between devices, moved(): lax.ppermute(array, 'blk', [(i, (i + steps[i % 4]) % blocks) for i in ran...  3 us
    ppermute x3, waiting for transfers between devices, exchanged(): lax.ppermute(array[k - 1], 'red', [(i, (i + k) % parts) for i in range(pa...  2.37 us
  transfers between devices with their start and end apart: 7, of which 4 were waited for; matrix products, arithmetic and copies ran while one was open for 0% of the time, Pallas kernels for 18%

profile of v13, /device:TPU:0, one launch (start us, length us, event | category | flops | bytes accessed | tf_op | source)
XLA Modules:
  0.0 20.0 jit_solution(8483496845589405727)
XLA Ops:
  0.0 1.4 %shard_map.56.own_ref.slab_ref = f32[200,256]{1,0:T(8,128)S(1)} custom-call(f32[256,768]{1,0:T(8,128)} %amp_ref.1, s32[1,256]{1,0:T(1,128)} %ij_ref.1, s32[1,768]{1,0:T(1,128)} %cd_ref.3), custom_call_target="tpu_custom_call" | custom-call | flops 786432 | bytes 995328 | tf_op jit(solution)/shard_map/pallas_call | solution.py:217
  1.4 3.0 %collective-permute-start.1 = (f32[200,256]{1,0:T(8,128)S(1)}, f32[200,256]{1,0:T(8,128)S(1)}, u32[]{:S(2)}, u32[]{:S(2)}) collective-permute-start(f32[200,256]{1,0:T(8,128)S(1)} %shard_map.56.own_ref.slab_ref), channel_id=1, source_target_pairs={{0,4},{2,6},{4,8},{6,10},{8,12},{10,14},{12,16},{14,18},{16,20},{1... | collective-permute-start | bytes 614408 | tf_op jit(solution)/shard_map/ppermute | solution.py:237
  4.4 0.0 collective-permute-start
  4.4 1.3 %shard_map.55 = (f32[256,192]{1,0:T(8,128)S(1)}, f32[256,128]{1,0:T(8,128)S(1)}) custom-call(f32[256,768]{1,0:T(8,128)} %v_ref.1, s32[1,256]{1,0:T(1,128)} %ab_ref.1, s32[1,768]{1,0:T(1,128)} %cd_ref.3), custom_call_target="tpu_custom_call" | custom-call | flops 9663676416 | bytes 1118208 | tf_op jit(solution)/shard_map/pallas_call | solution.py:217
  5.7 0.4 %shard_map.57 = (f32[128,128]{1,0:T(8,128)S(1)}, f32[1,64,128]{2,1,0:T(8,128)S(1)}) custom-call(f32[256,192]{1,0:T(8,128)S(1)} %get-tuple-element.17.rows_ref.refs_1_, f32[256,128]{1,0:T(8,128)S(1)} %get-tuple-element.18.column_ref.refs_2_.refs_3_, f32[200,256]{1,0:T(8,128)S(1)} %shard_map.56.own_ref.slab_ref), custom_call_target="tpu_custom_call" | custom-call | flops 150994944 | bytes 630784 | tf_op jit(solution)/shard_map/pallas_call | solution.py:217
  6.1 1.6 %collective-permute-start.4 = (f32[64,128]{1,0:T(8,128)S(1)}, f32[64,128]{1,0:T(8,128)S(1)}, u32[]{:S(2)}, u32[]{:S(2)}) collective-permute-start(f32[64,128]{1,0:T(8,128)S(1)} %bitcast.5), channel_id=1, source_target_pairs={{0,1},{1,0},{2,3},{3,2},{4,5},{5,4},{6,7},{7,6},{8,9},{9,8},{10,11... | collective-permute-start | bytes 98312 | tf_op jit(solution)/shard_map/ppermute | solution.py:241
  7.7 3.7 %collective-permute-done.mix_ref.refs_5_ = f32[200,256]{1,0:T(8,128)S(1)} collective-permute-done((f32[200,256]{1,0:T(8,128)S(1)}, f32[200,256]{1,0:T(8,128)S(1)}, u32[]{:S(2)}, u32[]{:S(2)}) %collective-permute-start) | collective-permute-done | bytes 204832 | tf_op jit(solution)/shard_map/ppermute | solution.py:237
  11.4 0.0 collective-permute-start.3
  11.4 0.3 %shard_map.59.mix_term = f32[128,128]{1,0:T(8,128)S(1)} custom-call(f32[256,192]{1,0:T(8,128)S(1)} %get-tuple-element.17.rows_ref.refs_1_, f32[256,128]{1,0:T(8,128)S(1)} %get-tuple-element.18.column_ref.refs_2_.refs_3_, f32[200,256]{1,0:T(8,128)S(1)} %collective-permute-done.mix_ref.refs_5_), custom_call_target="tpu_custom_call" | custom-call | flops 150994944 | bytes 598016 | tf_op jit(solution)/shard_map/pallas_call | solution.py:217
  11.7 0.0 collective-permute-done.4.refs_0_
  11.7 0.8 %collective-permute-done.1.two_ref.refs_4_ = f32[200,256]{1,0:T(8,128)S(1)} collective-permute-done((f32[200,256]{1,0:T(8,128)S(1)}, f32[200,256]{1,0:T(8,128)S(1)}, u32[]{:S(2)}, u32[]{:S(2)}) %collective-permute-start.1) | collective-permute-done | bytes 204832 | tf_op jit(solution)/shard_map/ppermute | solution.py:237
  12.5 0.0 collective-permute-start.5
  12.5 1.6 %collective-permute-start.2 = (f32[64,128]{1,0:T(8,128)S(1)}, f32[64,128]{1,0:T(8,128)S(1)}, u32[]{:S(2)}, u32[]{:S(2)}) collective-permute-start(f32[64,128]{1,0:T(8,128)S(1)} %bitcast.4), channel_id=1, source_target_pairs={{0,1},{1,0},{2,3},{3,2},{4,5},{5,4},{6,7},{7,6},{8,9},{9,8},{10,11... | collective-permute-start | bytes 98312 | tf_op jit(solution)/shard_map/ppermute | solution.py:241
  14.1 0.0 collective-permute-done.3.late_ref.refs_6_
  14.1 0.3 %shard_map.61.other_ref = f32[128,128]{1,0:T(8,128)S(1)} custom-call(f32[256,192]{1,0:T(8,128)S(1)} %get-tuple-element.17.rows_ref.refs_1_, f32[256,128]{1,0:T(8,128)S(1)} %get-tuple-element.18.column_ref.refs_2_.refs_3_, f32[200,256]{1,0:T(8,128)S(1)} %collective-permute-done.1.two_ref.refs_4_, f32[200,256]{1,0:T(8,128)S(1)} %collective-permute-done.3.late_ref.refs_6_), custom_call_target="tpu_custom_call" | custom-call | flops 150994944 | bytes 802816 | tf_op jit(solution)/shard_map/pallas_call | solution.py:217
  14.5 0.0 collective-permute-done.5.swap_ref.refs_7_
  14.5 0.3 %shard_map.62 = f32[1,128,128]{2,1,0:T(8,128)S(1)} custom-call(f32[256,192]{1,0:T(8,128)S(1)} %get-tuple-element.17.rows_ref.refs_1_, f32[256,128]{1,0:T(8,128)S(1)} %get-tuple-element.18.column_ref.refs_2_.refs_3_, f32[200,256]{1,0:T(8,128)S(1)} %collective-permute-done.5.swap_ref.refs_7_, f32[128,128]{1,0:T(8,128)S(1)} %shard_map.61.other_ref), custom_call_target="tpu_custom_call" | custom-call | flops 150994944 | bytes 663552 | tf_op jit(solution)/shard_map/pallas_call | solution.py:217
  14.8 1.1 %collective-permute-start.6 = (f32[128,128]{1,0:T(8,128)S(1)}, f32[128,128]{1,0:T(8,128)S(1)}, u32[]{:S(2)}, u32[]{:S(2)}) collective-permute-start(f32[128,128]{1,0:T(8,128)S(1)} %bitcast.3), channel_id=1, source_target_pairs={{0,1},{1,0},{2,3},{3,2},{4,5},{5,4},{6,7},{7,6},{8,9},{9,8},{10,11... | collective-permute-start | bytes 196616 | tf_op jit(solution)/shard_map/ppermute | solution.py:241
  15.9 0.6 %collective-permute-done.2.refs_0_ = f32[64,128]{1,0:T(8,128)S(1)} collective-permute-done((f32[64,128]{1,0:T(8,128)S(1)}, f32[64,128]{1,0:T(8,128)S(1)}, u32[]{:S(2)}, u32[]{:S(2)}) %collective-permute-start.2) | collective-permute-done | bytes 32800 | tf_op jit(solution)/shard_map/ppermute | solution.py:241
  16.5 0.9 %shard_map.63 = (f32[128,128]{1,0:T(8,128)S(1)}, f32[128,128]{1,0:T(8,128)S(1)}, f32[128,128]{1,0:T(8,128)S(1)}, f32[8,256]{1,0:T(8,128)S(1)}) custom-call(f32[64,128]{1,0:T(8,128)S(1)} %collective-permute-done.2.refs_0_, f32[256,192]{1,0:T(8,128)S(1)} %get-tuple-element.17.rows_ref.refs_1_, f32[256,128]{1,0:T(8,128)S(1)} %get-tuple-element.18.column_ref.refs_2_.refs_3_, ...), custom_call_target="tpu_custom_call" | custom-call | flops 2415919104 | bytes 1392640 | tf_op jit(solution)/shard_map/pallas_call | solution.py:217
  17.4 1.7 %collective-permute-done.6.refs_1_ = f32[128,128]{1,0:T(8,128)S(1)} collective-permute-done((f32[128,128]{1,0:T(8,128)S(1)}, f32[128,128]{1,0:T(8,128)S(1)}, u32[]{:S(2)}, u32[]{:S(2)}) %collective-permute-start.6) | collective-permute-done | bytes 65568 | tf_op jit(solution)/shard_map/ppermute | solution.py:241
  19.1 0.9 %shard_map.64 = f32[4,128,256]{2,1,0:T(8,128)} custom-call(f32[128,128]{1,0:T(8,128)S(1)} %get-tuple-element.19.own_keep, f32[128,128]{1,0:T(8,128)S(1)} %get-tuple-element.25.two_keep, f32[128,128]{1,0:T(8,128)S(1)} %get-tuple-element.26.three_keep, f32[128,128]{1,0:T(8,128)S(1)} %get-tuple-element.27.swap_keep, ...), custom_call_target="tpu_custom_call" | custom-call | flops 262144 | bytes 1024000 | tf_op jit(solution)/shard_map/pallas_call | solution.py:217
  (2 shorter events, 0.0 us)
Async XLA Ops:
  1.4 11.1 %collective-permute-start.1 = (f32[200,256]{1,0:T(8,128)S(1)}, f32[200,256]{1,0:T(8,128)S(1)}, u32[]{:S(2)}, u32[]{:S(2)}) collective-permute-start(f32[200,256]{1,0:T(8,128)S(1)} %shard_map.56.own_ref.slab_ref), channel_id=1, source_target_pairs={{0,4},{2,6},{4,8},{6,10},{8,12},{10,14},{12,16},{14,18},{16,20},{1... | collective-permute-start | bytes 614408 | tf_op jit(solution)/shard_map/ppermute | solution.py:237
  4.4 7.0 %collective-permute-start = (f32[200,256]{1,0:T(8,128)S(1)}, f32[200,256]{1,0:T(8,128)S(1)}, u32[]{:S(2)}, u32[]{:S(2)}) collective-permute-start(f32[200,256]{1,0:T(8,128)S(1)} %shard_map.56.own_ref.slab_ref), channel_id=1, source_target_pairs={{0,2},{2,8},{4,6},{6,4},{8,10},{10,16},{12,14},{14,12},{16,18},{18... | collective-permute-start | bytes 614408 | tf_op jit(solution)/shard_map/ppermute | solution.py:237
  6.1 5.6 %collective-permute-start.4 = (f32[64,128]{1,0:T(8,128)S(1)}, f32[64,128]{1,0:T(8,128)S(1)}, u32[]{:S(2)}, u32[]{:S(2)}) collective-permute-start(f32[64,128]{1,0:T(8,128)S(1)} %bitcast.5), channel_id=1, source_target_pairs={{0,1},{1,0},{2,3},{3,2},{4,5},{5,4},{6,7},{7,6},{8,9},{9,8},{10,11... | collective-permute-start | bytes 98312 | tf_op jit(solution)/shard_map/ppermute | solution.py:241
  11.4 2.7 %collective-permute-start.3 = (f32[200,256]{1,0:T(8,128)S(1)}, f32[200,256]{1,0:T(8,128)S(1)}, u32[]{:S(2)}, u32[]{:S(2)}) collective-permute-start(f32[200,256]{1,0:T(8,128)S(1)} %shard_map.56.own_ref.slab_ref), channel_id=1, source_target_pairs={{0,2},{2,0},{4,6},{6,12},{8,10},{10,8},{12,14},{14,20},{16,18},{18... | collective-permute-start | bytes 614408 | tf_op jit(solution)/shard_map/ppermute | solution.py:237
  12.5 2.0 %collective-permute-start.5 = (f32[200,256]{1,0:T(8,128)S(1)}, f32[200,256]{1,0:T(8,128)S(1)}, u32[]{:S(2)}, u32[]{:S(2)}) collective-permute-start(f32[200,256]{1,0:T(8,128)S(1)} %collective-permute-done.1.two_ref.refs_4_), channel_id=1, source_target_pairs={{0,2},{2,0},{4,6},{6,4},{8,10},{10,8},{12,14},{14,12},{16,18},{18,... | collective-permute-start | bytes 614408 | tf_op jit(solution)/shard_map/ppermute | solution.py:237
  12.5 4.0 %collective-permute-start.2 = (f32[64,128]{1,0:T(8,128)S(1)}, f32[64,128]{1,0:T(8,128)S(1)}, u32[]{:S(2)}, u32[]{:S(2)}) collective-permute-start(f32[64,128]{1,0:T(8,128)S(1)} %bitcast.4), channel_id=1, source_target_pairs={{0,1},{1,0},{2,3},{3,2},{4,5},{5,4},{6,7},{7,6},{8,9},{9,8},{10,11... | collective-permute-start | bytes 98312 | tf_op jit(solution)/shard_map/ppermute | solution.py:241
  14.8 4.3 %collective-permute-start.6 = (f32[128,128]{1,0:T(8,128)S(1)}, f32[128,128]{1,0:T(8,128)S(1)}, u32[]{:S(2)}, u32[]{:S(2)}) collective-permute-start(f32[128,128]{1,0:T(8,128)S(1)} %bitcast.3), channel_id=1, source_target_pairs={{0,1},{1,0},{2,3},{3,2},{4,5},{5,4},{6,7},{7,6},{8,9},{9,8},{10,11... | collective-permute-start | bytes 196616 | tf_op jit(solution)/shard_map/ppermute | solution.py:241

commit v14 on v8

v14 whole, which is shorter than its diff:
```python
import functools
import jax
import jax.numpy as jnp
from jax import lax
from jax.experimental import pallas as pl
from jax.experimental.pallas import tpu as pltpu
from jax.sharding import PartitionSpec as P

LANES = 128
F32 = jnp.float32
ONCHIP = pl.BlockSpec(memory_space=pltpu.VMEM)
OFFCHIP = pl.BlockSpec(memory_space=pltpu.HBM)


def column(labels):
    return jnp.broadcast_to(labels.astype(F32), (LANES, labels.shape[1])).T


def fold(rows, row_labels, cd_labels):
    tiles = rows.shape[1] // LANES
    kept = [
        jnp.where(row_labels == cd_labels[:, k * LANES:(k + 1) * LANES], rows[:, k * LANES:(k + 1) * LANES], 0.0)
        for k in range(tiles)
    ]
    kept = [kept[k] + kept[k + tiles // 2] for k in range(tiles // 2)]
    low = lower(kept[0].shape)
    first, middle, last = kept
    middle_turned, last_turned = turned(middle), turned(last)
    return first + jnp.where(low, middle_turned, last_turned), middle + last_turned


def lower(shape):
    return lax.broadcasted_iota(jnp.int32, shape, 1) < LANES // 2


def turned(array):
    return pltpu.roll(array, LANES // 2, 1)


def fetch(pairs, sems):
    copies = [pltpu.make_async_copy(src, dst, sems.at[i]) for i, (src, dst) in enumerate(pairs)]
    for copy in copies:
        copy.start()
    return copies


def pack_kernel(amp_ref, ij_ref, cd_ref, out_ref, amp, ij, cd, sems):
    pairs, width = amp.shape[0], out_ref.shape[0] - 8
    copies = fetch([(amp_ref, amp), (ij_ref, ij), (cd_ref, cd)], sems)
    copies[1].wait()
    copies[2].wait()
    rows = column(ij[...])
    labels = cd[...].astype(F32)
    out_ref[width:, :] = jnp.broadcast_to(ij[...].astype(F32), (8, pairs))
    copies[0].wait()
    for start in range(0, pairs, LANES):
        part = slice(start, start + LANES)
        first, second = fold(amp[part, :], rows[part], labels)
        out_ref[:LANES, part] = first.T
        out_ref[LANES:width, part] = second.T[:width - LANES]


def row_labels(rows):
    tile = rows[:, -LANES:]
    return jnp.where(lower(tile.shape), turned(tile), tile)


def narrowed(rows, slab_ref):
    width = slab_ref.shape[0] - 8
    full = jnp.dot(rows[:, :width], slab_ref[:width, :], precision=lax.Precision.HIGHEST, preferred_element_type=F32)
    slab_labels, own_labels = slab_ref[width:width + 1, :], row_labels(rows)
    total = None
    for start in range(0, full.shape[1], LANES):
        part = slice(start, start + LANES)
        kept = jnp.where(own_labels == slab_labels[:, part], full[:, part], 0.0)
        total = kept if total is None else total + kept
    return total + turned(total)


def beside(one, other):
    return jnp.where(lower(one.shape), one, other)


def apart(array):
    low, other = lower(array.shape), turned(array)
    return jnp.where(low, array, other), jnp.where(low, other, array)


def halved(term):
    half = term.shape[0] // 2
    return beside(term[:half], term[half:])


def unhalved(term):
    return jnp.concatenate(apart(term), axis=0)


def odd():
    return lax.rem(lax.axis_index("blk"), 2) == 1


def first_kernel(count, v_ref, ab_ref, cd_ref, rows_ref, v, ab, cd, labels, sems):
    parts = v.shape[0] // count
    mine = lax.axis_index("red")
    places = [pl.ds(pl.multiple_of(lax.rem(mine + k, parts) * count, count), count) for k in range(parts)]
    held = [pl.ds(k * count, count) for k in range(parts)]
    copies = fetch([(ab_ref, ab), (cd_ref, cd)] + [(v_ref.at[p], v.at[h]) for p, h in zip(places, held)], sems)
    copies[0].wait()
    copies[1].wait()
    labels[...] = column(ab[...])
    cd_labels = cd[...].astype(F32)
    for copy, p, h in zip(copies[2:], places, held):
        own_labels = labels[p, :]
        copy.wait()
        leading, last = fold(v[h, :], own_labels, cd_labels)
        rows_ref[h, :LANES] = leading
        rows_ref[h, LANES:] = beside(last, own_labels)


def labels_kernel(slab_ref, out_ref):
    out_ref[...] = slab_ref[slab_ref.shape[0] - 8:, :]


def own_kernel(rows_ref, own_ref, out_ref):
    out_ref[...] = narrowed(rows_ref[...], own_ref)


def near_kernel(rows_ref, twin_ref, below_ref, own_ref, mine_out, twin_out):
    @pl.when(odd())
    def _():
        mine_out[...] = narrowed(rows_ref[...], below_ref)
        twin_out[...] = narrowed(twin_ref[...], below_ref)

    @pl.when(~odd())
    def _():
        mine_out[...] = jnp.zeros_like(mine_out)
        twin_out[...] = narrowed(twin_ref[...], own_ref)


def far_terms(part, rows_ref, twin_ref, far_ref, third_ref):
    count = rows_ref[part, :].shape[0]
    both = narrowed(jnp.concatenate([rows_ref[part, :], twin_ref[part, :]], axis=0), far_ref)
    return both[:count], both[count:], narrowed(twin_ref[part, :], third_ref)


def send_kernel(rows_ref, twin_ref, far_ref, third_ref, own_term, mine_term, twin_term, send_ref):
    parts, count = send_ref.shape[0] + 1, send_ref.shape[1] // 3
    tail = slice(count, None)
    held = [slice(k * count, (k + 1) * count) for k in range(parts - 1)]

    @pl.when(odd())
    def _():
        mine, twin, third = far_terms(tail, rows_ref, twin_ref, far_ref, third_ref)
        second, last = beside(twin_term[tail, :], twin), beside(mine, third)
        for k, h in enumerate(held):
            send_ref[k, count:2 * count, :] = second[h]
            send_ref[k, 2 * count:, :] = last[h]

    @pl.when(~odd())
    def _():
        for k in range(parts - 1):
            send_ref[k, count:2 * count, :] = twin_term[(k + 1) * count:(k + 2) * count, :]
            send_ref[k, 2 * count:, :] = jnp.zeros((count, LANES), F32)

    first = beside(own_term[tail, :], mine_term[tail, :])
    for k, h in enumerate(held):
        send_ref[k, :count, :] = first[h]


def keep_kernel(rows_ref, twin_ref, below_ref, far_ref, third_ref, own_ref, twin_term, second_out, last_out, labels_out):
    count = second_out.shape[0]
    width = own_ref.shape[0] - 8
    head = slice(0, count)

    @pl.when(odd())
    def _():
        mine, twin, third = far_terms(head, rows_ref, twin_ref, far_ref, third_ref)
        second_out[...] = beside(twin_term[head, :], twin)
        last_out[...] = beside(mine, third)

    @pl.when(~odd())
    def _():
        second_out[...] = twin_term[head, :]
        last_out[...] = jnp.zeros_like(last_out)

    own = own_ref[width:width + 1, :]
    sent = [jnp.where(odd(), ref[width:width + 1, :], own) for ref in (below_ref, far_ref, third_ref)]
    tiles = [label[:, start:start + LANES] for label in sent for start in range(0, own.shape[1], LANES)]
    labels_out[...] = jnp.concatenate((tiles * 8)[:8], axis=0)


def sum_kernel(second_keep, last_keep, labels_ref, *refs):
    taken, (cross_ref, last_out) = refs[:-2], refs[-2:]
    count = second_keep.shape[0]
    last = sum([ref[2 * count:, :] for ref in taken], last_keep[...])
    cross_ref[:count, :] = sum([ref[count:2 * count, :] for ref in taken], second_keep[...])
    cross_ref[count:count + count // 2, :] = halved(apart(last)[1])
    cross_ref[count + count // 2:, :] = labels_ref[...]
    last_out[...] = last


def finish_kernel(parts, rows_ref, own_term, mine_term, last_ref, own_labels, below_ref, far_ref, cross_ref, *refs):
    taken, (out_ref, out, sems) = refs[:parts - 1], refs[parts - 1:]
    count = last_ref.shape[0]
    width = below_ref.shape[0] - 8
    tiles = out.shape[2] // LANES
    rows = row_labels(rows_ref[:count, :])
    copies = []

    def store(m, term, labels):
        for k in range(tiles):
            out[m, :, k * LANES:(k + 1) * LANES] = jnp.where(rows == labels[k], term, 0.0)
        copies.append(pltpu.make_async_copy(out.at[m], out_ref.at[m], sems.at[m]))
        copies[-1].start()

    def of(ref, row=width):
        return [ref[row:row + 1, k * LANES:(k + 1) * LANES] for k in range(tiles)]

    def pick(one, other):
        return [jnp.where(odd(), x, y) for x, y in zip(one, other)]

    start = count + count // 2
    labels = [[cross_ref[start + i * tiles + k:start + i * tiles + k + 1, :] for k in range(tiles)] for i in range(3)]
    pairs = [apart(ref[:count, :]) for ref in taken]
    store(0, sum([own for own, _ in pairs], own_term[:count, :]), of(own_labels, 0))
    mine = sum([mine for _, mine in pairs], mine_term[:count, :])
    one, two = apart(cross_ref[:count, :])
    store(1, one, labels[0])
    store(2, jnp.where(odd(), mine, two), pick(of(below_ref), labels[1]))
    far, three = apart(last_ref[...])[0], unhalved(cross_ref[count:start, :])
    store(3, jnp.where(odd(), far, three), pick(of(far_ref), labels[2]))
    for copy in copies:
        copy.wait()


def whole(*shape):
    return jax.ShapeDtypeStruct(shape, F32)


def call(kernel, out_shape, args, flops, off=0, scratch=(), out_specs=ONCHIP):
    moved = sum(a.size * 4 for a in list(args) + out_shape)
    args = [pltpu.with_memory_space_constraint(a, pltpu.HBM) for a in args[:off]] + list(args[off:])
    return pl.pallas_call(
        kernel,
        out_shape=out_shape,
        in_specs=[OFFCHIP] * off + [ONCHIP] * (len(args) - off),
        out_specs=[out_specs] * len(out_shape),
        scratch_shapes=list(scratch),
        cost_estimate=pl.CostEstimate(flops=flops, bytes_accessed=0, transcendentals=0),
        compiler_params=pltpu.CompilerParams(vmem_limit_bytes=32 * 1024 * 1024),
    )(*args)


def body(amplitudes, integrals, cd_irrep, ab_irrep, ij_irrep):
    blocks, parts = lax.axis_size("blk"), lax.axis_size("red")
    pairs, depth = amplitudes.shape
    row_count = integrals.shape[0]
    width = depth // 4
    count = row_count // parts
    one_product = 12 * row_count * width * pairs

    def moved(array, steps):
        return lax.ppermute(array, "blk", [(i, (i + steps[i % 4]) % blocks) for i in range(blocks)])

    def exchanged(array):
        return [
            lax.ppermute(array[k - 1], "red", [(i, (i + k) % parts) for i in range(parts)])
            for k in range(1, parts)
        ]

    def after(array, *earlier):
        return lax.optimization_barrier((array, *earlier))[0]

    def staging(array, labels, copies):
        return [
            pltpu.VMEM(array.shape, F32),
            pltpu.VMEM(labels.shape, jnp.int32),
            pltpu.VMEM(cd_irrep.shape, jnp.int32),
        ], pltpu.SemaphoreType.DMA((2 + copies,))

    stage, sems = staging(amplitudes, ij_irrep, 1)
    own, = call(pack_kernel, [whole(width + 8, pairs)], (amplitudes, ij_irrep, cd_irrep),
                4 * amplitudes.size, 3, stage + [sems])
    def up(array, step):
        pairs_of = [
            ((b, r), ((b + step) % blocks, r) if b % 2 else (b, (r + 1) % parts))
            for b in range(blocks) for r in range(parts)
        ]
        return lax.ppermute(array, ("blk", "red"), [(b * parts + r, c * parts + t) for (b, r), (c, t) in pairs_of])

    below = up(own, 2)
    own_labels, = call(labels_kernel, [whole(8, pairs)], (own,), 8 * pairs)
    stage, sems = staging(integrals, ab_irrep, parts)
    rows, = call(
        functools.partial(first_kernel, count), [whole(row_count, 2 * LANES)],
        (after(integrals, own_labels), ab_irrep, cd_irrep), 0, 3,
        stage + [pltpu.VMEM((row_count, LANES), F32), sems])
    far = moved(after(own, own_labels), (3, -1, 3, -1))
    twin = moved(rows, (1, -1, 1, -1))
    term = whole(row_count, LANES)
    own_term, = call(own_kernel, [term], (rows, own), 64 * one_product)
    third = up(after(own, own_term), 4)
    mine_term, twin_term = call(near_kernel, [term, term], (rows, twin, below, own), 0)
    send, = call(send_kernel, [whole(parts - 1, 3 * count, LANES)],
                 (rows, twin, far, third, own_term, mine_term, twin_term), 0)
    taken = exchanged(send)
    second_keep, last_keep, cross_labels = call(
        keep_kernel, [whole(count, LANES), whole(count, LANES), whole(8, LANES)],
        (rows, twin, below, far, after(third, send), own, twin_term), 0)
    summed, last = call(sum_kernel, [whole(count + count // 2 + 8, LANES), whole(count, LANES)],
                        (second_keep, last_keep, cross_labels, *taken), 0)
    cross = moved(summed, (1, -1, 1, -1))
    out, = call(functools.partial(finish_kernel, parts), [whole(4, count, pairs)],
                (rows, own_term, mine_term, last, own_labels, below, far, cross, *taken),
                4 * 2 * count * pairs, 0, [pltpu.VMEM((4, count, pairs), F32), pltpu.SemaphoreType.DMA((4,))], OFFCHIP)
    return out


def solution(mesh):
    in_specs = (P("blk", "red"), P("blk", "red"), P("red", None), P("blk", None), P("blk", None))
    out_specs = P(None, ("blk", "red"), None)
    return jax.shard_map(body, mesh=mesh, in_specs=in_specs, out_specs=out_specs, check_vma=False)
```

time: 20.8 us -> 22.6 us (1.087)
  waiting for transfers between devices: 8.93 us -> 10.3 us
  starting transfers between devices: 6.22 us -> 7.52 us
  Pallas kernels: 5.36 us -> 4.59 us
    ppermute x0 -> x2, starting transfers between devices: none -> 4.59 us  [up(): lax.ppermute(array, ('blk', 'red'), [(b * parts + r, c * parts + t) for (...]
    ppermute x0 -> x2, waiting for transfers between devices: none -> 3.78 us  [up(): lax.ppermute(array, ('blk', 'red'), [(b * parts + r, c * parts + t) for (...]
    ppermute x3, waiting for transfers between devices: 3.79 us -> 0.95 us  [moved(): lax.ppermute(array, 'blk', [(i, (i + steps[i % 4]) % blocks) for i in ran...]
    ppermute x3, starting transfers between devices: 3.05 us -> 1.34 us  [moved(): lax.ppermute(array, 'blk', [(i, (i + steps[i % 4]) % blocks) for i in ran...]
    ppermute x2 -> x1, starting transfers between devices: 3.17 us -> 1.58 us  [exchanged(): lax.ppermute(array[k - 1], 'red', [(i, (i + k) % parts) for i in range(pa...]
    pallas_call x7 -> x9, Pallas kernels: 5.36 us -> 4.59 us  [call(): pl.pallas_call(kernel, out_shape=out_shape, in_specs=[OFFCHIP] * off + [O...]
    ppermute x2 -> x1, waiting for transfers between devices: 5.14 us -> 5.53 us  [exchanged(): lax.ppermute(array[k - 1], 'red', [(i, (i + k) % parts) for i in range(pa...]
  transfers between devices with their start and end apart: 5 -> 6, of which waited for: 5 -> 3; matrix products, arithmetic and copies ran while one was open for 0% -> 0% of each run, Pallas kernels for 13% -> 10%
where the time goes in v14:
time: 22.6 us; the launch traced here: 22.4 us
  waiting for transfers between devices  10.3 us (46%)
  starting transfers between devices  7.52 us (33%)
  Pallas kernels  4.59 us (20%)
    ppermute x1, waiting for transfers between devices, exchanged(): lax.ppermute(array[k - 1], 'red', [(i, (i + k) % parts) for i in range(pa...  5.53 us
    ppermute x2, starting transfers between devices, up(): lax.ppermute(array, ('blk', 'red'), [(b * parts + r, c * parts + t) for (...  4.59 us
    pallas_call x9, Pallas kernels, call(): pl.pallas_call(kernel, out_shape=out_shape, in_specs=[OFFCHIP] * off + [O...  4.59 us
    ppermute x2, waiting for transfers between devices, up(): lax.ppermute(array, ('blk', 'red'), [(b * parts + r, c * parts + t) for (...  3.78 us
    ppermute x1, starting transfers between devices, exchanged(): lax.ppermute(array[k - 1], 'red', [(i, (i + k) % parts) for i in range(pa...  1.58 us
    ppermute x3, starting transfers between devices, moved(): lax.ppermute(array, 'blk', [(i, (i + steps[i % 4]) % blocks) for i in ran...  1.34 us
    ppermute x3, waiting for transfers between devices, moved(): lax.ppermute(array, 'blk', [(i, (i + steps[i % 4]) % blocks) for i in ran...  0.95 us
  transfers between devices with their start and end apart: 6, of which 3 were waited for; matrix products, arithmetic and copies ran while one was open for 0% of the time, Pallas kernels for 10%

profile of v14, /device:TPU:0, one launch (start us, length us, event | category | flops | bytes accessed | tf_op | source)
XLA Modules:
  0.0 22.4 jit_solution(13893831711348250868)
XLA Ops:
  0.0 1.4 %shard_map.55.slab_ref.own_ref = f32[200,256]{1,0:T(8,128)S(1)} custom-call(f32[256,768]{1,0:T(8,128)} %amp_ref.1, s32[1,256]{1,0:T(1,128)} %ij_ref.1, s32[1,768]{1,0:T(1,128)} %cd_ref.3), custom_call_target="tpu_custom_call" | custom-call | flops 786432 | tf_op jit(solution)/shard_map/pallas_call | solution.py:243
  1.4 3.0 %collective-permute-start.1 = (f32[200,256]{1,0:T(8,128)S(1)}, f32[200,256]{1,0:T(8,128)S(1)}, u32[]{:S(2)}, u32[]{:S(2)}) collective-permute-start(f32[200,256]{1,0:T(8,128)S(1)} %shard_map.55.slab_ref.own_ref), channel_id=1, source_target_pairs={{0,1},{1,0},{2,6},{3,7},{4,5},{5,4},{6,10},{7,11},{8,9},{9,8},{10,... | collective-permute-start | bytes 614408 | tf_op jit(solution)/shard_map/ppermute | solution.py:289
  4.4 0.7 %collective-permute-start.2 = (f32[200,256]{1,0:T(8,128)S(1)}, f32[200,256]{1,0:T(8,128)S(1)}, u32[]{:S(2)}, u32[]{:S(2)}) collective-permute-start(f32[200,256]{1,0:T(8,128)S(1)} %shard_map.55.slab_ref.own_ref), channel_id=1, source_target_pairs={{0,6},{2,0},{4,10},{6,4},{8,14},{10,8},{12,18},{14,12},{16,22},{18... | collective-permute-start | bytes 614408 | tf_op jit(solution)/shard_map/ppermute | solution.py:263
  5.1 1.3 %shard_map.57.rows_ref = f32[256,256]{1,0:T(8,128)S(1)} custom-call(f32[256,768]{1,0:T(8,128)} %v_ref, s32[1,256]{1,0:T(1,128)} %ab_ref.1, s32[1,768]{1,0:T(1,128)} %cd_ref.3), custom_call_target="tpu_custom_call" | custom-call | tf_op jit(solution)/shard_map/pallas_call | solution.py:243
  6.4 0.1 collective-permute-start
  6.5 0.4 %shard_map.58.own_term = f32[256,128]{1,0:T(8,128)S(1)} custom-call(f32[256,256]{1,0:T(8,128)S(1)} %shard_map.57.rows_ref, f32[200,256]{1,0:T(8,128)S(1)} %shard_map.55.slab_ref.own_ref), custom_call_target="tpu_custom_call" | custom-call | flops 9663676416 | tf_op jit(solution)/shard_map/pallas_call | solution.py:243
  6.9 1.6 %collective-permute-start.3 = (f32[200,256]{1,0:T(8,128)S(1)}, f32[200,256]{1,0:T(8,128)S(1)}, u32[]{:S(2)}, u32[]{:S(2)}) collective-permute-start(f32[200,256]{1,0:T(8,128)S(1)} %shard_map.55.slab_ref.own_ref), channel_id=1, source_target_pairs={{0,1},{1,0},{2,10},{3,11},{4,5},{5,4},{6,14},{7,15},{8,9},{9,8},{1... | collective-permute-start | bytes 614408 | tf_op jit(solution)/shard_map/ppermute | solution.py:289
  8.5 0.0 collective-permute-done.1.below_ref
  8.5 0.0 collective-permute-done.twin_ref
  8.5 0.4 %shard_map.59 = (f32[256,128]{1,0:T(8,128)S(1)}, f32[256,128]{1,0:T(8,128)S(1)}) custom-call(f32[256,256]{1,0:T(8,128)S(1)} %shard_map.57.rows_ref, f32[256,256]{1,0:T(8,128)S(1)} %collective-permute-done.twin_ref, f32[200,256]{1,0:T(8,128)S(1)} %collective-permute-done.1.below_ref, f32[200,256]{1,0:T(8,128)S(1)} %shard_map.55.slab_ref.own_ref), custom_call_target="tpu_custom_call" | custom-call | tf_op jit(solution)/shard_map/pallas_call | solution.py:243
  8.9 0.0 collective-permute-done.2.far_ref
  8.9 3.8 %collective-permute-done.3.third_ref = f32[200,256]{1,0:T(8,128)S(1)} collective-permute-done((f32[200,256]{1,0:T(8,128)S(1)}, f32[200,256]{1,0:T(8,128)S(1)}, u32[]{:S(2)}, u32[]{:S(2)}) %collective-permute-start.3) | collective-permute-done | bytes 204832 | tf_op jit(solution)/shard_map/ppermute | solution.py:289
  12.7 1.6 %collective-permute-start.4 = (f32[384,128]{1,0:T(8,128)S(1)}, f32[384,128]{1,0:T(8,128)S(1)}, u32[]{:S(2)}, u32[]{:S(2)}) collective-permute-start(f32[384,128]{1,0:T(8,128)S(1)} %bitcast.1), channel_id=1, source_target_pairs={{0,1},{1,0},{2,3},{3,2},{4,5},{5,4},{6,7},{7,6},{8,9},{9,8},{10,11... | collective-permute-start | bytes 589832 | tf_op jit(solution)/shard_map/ppermute | solution.py:267
  14.3 5.5 %collective-permute-done.4.refs_0_ = f32[384,128]{1,0:T(8,128)S(1)} collective-permute-done((f32[384,128]{1,0:T(8,128)S(1)}, f32[384,128]{1,0:T(8,128)S(1)}, u32[]{:S(2)}, u32[]{:S(2)}) %collective-permute-start.4) | collective-permute-done | bytes 196640 | tf_op jit(solution)/shard_map/ppermute | solution.py:267
  19.9 0.1 shard_map.62
  20.0 0.6 %collective-permute-start.5 = (f32[200,128]{1,0:T(8,128)S(1)}, f32[200,128]{1,0:T(8,128)S(1)}, u32[]{:S(2)}, u32[]{:S(2)}) collective-permute-start(f32[200,128]{1,0:T(8,128)S(1)} %get-tuple-element.26), channel_id=1, source_target_pairs={{0,2},{2,0},{4,6},{6,4},{8,10},{10,8},{12,14},{14,12},{16,18},{18,... | collective-permute-start | bytes 307208 | tf_op jit(solution)/shard_map/ppermute | solution.py:263
  20.5 0.9 %collective-permute-done.5.cross_ref = f32[200,128]{1,0:T(8,128)S(1)} collective-permute-done((f32[200,128]{1,0:T(8,128)S(1)}, f32[200,128]{1,0:T(8,128)S(1)}, u32[]{:S(2)}, u32[]{:S(2)}) %collective-permute-start.5) | collective-permute-done | bytes 102432 | tf_op jit(solution)/shard_map/ppermute | solution.py:263
  21.5 0.9 %shard_map.63 = f32[4,128,256]{2,1,0:T(8,128)} custom-call(f32[256,256]{1,0:T(8,128)S(1)} %shard_map.57.rows_ref, f32[256,128]{1,0:T(8,128)S(1)} %shard_map.58.own_term, f32[256,128]{1,0:T(8,128)S(1)} %get-tuple-element.17.mine_term, f32[128,128]{1,0:T(8,128)S(1)} %get-tuple-element.25.last_ref, f32[8,256]{1,0:T(8,128)S(1)} %shard_map.56.own_labels, ...), custom_call_target="tpu_custom_call" | custom-call | flops 262144 | tf_op jit(solution)/shard_map/pallas_call | solution.py:243
  (3 shorter events, 0.0 us)
Async XLA Ops:
  1.4 7.1 %collective-permute-start.1 = (f32[200,256]{1,0:T(8,128)S(1)}, f32[200,256]{1,0:T(8,128)S(1)}, u32[]{:S(2)}, u32[]{:S(2)}) collective-permute-start(f32[200,256]{1,0:T(8,128)S(1)} %shard_map.55.slab_ref.own_ref), channel_id=1, source_target_pairs={{0,1},{1,0},{2,6},{3,7},{4,5},{5,4},{6,10},{7,11},{8,9},{9,8},{10,... | collective-permute-start | bytes 614408 | tf_op jit(solution)/shard_map/ppermute | solution.py:289
  4.4 4.5 %collective-permute-start.2 = (f32[200,256]{1,0:T(8,128)S(1)}, f32[200,256]{1,0:T(8,128)S(1)}, u32[]{:S(2)}, u32[]{:S(2)}) collective-permute-start(f32[200,256]{1,0:T(8,128)S(1)} %shard_map.55.slab_ref.own_ref), channel_id=1, source_target_pairs={{0,6},{2,0},{4,10},{6,4},{8,14},{10,8},{12,18},{14,12},{16,22},{18... | collective-permute-start | bytes 614408 | tf_op jit(solution)/shard_map/ppermute | solution.py:263
  6.4 2.1 %collective-permute-start = (f32[256,256]{1,0:T(8,128)S(1)}, f32[256,256]{1,0:T(8,128)S(1)}, u32[]{:S(2)}, u32[]{:S(2)}) collective-permute-start(f32[256,256]{1,0:T(8,128)S(1)} %shard_map.57.rows_ref), channel_id=1, source_target_pairs={{0,2},{2,0},{4,6},{6,4},{8,10},{10,8},{12,14},{14,12},{16,18},{18,... | collective-permute-start | bytes 786440 | tf_op jit(solution)/shard_map/ppermute | solution.py:263
  6.9 5.8 %collective-permute-start.3 = (f32[200,256]{1,0:T(8,128)S(1)}, f32[200,256]{1,0:T(8,128)S(1)}, u32[]{:S(2)}, u32[]{:S(2)}) collective-permute-start(f32[200,256]{1,0:T(8,128)S(1)} %shard_map.55.slab_ref.own_ref), channel_id=1, source_target_pairs={{0,1},{1,0},{2,10},{3,11},{4,5},{5,4},{6,14},{7,15},{8,9},{9,8},{1... | collective-permute-start | bytes 614408 | tf_op jit(solution)/shard_map/ppermute | solution.py:289
  12.7 7.1 %collective-permute-start.4 = (f32[384,128]{1,0:T(8,128)S(1)}, f32[384,128]{1,0:T(8,128)S(1)}, u32[]{:S(2)}, u32[]{:S(2)}) collective-permute-start(f32[384,128]{1,0:T(8,128)S(1)} %bitcast.1), channel_id=1, source_target_pairs={{0,1},{1,0},{2,3},{3,2},{4,5},{5,4},{6,7},{7,6},{8,9},{9,8},{10,11... | collective-permute-start | bytes 589832 | tf_op jit(solution)/shard_map/ppermute | solution.py:267
  20.0 1.5 %collective-permute-start.5 = (f32[200,128]{1,0:T(8,128)S(1)}, f32[200,128]{1,0:T(8,128)S(1)}, u32[]{:S(2)}, u32[]{:S(2)}) collective-permute-start(f32[200,128]{1,0:T(8,128)S(1)} %get-tuple-element.26), channel_id=1, source_target_pairs={{0,2},{2,0},{4,6},{6,4},{8,10},{10,8},{12,14},{14,12},{16,18},{18,... | collective-permute-start | bytes 307208 | tf_op jit(solution)/shard_map/ppermute | solution.py:263

commit v15 on v14

--- a/solution.py
+++ b/solution.py
@@ -125,7 +125,23 @@
     out_ref[...] = narrowed(rows_ref[...], own_ref)
 
 
-def near_kernel(rows_ref, twin_ref, below_ref, own_ref, mine_out, twin_out):
+def early_kernel(twin_ref, own_ref, own_term, twin_out, send_ref):
+    parts, count = send_ref.shape[0] + 1, send_ref.shape[1]
+
+    @pl.when(~odd())
+    def _():
+        twin_out[...] = narrowed(twin_ref[...], own_ref)
+
+    @pl.when(odd())
+    def _():
+        twin_out[...] = jnp.zeros_like(twin_out)
+
+    both = beside(own_term[count:, :], twin_out[count:, :])
+    for k in range(parts - 1):
+        send_ref[k] = both[k * count:(k + 1) * count]
+
+
+def near_kernel(rows_ref, twin_ref, below_ref, mine_out, twin_out):
     @pl.when(odd())
     def _():
         mine_out[...] = narrowed(rows_ref[...], below_ref)
@@ -134,7 +150,7 @@
     @pl.when(~odd())
     def _():
         mine_out[...] = jnp.zeros_like(mine_out)
-        twin_out[...] = narrowed(twin_ref[...], own_ref)
+        twin_out[...] = jnp.zeros_like(twin_out)
 
 
 def far_terms(part, rows_ref, twin_ref, far_ref, third_ref):
@@ -143,44 +159,39 @@
     return both[:count], both[count:], narrowed(twin_ref[part, :], third_ref)
 
 
-def send_kernel(rows_ref, twin_ref, far_ref, third_ref, own_term, mine_term, twin_term, send_ref):
-    parts, count = send_ref.shape[0] + 1, send_ref.shape[1] // 3
+def send_kernel(rows_ref, twin_ref, far_ref, third_ref, mine_term, twin_term, send_ref):
+    parts, count = send_ref.shape[0] + 1, 2 * send_ref.shape[1] // 5
     tail = slice(count, None)
-    held = [slice(k * count, (k + 1) * count) for k in range(parts - 1)]
 
     @pl.when(odd())
     def _():
         mine, twin, third = far_terms(tail, rows_ref, twin_ref, far_ref, third_ref)
-        second, last = beside(twin_term[tail, :], twin), beside(mine, third)
-        for k, h in enumerate(held):
-            send_ref[k, count:2 * count, :] = second[h]
-            send_ref[k, 2 * count:, :] = last[h]
+        pair, last = beside(twin_term[tail, :], twin), beside(mine, third)
+        for k in range(parts - 1):
+            held = slice(k * count, (k + 1) * count)
+            send_ref[k, :count, :] = pair[held]
+            send_ref[k, count:2 * count, :] = last[held]
+            send_ref[k, 2 * count:, :] = halved(mine_term[(k + 1) * count:(k + 2) * count, :])
 
     @pl.when(~odd())
     def _():
-        for k in range(parts - 1):
-            send_ref[k, count:2 * count, :] = twin_term[(k + 1) * count:(k + 2) * count, :]
-            send_ref[k, 2 * count:, :] = jnp.zeros((count, LANES), F32)
-
-    first = beside(own_term[tail, :], mine_term[tail, :])
-    for k, h in enumerate(held):
-        send_ref[k, :count, :] = first[h]
-
-
-def keep_kernel(rows_ref, twin_ref, below_ref, far_ref, third_ref, own_ref, twin_term, second_out, last_out, labels_out):
-    count = second_out.shape[0]
+        send_ref[...] = jnp.zeros_like(send_ref)
+
+
+def keep_kernel(rows_ref, twin_ref, below_ref, far_ref, third_ref, own_ref, twin_term, early_term, pair_out, last_out, labels_out):
+    count = pair_out.shape[0]
     width = own_ref.shape[0] - 8
     head = slice(0, count)
 
     @pl.when(odd())
     def _():
         mine, twin, third = far_terms(head, rows_ref, twin_ref, far_ref, third_ref)
-        second_out[...] = beside(twin_term[head, :], twin)
+        pair_out[...] = beside(twin_term[head, :], twin)
         last_out[...] = beside(mine, third)
 
     @pl.when(~odd())
     def _():
-        second_out[...] = twin_term[head, :]
+        pair_out[...] = early_term[head, :]
         last_out[...] = jnp.zeros_like(last_out)
 
     own = own_ref[width:width + 1, :]
@@ -189,18 +200,21 @@
     labels_out[...] = jnp.concatenate((tiles * 8)[:8], axis=0)
 
 
-def sum_kernel(second_keep, last_keep, labels_ref, *refs):
-    taken, (cross_ref, last_out) = refs[:-2], refs[-2:]
-    count = second_keep.shape[0]
-    last = sum([ref[2 * count:, :] for ref in taken], last_keep[...])
-    cross_ref[:count, :] = sum([ref[count:2 * count, :] for ref in taken], second_keep[...])
+def sum_kernel(parts, pair_keep, last_keep, labels_ref, *refs):
+    early_in, late_in, (cross_ref, last_out) = refs[:parts - 1], refs[parts - 1:-2], refs[-2:]
+    count = pair_keep.shape[0]
+    pair, last = pair_keep[...], last_keep[...]
+    for early, late in zip(early_in, late_in):
+        pair = pair + jnp.where(odd(), late[:count, :], apart(early[...])[1])
+        last = last + late[count:2 * count, :]
+    cross_ref[:count, :] = pair
     cross_ref[count:count + count // 2, :] = halved(apart(last)[1])
     cross_ref[count + count // 2:, :] = labels_ref[...]
     last_out[...] = last
 
 
 def finish_kernel(parts, rows_ref, own_term, mine_term, last_ref, own_labels, below_ref, far_ref, cross_ref, *refs):
-    taken, (out_ref, out, sems) = refs[:parts - 1], refs[parts - 1:]
+    early_in, late_in, (out_ref, out, sems) = refs[:parts - 1], refs[parts - 1:-3], refs[-3:]
     count = last_ref.shape[0]
     width = below_ref.shape[0] - 8
     tiles = out.shape[2] // LANES
@@ -221,9 +235,8 @@
 
     start = count + count // 2
     labels = [[cross_ref[start + i * tiles + k:start + i * tiles + k + 1, :] for k in range(tiles)] for i in range(3)]
-    pairs = [apart(ref[:count, :]) for ref in taken]
-    store(0, sum([own for own, _ in pairs], own_term[:count, :]), of(own_labels, 0))
-    mine = sum([mine for _, mine in pairs], mine_term[:count, :])
+    store(0, sum([apart(ref[...])[0] for ref in early_in], own_term[:count, :]), of(own_labels, 0))
+    mine = sum([unhalved(ref[2 * count:, :]) for ref in late_in], mine_term[:count, :])
     one, two = apart(cross_ref[:count, :])
     store(1, one, labels[0])
     store(2, jnp.where(odd(), mine, two), pick(of(below_ref), labels[1]))
@@ -281,37 +294,39 @@
     stage, sems = staging(amplitudes, ij_irrep, 1)
     own, = call(pack_kernel, [whole(width + 8, pairs)], (amplitudes, ij_irrep, cd_irrep),
                 4 * amplitudes.size, 3, stage + [sems])
-    def up(array, step):
-        pairs_of = [
-            ((b, r), ((b + step) % blocks, r) if b % 2 else (b, (r + 1) % parts))
-            for b in range(blocks) for r in range(parts)
-        ]
-        return lax.ppermute(array, ("blk", "red"), [(b * parts + r, c * parts + t) for (b, r), (c, t) in pairs_of])
-
-    below = up(own, 2)
+    def routed(array, of_odd, of_even):
+        routes = [((b, r), (of_odd if b % 2 else of_even)(b, r)) for b in range(blocks) for r in range(parts)]
+        return lax.ppermute(array, ("blk", "red"),
+                            [(b * parts + r, c % blocks * parts + t % parts) for (b, r), (c, t) in routes])
+
+    below = routed(own, lambda b, r: (b + 2, r), lambda b, r: (b ^ 2, r))
     own_labels, = call(labels_kernel, [whole(8, pairs)], (own,), 8 * pairs)
     stage, sems = staging(integrals, ab_irrep, parts)
     rows, = call(
         functools.partial(first_kernel, count), [whole(row_count, 2 * LANES)],
-        (after(integrals, own_labels), ab_irrep, cd_irrep), 0, 3,
+        (after(integrals, own_labels), ab_irrep, cd_irrep), 0 * one_product, 3,
         stage + [pltpu.VMEM((row_count, LANES), F32), sems])
     far = moved(after(own, own_labels), (3, -1, 3, -1))
     twin = moved(rows, (1, -1, 1, -1))
     term = whole(row_count, LANES)
     own_term, = call(own_kernel, [term], (rows, own), 64 * one_product)
-    third = up(after(own, own_term), 4)
-    mine_term, twin_term = call(near_kernel, [term, term], (rows, twin, below, own), 0)
-    send, = call(send_kernel, [whole(parts - 1, 3 * count, LANES)],
-                 (rows, twin, far, third, own_term, mine_term, twin_term), 0)
-    taken = exchanged(send)
-    second_keep, last_keep, cross_labels = call(
+    third = routed(after(own, rows), lambda b, r: (b + 4, r), lambda b, r: (b, r + 1))
+    early_term, early_send = call(early_kernel, [term, whole(parts - 1, count, LANES)], (twin, own, own_term), 0)
+    early_in = exchanged(early_send)
+    mine_term, twin_term = call(near_kernel, [term, term], (rows, twin, after(below, *early_in)), 0)
+    send, = call(send_kernel, [whole(parts - 1, 5 * count // 2, LANES)],
+                 (rows, twin, far, third, mine_term, twin_term), 0)
+    late_in = [
+        routed(send[k - 1], lambda b, r: (b, r + k), lambda b, r: (b ^ 2, r)) for k in range(1, parts)
+    ]
+    pair_keep, last_keep, cross_labels = call(
         keep_kernel, [whole(count, LANES), whole(count, LANES), whole(8, LANES)],
-        (rows, twin, below, far, after(third, send), own, twin_term), 0)
-    summed, last = call(sum_kernel, [whole(count + count // 2 + 8, LANES), whole(count, LANES)],
-                        (second_keep, last_keep, cross_labels, *taken), 0)
+        (rows, twin, below, far, after(third, send), own, twin_term, early_term), 0)
+    summed, last = call(functools.partial(sum_kernel, parts), [whole(count + count // 2 + 8, LANES), whole(count, LANES)],
+                        (pair_keep, last_keep, cross_labels, *early_in, *late_in), 0)
     cross = moved(summed, (1, -1, 1, -1))
     out, = call(functools.partial(finish_kernel, parts), [whole(4, count, pairs)],
-                (rows, own_term, mine_term, last, own_labels, below, far, cross, *taken),
+                (rows, own_term, mine_term, last, own_labels, below, far, cross, *early_in, *late_in),
                 4 * 2 * count * pairs, 0, [pltpu.VMEM((4, count, pairs), F32), pltpu.SemaphoreType.DMA((4,))], OFFCHIP)
     return out
 

time: 22.6 us -> 21.7 us (0.960)
  waiting for transfers between devices: 10.3 us -> 8.76 us
  starting transfers between devices: 7.52 us -> 8.04 us
    ppermute x1, waiting for transfers between devices: 5.53 us -> 3.65 us  [exchanged(): lax.ppermute(array[k - 1], 'red', [(i, (i + k) % parts) for i in range(pa...]
    ppermute x2 -> x3, starting transfers between devices: 4.59 us -> 6.12 us  [routed(): lax.ppermute(array, ('blk', 'red'), [(b * parts + r, c % blocks * parts +...]
    ppermute x1, starting transfers between devices: 1.58 us -> 1.07 us  [exchanged(): lax.ppermute(array[k - 1], 'red', [(i, (i + k) % parts) for i in range(pa...]
    ppermute x3, starting transfers between devices: 1.34 us -> 0.85 us  [moved(): lax.ppermute(array, 'blk', [(i, (i + steps[i % 4]) % blocks) for i in ran...]
    ppermute x3, waiting for transfers between devices: 0.95 us -> 1.3 us  [moved(): lax.ppermute(array, 'blk', [(i, (i + steps[i % 4]) % blocks) for i in ran...]
    pallas_call x9 -> x10, Pallas kernels: 4.59 us -> 4.65 us  [call(): pl.pallas_call(kernel, out_shape=out_shape, in_specs=[OFFCHIP] * off + [O...]
    ppermute x2 -> x3, waiting for transfers between devices: 3.78 us -> 3.81 us  [routed(): lax.ppermute(array, ('blk', 'red'), [(b * parts + r, c % blocks * parts +...]
  transfers between devices with their start and end apart: 6 -> 7, of which waited for: 3 -> 3; matrix products, arithmetic and copies ran while one was open for 0% -> 0% of each run, Pallas kernels for 10% -> 10%
where the time goes in v15:
time: 21.7 us; the launch traced here: 21.5 us
  waiting for transfers between devices  8.76 us (40%)
  starting transfers between devices  8.04 us (37%)
  Pallas kernels  4.65 us (21%)
    ppermute x3, starting transfers between devices, routed(): lax.ppermute(array, ('blk', 'red'), [(b * parts + r, c % blocks * parts +...  6.12 us
    pallas_call x10, Pallas kernels, call(): pl.pallas_call(kernel, out_shape=out_shape, in_specs=[OFFCHIP] * off + [O...  4.65 us
    ppermute x3, waiting for transfers between devices, routed(): lax.ppermute(array, ('blk', 'red'), [(b * parts + r, c % blocks * parts +...  3.81 us
    ppermute x1, waiting for transfers between devices, exchanged(): lax.ppermute(array[k - 1], 'red', [(i, (i + k) % parts) for i in range(pa...  3.65 us
    ppermute x3, waiting for transfers between devices, moved(): lax.ppermute(array, 'blk', [(i, (i + steps[i % 4]) % blocks) for i in ran...  1.3 us
    ppermute x1, starting transfers between devices, exchanged(): lax.ppermute(array[k - 1], 'red', [(i, (i + k) % parts) for i in range(pa...  1.07 us
    ppermute x3, starting transfers between devices, moved(): lax.ppermute(array, 'blk', [(i, (i + steps[i % 4]) % blocks) for i in ran...  0.85 us
  transfers between devices with their start and end apart: 7, of which 3 were waited for; matrix products, arithmetic and copies ran while one was open for 0% of the time, Pallas kernels for 10%

profile of v15, /device:TPU:0, one launch (start us, length us, event | category | flops | bytes accessed | tf_op | source)
XLA Modules:
  0.0 21.5 jit_solution(17555794271369980627)
XLA Ops:
  0.0 1.4 %shard_map.55.slab_ref.own_ref = f32[200,256]{1,0:T(8,128)S(1)} custom-call(f32[256,768]{1,0:T(8,128)} %amp_ref.1, s32[1,256]{1,0:T(1,128)} %ij_ref.1, s32[1,768]{1,0:T(1,128)} %cd_ref.3), custom_call_target="tpu_custom_call" | custom-call | flops 786432 | tf_op jit(solution)/shard_map/pallas_call | solution.py:256
  1.4 3.0 %collective-permute-start.1 = (f32[200,256]{1,0:T(8,128)S(1)}, f32[200,256]{1,0:T(8,128)S(1)}, u32[]{:S(2)}, u32[]{:S(2)}) collective-permute-start(f32[200,256]{1,0:T(8,128)S(1)} %shard_map.55.slab_ref.own_ref), channel_id=1, source_target_pairs={{0,4},{1,5},{2,6},{3,7},{4,0},{5,1},{6,10},{7,11},{8,12},{9,13},{1... | collective-permute-start | bytes 614408 | tf_op jit(solution)/shard_map/ppermute | solution.py:299
  4.4 0.7 %collective-permute-start.3 = (f32[200,256]{1,0:T(8,128)S(1)}, f32[200,256]{1,0:T(8,128)S(1)}, u32[]{:S(2)}, u32[]{:S(2)}) collective-permute-start(f32[200,256]{1,0:T(8,128)S(1)} %shard_map.55.slab_ref.own_ref), channel_id=1, source_target_pairs={{0,6},{2,0},{4,10},{6,4},{8,14},{10,8},{12,18},{14,12},{16,22},{18... | collective-permute-start | bytes 614408 | tf_op jit(solution)/shard_map/ppermute | solution.py:276
  5.1 1.3 %shard_map.57.rows_ref = f32[256,256]{1,0:T(8,128)S(1)} custom-call(f32[256,768]{1,0:T(8,128)} %v_ref, s32[1,256]{1,0:T(1,128)} %ab_ref.1, s32[1,768]{1,0:T(1,128)} %cd_ref.3), custom_call_target="tpu_custom_call" | custom-call | tf_op jit(solution)/shard_map/pallas_call | solution.py:256
  6.4 0.1 collective-permute-start
  6.5 1.6 %collective-permute-start.4 = (f32[200,256]{1,0:T(8,128)S(1)}, f32[200,256]{1,0:T(8,128)S(1)}, u32[]{:S(2)}, u32[]{:S(2)}) collective-permute-start(f32[200,256]{1,0:T(8,128)S(1)} %shard_map.55.slab_ref.own_ref), channel_id=1, source_target_pairs={{0,1},{1,0},{2,10},{3,11},{4,5},{5,4},{6,14},{7,15},{8,9},{9,8},{1... | collective-permute-start | bytes 614408 | tf_op jit(solution)/shard_map/ppermute | solution.py:299
  8.0 0.4 %shard_map.58.own_term = f32[256,128]{1,0:T(8,128)S(1)} custom-call(f32[256,256]{1,0:T(8,128)S(1)} %shard_map.57.rows_ref, f32[200,256]{1,0:T(8,128)S(1)} %shard_map.55.slab_ref.own_ref), custom_call_target="tpu_custom_call" | custom-call | flops 9663676416 | tf_op jit(solution)/shard_map/pallas_call | solution.py:256
  8.5 0.0 collective-permute-done.twin_ref
  8.5 0.5 %shard_map.59 = (f32[256,128]{1,0:T(8,128)S(1)}, f32[1,128,128]{2,1,0:T(8,128)S(1)}) custom-call(f32[256,256]{1,0:T(8,128)S(1)} %collective-permute-done.twin_ref, f32[200,256]{1,0:T(8,128)S(1)} %shard_map.55.slab_ref.own_ref, f32[256,128]{1,0:T(8,128)S(1)} %shard_map.58.own_term), custom_call_target="tpu_custom_call" | custom-call | tf_op jit(solution)/shard_map/pallas_call | solution.py:256
  8.9 1.1 %collective-permute-start.2 = (f32[128,128]{1,0:T(8,128)S(1)}, f32[128,128]{1,0:T(8,128)S(1)}, u32[]{:S(2)}, u32[]{:S(2)}) collective-permute-start(f32[128,128]{1,0:T(8,128)S(1)} %bitcast.3), channel_id=1, source_target_pairs={{0,1},{1,0},{2,3},{3,2},{4,5},{5,4},{6,7},{7,6},{8,9},{9,8},{10,11... | collective-permute-start | bytes 196616 | tf_op jit(solution)/shard_map/ppermute | solution.py:280
  10.0 0.0 collective-permute-done.1.below_ref
  10.0 3.6 %collective-permute-done.2.refs_0_ = f32[128,128]{1,0:T(8,128)S(1)} collective-permute-done((f32[128,128]{1,0:T(8,128)S(1)}, f32[128,128]{1,0:T(8,128)S(1)}, u32[]{:S(2)}, u32[]{:S(2)}) %collective-permute-start.2) | collective-permute-done | bytes 65568 | tf_op jit(solution)/shard_map/ppermute | solution.py:280
  13.7 0.0 collective-permute-done.3.far_ref
  13.7 0.0 collective-permute-done.4.third_ref
  13.8 1.6 %collective-permute-start.5 = (f32[320,128]{1,0:T(8,128)S(1)}, f32[320,128]{1,0:T(8,128)S(1)}, u32[]{:S(2)}, u32[]{:S(2)}) collective-permute-start(f32[320,128]{1,0:T(8,128)S(1)} %bitcast.2), channel_id=1, source_target_pairs={{0,4},{1,5},{2,3},{3,2},{4,0},{5,1},{6,7},{7,6},{8,12},{9,13},{10,... | collective-permute-start | bytes 491528 | tf_op jit(solution)/shard_map/ppermute | solution.py:299
  15.3 3.8 %collective-permute-done.5.refs_1_ = f32[320,128]{1,0:T(8,128)S(1)} collective-permute-done((f32[320,128]{1,0:T(8,128)S(1)}, f32[320,128]{1,0:T(8,128)S(1)}, u32[]{:S(2)}, u32[]{:S(2)}) %collective-permute-start.5) | collective-permute-done | bytes 163872 | tf_op jit(solution)/shard_map/ppermute | solution.py:299
  19.1 0.1 shard_map.63
  19.2 0.1 collective-permute-start.6
  19.3 1.3 %collective-permute-done.6.cross_ref = f32[200,128]{1,0:T(8,128)S(1)} collective-permute-done((f32[200,128]{1,0:T(8,128)S(1)}, f32[200,128]{1,0:T(8,128)S(1)}, u32[]{:S(2)}, u32[]{:S(2)}) %collective-permute-start.6) | collective-permute-done | bytes 102432 | tf_op jit(solution)/shard_map/ppermute | solution.py:276
  20.6 0.9 %shard_map.64 = f32[4,128,256]{2,1,0:T(8,128)} custom-call(f32[256,256]{1,0:T(8,128)S(1)} %shard_map.57.rows_ref, f32[256,128]{1,0:T(8,128)S(1)} %shard_map.58.own_term, f32[256,128]{1,0:T(8,128)S(1)} %get-tuple-element.22.mine_term, f32[128,128]{1,0:T(8,128)S(1)} %get-tuple-element.31.last_ref, f32[8,256]{1,0:T(8,128)S(1)} %shard_map.56.own_labels, ...), custom_call_target="tpu_custom_call" | custom-call | flops 262144 | tf_op jit(solution)/shard_map/pallas_call | solution.py:256
  (4 shorter events, 0.1 us)
Async XLA Ops:
  1.4 8.6 %collective-permute-start.1 = (f32[200,256]{1,0:T(8,128)S(1)}, f32[200,256]{1,0:T(8,128)S(1)}, u32[]{:S(2)}, u32[]{:S(2)}) collective-permute-start(f32[200,256]{1,0:T(8,128)S(1)} %shard_map.55.slab_ref.own_ref), channel_id=1, source_target_pairs={{0,4},{1,5},{2,6},{3,7},{4,0},{5,1},{6,10},{7,11},{8,12},{9,13},{1... | collective-permute-start | bytes 614408 | tf_op jit(solution)/shard_map/ppermute | solution.py:299
  4.4 9.3 %collective-permute-start.3 = (f32[200,256]{1,0:T(8,128)S(1)}, f32[200,256]{1,0:T(8,128)S(1)}, u32[]{:S(2)}, u32[]{:S(2)}) collective-permute-start(f32[200,256]{1,0:T(8,128)S(1)} %shard_map.55.slab_ref.own_ref), channel_id=1, source_target_pairs={{0,6},{2,0},{4,10},{6,4},{8,14},{10,8},{12,18},{14,12},{16,22},{18... | collective-permute-start | bytes 614408 | tf_op jit(solution)/shard_map/ppermute | solution.py:276
  6.4 2.1 %collective-permute-start = (f32[256,256]{1,0:T(8,128)S(1)}, f32[256,256]{1,0:T(8,128)S(1)}, u32[]{:S(2)}, u32[]{:S(2)}) collective-permute-start(f32[256,256]{1,0:T(8,128)S(1)} %shard_map.57.rows_ref), channel_id=1, source_target_pairs={{0,2},{2,0},{4,6},{6,4},{8,10},{10,8},{12,14},{14,12},{16,18},{18,... | collective-permute-start | bytes 786440 | tf_op jit(solution)/shard_map/ppermute | solution.py:276
  6.5 7.2 %collective-permute-start.4 = (f32[200,256]{1,0:T(8,128)S(1)}, f32[200,256]{1,0:T(8,128)S(1)}, u32[]{:S(2)}, u32[]{:S(2)}) collective-permute-start(f32[200,256]{1,0:T(8,128)S(1)} %shard_map.55.slab_ref.own_ref), channel_id=1, source_target_pairs={{0,1},{1,0},{2,10},{3,11},{4,5},{5,4},{6,14},{7,15},{8,9},{9,8},{1... | collective-permute-start | bytes 614408 | tf_op jit(solution)/shard_map/ppermute | solution.py:299
  8.9 4.7 %collective-permute-start.2 = (f32[128,128]{1,0:T(8,128)S(1)}, f32[128,128]{1,0:T(8,128)S(1)}, u32[]{:S(2)}, u32[]{:S(2)}) collective-permute-start(f32[128,128]{1,0:T(8,128)S(1)} %bitcast.3), channel_id=1, source_target_pairs={{0,1},{1,0},{2,3},{3,2},{4,5},{5,4},{6,7},{7,6},{8,9},{9,8},{10,11... | collective-permute-start | bytes 196616 | tf_op jit(solution)/shard_map/ppermute | solution.py:280
  13.8 5.4 %collective-permute-start.5 = (f32[320,128]{1,0:T(8,128)S(1)}, f32[320,128]{1,0:T(8,128)S(1)}, u32[]{:S(2)}, u32[]{:S(2)}) collective-permute-start(f32[320,128]{1,0:T(8,128)S(1)} %bitcast.2), channel_id=1, source_target_pairs={{0,4},{1,5},{2,3},{3,2},{4,0},{5,1},{6,7},{7,6},{8,12},{9,13},{10,... | collective-permute-start | bytes 491528 | tf_op jit(solution)/shard_map/ppermute | solution.py:299
  19.2 1.4 %collective-permute-start.6 = (f32[200,128]{1,0:T(8,128)S(1)}, f32[200,128]{1,0:T(8,128)S(1)}, u32[]{:S(2)}, u32[]{:S(2)}) collective-permute-start(f32[200,128]{1,0:T(8,128)S(1)} %get-tuple-element.32), channel_id=1, source_target_pairs={{0,2},{2,0},{4,6},{6,4},{8,10},{10,8},{12,14},{14,12},{16,18},{18,... | collective-permute-start | bytes 307208 | tf_op jit(solution)/shard_map/ppermute | solution.py:276

commit v16 on v14

--- a/solution.py
+++ b/solution.py
@@ -125,11 +125,11 @@
     out_ref[...] = narrowed(rows_ref[...], own_ref)
 
 
-def near_kernel(rows_ref, twin_ref, below_ref, own_ref, mine_out, twin_out):
+def far_kernel(rows_ref, twin_ref, far_ref, own_ref, mine_out, twin_out):
     @pl.when(odd())
     def _():
-        mine_out[...] = narrowed(rows_ref[...], below_ref)
-        twin_out[...] = narrowed(twin_ref[...], below_ref)
+        mine_out[...] = narrowed(rows_ref[...], far_ref)
+        twin_out[...] = narrowed(twin_ref[...], far_ref)
 
     @pl.when(~odd())
     def _():
@@ -137,20 +137,20 @@
         twin_out[...] = narrowed(twin_ref[...], own_ref)
 
 
-def far_terms(part, rows_ref, twin_ref, far_ref, third_ref):
+def near_terms(part, rows_ref, twin_ref, near_ref, third_ref):
     count = rows_ref[part, :].shape[0]
-    both = narrowed(jnp.concatenate([rows_ref[part, :], twin_ref[part, :]], axis=0), far_ref)
+    both = narrowed(jnp.concatenate([rows_ref[part, :], twin_ref[part, :]], axis=0), near_ref)
     return both[:count], both[count:], narrowed(twin_ref[part, :], third_ref)
 
 
-def send_kernel(rows_ref, twin_ref, far_ref, third_ref, own_term, mine_term, twin_term, send_ref):
+def send_kernel(rows_ref, twin_ref, near_ref, third_ref, own_term, mine_term, twin_term, send_ref):
     parts, count = send_ref.shape[0] + 1, send_ref.shape[1] // 3
     tail = slice(count, None)
     held = [slice(k * count, (k + 1) * count) for k in range(parts - 1)]
 
     @pl.when(odd())
     def _():
-        mine, twin, third = far_terms(tail, rows_ref, twin_ref, far_ref, third_ref)
+        mine, twin, third = near_terms(tail, rows_ref, twin_ref, near_ref, third_ref)
         second, last = beside(twin_term[tail, :], twin), beside(mine, third)
         for k, h in enumerate(held):
             send_ref[k, count:2 * count, :] = second[h]
@@ -167,14 +167,14 @@
         send_ref[k, :count, :] = first[h]
 
 
-def keep_kernel(rows_ref, twin_ref, below_ref, far_ref, third_ref, own_ref, twin_term, second_out, last_out, labels_out):
+def keep_kernel(rows_ref, twin_ref, far_ref, near_ref, third_ref, own_ref, twin_term, second_out, last_out, labels_out):
     count = second_out.shape[0]
     width = own_ref.shape[0] - 8
     head = slice(0, count)
 
     @pl.when(odd())
     def _():
-        mine, twin, third = far_terms(head, rows_ref, twin_ref, far_ref, third_ref)
+        mine, twin, third = near_terms(head, rows_ref, twin_ref, near_ref, third_ref)
         second_out[...] = beside(twin_term[head, :], twin)
         last_out[...] = beside(mine, third)
 
@@ -184,7 +184,7 @@
         last_out[...] = jnp.zeros_like(last_out)
 
     own = own_ref[width:width + 1, :]
-    sent = [jnp.where(odd(), ref[width:width + 1, :], own) for ref in (below_ref, far_ref, third_ref)]
+    sent = [jnp.where(odd(), ref[width:width + 1, :], own) for ref in (far_ref, near_ref, third_ref)]
     tiles = [label[:, start:start + LANES] for label in sent for start in range(0, own.shape[1], LANES)]
     labels_out[...] = jnp.concatenate((tiles * 8)[:8], axis=0)
 
@@ -199,10 +199,10 @@
     last_out[...] = last
 
 
-def finish_kernel(parts, rows_ref, own_term, mine_term, last_ref, own_labels, below_ref, far_ref, cross_ref, *refs):
+def finish_kernel(parts, rows_ref, own_term, mine_term, last_ref, own_labels, far_ref, near_ref, cross_ref, *refs):
     taken, (out_ref, out, sems) = refs[:parts - 1], refs[parts - 1:]
     count = last_ref.shape[0]
-    width = below_ref.shape[0] - 8
+    width = far_ref.shape[0] - 8
     tiles = out.shape[2] // LANES
     rows = row_labels(rows_ref[:count, :])
     copies = []
@@ -224,11 +224,10 @@
     pairs = [apart(ref[:count, :]) for ref in taken]
     store(0, sum([own for own, _ in pairs], own_term[:count, :]), of(own_labels, 0))
     mine = sum([mine for _, mine in pairs], mine_term[:count, :])
-    one, two = apart(cross_ref[:count, :])
-    store(1, one, labels[0])
-    store(2, jnp.where(odd(), mine, two), pick(of(below_ref), labels[1]))
-    far, three = apart(last_ref[...])[0], unhalved(cross_ref[count:start, :])
-    store(3, jnp.where(odd(), far, three), pick(of(far_ref), labels[2]))
+    two, one = apart(cross_ref[:count, :])
+    store(1, one, labels[1])
+    store(2, jnp.where(odd(), apart(last_ref[...])[0], two), pick(of(near_ref), labels[0]))
+    store(3, jnp.where(odd(), mine, unhalved(cross_ref[count:start, :])), pick(of(far_ref), labels[2]))
     for copy in copies:
         copy.wait()
 
@@ -281,38 +280,32 @@
     stage, sems = staging(amplitudes, ij_irrep, 1)
     own, = call(pack_kernel, [whole(width + 8, pairs)], (amplitudes, ij_irrep, cd_irrep),
                 4 * amplitudes.size, 3, stage + [sems])
-    def up(array, step):
-        pairs_of = [
-            ((b, r), ((b + step) % blocks, r) if b % 2 else (b, (r + 1) % parts))
-            for b in range(blocks) for r in range(parts)
-        ]
-        return lax.ppermute(array, ("blk", "red"), [(b * parts + r, c * parts + t) for (b, r), (c, t) in pairs_of])
-
-    below = up(own, 2)
-    own_labels, = call(labels_kernel, [whole(8, pairs)], (own,), 8 * pairs)
+    far = moved(own, (3, -1, 3, -1))
+    own_labels, = call(labels_kernel, [whole(8, pairs)], (own,), 0)
+    other = moved(after(own, own_labels), (1, -1, 1, -1))
     stage, sems = staging(integrals, ab_irrep, parts)
     rows, = call(
         functools.partial(first_kernel, count), [whole(row_count, 2 * LANES)],
         (after(integrals, own_labels), ab_irrep, cd_irrep), 0, 3,
         stage + [pltpu.VMEM((row_count, LANES), F32), sems])
-    far = moved(after(own, own_labels), (3, -1, 3, -1))
+    near = moved(other, (3, -1, 3, -1))
     twin = moved(rows, (1, -1, 1, -1))
     term = whole(row_count, LANES)
     own_term, = call(own_kernel, [term], (rows, own), 64 * one_product)
-    third = up(after(own, own_term), 4)
-    mine_term, twin_term = call(near_kernel, [term, term], (rows, twin, below, own), 0)
+    third = moved(after(other, own_term), (5, -1, 5, -1))
+    mine_term, twin_term = call(far_kernel, [term, term], (rows, twin, far, own), 0)
     send, = call(send_kernel, [whole(parts - 1, 3 * count, LANES)],
-                 (rows, twin, far, third, own_term, mine_term, twin_term), 0)
+                 (rows, twin, near, third, own_term, mine_term, twin_term), 0)
     taken = exchanged(send)
-    second_keep, last_keep, cross_labels = call(
+    pair_keep, last_keep, cross_labels = call(
         keep_kernel, [whole(count, LANES), whole(count, LANES), whole(8, LANES)],
-        (rows, twin, below, far, after(third, send), own, twin_term), 0)
+        (rows, twin, far, near, after(third, send), own, twin_term), 0)
     summed, last = call(sum_kernel, [whole(count + count // 2 + 8, LANES), whole(count, LANES)],
-                        (second_keep, last_keep, cross_labels, *taken), 0)
+                        (pair_keep, last_keep, cross_labels, *taken), 0)
     cross = moved(summed, (1, -1, 1, -1))
     out, = call(functools.partial(finish_kernel, parts), [whole(4, count, pairs)],
-                (rows, own_term, mine_term, last, own_labels, below, far, cross, *taken),
-                4 * 2 * count * pairs, 0, [pltpu.VMEM((4, count, pairs), F32), pltpu.SemaphoreType.DMA((4,))], OFFCHIP)
+                (rows, own_term, mine_term, last, own_labels, far, near, cross, *taken),
+                0, 0, [pltpu.VMEM((4, count, pairs), F32), pltpu.SemaphoreType.DMA((4,))], OFFCHIP)
     return out
 
 

time: 22.6 us -> 21.8 us (0.965)
  the two profiles are of different devices: /device:TPU:0 before, /device:TPU:19 now
where the time goes in v16:
time: 21.8 us; the launch traced here: 21.6 us
  waiting for transfers between devices  10.4 us (48%)
  Pallas kernels  5.94 us (27%)
  starting transfers between devices  5.19 us (24%)
    ppermute x6, waiting for transfers between devices, moved(): lax.ppermute(array, 'blk', [(i, (i + steps[i % 4]) % blocks) for i in ran...  5.94 us
    pallas_call x9, Pallas kernels, call(): pl.pallas_call(kernel, out_shape=out_shape, in_specs=[OFFCHIP] * off + [O...  5.94 us
    ppermute x1, waiting for transfers between devices, exchanged(): lax.ppermute(array[k - 1], 'red', [(i, (i + k) % parts) for i in range(pa...  4.48 us
    ppermute x6, starting transfers between devices, moved(): lax.ppermute(array, 'blk', [(i, (i + steps[i % 4]) % blocks) for i in ran...  3.88 us
    ppermute x1, starting transfers between devices, exchanged(): lax.ppermute(array[k - 1], 'red', [(i, (i + k) % parts) for i in range(pa...  1.31 us
  transfers between devices with their start and end apart: 7, of which 4 were waited for; matrix products, arithmetic and copies ran while one was open for 0% of the time, Pallas kernels for 14%

profile of v16, /device:TPU:19, one launch (start us, length us, event | category | flops | bytes accessed | tf_op | source)
XLA Modules:
  0.0 21.6 jit_solution(6292509041065726403)
XLA Ops:
  0.0 1.4 %shard_map.55.slab_ref.own_ref = f32[200,256]{1,0:T(8,128)S(1)} custom-call(f32[256,768]{1,0:T(8,128)} %amp_ref.1, s32[1,256]{1,0:T(1,128)} %ij_ref.1, s32[1,768]{1,0:T(1,128)} %cd_ref.3), custom_call_target="tpu_custom_call" | custom-call | flops 786432 | tf_op jit(solution)/shard_map/pallas_call | solution.py:242
  1.4 0.7 %collective-permute-start.1 = (f32[200,256]{1,0:T(8,128)S(1)}, f32[200,256]{1,0:T(8,128)S(1)}, u32[]{:S(2)}, u32[]{:S(2)}) collective-permute-start(f32[200,256]{1,0:T(8,128)S(1)} %shard_map.55.slab_ref.own_ref), channel_id=1, source_target_pairs={{0,6},{2,0},{4,10},{6,4},{8,14},{10,8},{12,18},{14,12},{16,22},{18... | collective-permute-start | bytes 614408 | tf_op jit(solution)/shard_map/ppermute | solution.py:262
  2.1 1.0 %collective-permute-start.2 = (f32[200,256]{1,0:T(8,128)S(1)}, f32[200,256]{1,0:T(8,128)S(1)}, u32[]{:S(2)}, u32[]{:S(2)}) collective-permute-start(f32[200,256]{1,0:T(8,128)S(1)} %shard_map.55.slab_ref.own_ref), channel_id=1, source_target_pairs={{0,2},{2,0},{4,6},{6,4},{8,10},{10,8},{12,14},{14,12},{16,18},{18,... | collective-permute-start | bytes 614408 | tf_op jit(solution)/shard_map/ppermute | solution.py:262
  3.1 1.3 %shard_map.57.rows_ref = f32[256,256]{1,0:T(8,128)S(1)} custom-call(f32[256,768]{1,0:T(8,128)} %v_ref, s32[1,256]{1,0:T(1,128)} %ab_ref.1, s32[1,768]{1,0:T(1,128)} %cd_ref.3), custom_call_target="tpu_custom_call" | custom-call | tf_op jit(solution)/shard_map/pallas_call | solution.py:242
  4.4 0.1 collective-permute-start
  4.5 0.4 %shard_map.58.own_term = f32[256,128]{1,0:T(8,128)S(1)} custom-call(f32[256,256]{1,0:T(8,128)S(1)} %shard_map.57.rows_ref, f32[200,256]{1,0:T(8,128)S(1)} %shard_map.55.slab_ref.own_ref), custom_call_target="tpu_custom_call" | custom-call | flops 9663676416 | tf_op jit(solution)/shard_map/pallas_call | solution.py:242
  4.9 0.0 collective-permute-done.2
  4.9 0.5 %collective-permute-start.3 = (f32[200,256]{1,0:T(8,128)S(1)}, f32[200,256]{1,0:T(8,128)S(1)}, u32[]{:S(2)}, u32[]{:S(2)}) collective-permute-start(f32[200,256]{1,0:T(8,128)S(1)} %collective-permute-done.2), channel_id=1, source_target_pairs={{0,6},{2,0},{4,10},{6,4},{8,14},{10,8},{12,18},{14,12},{16,22},{18... | collective-permute-start | bytes 614408 | tf_op jit(solution)/shard_map/ppermute | solution.py:262
  5.5 1.1 %collective-permute-start.4 = (f32[200,256]{1,0:T(8,128)S(1)}, f32[200,256]{1,0:T(8,128)S(1)}, u32[]{:S(2)}, u32[]{:S(2)}) collective-permute-start(f32[200,256]{1,0:T(8,128)S(1)} %collective-permute-done.2), channel_id=1, source_target_pairs={{0,10},{2,0},{4,14},{6,4},{8,18},{10,8},{12,22},{14,12},{16,26},{1... | collective-permute-start | bytes 614408 | tf_op jit(solution)/shard_map/ppermute | solution.py:262
  6.6 0.0 collective-permute-done.1.far_ref
  6.6 0.0 collective-permute-done.twin_ref
  6.6 0.7 %shard_map.59 = (f32[256,128]{1,0:T(8,128)S(1)}, f32[256,128]{1,0:T(8,128)S(1)}) custom-call(f32[256,256]{1,0:T(8,128)S(1)} %shard_map.57.rows_ref, f32[256,256]{1,0:T(8,128)S(1)} %collective-permute-done.twin_ref, f32[200,256]{1,0:T(8,128)S(1)} %collective-permute-done.1.far_ref, f32[200,256]{1,0:T(8,128)S(1)} %shard_map.55.slab_ref.own_ref), custom_call_target="tpu_custom_call" | custom-call | tf_op jit(solution)/shard_map/pallas_call | solution.py:242
  7.3 2.8 %collective-permute-done.3.near_ref = f32[200,256]{1,0:T(8,128)S(1)} collective-permute-done((f32[200,256]{1,0:T(8,128)S(1)}, f32[200,256]{1,0:T(8,128)S(1)}, u32[]{:S(2)}, u32[]{:S(2)}) %collective-permute-start.3) | collective-permute-done | bytes 204832 | tf_op jit(solution)/shard_map/ppermute | solution.py:262
  10.2 2.1 %collective-permute-done.4.third_ref = f32[200,256]{1,0:T(8,128)S(1)} collective-permute-done((f32[200,256]{1,0:T(8,128)S(1)}, f32[200,256]{1,0:T(8,128)S(1)}, u32[]{:S(2)}, u32[]{:S(2)}) %collective-permute-start.4) | collective-permute-done | bytes 204832 | tf_op jit(solution)/shard_map/ppermute | solution.py:262
  12.3 0.6 %shard_map.60 = f32[1,384,128]{2,1,0:T(8,128)S(1)} custom-call(f32[256,256]{1,0:T(8,128)S(1)} %shard_map.57.rows_ref, f32[256,256]{1,0:T(8,128)S(1)} %collective-permute-done.twin_ref, f32[200,256]{1,0:T(8,128)S(1)} %collective-permute-done.3.near_ref, f32[200,256]{1,0:T(8,128)S(1)} %collective-permute-done.4.third_ref, f32[256,128]{1,0:T(8,128)S(1)} %shard_map.58.own_term, ...), custom_call_target="tpu_custom_call" | custom-call | tf_op jit(solution)/shard_map/pallas_call | solution.py:242
  12.9 1.3 %collective-permute-start.5 = (f32[384,128]{1,0:T(8,128)S(1)}, f32[384,128]{1,0:T(8,128)S(1)}, u32[]{:S(2)}, u32[]{:S(2)}) collective-permute-start(f32[384,128]{1,0:T(8,128)S(1)} %bitcast.1), channel_id=1, source_target_pairs={{0,1},{1,0},{2,3},{3,2},{4,5},{5,4},{6,7},{7,6},{8,9},{9,8},{10,11... | collective-permute-start | bytes 589832 | tf_op jit(solution)/shard_map/ppermute | solution.py:266
  14.2 0.6 %shard_map.61 = (f32[128,128]{1,0:T(8,128)S(1)}, f32[128,128]{1,0:T(8,128)S(1)}, f32[8,128]{1,0:T(8,128)S(1)}) custom-call(f32[256,256]{1,0:T(8,128)S(1)} %shard_map.57.rows_ref, f32[256,256]{1,0:T(8,128)S(1)} %collective-permute-done.twin_ref, f32[200,256]{1,0:T(8,128)S(1)} %collective-permute-done.1.far_ref, ...), custom_call_target="tpu_custom_call" | custom-call | tf_op jit(solution)/shard_map/pallas_call | solution.py:242
  14.8 4.5 %collective-permute-done.5.refs_0_ = f32[384,128]{1,0:T(8,128)S(1)} collective-permute-done((f32[384,128]{1,0:T(8,128)S(1)}, f32[384,128]{1,0:T(8,128)S(1)}, u32[]{:S(2)}, u32[]{:S(2)}) %collective-permute-start.5) | collective-permute-done | bytes 196640 | tf_op jit(solution)/shard_map/ppermute | solution.py:266
  19.2 0.1 shard_map.62
  19.3 0.4 %collective-permute-start.6 = (f32[200,128]{1,0:T(8,128)S(1)}, f32[200,128]{1,0:T(8,128)S(1)}, u32[]{:S(2)}, u32[]{:S(2)}) collective-permute-start(f32[200,128]{1,0:T(8,128)S(1)} %get-tuple-element.26), channel_id=1, source_target_pairs={{0,2},{2,0},{4,6},{6,4},{8,10},{10,8},{12,14},{14,12},{16,18},{18,... | collective-permute-start | bytes 307208 | tf_op jit(solution)/shard_map/ppermute | solution.py:262
  19.8 0.9 %collective-permute-done.6.cross_ref = f32[200,128]{1,0:T(8,128)S(1)} collective-permute-done((f32[200,128]{1,0:T(8,128)S(1)}, f32[200,128]{1,0:T(8,128)S(1)}, u32[]{:S(2)}, u32[]{:S(2)}) %collective-permute-start.6) | collective-permute-done | bytes 102432 | tf_op jit(solution)/shard_map/ppermute | solution.py:262
  20.7 0.9 %shard_map.63 = f32[4,128,256]{2,1,0:T(8,128)} custom-call(f32[256,256]{1,0:T(8,128)S(1)} %shard_map.57.rows_ref, f32[256,128]{1,0:T(8,128)S(1)} %shard_map.58.own_term, f32[256,128]{1,0:T(8,128)S(1)} %get-tuple-element.17.mine_term, f32[128,128]{1,0:T(8,128)S(1)} %get-tuple-element.25.last_ref, f32[8,256]{1,0:T(8,128)S(1)} %shard_map.56.own_labels, ...), custom_call_target="tpu_custom_call" | custom-call | tf_op jit(solution)/shard_map/pallas_call | solution.py:242
  (1 shorter events, 0.0 us)
Async XLA Ops:
  1.4 5.2 %collective-permute-start.1 = (f32[200,256]{1,0:T(8,128)S(1)}, f32[200,256]{1,0:T(8,128)S(1)}, u32[]{:S(2)}, u32[]{:S(2)}) collective-permute-start(f32[200,256]{1,0:T(8,128)S(1)} %shard_map.55.slab_ref.own_ref), channel_id=1, source_target_pairs={{0,6},{2,0},{4,10},{6,4},{8,14},{10,8},{12,18},{14,12},{16,22},{18... | collective-permute-start | bytes 614408 | tf_op jit(solution)/shard_map/ppermute | solution.py:262
  2.1 2.8 %collective-permute-start.2 = (f32[200,256]{1,0:T(8,128)S(1)}, f32[200,256]{1,0:T(8,128)S(1)}, u32[]{:S(2)}, u32[]{:S(2)}) collective-permute-start(f32[200,256]{1,0:T(8,128)S(1)} %shard_map.55.slab_ref.own_ref), channel_id=1, source_target_pairs={{0,2},{2,0},{4,6},{6,4},{8,10},{10,8},{12,14},{14,12},{16,18},{18,... | collective-permute-start | bytes 614408 | tf_op jit(solution)/shard_map/ppermute | solution.py:262
  4.4 2.2 %collective-permute-start = (f32[256,256]{1,0:T(8,128)S(1)}, f32[256,256]{1,0:T(8,128)S(1)}, u32[]{:S(2)}, u32[]{:S(2)}) collective-permute-start(f32[256,256]{1,0:T(8,128)S(1)} %shard_map.57.rows_ref), channel_id=1, source_target_pairs={{0,2},{2,0},{4,6},{6,4},{8,10},{10,8},{12,14},{14,12},{16,18},{18,... | collective-permute-start | bytes 786440 | tf_op jit(solution)/shard_map/ppermute | solution.py:262
  4.9 5.2 %collective-permute-start.3 = (f32[200,256]{1,0:T(8,128)S(1)}, f32[200,256]{1,0:T(8,128)S(1)}, u32[]{:S(2)}, u32[]{:S(2)}) collective-permute-start(f32[200,256]{1,0:T(8,128)S(1)} %collective-permute-done.2), channel_id=1, source_target_pairs={{0,6},{2,0},{4,10},{6,4},{8,14},{10,8},{12,18},{14,12},{16,22},{18... | collective-permute-start | bytes 614408 | tf_op jit(solution)/shard_map/ppermute | solution.py:262
  5.5 6.8 %collective-permute-start.4 = (f32[200,256]{1,0:T(8,128)S(1)}, f32[200,256]{1,0:T(8,128)S(1)}, u32[]{:S(2)}, u32[]{:S(2)}) collective-permute-start(f32[200,256]{1,0:T(8,128)S(1)} %collective-permute-done.2), channel_id=1, source_target_pairs={{0,10},{2,0},{4,14},{6,4},{8,18},{10,8},{12,22},{14,12},{16,26},{1... | collective-permute-start | bytes 614408 | tf_op jit(solution)/shard_map/ppermute | solution.py:262
  12.9 6.4 %collective-permute-start.5 = (f32[384,128]{1,0:T(8,128)S(1)}, f32[384,128]{1,0:T(8,128)S(1)}, u32[]{:S(2)}, u32[]{:S(2)}) collective-permute-start(f32[384,128]{1,0:T(8,128)S(1)} %bitcast.1), channel_id=1, source_target_pairs={{0,1},{1,0},{2,3},{3,2},{4,5},{5,4},{6,7},{7,6},{8,9},{9,8},{10,11... | collective-permute-start | bytes 589832 | tf_op jit(solution)/shard_map/ppermute | solution.py:266
  19.3 1.4 %collective-permute-start.6 = (f32[200,128]{1,0:T(8,128)S(1)}, f32[200,128]{1,0:T(8,128)S(1)}, u32[]{:S(2)}, u32[]{:S(2)}) collective-permute-start(f32[200,128]{1,0:T(8,128)S(1)} %get-tuple-element.26), channel_id=1, source_target_pairs={{0,2},{2,0},{4,6},{6,4},{8,10},{10,8},{12,14},{14,12},{16,18},{18,... | collective-permute-start | bytes 307208 | tf_op jit(solution)/shard_map/ppermute | solution.py:262

commit v17 on v13

--- a/solution.py
+++ b/solution.py
@@ -132,26 +132,25 @@
             out_ref[...] = narrowed(rows, ref, labels)
 
 
-def mix_kernel(rows_ref, column_ref, mix_ref, out_ref):
+def sent_kernel(rows_ref, column_ref, slab_ref, out_ref):
     count = rows_ref.shape[0] - out_ref.shape[0]
-    out_ref[...] = narrowed(rows_ref[count:, :], mix_ref, column_ref[count:, :])
-
-
-def early_kernel(rows_ref, column_ref, mix_term, two_ref, send_ref, term):
+    out_ref[...] = narrowed(rows_ref[count:, :], slab_ref, column_ref[count:, :])
+
+
+def early_kernel(mix_term, two_term, send_ref):
     parts, count = send_ref.shape[0] + 1, 2 * send_ref.shape[1]
-    term[...] = mix_term[...]
+    term = jnp.where(second(), two_term[...], mix_term[...])
+    for k in range(1, parts):
+        send_ref[k - 1] = halved(term[(k - 1) * count:k * count, :])
+
+
+def other_kernel(rows_ref, column_ref, two_term, late_ref, out_ref):
+    count = rows_ref.shape[0] - out_ref.shape[0]
+    out_ref[...] = two_term[...]
 
     @pl.when(second())
     def _():
-        term[...] = narrowed(rows_ref[count:, :], two_ref, column_ref[count:, :])
-
-    for k in range(1, parts):
-        send_ref[k - 1] = halved(term[(k - 1) * count:k * count, :])
-
-
-def other_kernel(rows_ref, column_ref, two_ref, late_ref, out_ref):
-    count = rows_ref.shape[0] - out_ref.shape[0]
-    either(second(), late_ref, two_ref, out_ref, rows_ref[count:, :], column_ref[count:, :])
+        out_ref[...] = narrowed(rows_ref[count:, :], late_ref, column_ref[count:, :])
 
 
 def swap_kernel(rows_ref, column_ref, swap_ref, other_ref, send_ref):
@@ -268,12 +267,12 @@
     own_in = exchanged(own_send)
     late = moved(after(own, own_keep, mix), (1, -1, 1, 3))
     rest = whole(row_count - count, LANES)
-    mix_term, = call(mix_kernel, [rest], (rows, labels, mix), one_product)
-    early_send, = call(early_kernel, [whole(parts - 1, count // 2, LANES)], (rows, labels, mix_term, two),
-                       one_product, 0, [pltpu.VMEM(rest.shape, F32)])
+    mix_term, = call(sent_kernel, [rest], (rows, labels, mix), one_product)
+    swap = moved(after(two, mix_term, *own_in), (1, -1, 1, -1))
+    two_term, = call(sent_kernel, [rest], (rows, labels, two), one_product)
+    early_send, = call(early_kernel, [whole(parts - 1, count // 2, LANES)], (mix_term, two_term), 0)
     early_in = exchanged(early_send)
-    swap = moved(after(two, mix_term, *own_in), (1, -1, 1, -1))
-    other_term, = call(other_kernel, [rest], (rows, labels, two, late), one_product)
+    other_term, = call(other_kernel, [rest], (rows, labels, two_term, late), one_product)
     late_send, = call(swap_kernel, [whole(parts - 1, count, LANES)], (rows, labels, swap, other_term), one_product)
     late_in = exchanged(late_send)
     two_keep, three_keep, swap_keep, slab_labels = call(

time: 20.2 us -> 20.2 us (level)
    pallas_call x10 -> x11, Pallas kernels: 5.93 us -> 5.92 us  [call(): pl.pallas_call(kernel, out_shape=out_shape, in_specs=[OFFCHIP] * off + [O...]
where the time goes in v17:
time: 20.2 us; the launch traced here: 20.1 us
  starting transfers between devices  7.22 us (36%)
  waiting for transfers between devices  6.82 us (34%)
  Pallas kernels  5.92 us (29%)
    pallas_call x11, Pallas kernels, call(): pl.pallas_call(kernel, out_shape=out_shape, in_specs=[OFFCHIP] * off + [O...  5.92 us
    ppermute x4, waiting for transfers between devices, moved(): lax.ppermute(array, 'blk', [(i, (i + steps[i % 4]) % blocks) for i in ran...  4.44 us
    ppermute x3, starting transfers between devices, exchanged(): lax.ppermute(array[k - 1], 'red', [(i, (i + k) % parts) for i in range(pa...  4.22 us
    ppermute x4, starting transfers between devices, moved(): lax.ppermute(array, 'blk', [(i, (i + steps[i % 4]) % blocks) for i in ran...  3 us
    ppermute x3, waiting for transfers between devices, exchanged(): lax.ppermute(array[k - 1], 'red', [(i, (i + k) % parts) for i in range(pa...  2.38 us
  transfers between devices with their start and end apart: 7, of which 4 were waited for; matrix products, arithmetic and copies ran while one was open for 0% of the time, Pallas kernels for 18%

profile of v17, /device:TPU:0, one launch (start us, length us, event | category | flops | bytes accessed | tf_op | source)
XLA Modules:
  0.0 20.1 jit_solution(6119461586168269143)
XLA Ops:
  0.0 1.4 %shard_map.56.own_ref.slab_ref = f32[200,256]{1,0:T(8,128)S(1)} custom-call(f32[256,768]{1,0:T(8,128)} %amp_ref.1, s32[1,256]{1,0:T(1,128)} %ij_ref.1, s32[1,768]{1,0:T(1,128)} %cd_ref.3), custom_call_target="tpu_custom_call" | custom-call | flops 786432 | bytes 995328 | tf_op jit(solution)/shard_map/pallas_call | solution.py:216
  1.4 3.0 %collective-permute-start.1 = (f32[200,256]{1,0:T(8,128)S(1)}, f32[200,256]{1,0:T(8,128)S(1)}, u32[]{:S(2)}, u32[]{:S(2)}) collective-permute-start(f32[200,256]{1,0:T(8,128)S(1)} %shard_map.56.own_ref.slab_ref), channel_id=1, source_target_pairs={{0,4},{2,6},{4,8},{6,10},{8,12},{10,14},{12,16},{14,18},{16,20},{1... | collective-permute-start | bytes 614408 | tf_op jit(solution)/shard_map/ppermute | solution.py:236
  4.4 0.0 collective-permute-start
  4.4 1.3 %shard_map.55 = (f32[256,192]{1,0:T(8,128)S(1)}, f32[256,128]{1,0:T(8,128)S(1)}) custom-call(f32[256,768]{1,0:T(8,128)} %v_ref.1, s32[1,256]{1,0:T(1,128)} %ab_ref.1, s32[1,768]{1,0:T(1,128)} %cd_ref.3), custom_call_target="tpu_custom_call" | custom-call | flops 9663676416 | bytes 1118208 | tf_op jit(solution)/shard_map/pallas_call | solution.py:216
  5.7 0.4 %shard_map.57 = (f32[128,128]{1,0:T(8,128)S(1)}, f32[1,64,128]{2,1,0:T(8,128)S(1)}) custom-call(f32[256,192]{1,0:T(8,128)S(1)} %get-tuple-element.17.rows_ref.refs_1_, f32[256,128]{1,0:T(8,128)S(1)} %get-tuple-element.18.column_ref.refs_2_.refs_3_, f32[200,256]{1,0:T(8,128)S(1)} %shard_map.56.own_ref.slab_ref), custom_call_target="tpu_custom_call" | custom-call | flops 150994944 | bytes 630784 | tf_op jit(solution)/shard_map/pallas_call | solution.py:216
  6.1 1.6 %collective-permute-start.4 = (f32[64,128]{1,0:T(8,128)S(1)}, f32[64,128]{1,0:T(8,128)S(1)}, u32[]{:S(2)}, u32[]{:S(2)}) collective-permute-start(f32[64,128]{1,0:T(8,128)S(1)} %bitcast.5), channel_id=1, source_target_pairs={{0,1},{1,0},{2,3},{3,2},{4,5},{5,4},{6,7},{7,6},{8,9},{9,8},{10,11... | collective-permute-start | bytes 98312 | tf_op jit(solution)/shard_map/ppermute | solution.py:240
  7.7 3.7 %collective-permute-done.slab_ref.refs_5_ = f32[200,256]{1,0:T(8,128)S(1)} collective-permute-done((f32[200,256]{1,0:T(8,128)S(1)}, f32[200,256]{1,0:T(8,128)S(1)}, u32[]{:S(2)}, u32[]{:S(2)}) %collective-permute-start) | collective-permute-done | bytes 204832 | tf_op jit(solution)/shard_map/ppermute | solution.py:236
  11.4 0.0 collective-permute-start.3
  11.4 0.3 %shard_map.59.mix_term = f32[128,128]{1,0:T(8,128)S(1)} custom-call(f32[256,192]{1,0:T(8,128)S(1)} %get-tuple-element.17.rows_ref.refs_1_, f32[256,128]{1,0:T(8,128)S(1)} %get-tuple-element.18.column_ref.refs_2_.refs_3_, f32[200,256]{1,0:T(8,128)S(1)} %collective-permute-done.slab_ref.refs_5_), custom_call_target="tpu_custom_call" | custom-call | flops 150994944 | bytes 598016 | tf_op jit(solution)/shard_map/pallas_call | solution.py:216
  11.7 0.0 collective-permute-done.4.refs_0_
  11.7 0.8 %collective-permute-done.1.slab_ref.refs_4_ = f32[200,256]{1,0:T(8,128)S(1)} collective-permute-done((f32[200,256]{1,0:T(8,128)S(1)}, f32[200,256]{1,0:T(8,128)S(1)}, u32[]{:S(2)}, u32[]{:S(2)}) %collective-permute-start.1) | collective-permute-done | bytes 204832 | tf_op jit(solution)/shard_map/ppermute | solution.py:236
  12.5 0.0 collective-permute-start.5
  12.5 0.3 %shard_map.60.two_term = f32[128,128]{1,0:T(8,128)S(1)} custom-call(f32[256,192]{1,0:T(8,128)S(1)} %get-tuple-element.17.rows_ref.refs_1_, f32[256,128]{1,0:T(8,128)S(1)} %get-tuple-element.18.column_ref.refs_2_.refs_3_, f32[200,256]{1,0:T(8,128)S(1)} %collective-permute-done.1.slab_ref.refs_4_), custom_call_target="tpu_custom_call" | custom-call | flops 150994944 | bytes 598016 | tf_op jit(solution)/shard_map/pallas_call | solution.py:216
  12.9 1.6 %collective-permute-start.2 = (f32[64,128]{1,0:T(8,128)S(1)}, f32[64,128]{1,0:T(8,128)S(1)}, u32[]{:S(2)}, u32[]{:S(2)}) collective-permute-start(f32[64,128]{1,0:T(8,128)S(1)} %bitcast.4), channel_id=1, source_target_pairs={{0,1},{1,0},{2,3},{3,2},{4,5},{5,4},{6,7},{7,6},{8,9},{9,8},{10,11... | collective-permute-start | bytes 98312 | tf_op jit(solution)/shard_map/ppermute | solution.py:240
  14.4 0.0 collective-permute-done.3.late_ref.refs_6_
  14.5 0.0 collective-permute-done.5.swap_ref.refs_7_
  14.5 0.3 %shard_map.63 = f32[1,128,128]{2,1,0:T(8,128)S(1)} custom-call(f32[256,192]{1,0:T(8,128)S(1)} %get-tuple-element.17.rows_ref.refs_1_, f32[256,128]{1,0:T(8,128)S(1)} %get-tuple-element.18.column_ref.refs_2_.refs_3_, f32[200,256]{1,0:T(8,128)S(1)} %collective-permute-done.5.swap_ref.refs_7_, f32[128,128]{1,0:T(8,128)S(1)} %shard_map.62.other_ref), custom_call_target="tpu_custom_call" | custom-call | flops 150994944 | bytes 663552 | tf_op jit(solution)/shard_map/pallas_call | solution.py:216
  14.8 1.1 %collective-permute-start.6 = (f32[128,128]{1,0:T(8,128)S(1)}, f32[128,128]{1,0:T(8,128)S(1)}, u32[]{:S(2)}, u32[]{:S(2)}) collective-permute-start(f32[128,128]{1,0:T(8,128)S(1)} %bitcast.3), channel_id=1, source_target_pairs={{0,1},{1,0},{2,3},{3,2},{4,5},{5,4},{6,7},{7,6},{8,9},{9,8},{10,11... | collective-permute-start | bytes 196616 | tf_op jit(solution)/shard_map/ppermute | solution.py:240
  15.9 1.0 %collective-permute-done.2.refs_0_ = f32[64,128]{1,0:T(8,128)S(1)} collective-permute-done((f32[64,128]{1,0:T(8,128)S(1)}, f32[64,128]{1,0:T(8,128)S(1)}, u32[]{:S(2)}, u32[]{:S(2)}) %collective-permute-start.2) | collective-permute-done | bytes 32800 | tf_op jit(solution)/shard_map/ppermute | solution.py:240
  16.8 0.9 %shard_map.64 = (f32[128,128]{1,0:T(8,128)S(1)}, f32[128,128]{1,0:T(8,128)S(1)}, f32[128,128]{1,0:T(8,128)S(1)}, f32[8,256]{1,0:T(8,128)S(1)}) custom-call(f32[64,128]{1,0:T(8,128)S(1)} %collective-permute-done.2.refs_0_, f32[256,192]{1,0:T(8,128)S(1)} %get-tuple-element.17.rows_ref.refs_1_, f32[256,128]{1,0:T(8,128)S(1)} %get-tuple-element.18.column_ref.refs_2_.refs_3_, ...), custom_call_target="tpu_custom_call" | custom-call | flops 2415919104 | bytes 1392640 | tf_op jit(solution)/shard_map/pallas_call | solution.py:216
  17.7 1.4 %collective-permute-done.6.refs_1_ = f32[128,128]{1,0:T(8,128)S(1)} collective-permute-done((f32[128,128]{1,0:T(8,128)S(1)}, f32[128,128]{1,0:T(8,128)S(1)}, u32[]{:S(2)}, u32[]{:S(2)}) %collective-permute-start.6) | collective-permute-done | bytes 65568 | tf_op jit(solution)/shard_map/ppermute | solution.py:240
  19.1 0.9 %shard_map.65 = f32[4,128,256]{2,1,0:T(8,128)} custom-call(f32[128,128]{1,0:T(8,128)S(1)} %get-tuple-element.19.own_keep, f32[128,128]{1,0:T(8,128)S(1)} %get-tuple-element.25.two_keep, f32[128,128]{1,0:T(8,128)S(1)} %get-tuple-element.26.three_keep, f32[128,128]{1,0:T(8,128)S(1)} %get-tuple-element.27.swap_keep, ...), custom_call_target="tpu_custom_call" | custom-call | flops 262144 | bytes 1024000 | tf_op jit(solution)/shard_map/pallas_call | solution.py:216
  (3 shorter events, 0.0 us)
Async XLA Ops:
  1.4 11.1 %collective-permute-start.1 = (f32[200,256]{1,0:T(8,128)S(1)}, f32[200,256]{1,0:T(8,128)S(1)}, u32[]{:S(2)}, u32[]{:S(2)}) collective-permute-start(f32[200,256]{1,0:T(8,128)S(1)} %shard_map.56.own_ref.slab_ref), channel_id=1, source_target_pairs={{0,4},{2,6},{4,8},{6,10},{8,12},{10,14},{12,16},{14,18},{16,20},{1... | collective-permute-start | bytes 614408 | tf_op jit(solution)/shard_map/ppermute | solution.py:236
  4.4 7.0 %collective-permute-start = (f32[200,256]{1,0:T(8,128)S(1)}, f32[200,256]{1,0:T(8,128)S(1)}, u32[]{:S(2)}, u32[]{:S(2)}) collective-permute-start(f32[200,256]{1,0:T(8,128)S(1)} %shard_map.56.own_ref.slab_ref), channel_id=1, source_target_pairs={{0,2},{2,8},{4,6},{6,4},{8,10},{10,16},{12,14},{14,12},{16,18},{18... | collective-permute-start | bytes 614408 | tf_op jit(solution)/shard_map/ppermute | solution.py:236
  6.1 5.6 %collective-permute-start.4 = (f32[64,128]{1,0:T(8,128)S(1)}, f32[64,128]{1,0:T(8,128)S(1)}, u32[]{:S(2)}, u32[]{:S(2)}) collective-permute-start(f32[64,128]{1,0:T(8,128)S(1)} %bitcast.5), channel_id=1, source_target_pairs={{0,1},{1,0},{2,3},{3,2},{4,5},{5,4},{6,7},{7,6},{8,9},{9,8},{10,11... | collective-permute-start | bytes 98312 | tf_op jit(solution)/shard_map/ppermute | solution.py:240
  11.4 3.1 %collective-permute-start.3 = (f32[200,256]{1,0:T(8,128)S(1)}, f32[200,256]{1,0:T(8,128)S(1)}, u32[]{:S(2)}, u32[]{:S(2)}) collective-permute-start(f32[200,256]{1,0:T(8,128)S(1)} %shard_map.56.own_ref.slab_ref), channel_id=1, source_target_pairs={{0,2},{2,0},{4,6},{6,12},{8,10},{10,8},{12,14},{14,20},{16,18},{18... | collective-permute-start | bytes 614408 | tf_op jit(solution)/shard_map/ppermute | solution.py:236
  12.5 2.0 %collective-permute-start.5 = (f32[200,256]{1,0:T(8,128)S(1)}, f32[200,256]{1,0:T(8,128)S(1)}, u32[]{:S(2)}, u32[]{:S(2)}) collective-permute-start(f32[200,256]{1,0:T(8,128)S(1)} %collective-permute-done.1.slab_ref.refs_4_), channel_id=1, source_target_pairs={{0,2},{2,0},{4,6},{6,4},{8,10},{10,8},{12,14},{14,12},{16,18},{18,... | collective-permute-start | bytes 614408 | tf_op jit(solution)/shard_map/ppermute | solution.py:236
  12.9 4.0 %collective-permute-start.2 = (f32[64,128]{1,0:T(8,128)S(1)}, f32[64,128]{1,0:T(8,128)S(1)}, u32[]{:S(2)}, u32[]{:S(2)}) collective-permute-start(f32[64,128]{1,0:T(8,128)S(1)} %bitcast.4), channel_id=1, source_target_pairs={{0,1},{1,0},{2,3},{3,2},{4,5},{5,4},{6,7},{7,6},{8,9},{9,8},{10,11... | collective-permute-start | bytes 98312 | tf_op jit(solution)/shard_map/ppermute | solution.py:240
  14.8 4.3 %collective-permute-start.6 = (f32[128,128]{1,0:T(8,128)S(1)}, f32[128,128]{1,0:T(8,128)S(1)}, u32[]{:S(2)}, u32[]{:S(2)}) collective-permute-start(f32[128,128]{1,0:T(8,128)S(1)} %bitcast.3), channel_id=1, source_target_pairs={{0,1},{1,0},{2,3},{3,2},{4,5},{5,4},{6,7},{7,6},{8,9},{9,8},{10,11... | collective-permute-start | bytes 196616 | tf_op jit(solution)/shard_map/ppermute | solution.py:240

commit v18 on v8

v18 whole, which is shorter than its diff:
```python
import functools
import jax
import jax.numpy as jnp
from jax import lax
from jax.experimental import pallas as pl
from jax.experimental.pallas import tpu as pltpu
from jax.sharding import PartitionSpec as P

LANES = 128
F32 = jnp.float32
ONCHIP = pl.BlockSpec(memory_space=pltpu.VMEM)
OFFCHIP = pl.BlockSpec(memory_space=pltpu.HBM)


def column(labels):
    return jnp.broadcast_to(labels.astype(F32), (LANES, labels.shape[1])).T


def fold(rows, row_labels, cd_labels):
    tiles = rows.shape[1] // LANES
    kept = [
        jnp.where(row_labels == cd_labels[:, k * LANES:(k + 1) * LANES], rows[:, k * LANES:(k + 1) * LANES], 0.0)
        for k in range(tiles)
    ]
    kept = [kept[k] + kept[k + tiles // 2] for k in range(tiles // 2)]
    low = lower(kept[0].shape)
    first, middle, last = kept
    middle_turned, last_turned = turned(middle), turned(last)
    return first + jnp.where(low, middle_turned, last_turned), middle + last_turned


def lower(shape):
    return lax.broadcasted_iota(jnp.int32, shape, 1) < LANES // 2


def turned(array):
    return pltpu.roll(array, LANES // 2, 1)


def fetch(pairs, sems):
    copies = [pltpu.make_async_copy(src, dst, sems.at[i]) for i, (src, dst) in enumerate(pairs)]
    for copy in copies:
        copy.start()
    return copies


def pack_kernel(amp_ref, ij_ref, cd_ref, out_ref, amp, ij, cd, sems):
    pairs, width = amp.shape[0], out_ref.shape[0] - 8
    copies = fetch([(amp_ref, amp), (ij_ref, ij), (cd_ref, cd)], sems)
    copies[1].wait()
    copies[2].wait()
    rows = column(ij[...])
    labels = cd[...].astype(F32)
    out_ref[width:, :] = jnp.broadcast_to(ij[...].astype(F32), (8, pairs))
    copies[0].wait()
    for start in range(0, pairs, LANES):
        part = slice(start, start + LANES)
        first, second = fold(amp[part, :], rows[part], labels)
        out_ref[:LANES, part] = first.T
        out_ref[LANES:width, part] = second.T[:width - LANES]


def row_labels(rows):
    tile = rows[:, -LANES:]
    return jnp.where(lower(tile.shape), turned(tile), tile)


def narrowed(rows, slab_ref):
    width = slab_ref.shape[0] - 8
    full = jnp.dot(rows[:, :width], slab_ref[:width, :], precision=lax.Precision.HIGHEST, preferred_element_type=F32)
    slab_labels, own_labels = slab_ref[width:width + 1, :], row_labels(rows)
    total = None
    for start in range(0, full.shape[1], LANES):
        part = slice(start, start + LANES)
        kept = jnp.where(own_labels == slab_labels[:, part], full[:, part], 0.0)
        total = kept if total is None else total + kept
    return total + turned(total)


def beside(one, other):
    return jnp.where(lower(one.shape), one, other)


def apart(array):
    low, other = lower(array.shape), turned(array)
    return jnp.where(low, array, other), jnp.where(low, other, array)


def halved(term):
    half = term.shape[0] // 2
    return beside(term[:half], term[half:])


def unhalved(term):
    return jnp.concatenate(apart(term), axis=0)


def odd():
    return lax.rem(lax.axis_index("blk"), 2) == 1


def first_kernel(count, v_ref, ab_ref, cd_ref, rows_ref, v, ab, cd, labels, sems):
    parts = v.shape[0] // count
    mine = lax.axis_index("red")
    places = [pl.ds(pl.multiple_of(lax.rem(mine + k, parts) * count, count), count) for k in range(parts)]
    held = [pl.ds(k * count, count) for k in range(parts)]
    copies = fetch([(ab_ref, ab), (cd_ref, cd)] + [(v_ref.at[p], v.at[h]) for p, h in zip(places, held)], sems)
    copies[0].wait()
    copies[1].wait()
    labels[...] = column(ab[...])
    cd_labels = cd[...].astype(F32)
    for copy, p, h in zip(copies[2:], places, held):
        own_labels = labels[p, :]
        copy.wait()
        leading, last = fold(v[h, :], own_labels, cd_labels)
        rows_ref[h, :LANES] = leading
        rows_ref[h, LANES:] = beside(last, own_labels)


def labels_kernel(slab_ref, out_ref):
    out_ref[...] = slab_ref[slab_ref.shape[0] - 8:, :]


def second():
    return lax.rem(lax.axis_index("blk"), 4) == 2


def own_kernel(rows_ref, own_ref, keep_ref, send_ref):
    count = keep_ref.shape[0]
    term = narrowed(rows_ref[...], own_ref)
    keep_ref[...] = term[:count]
    for k in range(1, send_ref.shape[0] + 1):
        send_ref[k - 1] = halved(term[k * count:(k + 1) * count])


def sent_kernel(rows_ref, slab_ref, out_ref):
    count = rows_ref.shape[0] - out_ref.shape[0]
    out_ref[...] = narrowed(rows_ref[count:, :], slab_ref)


def pair_kernel(rows_ref, two_ref, late_ref, mix_term, send_ref, third):
    parts, count = send_ref.shape[0] + 1, send_ref.shape[1]
    third[...] = mix_term[...]

    @pl.when(second())
    def _():
        third[...] = narrowed(rows_ref[count:, :], late_ref)

    both = beside(narrowed(rows_ref[count:, :], two_ref), third[...])
    for k in range(1, parts):
        send_ref[k - 1] = both[(k - 1) * count:k * count]


def cross_kernel(twin_ref, two_ref, core_ref, diagonal_ref):
    parts, half = diagonal_ref.shape[0] + 1, diagonal_ref.shape[1]
    term = narrowed(twin_ref[...], two_ref)
    width = two_ref.shape[0] - 8
    labels = two_ref[width:width + 1, :]
    tiles = [labels[:, start:start + LANES] for start in range(0, labels.shape[1], LANES)]
    core_ref[:half, :] = halved(term[:2 * half])
    core_ref[half:, :] = jnp.concatenate((tiles * 8)[:8], axis=0)
    for k in range(1, parts):
        diagonal_ref[k - 1] = halved(term[2 * k * half:2 * (k + 1) * half])


def keep_kernel(rows_ref, two_ref, mix_ref, late_ref, two_out, third_out):
    count = two_out.shape[0]
    two_out[...] = narrowed(rows_ref[:count, :], two_ref)

    @pl.when(second())
    def _():
        third_out[...] = narrowed(rows_ref[:count, :], late_ref)

    @pl.when(~second())
    def _():
        third_out[...] = narrowed(rows_ref[:count, :], mix_ref)


def finish_kernel(parts, rows_ref, own_keep, two_keep, third_keep, own_labels, two_ref, mix_ref, late_ref, core_ref, *refs):
    own_in, pair_in, diagonal_in = [refs[i * (parts - 1):(i + 1) * (parts - 1)] for i in range(3)]
    out_ref, out, sems = refs[-3:]
    count = own_keep.shape[0]
    width = two_ref.shape[0] - 8
    tiles = out.shape[2] // LANES
    rows = row_labels(rows_ref[:count, :])
    copies = []

    def store(m, term, labels):
        for k in range(tiles):
            out[m, :, k * LANES:(k + 1) * LANES] = jnp.where(rows == labels[k], term, 0.0)
        copies.append(pltpu.make_async_copy(out.at[m], out_ref.at[m], sems.at[m]))
        copies[-1].start()

    def of(ref, row=width):
        return [ref[row:row + 1, k * LANES:(k + 1) * LANES] for k in range(tiles)]

    def pick(here, one, other):
        return [jnp.where(here, x, y) for x, y in zip(one, other)]

    pairs = [apart(ref[...]) for ref in pair_in]
    store(0, sum([unhalved(ref[...]) for ref in own_in], own_keep[...]), of(own_labels, 0))
    store(2, sum([two for two, _ in pairs], two_keep[...]), of(two_ref))
    third = sum([third for _, third in pairs], third_keep[...])
    crossed = sum([unhalved(ref[...]) for ref in diagonal_in], unhalved(core_ref[:count // 2, :]))
    crossed_labels = [core_ref[count // 2 + k:count // 2 + k + 1, :] for k in range(tiles)]
    third_labels = pick(second(), of(late_ref), of(mix_ref))
    store(1, jnp.where(odd(), third, crossed), pick(odd(), third_labels, crossed_labels))
    store(3, jnp.where(odd(), crossed, third), pick(odd(), crossed_labels, third_labels))
    for copy in copies:
        copy.wait()


def whole(*shape):
    return jax.ShapeDtypeStruct(shape, F32)


def call(kernel, out_shape, args, flops, off=0, scratch=(), out_specs=ONCHIP):
    moved = sum(a.size * 4 for a in list(args) + out_shape)
    args = [pltpu.with_memory_space_constraint(a, pltpu.HBM) for a in args[:off]] + list(args[off:])
    return pl.pallas_call(
        kernel,
        out_shape=out_shape,
        in_specs=[OFFCHIP] * off + [ONCHIP] * (len(args) - off),
        out_specs=[out_specs] * len(out_shape),
        scratch_shapes=list(scratch),
        cost_estimate=pl.CostEstimate(flops=flops, bytes_accessed=0, transcendentals=0),
        compiler_params=pltpu.CompilerParams(vmem_limit_bytes=32 * 1024 * 1024),
    )(*args)


def body(amplitudes, integrals, cd_irrep, ab_irrep, ij_irrep):
    blocks, parts = lax.axis_size("blk"), lax.axis_size("red")
    pairs, depth = amplitudes.shape
    row_count = integrals.shape[0]
    width = depth // 4
    count = row_count // parts
    one_product = 12 * row_count * width * pairs

    def moved(array, steps):
        return lax.ppermute(array, "blk", [(i, (i + steps[i % 4]) % blocks) for i in range(blocks)])

    def exchanged(array):
        return [
            lax.ppermute(array[k - 1], "red", [(i, (i + k) % parts) for i in range(parts)])
            for k in range(1, parts)
        ]

    def after(array, *earlier):
        return lax.optimization_barrier((array, *earlier))[0]

    def staging(array, labels, copies):
        return [
            pltpu.VMEM(array.shape, F32),
            pltpu.VMEM(labels.shape, jnp.int32),
            pltpu.VMEM(cd_irrep.shape, jnp.int32),
        ], pltpu.SemaphoreType.DMA((2 + copies,))

    stage, sems = staging(amplitudes, ij_irrep, 1)
    own, = call(pack_kernel, [whole(width + 8, pairs)], (amplitudes, ij_irrep, cd_irrep),
                4 * amplitudes.size, 3, stage + [sems])
    def crossed(array, step):
        routes = [((b, r), (b ^ 1, (r + step) % parts)) for b in range(blocks) for r in range(parts)]
        return lax.ppermute(array, ("blk", "red"), [(b * parts + r, c * parts + t) for (b, r), (c, t) in routes])

    two = moved(own, (2, 2, 2, 2))
    own_labels, = call(labels_kernel, [whole(8, pairs)], (own,), 0)
    mix = moved(after(own, own_labels), (1, 3, 1, -1))
    stage, sems = staging(integrals, ab_irrep, parts)
    rows, = call(
        functools.partial(first_kernel, count), [whole(row_count, 2 * LANES)],
        (after(integrals, own_labels), ab_irrep, cd_irrep), 0, 3,
        stage + [pltpu.VMEM((row_count, LANES), F32), sems])
    twin = moved(rows, (1, -1, 1, -1))
    own_keep, own_send = call(
        own_kernel, [whole(count, LANES), whole(parts - 1, count // 2, LANES)], (rows, own), 64 * one_product)
    own_in = exchanged(own_send)
    late = moved(after(own, own_keep), (1, -1, 1, 3))
    rest = whole(row_count - count, LANES)
    mix_term, = call(sent_kernel, [rest], (rows, mix), 64 * one_product)
    pair_send, = call(pair_kernel, [whole(parts - 1, count, LANES)], (rows, after(two, mix_term, *own_in), late, mix_term),
                      0, 0, [pltpu.VMEM(rest.shape, F32)])
    pair_in = exchanged(pair_send)
    core_send, diagonal_send = call(
        cross_kernel, [whole(count // 2 + 8, LANES), whole(parts - 1, count // 2, LANES)],
        (twin, after(two, pair_send)), 0)
    diagonal_in = [crossed(diagonal_send[k - 1], k) for k in range(1, parts)]
    core_in = moved(core_send, (1, -1, 1, -1))
    two_keep, third_keep = call(keep_kernel, [whole(count, LANES)] * 2,
                                (rows, after(two, diagonal_send), mix, late), 64 * one_product)
    out, = call(functools.partial(finish_kernel, parts), [whole(4, count, pairs)],
                (rows, own_keep, two_keep, third_keep, own_labels, two, mix, late, core_in, *own_in, *pair_in, *diagonal_in),
                0, 0, [pltpu.VMEM((4, count, pairs), F32), pltpu.SemaphoreType.DMA((4,))], OFFCHIP)
    return out


def solution(mesh):
    in_specs = (P("blk", "red"), P("blk", "red"), P("red", None), P("blk", None), P("blk", None))
    out_specs = P(None, ("blk", "red"), None)
    return jax.shard_map(body, mesh=mesh, in_specs=in_specs, out_specs=out_specs, check_vma=False)
```

time: 20.8 us -> 20.7 us (level)
  the two profiles are of different devices: /device:TPU:0 before, /device:TPU:3 now
where the time goes in v18:
time: 20.7 us; the launch traced here: 20.5 us
  starting transfers between devices  10.8 us (52%)
  Pallas kernels  5.8 us (28%)
  waiting for transfers between devices  3.81 us (18%)
    pallas_call x9, Pallas kernels, call(): pl.pallas_call(kernel, out_shape=out_shape, in_specs=[OFFCHIP] * off + [O...  5.8 us
    ppermute x1, starting transfers between devices, crossed(): lax.ppermute(array, ('blk', 'red'), [(b * parts + r, c * parts + t) for (...  4.9 us
    ppermute x5, starting transfers between devices, moved(): lax.ppermute(array, 'blk', [(i, (i + steps[i % 4]) % blocks) for i in ran...  4.31 us
    ppermute x5, waiting for transfers between devices, moved(): lax.ppermute(array, 'blk', [(i, (i + steps[i % 4]) % blocks) for i in ran...  2.35 us
    ppermute x2, starting transfers between devices, exchanged(): lax.ppermute(array[k - 1], 'red', [(i, (i + k) % parts) for i in range(pa...  1.6 us
    ppermute x1, waiting for transfers between devices, crossed(): lax.ppermute(array, ('blk', 'red'), [(b * parts + r, c * parts + t) for (...  1.45 us
  transfers between devices with their start and end apart: 8, of which 2 were waited for; matrix products, arithmetic and copies ran while one was open for 0% of the time, Pallas kernels for 17%

profile of v18, /device:TPU:3, one launch (start us, length us, event | category | flops | bytes accessed | tf_op | source)
XLA Modules:
  0.0 20.5 jit_solution(7065193362348352791)
XLA Ops:
  0.0 1.4 %shard_map.55.slab_ref.own_ref = f32[200,256]{1,0:T(8,128)S(1)} custom-call(f32[256,768]{1,0:T(8,128)} %amp_ref.1, s32[1,256]{1,0:T(1,128)} %ij_ref.1, s32[1,768]{1,0:T(1,128)} %cd_ref.3), custom_call_target="tpu_custom_call" | custom-call | flops 786432 | tf_op jit(solution)/shard_map/pallas_call | solution.py:220
  1.4 1.3 %collective-permute-start = (f32[200,256]{1,0:T(8,128)S(1)}, f32[200,256]{1,0:T(8,128)S(1)}, u32[]{:S(2)}, u32[]{:S(2)}) collective-permute-start(f32[200,256]{1,0:T(8,128)S(1)} %shard_map.55.slab_ref.own_ref), channel_id=1, source_target_pairs={{0,4},{2,6},{4,8},{6,10},{8,12},{10,14},{12,16},{14,18},{16,20},{1... | collective-permute-start | bytes 614408 | tf_op jit(solution)/shard_map/ppermute | solution.py:240
  2.7 1.0 %collective-permute-start.2 = (f32[200,256]{1,0:T(8,128)S(1)}, f32[200,256]{1,0:T(8,128)S(1)}, u32[]{:S(2)}, u32[]{:S(2)}) collective-permute-start(f32[200,256]{1,0:T(8,128)S(1)} %shard_map.55.slab_ref.own_ref), channel_id=1, source_target_pairs={{0,2},{2,8},{4,6},{6,4},{8,10},{10,16},{12,14},{14,12},{16,18},{18... | collective-permute-start | bytes 614408 | tf_op jit(solution)/shard_map/ppermute | solution.py:240
  3.7 1.3 %shard_map.57.rows_ref = f32[256,256]{1,0:T(8,128)S(1)} custom-call(f32[256,768]{1,0:T(8,128)} %v_ref, s32[1,256]{1,0:T(1,128)} %ab_ref.1, s32[1,768]{1,0:T(1,128)} %cd_ref.3), custom_call_target="tpu_custom_call" | custom-call | tf_op jit(solution)/shard_map/pallas_call | solution.py:220
  5.0 0.1 collective-permute-start.1
  5.0 0.4 %shard_map.58 = (f32[128,128]{1,0:T(8,128)S(1)}, f32[1,64,128]{2,1,0:T(8,128)S(1)}) custom-call(f32[256,256]{1,0:T(8,128)S(1)} %shard_map.57.rows_ref, f32[200,256]{1,0:T(8,128)S(1)} %shard_map.55.slab_ref.own_ref), custom_call_target="tpu_custom_call" | custom-call | flops 9663676416 | tf_op jit(solution)/shard_map/pallas_call | solution.py:220
  5.5 1.3 %collective-permute-start.3 = (f32[64,128]{1,0:T(8,128)S(1)}, f32[64,128]{1,0:T(8,128)S(1)}, u32[]{:S(2)}, u32[]{:S(2)}) collective-permute-start(f32[64,128]{1,0:T(8,128)S(1)} %bitcast.5), channel_id=1, source_target_pairs={{0,1},{1,0},{2,3},{3,2},{4,5},{5,4},{6,7},{7,6},{8,9},{9,8},{10,11... | collective-permute-start | bytes 98312 | tf_op jit(solution)/shard_map/ppermute | solution.py:244
  6.8 2.0 %collective-permute-start.4 = (f32[200,256]{1,0:T(8,128)S(1)}, f32[200,256]{1,0:T(8,128)S(1)}, u32[]{:S(2)}, u32[]{:S(2)}) collective-permute-start(f32[200,256]{1,0:T(8,128)S(1)} %shard_map.55.slab_ref.own_ref), channel_id=1, source_target_pairs={{0,2},{2,0},{4,6},{6,12},{8,10},{10,8},{12,14},{14,20},{16,18},{18... | collective-permute-start | bytes 614408 | tf_op jit(solution)/shard_map/ppermute | solution.py:240
  8.7 0.0 collective-permute-done.2.slab_ref.mix_ref
  8.7 0.3 %shard_map.59.mix_term = f32[128,128]{1,0:T(8,128)S(1)} custom-call(f32[256,256]{1,0:T(8,128)S(1)} %shard_map.57.rows_ref, f32[200,256]{1,0:T(8,128)S(1)} %collective-permute-done.2.slab_ref.mix_ref), custom_call_target="tpu_custom_call" | custom-call | flops 9663676416 | tf_op jit(solution)/shard_map/pallas_call | solution.py:220
  9.1 0.0 collective-permute-done.3.refs_0_
  9.1 0.0 collective-permute-done.two_ref
  9.1 2.3 %collective-permute-done.4.late_ref = f32[200,256]{1,0:T(8,128)S(1)} collective-permute-done((f32[200,256]{1,0:T(8,128)S(1)}, f32[200,256]{1,0:T(8,128)S(1)}, u32[]{:S(2)}, u32[]{:S(2)}) %collective-permute-start.4) | collective-permute-done | bytes 204832 | tf_op jit(solution)/shard_map/ppermute | solution.py:240
  11.4 0.3 %shard_map.60 = f32[1,128,128]{2,1,0:T(8,128)S(1)} custom-call(f32[256,256]{1,0:T(8,128)S(1)} %shard_map.57.rows_ref, f32[200,256]{1,0:T(8,128)S(1)} %collective-permute-done.two_ref, f32[200,256]{1,0:T(8,128)S(1)} %collective-permute-done.4.late_ref, f32[128,128]{1,0:T(8,128)S(1)} %shard_map.59.mix_term), custom_call_target="tpu_custom_call" | custom-call | tf_op jit(solution)/shard_map/pallas_call | solution.py:220
  11.8 0.3 %collective-permute-start.6 = (f32[128,128]{1,0:T(8,128)S(1)}, f32[128,128]{1,0:T(8,128)S(1)}, u32[]{:S(2)}, u32[]{:S(2)}) collective-permute-start(f32[128,128]{1,0:T(8,128)S(1)} %bitcast.3), channel_id=1, source_target_pairs={{0,1},{1,0},{2,3},{3,2},{4,5},{5,4},{6,7},{7,6},{8,9},{9,8},{10,11... | collective-permute-start | bytes 196616 | tf_op jit(solution)/shard_map/ppermute | solution.py:244
  12.1 0.0 collective-permute-done.1.twin_ref
  12.1 0.4 %shard_map.61 = (f32[72,128]{1,0:T(8,128)S(1)}, f32[1,64,128]{2,1,0:T(8,128)S(1)}) custom-call(f32[256,256]{1,0:T(8,128)S(1)} %collective-permute-done.1.twin_ref, f32[200,256]{1,0:T(8,128)S(1)} %collective-permute-done.two_ref), custom_call_target="tpu_custom_call" | custom-call | tf_op jit(solution)/shard_map/pallas_call | solution.py:220
  12.5 4.9 %collective-permute-start.7 = (f32[64,128]{1,0:T(8,128)S(1)}, f32[64,128]{1,0:T(8,128)S(1)}, u32[]{:S(2)}, u32[]{:S(2)}) collective-permute-start(f32[64,128]{1,0:T(8,128)S(1)} %bitcast.4), channel_id=1, source_target_pairs={{0,3},{1,2},{2,1},{3,0},{4,7},{5,6},{6,5},{7,4},{8,11},{9,10},{10,... | collective-permute-start | bytes 98312 | tf_op jit(solution)/shard_map/ppermute | solution.py:263
  17.4 0.0 collective-permute-start.5
  17.4 0.7 %shard_map.62 = (f32[128,128]{1,0:T(8,128)S(1)}, f32[128,128]{1,0:T(8,128)S(1)}) custom-call(f32[256,256]{1,0:T(8,128)S(1)} %shard_map.57.rows_ref, f32[200,256]{1,0:T(8,128)S(1)} %collective-permute-done.two_ref, f32[200,256]{1,0:T(8,128)S(1)} %collective-permute-done.2.slab_ref.mix_ref, f32[200,256]{1,0:T(8,128)S(1)} %collective-permute-done.4.late_ref), custom_call_target="tpu_custom_call" | custom-call | flops 9663676416 | tf_op jit(solution)/shard_map/pallas_call | solution.py:220
  18.1 0.0 collective-permute-done.6.refs_1_
  18.1 1.4 %collective-permute-done.7.refs_2_ = f32[64,128]{1,0:T(8,128)S(1)} collective-permute-done((f32[64,128]{1,0:T(8,128)S(1)}, f32[64,128]{1,0:T(8,128)S(1)}, u32[]{:S(2)}, u32[]{:S(2)}) %collective-permute-start.7) | collective-permute-done | bytes 32800 | tf_op jit(solution)/shard_map/ppermute | solution.py:263
  19.6 0.0 collective-permute-done.5.core_ref
  19.6 0.9 %shard_map.63 = f32[4,128,256]{2,1,0:T(8,128)} custom-call(f32[256,256]{1,0:T(8,128)S(1)} %shard_map.57.rows_ref, f32[128,128]{1,0:T(8,128)S(1)} %get-tuple-element.18.own_keep, f32[128,128]{1,0:T(8,128)S(1)} %get-tuple-element.26.two_keep, f32[128,128]{1,0:T(8,128)S(1)} %get-tuple-element.27.third_keep, f32[8,256]{1,0:T(8,128)S(1)} %shard_map.56.own_labels, ...), custom_call_target="tpu_custom_call" | custom-call | tf_op jit(solution)/shard_map/pallas_call | solution.py:220
  (1 shorter events, 0.0 us)
Async XLA Ops:
  1.4 7.7 %collective-permute-start = (f32[200,256]{1,0:T(8,128)S(1)}, f32[200,256]{1,0:T(8,128)S(1)}, u32[]{:S(2)}, u32[]{:S(2)}) collective-permute-start(f32[200,256]{1,0:T(8,128)S(1)} %shard_map.55.slab_ref.own_ref), channel_id=1, source_target_pairs={{0,4},{2,6},{4,8},{6,10},{8,12},{10,14},{12,16},{14,18},{16,20},{1... | collective-permute-start | bytes 614408 | tf_op jit(solution)/shard_map/ppermute | solution.py:240
  2.7 6.0 %collective-permute-start.2 = (f32[200,256]{1,0:T(8,128)S(1)}, f32[200,256]{1,0:T(8,128)S(1)}, u32[]{:S(2)}, u32[]{:S(2)}) collective-permute-start(f32[200,256]{1,0:T(8,128)S(1)} %shard_map.55.slab_ref.own_ref), channel_id=1, source_target_pairs={{0,2},{2,8},{4,6},{6,4},{8,10},{10,16},{12,14},{14,12},{16,18},{18... | collective-permute-start | bytes 614408 | tf_op jit(solution)/shard_map/ppermute | solution.py:240
  5.0 7.1 %collective-permute-start.1 = (f32[256,256]{1,0:T(8,128)S(1)}, f32[256,256]{1,0:T(8,128)S(1)}, u32[]{:S(2)}, u32[]{:S(2)}) collective-permute-start(f32[256,256]{1,0:T(8,128)S(1)} %shard_map.57.rows_ref), channel_id=1, source_target_pairs={{0,2},{2,0},{4,6},{6,4},{8,10},{10,8},{12,14},{14,12},{16,18},{18,... | collective-permute-start | bytes 786440 | tf_op jit(solution)/shard_map/ppermute | solution.py:240
  5.5 3.6 %collective-permute-start.3 = (f32[64,128]{1,0:T(8,128)S(1)}, f32[64,128]{1,0:T(8,128)S(1)}, u32[]{:S(2)}, u32[]{:S(2)}) collective-permute-start(f32[64,128]{1,0:T(8,128)S(1)} %bitcast.5), channel_id=1, source_target_pairs={{0,1},{1,0},{2,3},{3,2},{4,5},{5,4},{6,7},{7,6},{8,9},{9,8},{10,11... | collective-permute-start | bytes 98312 | tf_op jit(solution)/shard_map/ppermute | solution.py:244
  6.8 4.7 %collective-permute-start.4 = (f32[200,256]{1,0:T(8,128)S(1)}, f32[200,256]{1,0:T(8,128)S(1)}, u32[]{:S(2)}, u32[]{:S(2)}) collective-permute-start(f32[200,256]{1,0:T(8,128)S(1)} %shard_map.55.slab_ref.own_ref), channel_id=1, source_target_pairs={{0,2},{2,0},{4,6},{6,12},{8,10},{10,8},{12,14},{14,20},{16,18},{18... | collective-permute-start | bytes 614408 | tf_op jit(solution)/shard_map/ppermute | solution.py:240
  11.8 6.3 %collective-permute-start.6 = (f32[128,128]{1,0:T(8,128)S(1)}, f32[128,128]{1,0:T(8,128)S(1)}, u32[]{:S(2)}, u32[]{:S(2)}) collective-permute-start(f32[128,128]{1,0:T(8,128)S(1)} %bitcast.3), channel_id=1, source_target_pairs={{0,1},{1,0},{2,3},{3,2},{4,5},{5,4},{6,7},{7,6},{8,9},{9,8},{10,11... | collective-permute-start | bytes 196616 | tf_op jit(solution)/shard_map/ppermute | solution.py:244
  12.5 7.0 %collective-permute-start.7 = (f32[64,128]{1,0:T(8,128)S(1)}, f32[64,128]{1,0:T(8,128)S(1)}, u32[]{:S(2)}, u32[]{:S(2)}) collective-permute-start(f32[64,128]{1,0:T(8,128)S(1)} %bitcast.4), channel_id=1, source_target_pairs={{0,3},{1,2},{2,1},{3,0},{4,7},{5,6},{6,5},{7,4},{8,11},{9,10},{10,... | collective-permute-start | bytes 98312 | tf_op jit(solution)/shard_map/ppermute | solution.py:263
  17.4 2.1 %collective-permute-start.5 = (f32[72,128]{1,0:T(8,128)S(1)}, f32[72,128]{1,0:T(8,128)S(1)}, u32[]{:S(2)}, u32[]{:S(2)}) collective-permute-start(f32[72,128]{1,0:T(8,128)S(1)} %get-tuple-element.28), channel_id=1, source_target_pairs={{0,2},{2,0},{4,6},{6,4},{8,10},{10,8},{12,14},{14,12},{16,18},{18,... | collective-permute-start | bytes 110600 | tf_op jit(solution)/shard_map/ppermute | solution.py:240

commit v19 on v18

--- a/solution.py
+++ b/solution.py
@@ -276,7 +276,7 @@
     own_in = exchanged(own_send)
     late = moved(after(own, own_keep), (1, -1, 1, 3))
     rest = whole(row_count - count, LANES)
-    mix_term, = call(sent_kernel, [rest], (rows, mix), 64 * one_product)
+    mix_term, = call(sent_kernel, [rest], (rows, mix), 0)
     pair_send, = call(pair_kernel, [whole(parts - 1, count, LANES)], (rows, after(two, mix_term, *own_in), late, mix_term),
                       0, 0, [pltpu.VMEM(rest.shape, F32)])
     pair_in = exchanged(pair_send)

time: 20.7 us -> 19.6 us (0.947)
  the two profiles are of different devices: /device:TPU:3 before, /device:TPU:0 now
where the time goes in v19:
time: 19.6 us; the launch traced here: 19.2 us
  starting transfers between devices  8.66 us (44%)
  Pallas kernels  5.81 us (30%)
  waiting for transfers between devices  4.69 us (24%)
    pallas_call x9, Pallas kernels, call(): pl.pallas_call(kernel, out_shape=out_shape, in_specs=[OFFCHIP] * off + [O...  5.81 us
    ppermute x5, starting transfers between devices, moved(): lax.ppermute(array, 'blk', [(i, (i + steps[i % 4]) % blocks) for i in ran...  5.42 us
    ppermute x2, starting transfers between devices, exchanged(): lax.ppermute(array[k - 1], 'red', [(i, (i + k) % parts) for i in range(pa...  3.17 us
    ppermute x5, waiting for transfers between devices, moved(): lax.ppermute(array, 'blk', [(i, (i + steps[i % 4]) % blocks) for i in ran...  2.43 us
    ppermute x2, waiting for transfers between devices, exchanged(): lax.ppermute(array[k - 1], 'red', [(i, (i + k) % parts) for i in range(pa...  1.16 us
    ppermute x1, waiting for transfers between devices, crossed(): lax.ppermute(array, ('blk', 'red'), [(b * parts + r, c * parts + t) for (...  1.1 us
  transfers between devices with their start and end apart: 8, of which 5 were waited for; matrix products, arithmetic and copies ran while one was open for 0% of the time, Pallas kernels for 18%

profile of v19, /device:TPU:0, one launch (start us, length us, event | category | flops | bytes accessed | tf_op | source)
XLA Modules:
  0.0 19.2 jit_solution(17798939898115009476)
XLA Ops:
  0.0 1.4 %shard_map.55.slab_ref.own_ref = f32[200,256]{1,0:T(8,128)S(1)} custom-call(f32[256,768]{1,0:T(8,128)} %amp_ref.1, s32[1,256]{1,0:T(1,128)} %ij_ref.1, s32[1,768]{1,0:T(1,128)} %cd_ref.3), custom_call_target="tpu_custom_call" | custom-call | flops 786432 | tf_op jit(solution)/shard_map/pallas_call | solution.py:220
  1.4 3.0 %collective-permute-start = (f32[200,256]{1,0:T(8,128)S(1)}, f32[200,256]{1,0:T(8,128)S(1)}, u32[]{:S(2)}, u32[]{:S(2)}) collective-permute-start(f32[200,256]{1,0:T(8,128)S(1)} %shard_map.55.slab_ref.own_ref), channel_id=1, source_target_pairs={{0,4},{2,6},{4,8},{6,10},{8,12},{10,14},{12,16},{14,18},{16,20},{1... | collective-permute-start | bytes 614408 | tf_op jit(solution)/shard_map/ppermute | solution.py:240
  4.4 0.0 collective-permute-start.2
  4.4 1.3 %shard_map.57.rows_ref = f32[256,256]{1,0:T(8,128)S(1)} custom-call(f32[256,768]{1,0:T(8,128)} %v_ref, s32[1,256]{1,0:T(1,128)} %ab_ref.1, s32[1,768]{1,0:T(1,128)} %cd_ref.3), custom_call_target="tpu_custom_call" | custom-call | tf_op jit(solution)/shard_map/pallas_call | solution.py:220
  5.7 1.8 %collective-permute-start.1 = (f32[256,256]{1,0:T(8,128)S(1)}, f32[256,256]{1,0:T(8,128)S(1)}, u32[]{:S(2)}, u32[]{:S(2)}) collective-permute-start(f32[256,256]{1,0:T(8,128)S(1)} %shard_map.57.rows_ref), channel_id=1, source_target_pairs={{0,2},{2,0},{4,6},{6,4},{8,10},{10,8},{12,14},{14,12},{16,18},{18,... | collective-permute-start | bytes 786440 | tf_op jit(solution)/shard_map/ppermute | solution.py:240
  7.4 0.4 %shard_map.58 = (f32[128,128]{1,0:T(8,128)S(1)}, f32[1,64,128]{2,1,0:T(8,128)S(1)}) custom-call(f32[256,256]{1,0:T(8,128)S(1)} %shard_map.57.rows_ref, f32[200,256]{1,0:T(8,128)S(1)} %shard_map.55.slab_ref.own_ref), custom_call_target="tpu_custom_call" | custom-call | flops 9663676416 | tf_op jit(solution)/shard_map/pallas_call | solution.py:220
  7.9 0.1 collective-permute-start.4
  7.9 1.6 %collective-permute-start.3 = (f32[64,128]{1,0:T(8,128)S(1)}, f32[64,128]{1,0:T(8,128)S(1)}, u32[]{:S(2)}, u32[]{:S(2)}) collective-permute-start(f32[64,128]{1,0:T(8,128)S(1)} %bitcast.5), channel_id=1, source_target_pairs={{0,1},{1,0},{2,3},{3,2},{4,5},{5,4},{6,7},{7,6},{8,9},{9,8},{10,11... | collective-permute-start | bytes 98312 | tf_op jit(solution)/shard_map/ppermute | solution.py:244
  9.5 1.8 %collective-permute-done.2.slab_ref.mix_ref = f32[200,256]{1,0:T(8,128)S(1)} collective-permute-done((f32[200,256]{1,0:T(8,128)S(1)}, f32[200,256]{1,0:T(8,128)S(1)}, u32[]{:S(2)}, u32[]{:S(2)}) %collective-permute-start.2) | collective-permute-done | bytes 204832 | tf_op jit(solution)/shard_map/ppermute | solution.py:240
  11.4 0.3 %shard_map.59.mix_term = f32[128,128]{1,0:T(8,128)S(1)} custom-call(f32[256,256]{1,0:T(8,128)S(1)} %shard_map.57.rows_ref, f32[200,256]{1,0:T(8,128)S(1)} %collective-permute-done.2.slab_ref.mix_ref), custom_call_target="tpu_custom_call" | custom-call | tf_op jit(solution)/shard_map/pallas_call | solution.py:220
  11.7 0.2 %collective-permute-done.3.refs_0_ = f32[64,128]{1,0:T(8,128)S(1)} collective-permute-done((f32[64,128]{1,0:T(8,128)S(1)}, f32[64,128]{1,0:T(8,128)S(1)}, u32[]{:S(2)}, u32[]{:S(2)}) %collective-permute-start.3) | collective-permute-done | bytes 32800 | tf_op jit(solution)/shard_map/ppermute | solution.py:244
  11.9 0.6 %collective-permute-done.two_ref = f32[200,256]{1,0:T(8,128)S(1)} collective-permute-done((f32[200,256]{1,0:T(8,128)S(1)}, f32[200,256]{1,0:T(8,128)S(1)}, u32[]{:S(2)}, u32[]{:S(2)}) %collective-permute-start) | collective-permute-done | bytes 204832 | tf_op jit(solution)/shard_map/ppermute | solution.py:240
  12.5 0.0 collective-permute-done.4.late_ref
  12.5 0.3 %shard_map.60 = f32[1,128,128]{2,1,0:T(8,128)S(1)} custom-call(f32[256,256]{1,0:T(8,128)S(1)} %shard_map.57.rows_ref, f32[200,256]{1,0:T(8,128)S(1)} %collective-permute-done.two_ref, f32[200,256]{1,0:T(8,128)S(1)} %collective-permute-done.4.late_ref, f32[128,128]{1,0:T(8,128)S(1)} %shard_map.59.mix_term), custom_call_target="tpu_custom_call" | custom-call | tf_op jit(solution)/shard_map/pallas_call | solution.py:220
  12.8 1.6 %collective-permute-start.6 = (f32[128,128]{1,0:T(8,128)S(1)}, f32[128,128]{1,0:T(8,128)S(1)}, u32[]{:S(2)}, u32[]{:S(2)}) collective-permute-start(f32[128,128]{1,0:T(8,128)S(1)} %bitcast.3), channel_id=1, source_target_pairs={{0,1},{1,0},{2,3},{3,2},{4,5},{5,4},{6,7},{7,6},{8,9},{9,8},{10,11... | collective-permute-start | bytes 196616 | tf_op jit(solution)/shard_map/ppermute | solution.py:244
  14.4 0.0 collective-permute-done.1.twin_ref
  14.4 0.4 %shard_map.61 = (f32[72,128]{1,0:T(8,128)S(1)}, f32[1,64,128]{2,1,0:T(8,128)S(1)}) custom-call(f32[256,256]{1,0:T(8,128)S(1)} %collective-permute-done.1.twin_ref, f32[200,256]{1,0:T(8,128)S(1)} %collective-permute-done.two_ref), custom_call_target="tpu_custom_call" | custom-call | tf_op jit(solution)/shard_map/pallas_call | solution.py:220
  14.9 0.1 collective-permute-start.7
  15.0 0.6 %collective-permute-start.5 = (f32[72,128]{1,0:T(8,128)S(1)}, f32[72,128]{1,0:T(8,128)S(1)}, u32[]{:S(2)}, u32[]{:S(2)}) collective-permute-start(f32[72,128]{1,0:T(8,128)S(1)} %get-tuple-element.28), channel_id=1, source_target_pairs={{0,2},{2,0},{4,6},{6,4},{8,10},{10,8},{12,14},{14,12},{16,18},{18,... | collective-permute-start | bytes 110600 | tf_op jit(solution)/shard_map/ppermute | solution.py:240
  15.6 0.7 %shard_map.62 = (f32[128,128]{1,0:T(8,128)S(1)}, f32[128,128]{1,0:T(8,128)S(1)}) custom-call(f32[256,256]{1,0:T(8,128)S(1)} %shard_map.57.rows_ref, f32[200,256]{1,0:T(8,128)S(1)} %collective-permute-done.two_ref, f32[200,256]{1,0:T(8,128)S(1)} %collective-permute-done.2.slab_ref.mix_ref, f32[200,256]{1,0:T(8,128)S(1)} %collective-permute-done.4.late_ref), custom_call_target="tpu_custom_call" | custom-call | flops 9663676416 | tf_op jit(solution)/shard_map/pallas_call | solution.py:220
  16.2 0.9 %collective-permute-done.6.refs_1_ = f32[128,128]{1,0:T(8,128)S(1)} collective-permute-done((f32[128,128]{1,0:T(8,128)S(1)}, f32[128,128]{1,0:T(8,128)S(1)}, u32[]{:S(2)}, u32[]{:S(2)}) %collective-permute-start.6) | collective-permute-done | bytes 65568 | tf_op jit(solution)/shard_map/ppermute | solution.py:244
  17.2 1.1 %collective-permute-done.7.refs_2_ = f32[64,128]{1,0:T(8,128)S(1)} collective-permute-done((f32[64,128]{1,0:T(8,128)S(1)}, f32[64,128]{1,0:T(8,128)S(1)}, u32[]{:S(2)}, u32[]{:S(2)}) %collective-permute-start.7) | collective-permute-done | bytes 32800 | tf_op jit(solution)/shard_map/ppermute | solution.py:263
  18.3 0.0 collective-permute-done.5.core_ref
  18.3 0.9 %shard_map.63 = f32[4,128,256]{2,1,0:T(8,128)} custom-call(f32[256,256]{1,0:T(8,128)S(1)} %shard_map.57.rows_ref, f32[128,128]{1,0:T(8,128)S(1)} %get-tuple-element.18.own_keep, f32[128,128]{1,0:T(8,128)S(1)} %get-tuple-element.26.two_keep, f32[128,128]{1,0:T(8,128)S(1)} %get-tuple-element.27.third_keep, f32[8,256]{1,0:T(8,128)S(1)} %shard_map.56.own_labels, ...), custom_call_target="tpu_custom_call" | custom-call | tf_op jit(solution)/shard_map/pallas_call | solution.py:220
  (1 shorter events, 0.0 us)
Async XLA Ops:
  1.4 11.1 %collective-permute-start = (f32[200,256]{1,0:T(8,128)S(1)}, f32[200,256]{1,0:T(8,128)S(1)}, u32[]{:S(2)}, u32[]{:S(2)}) collective-permute-start(f32[200,256]{1,0:T(8,128)S(1)} %shard_map.55.slab_ref.own_ref), channel_id=1, source_target_pairs={{0,4},{2,6},{4,8},{6,10},{8,12},{10,14},{12,16},{14,18},{16,20},{1... | collective-permute-start | bytes 614408 | tf_op jit(solution)/shard_map/ppermute | solution.py:240
  4.4 7.0 %collective-permute-start.2 = (f32[200,256]{1,0:T(8,128)S(1)}, f32[200,256]{1,0:T(8,128)S(1)}, u32[]{:S(2)}, u32[]{:S(2)}) collective-permute-start(f32[200,256]{1,0:T(8,128)S(1)} %shard_map.55.slab_ref.own_ref), channel_id=1, source_target_pairs={{0,2},{2,8},{4,6},{6,4},{8,10},{10,16},{12,14},{14,12},{16,18},{18... | collective-permute-start | bytes 614408 | tf_op jit(solution)/shard_map/ppermute | solution.py:240
  5.7 8.8 %collective-permute-start.1 = (f32[256,256]{1,0:T(8,128)S(1)}, f32[256,256]{1,0:T(8,128)S(1)}, u32[]{:S(2)}, u32[]{:S(2)}) collective-permute-start(f32[256,256]{1,0:T(8,128)S(1)} %shard_map.57.rows_ref), channel_id=1, source_target_pairs={{0,2},{2,0},{4,6},{6,4},{8,10},{10,8},{12,14},{14,12},{16,18},{18,... | collective-permute-start | bytes 786440 | tf_op jit(solution)/shard_map/ppermute | solution.py:240
  7.9 4.6 %collective-permute-start.4 = (f32[200,256]{1,0:T(8,128)S(1)}, f32[200,256]{1,0:T(8,128)S(1)}, u32[]{:S(2)}, u32[]{:S(2)}) collective-permute-start(f32[200,256]{1,0:T(8,128)S(1)} %shard_map.55.slab_ref.own_ref), channel_id=1, source_target_pairs={{0,2},{2,0},{4,6},{6,12},{8,10},{10,8},{12,14},{14,20},{16,18},{18... | collective-permute-start | bytes 614408 | tf_op jit(solution)/shard_map/ppermute | solution.py:240
  7.9 4.0 %collective-permute-start.3 = (f32[64,128]{1,0:T(8,128)S(1)}, f32[64,128]{1,0:T(8,128)S(1)}, u32[]{:S(2)}, u32[]{:S(2)}) collective-permute-start(f32[64,128]{1,0:T(8,128)S(1)} %bitcast.5), channel_id=1, source_target_pairs={{0,1},{1,0},{2,3},{3,2},{4,5},{5,4},{6,7},{7,6},{8,9},{9,8},{10,11... | collective-permute-start | bytes 98312 | tf_op jit(solution)/shard_map/ppermute | solution.py:244
  12.8 4.3 %collective-permute-start.6 = (f32[128,128]{1,0:T(8,128)S(1)}, f32[128,128]{1,0:T(8,128)S(1)}, u32[]{:S(2)}, u32[]{:S(2)}) collective-permute-start(f32[128,128]{1,0:T(8,128)S(1)} %bitcast.3), channel_id=1, source_target_pairs={{0,1},{1,0},{2,3},{3,2},{4,5},{5,4},{6,7},{7,6},{8,9},{9,8},{10,11... | collective-permute-start | bytes 196616 | tf_op jit(solution)/shard_map/ppermute | solution.py:244
  14.9 3.4 %collective-permute-start.7 = (f32[64,128]{1,0:T(8,128)S(1)}, f32[64,128]{1,0:T(8,128)S(1)}, u32[]{:S(2)}, u32[]{:S(2)}) collective-permute-start(f32[64,128]{1,0:T(8,128)S(1)} %bitcast.4), channel_id=1, source_target_pairs={{0,3},{1,2},{2,1},{3,0},{4,7},{5,6},{6,5},{7,4},{8,11},{9,10},{10,... | collective-permute-start | bytes 98312 | tf_op jit(solution)/shard_map/ppermute | solution.py:263
  15.0 3.3 %collective-permute-start.5 = (f32[72,128]{1,0:T(8,128)S(1)}, f32[72,128]{1,0:T(8,128)S(1)}, u32[]{:S(2)}, u32[]{:S(2)}) collective-permute-start(f32[72,128]{1,0:T(8,128)S(1)} %get-tuple-element.28), channel_id=1, source_target_pairs={{0,2},{2,0},{4,6},{6,4},{8,10},{10,8},{12,14},{14,12},{16,18},{18,... | collective-permute-start | bytes 110600 | tf_op jit(solution)/shard_map/ppermute | solution.py:240

commit v20 on v19

--- a/solution.py
+++ b/solution.py
@@ -152,15 +152,15 @@
 
 
 def cross_kernel(twin_ref, two_ref, core_ref, diagonal_ref):
-    parts, half = diagonal_ref.shape[0] + 1, diagonal_ref.shape[1]
+    parts, count = diagonal_ref.shape[0] + 1, diagonal_ref.shape[1] - 8
     term = narrowed(twin_ref[...], two_ref)
     width = two_ref.shape[0] - 8
     labels = two_ref[width:width + 1, :]
     tiles = [labels[:, start:start + LANES] for start in range(0, labels.shape[1], LANES)]
-    core_ref[:half, :] = halved(term[:2 * half])
-    core_ref[half:, :] = jnp.concatenate((tiles * 8)[:8], axis=0)
+    core_ref[...] = halved(term[:count])
     for k in range(1, parts):
-        diagonal_ref[k - 1] = halved(term[2 * k * half:2 * (k + 1) * half])
+        diagonal_ref[k - 1, :count, :] = term[k * count:(k + 1) * count]
+        diagonal_ref[k - 1, count:, :] = jnp.concatenate((tiles * 8)[:8], axis=0)
 
 
 def keep_kernel(rows_ref, two_ref, mix_ref, late_ref, two_out, third_out):
@@ -201,8 +201,8 @@
     store(0, sum([unhalved(ref[...]) for ref in own_in], own_keep[...]), of(own_labels, 0))
     store(2, sum([two for two, _ in pairs], two_keep[...]), of(two_ref))
     third = sum([third for _, third in pairs], third_keep[...])
-    crossed = sum([unhalved(ref[...]) for ref in diagonal_in], unhalved(core_ref[:count // 2, :]))
-    crossed_labels = [core_ref[count // 2 + k:count // 2 + k + 1, :] for k in range(tiles)]
+    crossed = sum([ref[:count, :] for ref in diagonal_in], unhalved(core_ref[...]))
+    crossed_labels = [diagonal_in[0][count + k:count + k + 1, :] for k in range(tiles)]
     third_labels = pick(second(), of(late_ref), of(mix_ref))
     store(1, jnp.where(odd(), third, crossed), pick(odd(), third_labels, crossed_labels))
     store(3, jnp.where(odd(), crossed, third), pick(odd(), crossed_labels, third_labels))
@@ -277,16 +277,16 @@
     late = moved(after(own, own_keep), (1, -1, 1, 3))
     rest = whole(row_count - count, LANES)
     mix_term, = call(sent_kernel, [rest], (rows, mix), 0)
-    pair_send, = call(pair_kernel, [whole(parts - 1, count, LANES)], (rows, after(two, mix_term, *own_in), late, mix_term),
+    core_send, diagonal_send = call(
+        cross_kernel, [whole(count // 2, LANES), whole(parts - 1, count + 8, LANES)],
+        (twin, after(two, mix_term, *own_in)), 0)
+    diagonal_in = [crossed(diagonal_send[k - 1], k) for k in range(1, parts)]
+    pair_send, = call(pair_kernel, [whole(parts - 1, count, LANES)], (rows, after(two, diagonal_send), late, mix_term),
                       0, 0, [pltpu.VMEM(rest.shape, F32)])
     pair_in = exchanged(pair_send)
-    core_send, diagonal_send = call(
-        cross_kernel, [whole(count // 2 + 8, LANES), whole(parts - 1, count // 2, LANES)],
-        (twin, after(two, pair_send)), 0)
-    diagonal_in = [crossed(diagonal_send[k - 1], k) for k in range(1, parts)]
-    core_in = moved(core_send, (1, -1, 1, -1))
+    core_in = moved(after(core_send, pair_send), (1, -1, 1, -1))
     two_keep, third_keep = call(keep_kernel, [whole(count, LANES)] * 2,
-                                (rows, after(two, diagonal_send), mix, late), 64 * one_product)
+                                (rows, after(two, pair_send), mix, late), 0)
     out, = call(functools.partial(finish_kernel, parts), [whole(4, count, pairs)],
                 (rows, own_keep, two_keep, third_keep, own_labels, two, mix, late, core_in, *own_in, *pair_in, *diagonal_in),
                 0, 0, [pltpu.VMEM((4, count, pairs), F32), pltpu.SemaphoreType.DMA((4,))], OFFCHIP)

time: 19.6 us -> 19.8 us (1.010)
  waiting for transfers between devices: 4.69 us -> 5.34 us
  starting transfers between devices: 8.66 us -> 8.39 us
    ppermute x2, waiting for transfers between devices: 1.16 us -> 2.69 us  [exchanged(): lax.ppermute(array[k - 1], 'red', [(i, (i + k) % parts) for i in range(pa...]
    ppermute x1, waiting for transfers between devices: 1.1 us -> 0.01 us  [crossed(): lax.ppermute(array, ('blk', 'red'), [(b * parts + r, c * parts + t) for (...]
    ppermute x5, starting transfers between devices: 5.42 us -> 5.12 us  [moved(): lax.ppermute(array, 'blk', [(i, (i + steps[i % 4]) % blocks) for i in ran...]
    ppermute x5, waiting for transfers between devices: 2.43 us -> 2.65 us  [moved(): lax.ppermute(array, 'blk', [(i, (i + steps[i % 4]) % blocks) for i in ran...]
where the time goes in v20:
time: 19.8 us; the launch traced here: 19.6 us
  starting transfers between devices  8.39 us (42%)
  Pallas kernels  5.8 us (29%)
  waiting for transfers between devices  5.34 us (27%)
    pallas_call x9, Pallas kernels, call(): pl.pallas_call(kernel, out_shape=out_shape, in_specs=[OFFCHIP] * off + [O...  5.8 us
    ppermute x5, starting transfers between devices, moved(): lax.ppermute(array, 'blk', [(i, (i + steps[i % 4]) % blocks) for i in ran...  5.12 us
    ppermute x2, starting transfers between devices, exchanged(): lax.ppermute(array[k - 1], 'red', [(i, (i + k) % parts) for i in range(pa...  3.01 us
    ppermute x2, waiting for transfers between devices, exchanged(): lax.ppermute(array[k - 1], 'red', [(i, (i + k) % parts) for i in range(pa...  2.69 us
    ppermute x5, waiting for transfers between devices, moved(): lax.ppermute(array, 'blk', [(i, (i + steps[i % 4]) % blocks) for i in ran...  2.65 us
  transfers between devices with their start and end apart: 8, of which 5 were waited for; matrix products, arithmetic and copies ran while one was open for 0% of the time, Pallas kernels for 18%

profile of v20, /device:TPU:0, one launch (start us, length us, event | category | flops | bytes accessed | tf_op | source)
XLA Modules:
  0.0 19.6 jit_solution(11633629392207605126)
XLA Ops:
  0.0 1.4 %shard_map.55.slab_ref.own_ref = f32[200,256]{1,0:T(8,128)S(1)} custom-call(f32[256,768]{1,0:T(8,128)} %amp_ref.1, s32[1,256]{1,0:T(1,128)} %ij_ref.1, s32[1,768]{1,0:T(1,128)} %cd_ref.3), custom_call_target="tpu_custom_call" | custom-call | flops 786432 | tf_op jit(solution)/shard_map/pallas_call | solution.py:220
  1.4 3.0 %collective-permute-start = (f32[200,256]{1,0:T(8,128)S(1)}, f32[200,256]{1,0:T(8,128)S(1)}, u32[]{:S(2)}, u32[]{:S(2)}) collective-permute-start(f32[200,256]{1,0:T(8,128)S(1)} %shard_map.55.slab_ref.own_ref), channel_id=1, source_target_pairs={{0,4},{2,6},{4,8},{6,10},{8,12},{10,14},{12,16},{14,18},{16,20},{1... | collective-permute-start | bytes 614408 | tf_op jit(solution)/shard_map/ppermute | solution.py:240
  4.4 0.0 collective-permute-start.2
  4.4 1.3 %shard_map.57.rows_ref = f32[256,256]{1,0:T(8,128)S(1)} custom-call(f32[256,768]{1,0:T(8,128)} %v_ref, s32[1,256]{1,0:T(1,128)} %ab_ref.1, s32[1,768]{1,0:T(1,128)} %cd_ref.3), custom_call_target="tpu_custom_call" | custom-call | tf_op jit(solution)/shard_map/pallas_call | solution.py:220
  5.7 1.8 %collective-permute-start.1 = (f32[256,256]{1,0:T(8,128)S(1)}, f32[256,256]{1,0:T(8,128)S(1)}, u32[]{:S(2)}, u32[]{:S(2)}) collective-permute-start(f32[256,256]{1,0:T(8,128)S(1)} %shard_map.57.rows_ref), channel_id=1, source_target_pairs={{0,2},{2,0},{4,6},{6,4},{8,10},{10,8},{12,14},{14,12},{16,18},{18,... | collective-permute-start | bytes 786440 | tf_op jit(solution)/shard_map/ppermute | solution.py:240
  7.4 0.4 %shard_map.58 = (f32[128,128]{1,0:T(8,128)S(1)}, f32[1,64,128]{2,1,0:T(8,128)S(1)}) custom-call(f32[256,256]{1,0:T(8,128)S(1)} %shard_map.57.rows_ref, f32[200,256]{1,0:T(8,128)S(1)} %shard_map.55.slab_ref.own_ref), custom_call_target="tpu_custom_call" | custom-call | flops 9663676416 | tf_op jit(solution)/shard_map/pallas_call | solution.py:220
  7.9 0.1 collective-permute-start.4
  7.9 1.6 %collective-permute-start.3 = (f32[64,128]{1,0:T(8,128)S(1)}, f32[64,128]{1,0:T(8,128)S(1)}, u32[]{:S(2)}, u32[]{:S(2)}) collective-permute-start(f32[64,128]{1,0:T(8,128)S(1)} %bitcast.5), channel_id=1, source_target_pairs={{0,1},{1,0},{2,3},{3,2},{4,5},{5,4},{6,7},{7,6},{8,9},{9,8},{10,11... | collective-permute-start | bytes 98312 | tf_op jit(solution)/shard_map/ppermute | solution.py:244
  9.5 1.8 %collective-permute-done.2.slab_ref.mix_ref = f32[200,256]{1,0:T(8,128)S(1)} collective-permute-done((f32[200,256]{1,0:T(8,128)S(1)}, f32[200,256]{1,0:T(8,128)S(1)}, u32[]{:S(2)}, u32[]{:S(2)}) %collective-permute-start.2) | collective-permute-done | bytes 204832 | tf_op jit(solution)/shard_map/ppermute | solution.py:240
  11.4 0.3 %shard_map.59.mix_term = f32[128,128]{1,0:T(8,128)S(1)} custom-call(f32[256,256]{1,0:T(8,128)S(1)} %shard_map.57.rows_ref, f32[200,256]{1,0:T(8,128)S(1)} %collective-permute-done.2.slab_ref.mix_ref), custom_call_target="tpu_custom_call" | custom-call | tf_op jit(solution)/shard_map/pallas_call | solution.py:220
  11.7 0.2 %collective-permute-done.3.refs_0_ = f32[64,128]{1,0:T(8,128)S(1)} collective-permute-done((f32[64,128]{1,0:T(8,128)S(1)}, f32[64,128]{1,0:T(8,128)S(1)}, u32[]{:S(2)}, u32[]{:S(2)}) %collective-permute-start.3) | collective-permute-done | bytes 32800 | tf_op jit(solution)/shard_map/ppermute | solution.py:244
  11.9 0.6 %collective-permute-done.two_ref = f32[200,256]{1,0:T(8,128)S(1)} collective-permute-done((f32[200,256]{1,0:T(8,128)S(1)}, f32[200,256]{1,0:T(8,128)S(1)}, u32[]{:S(2)}, u32[]{:S(2)}) %collective-permute-start) | collective-permute-done | bytes 204832 | tf_op jit(solution)/shard_map/ppermute | solution.py:240
  12.5 0.0 collective-permute-done.1.twin_ref
  12.5 0.4 %shard_map.60 = (f32[64,128]{1,0:T(8,128)S(1)}, f32[1,136,128]{2,1,0:T(8,128)S(1)}) custom-call(f32[256,256]{1,0:T(8,128)S(1)} %collective-permute-done.1.twin_ref, f32[200,256]{1,0:T(8,128)S(1)} %collective-permute-done.two_ref), custom_call_target="tpu_custom_call" | custom-call | tf_op jit(solution)/shard_map/pallas_call | solution.py:220
  12.9 0.3 %collective-permute-start.7 = (f32[136,128]{1,0:T(8,128)S(1)}, f32[136,128]{1,0:T(8,128)S(1)}, u32[]{:S(2)}, u32[]{:S(2)}) collective-permute-start(f32[136,128]{1,0:T(8,128)S(1)} %bitcast.4), channel_id=1, source_target_pairs={{0,3},{1,2},{2,1},{3,0},{4,7},{5,6},{6,5},{7,4},{8,11},{9,10},{10,... | collective-permute-start | bytes 208904 | tf_op jit(solution)/shard_map/ppermute | solution.py:263
  13.2 0.0 collective-permute-done.4.late_ref
  13.2 0.3 %shard_map.61 = f32[1,128,128]{2,1,0:T(8,128)S(1)} custom-call(f32[256,256]{1,0:T(8,128)S(1)} %shard_map.57.rows_ref, f32[200,256]{1,0:T(8,128)S(1)} %collective-permute-done.two_ref, f32[200,256]{1,0:T(8,128)S(1)} %collective-permute-done.4.late_ref, f32[128,128]{1,0:T(8,128)S(1)} %shard_map.59.mix_term), custom_call_target="tpu_custom_call" | custom-call | tf_op jit(solution)/shard_map/pallas_call | solution.py:220
  13.5 1.4 %collective-permute-start.6 = (f32[128,128]{1,0:T(8,128)S(1)}, f32[128,128]{1,0:T(8,128)S(1)}, u32[]{:S(2)}, u32[]{:S(2)}) collective-permute-start(f32[128,128]{1,0:T(8,128)S(1)} %bitcast.3), channel_id=1, source_target_pairs={{0,1},{1,0},{2,3},{3,2},{4,5},{5,4},{6,7},{7,6},{8,9},{9,8},{10,11... | collective-permute-start | bytes 196616 | tf_op jit(solution)/shard_map/ppermute | solution.py:244
  15.0 0.3 %collective-permute-start.5 = (f32[64,128]{1,0:T(8,128)S(1)}, f32[64,128]{1,0:T(8,128)S(1)}, u32[]{:S(2)}, u32[]{:S(2)}) collective-permute-start(f32[64,128]{1,0:T(8,128)S(1)} %get-tuple-element.30), channel_id=1, source_target_pairs={{0,2},{2,0},{4,6},{6,4},{8,10},{10,8},{12,14},{14,12},{16,18},{18,... | collective-permute-start | bytes 98312 | tf_op jit(solution)/shard_map/ppermute | solution.py:240
  15.3 0.7 %shard_map.62 = (f32[128,128]{1,0:T(8,128)S(1)}, f32[128,128]{1,0:T(8,128)S(1)}) custom-call(f32[256,256]{1,0:T(8,128)S(1)} %shard_map.57.rows_ref, f32[200,256]{1,0:T(8,128)S(1)} %collective-permute-done.two_ref, f32[200,256]{1,0:T(8,128)S(1)} %collective-permute-done.2.slab_ref.mix_ref, f32[200,256]{1,0:T(8,128)S(1)} %collective-permute-done.4.late_ref), custom_call_target="tpu_custom_call" | custom-call | tf_op jit(solution)/shard_map/pallas_call | solution.py:220
  16.0 0.2 %collective-permute-done.5.core_ref = f32[64,128]{1,0:T(8,128)S(1)} collective-permute-done((f32[64,128]{1,0:T(8,128)S(1)}, f32[64,128]{1,0:T(8,128)S(1)}, u32[]{:S(2)}, u32[]{:S(2)}) %collective-permute-start.5) | collective-permute-done | bytes 32800 | tf_op jit(solution)/shard_map/ppermute | solution.py:240
  16.2 2.5 %collective-permute-done.6.refs_1_ = f32[128,128]{1,0:T(8,128)S(1)} collective-permute-done((f32[128,128]{1,0:T(8,128)S(1)}, f32[128,128]{1,0:T(8,128)S(1)}, u32[]{:S(2)}, u32[]{:S(2)}) %collective-permute-start.6) | collective-permute-done | bytes 65568 | tf_op jit(solution)/shard_map/ppermute | solution.py:244
  18.7 0.0 collective-permute-done.7.refs_2_
  18.7 0.9 %shard_map.63 = f32[4,128,256]{2,1,0:T(8,128)} custom-call(f32[256,256]{1,0:T(8,128)S(1)} %shard_map.57.rows_ref, f32[128,128]{1,0:T(8,128)S(1)} %get-tuple-element.19.own_keep, f32[128,128]{1,0:T(8,128)S(1)} %get-tuple-element.27.two_keep, f32[128,128]{1,0:T(8,128)S(1)} %get-tuple-element.28.third_keep, f32[8,256]{1,0:T(8,128)S(1)} %shard_map.56.own_labels, ...), custom_call_target="tpu_custom_call" | custom-call | tf_op jit(solution)/shard_map/pallas_call | solution.py:220
  (1 shorter events, 0.0 us)
Async XLA Ops:
  1.4 11.1 %collective-permute-start = (f32[200,256]{1,0:T(8,128)S(1)}, f32[200,256]{1,0:T(8,128)S(1)}, u32[]{:S(2)}, u32[]{:S(2)}) collective-permute-start(f32[200,256]{1,0:T(8,128)S(1)} %shard_map.55.slab_ref.own_ref), channel_id=1, source_target_pairs={{0,4},{2,6},{4,8},{6,10},{8,12},{10,14},{12,16},{14,18},{16,20},{1... | collective-permute-start | bytes 614408 | tf_op jit(solution)/shard_map/ppermute | solution.py:240
  4.4 7.0 %collective-permute-start.2 = (f32[200,256]{1,0:T(8,128)S(1)}, f32[200,256]{1,0:T(8,128)S(1)}, u32[]{:S(2)}, u32[]{:S(2)}) collective-permute-start(f32[200,256]{1,0:T(8,128)S(1)} %shard_map.55.slab_ref.own_ref), channel_id=1, source_target_pairs={{0,2},{2,8},{4,6},{6,4},{8,10},{10,16},{12,14},{14,12},{16,18},{18... | collective-permute-start | bytes 614408 | tf_op jit(solution)/shard_map/ppermute | solution.py:240
  5.7 6.8 %collective-permute-start.1 = (f32[256,256]{1,0:T(8,128)S(1)}, f32[256,256]{1,0:T(8,128)S(1)}, u32[]{:S(2)}, u32[]{:S(2)}) collective-permute-start(f32[256,256]{1,0:T(8,128)S(1)} %shard_map.57.rows_ref), channel_id=1, source_target_pairs={{0,2},{2,0},{4,6},{6,4},{8,10},{10,8},{12,14},{14,12},{16,18},{18,... | collective-permute-start | bytes 786440 | tf_op jit(solution)/shard_map/ppermute | solution.py:240
  7.9 5.3 %collective-permute-start.4 = (f32[200,256]{1,0:T(8,128)S(1)}, f32[200,256]{1,0:T(8,128)S(1)}, u32[]{:S(2)}, u32[]{:S(2)}) collective-permute-start(f32[200,256]{1,0:T(8,128)S(1)} %shard_map.55.slab_ref.own_ref), channel_id=1, source_target_pairs={{0,2},{2,0},{4,6},{6,12},{8,10},{10,8},{12,14},{14,20},{16,18},{18... | collective-permute-start | bytes 614408 | tf_op jit(solution)/shard_map/ppermute | solution.py:240
  7.9 4.0 %collective-permute-start.3 = (f32[64,128]{1,0:T(8,128)S(1)}, f32[64,128]{1,0:T(8,128)S(1)}, u32[]{:S(2)}, u32[]{:S(2)}) collective-permute-start(f32[64,128]{1,0:T(8,128)S(1)} %bitcast.5), channel_id=1, source_target_pairs={{0,1},{1,0},{2,3},{3,2},{4,5},{5,4},{6,7},{7,6},{8,9},{9,8},{10,11... | collective-permute-start | bytes 98312 | tf_op jit(solution)/shard_map/ppermute | solution.py:244
  12.9 5.7 %collective-permute-start.7 = (f32[136,128]{1,0:T(8,128)S(1)}, f32[136,128]{1,0:T(8,128)S(1)}, u32[]{:S(2)}, u32[]{:S(2)}) collective-permute-start(f32[136,128]{1,0:T(8,128)S(1)} %bitcast.4), channel_id=1, source_target_pairs={{0,3},{1,2},{2,1},{3,0},{4,7},{5,6},{6,5},{7,4},{8,11},{9,10},{10,... | collective-permute-start | bytes 208904 | tf_op jit(solution)/shard_map/ppermute | solution.py:263
  13.5 5.1 %collective-permute-start.6 = (f32[128,128]{1,0:T(8,128)S(1)}, f32[128,128]{1,0:T(8,128)S(1)}, u32[]{:S(2)}, u32[]{:S(2)}) collective-permute-start(f32[128,128]{1,0:T(8,128)S(1)} %bitcast.3), channel_id=1, source_target_pairs={{0,1},{1,0},{2,3},{3,2},{4,5},{5,4},{6,7},{7,6},{8,9},{9,8},{10,11... | collective-permute-start | bytes 196616 | tf_op jit(solution)/shard_map/ppermute | solution.py:244
  15.0 1.2 %collective-permute-start.5 = (f32[64,128]{1,0:T(8,128)S(1)}, f32[64,128]{1,0:T(8,128)S(1)}, u32[]{:S(2)}, u32[]{:S(2)}) collective-permute-start(f32[64,128]{1,0:T(8,128)S(1)} %get-tuple-element.30), channel_id=1, source_target_pairs={{0,2},{2,0},{4,6},{6,4},{8,10},{10,8},{12,14},{14,12},{16,18},{18,... | collective-permute-start | bytes 98312 | tf_op jit(solution)/shard_map/ppermute | solution.py:240

commit v21 on v20

--- a/solution.py
+++ b/solution.py
@@ -152,19 +152,22 @@
 
 
 def cross_kernel(twin_ref, two_ref, core_ref, diagonal_ref):
-    parts, count = diagonal_ref.shape[0] + 1, diagonal_ref.shape[1] - 8
+    parts, half = diagonal_ref.shape[0] + 1, diagonal_ref.shape[1]
     term = narrowed(twin_ref[...], two_ref)
     width = two_ref.shape[0] - 8
     labels = two_ref[width:width + 1, :]
     tiles = [labels[:, start:start + LANES] for start in range(0, labels.shape[1], LANES)]
-    core_ref[...] = halved(term[:count])
+    core_ref[:half, :] = halved(term[:2 * half])
+    core_ref[half:, :] = jnp.concatenate((tiles * 8)[:8], axis=0)
     for k in range(1, parts):
-        diagonal_ref[k - 1, :count, :] = term[k * count:(k + 1) * count]
-        diagonal_ref[k - 1, count:, :] = jnp.concatenate((tiles * 8)[:8], axis=0)
-
-
-def keep_kernel(rows_ref, two_ref, mix_ref, late_ref, two_out, third_out):
+        diagonal_ref[k - 1] = halved(term[2 * k * half:2 * (k + 1) * half])
+
+
+def keep_kernel(rows_ref, two_ref, mix_ref, late_ref, *refs):
+    diagonal_in, (two_out, third_out, crossed_out) = refs[:-3], refs[-3:]
     count = two_out.shape[0]
+    terms = [unhalved(ref[...]) for ref in diagonal_in]
+    crossed_out[...] = sum(terms[1:], terms[0])
     two_out[...] = narrowed(rows_ref[:count, :], two_ref)
 
     @pl.when(second())
@@ -176,9 +179,13 @@
         third_out[...] = narrowed(rows_ref[:count, :], mix_ref)
 
 
-def finish_kernel(parts, rows_ref, own_keep, two_keep, third_keep, own_labels, two_ref, mix_ref, late_ref, core_ref, *refs):
-    own_in, pair_in, diagonal_in = [refs[i * (parts - 1):(i + 1) * (parts - 1)] for i in range(3)]
-    out_ref, out, sems = refs[-3:]
+def total_kernel(*refs):
+    terms, out_ref = [ref[...] for ref in refs[:-1]], refs[-1]
+    out_ref[...] = sum(terms[1:], terms[0])
+
+
+def finish_kernel(parts, rows_ref, own_keep, two_keep, third_keep, crossed_ref, own_labels, two_ref, mix_ref, late_ref, core_ref, *refs):
+    own_in, (pair_ref, out_ref, out, sems) = refs[:parts - 1], refs[parts - 1:]
     count = own_keep.shape[0]
     width = two_ref.shape[0] - 8
     tiles = out.shape[2] // LANES
@@ -197,12 +204,12 @@
     def pick(here, one, other):
         return [jnp.where(here, x, y) for x, y in zip(one, other)]
 
-    pairs = [apart(ref[...]) for ref in pair_in]
+    two, third = apart(pair_ref[...])
     store(0, sum([unhalved(ref[...]) for ref in own_in], own_keep[...]), of(own_labels, 0))
-    store(2, sum([two for two, _ in pairs], two_keep[...]), of(two_ref))
-    third = sum([third for _, third in pairs], third_keep[...])
-    crossed = sum([ref[:count, :] for ref in diagonal_in], unhalved(core_ref[...]))
-    crossed_labels = [diagonal_in[0][count + k:count + k + 1, :] for k in range(tiles)]
+    store(2, two + two_keep[...], of(two_ref))
+    third = third + third_keep[...]
+    crossed = crossed_ref[...] + unhalved(core_ref[:count // 2, :])
+    crossed_labels = [core_ref[count // 2 + k:count // 2 + k + 1, :] for k in range(tiles)]
     third_labels = pick(second(), of(late_ref), of(mix_ref))
     store(1, jnp.where(odd(), third, crossed), pick(odd(), third_labels, crossed_labels))
     store(3, jnp.where(odd(), crossed, third), pick(odd(), crossed_labels, third_labels))
@@ -278,17 +285,18 @@
     rest = whole(row_count - count, LANES)
     mix_term, = call(sent_kernel, [rest], (rows, mix), 0)
     core_send, diagonal_send = call(
-        cross_kernel, [whole(count // 2, LANES), whole(parts - 1, count + 8, LANES)],
+        cross_kernel, [whole(count // 2 + 8, LANES), whole(parts - 1, count // 2, LANES)],
         (twin, after(two, mix_term, *own_in)), 0)
     diagonal_in = [crossed(diagonal_send[k - 1], k) for k in range(1, parts)]
     pair_send, = call(pair_kernel, [whole(parts - 1, count, LANES)], (rows, after(two, diagonal_send), late, mix_term),
                       0, 0, [pltpu.VMEM(rest.shape, F32)])
     pair_in = exchanged(pair_send)
     core_in = moved(after(core_send, pair_send), (1, -1, 1, -1))
-    two_keep, third_keep = call(keep_kernel, [whole(count, LANES)] * 2,
-                                (rows, after(two, pair_send), mix, late), 0)
+    two_keep, third_keep, crossed_sum = call(
+        keep_kernel, [whole(count, LANES)] * 3, (rows, after(two, pair_send), mix, late, *diagonal_in), 4 * one_product)
+    pair_sum, = call(total_kernel, [whole(count, LANES)], tuple(pair_in), 0)
     out, = call(functools.partial(finish_kernel, parts), [whole(4, count, pairs)],
-                (rows, own_keep, two_keep, third_keep, own_labels, two, mix, late, core_in, *own_in, *pair_in, *diagonal_in),
+                (rows, own_keep, two_keep, third_keep, crossed_sum, own_labels, two, mix, late, core_in, *own_in, pair_sum),
                 0, 0, [pltpu.VMEM((4, count, pairs), F32), pltpu.SemaphoreType.DMA((4,))], OFFCHIP)
     return out
 

time: 19.8 us -> 19.3 us (0.975)
  waiting for transfers between devices: 5.34 us -> 4.86 us
    ppermute x2, waiting for transfers between devices: 2.69 us -> 1.1 us  [exchanged(): lax.ppermute(array[k - 1], 'red', [(i, (i + k) % parts) for i in range(pa...]
    ppermute x1, waiting for transfers between devices: 0.01 us -> 1.33 us  [crossed(): lax.ppermute(array, ('blk', 'red'), [(b * parts + r, c * parts + t) for (...]
    ppermute x5, waiting for transfers between devices: 2.65 us -> 2.43 us  [moved(): lax.ppermute(array, 'blk', [(i, (i + steps[i % 4]) % blocks) for i in ran...]
    pallas_call x9 -> x10, Pallas kernels: 5.8 us -> 5.8 us  [call(): pl.pallas_call(kernel, out_shape=out_shape, in_specs=[OFFCHIP] * off + [O...]
where the time goes in v21:
time: 19.3 us; the launch traced here: 19.1 us
  starting transfers between devices  8.38 us (43%)
  Pallas kernels  5.8 us (30%)
  waiting for transfers between devices  4.86 us (25%)
    pallas_call x10, Pallas kernels, call(): pl.pallas_call(kernel, out_shape=out_shape, in_specs=[OFFCHIP] * off + [O...  5.8 us
    ppermute x5, starting transfers between devices, moved(): lax.ppermute(array, 'blk', [(i, (i + steps[i % 4]) % blocks) for i in ran...  5.12 us
    ppermute x2, starting transfers between devices, exchanged(): lax.ppermute(array[k - 1], 'red', [(i, (i + k) % parts) for i in range(pa...  3.01 us
    ppermute x5, waiting for transfers between devices, moved(): lax.ppermute(array, 'blk', [(i, (i + steps[i % 4]) % blocks) for i in ran...  2.43 us
    ppermute x1, waiting for transfers between devices, crossed(): lax.ppermute(array, ('blk', 'red'), [(b * parts + r, c * parts + t) for (...  1.33 us
    ppermute x2, waiting for transfers between devices, exchanged(): lax.ppermute(array[k - 1], 'red', [(i, (i + k) % parts) for i in range(pa...  1.1 us
  transfers between devices with their start and end apart: 8, of which 5 were waited for; matrix products, arithmetic and copies ran while one was open for 0% of the time, Pallas kernels for 18%

profile of v21, /device:TPU:0, one launch (start us, length us, event | category | flops | bytes accessed | tf_op | source)
XLA Modules:
  0.0 19.1 jit_solution(3006500877757944339)
XLA Ops:
  0.0 1.4 %shard_map.55.slab_ref.own_ref = f32[200,256]{1,0:T(8,128)S(1)} custom-call(f32[256,768]{1,0:T(8,128)} %amp_ref.1, s32[1,256]{1,0:T(1,128)} %ij_ref.1, s32[1,768]{1,0:T(1,128)} %cd_ref.3), custom_call_target="tpu_custom_call" | custom-call | flops 786432 | tf_op jit(solution)/shard_map/pallas_call | solution.py:227
  1.4 3.0 %collective-permute-start = (f32[200,256]{1,0:T(8,128)S(1)}, f32[200,256]{1,0:T(8,128)S(1)}, u32[]{:S(2)}, u32[]{:S(2)}) collective-permute-start(f32[200,256]{1,0:T(8,128)S(1)} %shard_map.55.slab_ref.own_ref), channel_id=1, source_target_pairs={{0,4},{2,6},{4,8},{6,10},{8,12},{10,14},{12,16},{14,18},{16,20},{1... | collective-permute-start | bytes 614408 | tf_op jit(solution)/shard_map/ppermute | solution.py:247
  4.4 0.0 collective-permute-start.2
  4.4 1.3 %shard_map.57.rows_ref = f32[256,256]{1,0:T(8,128)S(1)} custom-call(f32[256,768]{1,0:T(8,128)} %v_ref, s32[1,256]{1,0:T(1,128)} %ab_ref.1, s32[1,768]{1,0:T(1,128)} %cd_ref.3), custom_call_target="tpu_custom_call" | custom-call | tf_op jit(solution)/shard_map/pallas_call | solution.py:227
  5.7 1.8 %collective-permute-start.1 = (f32[256,256]{1,0:T(8,128)S(1)}, f32[256,256]{1,0:T(8,128)S(1)}, u32[]{:S(2)}, u32[]{:S(2)}) collective-permute-start(f32[256,256]{1,0:T(8,128)S(1)} %shard_map.57.rows_ref), channel_id=1, source_target_pairs={{0,2},{2,0},{4,6},{6,4},{8,10},{10,8},{12,14},{14,12},{16,18},{18,... | collective-permute-start | bytes 786440 | tf_op jit(solution)/shard_map/ppermute | solution.py:247
  7.4 0.4 %shard_map.58 = (f32[128,128]{1,0:T(8,128)S(1)}, f32[1,64,128]{2,1,0:T(8,128)S(1)}) custom-call(f32[256,256]{1,0:T(8,128)S(1)} %shard_map.57.rows_ref, f32[200,256]{1,0:T(8,128)S(1)} %shard_map.55.slab_ref.own_ref), custom_call_target="tpu_custom_call" | custom-call | flops 9663676416 | tf_op jit(solution)/shard_map/pallas_call | solution.py:227
  7.9 0.1 collective-permute-start.4
  7.9 1.6 %collective-permute-start.3 = (f32[64,128]{1,0:T(8,128)S(1)}, f32[64,128]{1,0:T(8,128)S(1)}, u32[]{:S(2)}, u32[]{:S(2)}) collective-permute-start(f32[64,128]{1,0:T(8,128)S(1)} %bitcast.5), channel_id=1, source_target_pairs={{0,1},{1,0},{2,3},{3,2},{4,5},{5,4},{6,7},{7,6},{8,9},{9,8},{10,11... | collective-permute-start | bytes 98312 | tf_op jit(solution)/shard_map/ppermute | solution.py:251
  9.5 1.8 %collective-permute-done.2.slab_ref.mix_ref = f32[200,256]{1,0:T(8,128)S(1)} collective-permute-done((f32[200,256]{1,0:T(8,128)S(1)}, f32[200,256]{1,0:T(8,128)S(1)}, u32[]{:S(2)}, u32[]{:S(2)}) %collective-permute-start.2) | collective-permute-done | bytes 204832 | tf_op jit(solution)/shard_map/ppermute | solution.py:247
  11.4 0.3 %shard_map.59.mix_term = f32[128,128]{1,0:T(8,128)S(1)} custom-call(f32[256,256]{1,0:T(8,128)S(1)} %shard_map.57.rows_ref, f32[200,256]{1,0:T(8,128)S(1)} %collective-permute-done.2.slab_ref.mix_ref), custom_call_target="tpu_custom_call" | custom-call | tf_op jit(solution)/shard_map/pallas_call | solution.py:227
  11.7 0.2 %collective-permute-done.3.refs_0_ = f32[64,128]{1,0:T(8,128)S(1)} collective-permute-done((f32[64,128]{1,0:T(8,128)S(1)}, f32[64,128]{1,0:T(8,128)S(1)}, u32[]{:S(2)}, u32[]{:S(2)}) %collective-permute-start.3) | collective-permute-done | bytes 32800 | tf_op jit(solution)/shard_map/ppermute | solution.py:251
  11.9 0.6 %collective-permute-done.two_ref = f32[200,256]{1,0:T(8,128)S(1)} collective-permute-done((f32[200,256]{1,0:T(8,128)S(1)}, f32[200,256]{1,0:T(8,128)S(1)}, u32[]{:S(2)}, u32[]{:S(2)}) %collective-permute-start) | collective-permute-done | bytes 204832 | tf_op jit(solution)/shard_map/ppermute | solution.py:247
  12.5 0.0 collective-permute-done.1.twin_ref
  12.5 0.4 %shard_map.60 = (f32[72,128]{1,0:T(8,128)S(1)}, f32[1,64,128]{2,1,0:T(8,128)S(1)}) custom-call(f32[256,256]{1,0:T(8,128)S(1)} %collective-permute-done.1.twin_ref, f32[200,256]{1,0:T(8,128)S(1)} %collective-permute-done.two_ref), custom_call_target="tpu_custom_call" | custom-call | tf_op jit(solution)/shard_map/pallas_call | solution.py:227
  12.9 0.3 %collective-permute-start.5 = (f32[64,128]{1,0:T(8,128)S(1)}, f32[64,128]{1,0:T(8,128)S(1)}, u32[]{:S(2)}, u32[]{:S(2)}) collective-permute-start(f32[64,128]{1,0:T(8,128)S(1)} %bitcast.4), channel_id=1, source_target_pairs={{0,3},{1,2},{2,1},{3,0},{4,7},{5,6},{6,5},{7,4},{8,11},{9,10},{10,... | collective-permute-start | bytes 98312 | tf_op jit(solution)/shard_map/ppermute | solution.py:270
  13.2 0.0 collective-permute-done.4.late_ref
  13.2 0.3 %shard_map.61 = f32[1,128,128]{2,1,0:T(8,128)S(1)} custom-call(f32[256,256]{1,0:T(8,128)S(1)} %shard_map.57.rows_ref, f32[200,256]{1,0:T(8,128)S(1)} %collective-permute-done.two_ref, f32[200,256]{1,0:T(8,128)S(1)} %collective-permute-done.4.late_ref, f32[128,128]{1,0:T(8,128)S(1)} %shard_map.59.mix_term), custom_call_target="tpu_custom_call" | custom-call | tf_op jit(solution)/shard_map/pallas_call | solution.py:227
  13.5 1.4 %collective-permute-start.7 = (f32[128,128]{1,0:T(8,128)S(1)}, f32[128,128]{1,0:T(8,128)S(1)}, u32[]{:S(2)}, u32[]{:S(2)}) collective-permute-start(f32[128,128]{1,0:T(8,128)S(1)} %bitcast.3), channel_id=1, source_target_pairs={{0,1},{1,0},{2,3},{3,2},{4,5},{5,4},{6,7},{7,6},{8,9},{9,8},{10,11... | collective-permute-start | bytes 196616 | tf_op jit(solution)/shard_map/ppermute | solution.py:251
  15.0 0.3 %collective-permute-start.6 = (f32[72,128]{1,0:T(8,128)S(1)}, f32[72,128]{1,0:T(8,128)S(1)}, u32[]{:S(2)}, u32[]{:S(2)}) collective-permute-start(f32[72,128]{1,0:T(8,128)S(1)} %get-tuple-element.32), channel_id=1, source_target_pairs={{0,2},{2,0},{4,6},{6,4},{8,10},{10,8},{12,14},{14,12},{16,18},{18,... | collective-permute-start | bytes 110600 | tf_op jit(solution)/shard_map/ppermute | solution.py:247
  15.3 1.3 %collective-permute-done.5.refs_0_ = f32[64,128]{1,0:T(8,128)S(1)} collective-permute-done((f32[64,128]{1,0:T(8,128)S(1)}, f32[64,128]{1,0:T(8,128)S(1)}, u32[]{:S(2)}, u32[]{:S(2)}) %collective-permute-start.5) | collective-permute-done | bytes 32800 | tf_op jit(solution)/shard_map/ppermute | solution.py:270
  16.6 0.7 %shard_map.62 = (f32[128,128]{1,0:T(8,128)S(1)}, f32[128,128]{1,0:T(8,128)S(1)}, f32[128,128]{1,0:T(8,128)S(1)}) custom-call(f32[256,256]{1,0:T(8,128)S(1)} %shard_map.57.rows_ref, f32[200,256]{1,0:T(8,128)S(1)} %collective-permute-done.two_ref, f32[200,256]{1,0:T(8,128)S(1)} %collective-permute-done.2.slab_ref.mix_ref, ...), custom_call_target="tpu_custom_call" | custom-call | flops 603979776 | tf_op jit(solution)/shard_map/pallas_call | solution.py:227
  17.3 0.9 %collective-permute-done.7.refs_0_ = f32[128,128]{1,0:T(8,128)S(1)} collective-permute-done((f32[128,128]{1,0:T(8,128)S(1)}, f32[128,128]{1,0:T(8,128)S(1)}, u32[]{:S(2)}, u32[]{:S(2)}) %collective-permute-start.7) | collective-permute-done | bytes 65568 | tf_op jit(solution)/shard_map/ppermute | solution.py:251
  18.2 0.0 collective-permute-done.6.core_ref
  18.2 0.9 %shard_map.64 = f32[4,128,256]{2,1,0:T(8,128)} custom-call(f32[256,256]{1,0:T(8,128)S(1)} %shard_map.57.rows_ref, f32[128,128]{1,0:T(8,128)S(1)} %get-tuple-element.20.own_keep, f32[128,128]{1,0:T(8,128)S(1)} %get-tuple-element.28.two_keep, f32[128,128]{1,0:T(8,128)S(1)} %get-tuple-element.29.third_keep, f32[128,128]{1,0:T(8,128)S(1)} %get-tuple-element.30.crossed_ref, ...), custom_call_target="tpu_custom_call" | custom-call | tf_op jit(solution)/shard_map/pallas_call | solution.py:227
  (2 shorter events, 0.0 us)
Async XLA Ops:
  1.4 11.1 %collective-permute-start = (f32[200,256]{1,0:T(8,128)S(1)}, f32[200,256]{1,0:T(8,128)S(1)}, u32[]{:S(2)}, u32[]{:S(2)}) collective-permute-start(f32[200,256]{1,0:T(8,128)S(1)} %shard_map.55.slab_ref.own_ref), channel_id=1, source_target_pairs={{0,4},{2,6},{4,8},{6,10},{8,12},{10,14},{12,16},{14,18},{16,20},{1... | collective-permute-start | bytes 614408 | tf_op jit(solution)/shard_map/ppermute | solution.py:247
  4.4 7.0 %collective-permute-start.2 = (f32[200,256]{1,0:T(8,128)S(1)}, f32[200,256]{1,0:T(8,128)S(1)}, u32[]{:S(2)}, u32[]{:S(2)}) collective-permute-start(f32[200,256]{1,0:T(8,128)S(1)} %shard_map.55.slab_ref.own_ref), channel_id=1, source_target_pairs={{0,2},{2,8},{4,6},{6,4},{8,10},{10,16},{12,14},{14,12},{16,18},{18... | collective-permute-start | bytes 614408 | tf_op jit(solution)/shard_map/ppermute | solution.py:247
  5.7 6.8 %collective-permute-start.1 = (f32[256,256]{1,0:T(8,128)S(1)}, f32[256,256]{1,0:T(8,128)S(1)}, u32[]{:S(2)}, u32[]{:S(2)}) collective-permute-start(f32[256,256]{1,0:T(8,128)S(1)} %shard_map.57.rows_ref), channel_id=1, source_target_pairs={{0,2},{2,0},{4,6},{6,4},{8,10},{10,8},{12,14},{14,12},{16,18},{18,... | collective-permute-start | bytes 786440 | tf_op jit(solution)/shard_map/ppermute | solution.py:247
  7.9 5.3 %collective-permute-start.4 = (f32[200,256]{1,0:T(8,128)S(1)}, f32[200,256]{1,0:T(8,128)S(1)}, u32[]{:S(2)}, u32[]{:S(2)}) collective-permute-start(f32[200,256]{1,0:T(8,128)S(1)} %shard_map.55.slab_ref.own_ref), channel_id=1, source_target_pairs={{0,2},{2,0},{4,6},{6,12},{8,10},{10,8},{12,14},{14,20},{16,18},{18... | collective-permute-start | bytes 614408 | tf_op jit(solution)/shard_map/ppermute | solution.py:247
  7.9 4.0 %collective-permute-start.3 = (f32[64,128]{1,0:T(8,128)S(1)}, f32[64,128]{1,0:T(8,128)S(1)}, u32[]{:S(2)}, u32[]{:S(2)}) collective-permute-start(f32[64,128]{1,0:T(8,128)S(1)} %bitcast.5), channel_id=1, source_target_pairs={{0,1},{1,0},{2,3},{3,2},{4,5},{5,4},{6,7},{7,6},{8,9},{9,8},{10,11... | collective-permute-start | bytes 98312 | tf_op jit(solution)/shard_map/ppermute | solution.py:251
  12.9 3.7 %collective-permute-start.5 = (f32[64,128]{1,0:T(8,128)S(1)}, f32[64,128]{1,0:T(8,128)S(1)}, u32[]{:S(2)}, u32[]{:S(2)}) collective-permute-start(f32[64,128]{1,0:T(8,128)S(1)} %bitcast.4), channel_id=1, source_target_pairs={{0,3},{1,2},{2,1},{3,0},{4,7},{5,6},{6,5},{7,4},{8,11},{9,10},{10,... | collective-permute-start | bytes 98312 | tf_op jit(solution)/shard_map/ppermute | solution.py:270
  13.5 4.6 %collective-permute-start.7 = (f32[128,128]{1,0:T(8,128)S(1)}, f32[128,128]{1,0:T(8,128)S(1)}, u32[]{:S(2)}, u32[]{:S(2)}) collective-permute-start(f32[128,128]{1,0:T(8,128)S(1)} %bitcast.3), channel_id=1, source_target_pairs={{0,1},{1,0},{2,3},{3,2},{4,5},{5,4},{6,7},{7,6},{8,9},{9,8},{10,11... | collective-permute-start | bytes 196616 | tf_op jit(solution)/shard_map/ppermute | solution.py:251
  15.0 3.2 %collective-permute-start.6 = (f32[72,128]{1,0:T(8,128)S(1)}, f32[72,128]{1,0:T(8,128)S(1)}, u32[]{:S(2)}, u32[]{:S(2)}) collective-permute-start(f32[72,128]{1,0:T(8,128)S(1)} %get-tuple-element.32), channel_id=1, source_target_pairs={{0,2},{2,0},{4,6},{6,4},{8,10},{10,8},{12,14},{14,12},{16,18},{18,... | collective-permute-start | bytes 110600 | tf_op jit(solution)/shard_map/ppermute | solution.py:247

commit v22 on v21

--- a/solution.py
+++ b/solution.py
@@ -65,9 +65,23 @@
     return jnp.where(lower(tile.shape), turned(tile), tile)
 
 
+def split(array):
+    high = array.astype(jnp.bfloat16)
+    return high, (array - high.astype(F32)).astype(jnp.bfloat16)
+
+
+def product(one, other):
+    (one_high, one_low), (other_high, other_low) = split(one), split(other)
+
+    def dot(left, right):
+        return jnp.dot(left, right, preferred_element_type=F32)
+
+    return dot(one_high, other_high) + (dot(one_high, other_low) + dot(one_low, other_high))
+
+
 def narrowed(rows, slab_ref):
     width = slab_ref.shape[0] - 8
-    full = jnp.dot(rows[:, :width], slab_ref[:width, :], precision=lax.Precision.HIGHEST, preferred_element_type=F32)
+    full = product(rows[:, :width], slab_ref[:width, :])
     slab_labels, own_labels = slab_ref[width:width + 1, :], row_labels(rows)
     total = None
     for start in range(0, full.shape[1], LANES):
@@ -151,16 +165,20 @@
         send_ref[k - 1] = both[(k - 1) * count:k * count]
 
 
-def cross_kernel(twin_ref, two_ref, core_ref, diagonal_ref):
-    parts, half = diagonal_ref.shape[0] + 1, diagonal_ref.shape[1]
-    term = narrowed(twin_ref[...], two_ref)
+def diagonal_kernel(twin_ref, two_ref, send_ref):
+    parts, half = send_ref.shape[0] + 1, send_ref.shape[1]
+    term = narrowed(twin_ref[2 * half:, :], two_ref)
+    for k in range(1, parts):
+        send_ref[k - 1] = halved(term[2 * (k - 1) * half:2 * k * half])
+
+
+def core_kernel(twin_ref, two_ref, send_ref):
+    half = send_ref.shape[0] - 8
     width = two_ref.shape[0] - 8
     labels = two_ref[width:width + 1, :]
     tiles = [labels[:, start:start + LANES] for start in range(0, labels.shape[1], LANES)]
-    core_ref[:half, :] = halved(term[:2 * half])
-    core_ref[half:, :] = jnp.concatenate((tiles * 8)[:8], axis=0)
-    for k in range(1, parts):
-        diagonal_ref[k - 1] = halved(term[2 * k * half:2 * (k + 1) * half])
+    send_ref[:half, :] = halved(narrowed(twin_ref[:2 * half, :], two_ref))
+    send_ref[half:, :] = jnp.concatenate((tiles * 8)[:8], axis=0)
 
 
 def keep_kernel(rows_ref, two_ref, mix_ref, late_ref, *refs):
@@ -284,14 +302,14 @@
     late = moved(after(own, own_keep), (1, -1, 1, 3))
     rest = whole(row_count - count, LANES)
     mix_term, = call(sent_kernel, [rest], (rows, mix), 0)
-    core_send, diagonal_send = call(
-        cross_kernel, [whole(count // 2 + 8, LANES), whole(parts - 1, count // 2, LANES)],
-        (twin, after(two, mix_term, *own_in)), 0)
+    diagonal_send, = call(diagonal_kernel, [whole(parts - 1, count // 2, LANES)],
+                          (twin, after(two, mix_term, *own_in)), 0)
     diagonal_in = [crossed(diagonal_send[k - 1], k) for k in range(1, parts)]
     pair_send, = call(pair_kernel, [whole(parts - 1, count, LANES)], (rows, after(two, diagonal_send), late, mix_term),
                       0, 0, [pltpu.VMEM(rest.shape, F32)])
     pair_in = exchanged(pair_send)
-    core_in = moved(after(core_send, pair_send), (1, -1, 1, -1))
+    core_send, = call(core_kernel, [whole(count // 2 + 8, LANES)], (twin, after(two, pair_send)), 0)
+    core_in = moved(core_send, (1, -1, 1, -1))
     two_keep, third_keep, crossed_sum = call(
         keep_kernel, [whole(count, LANES)] * 3, (rows, after(two, pair_send), mix, late, *diagonal_in), 4 * one_product)
     pair_sum, = call(total_kernel, [whole(count, LANES)], tuple(pair_in), 0)

time: 19.3 us -> 19.1 us (0.990)
    ppermute x1, waiting for transfers between devices: 1.33 us -> 1.03 us  [crossed(): lax.ppermute(array, ('blk', 'red'), [(b * parts + r, c * parts + t) for (...]
    pallas_call x10 -> x11, Pallas kernels: 5.8 us -> 5.63 us  [call(): pl.pallas_call(kernel, out_shape=out_shape, in_specs=[OFFCHIP] * off + [O...]
where the time goes in v22:
time: 19.1 us; the launch traced here: 18.9 us
  starting transfers between devices  8.45 us (44%)
  Pallas kernels  5.63 us (29%)
  waiting for transfers between devices  4.74 us (25%)
    pallas_call x11, Pallas kernels, call(): pl.pallas_call(kernel, out_shape=out_shape, in_specs=[OFFCHIP] * off + [O...  5.63 us
    ppermute x5, starting transfers between devices, moved(): lax.ppermute(array, 'blk', [(i, (i + steps[i % 4]) % blocks) for i in ran...  5.19 us
    ppermute x2, starting transfers between devices, exchanged(): lax.ppermute(array[k - 1], 'red', [(i, (i + k) % parts) for i in range(pa...  3.01 us
    ppermute x5, waiting for transfers between devices, moved(): lax.ppermute(array, 'blk', [(i, (i + steps[i % 4]) % blocks) for i in ran...  2.62 us
    ppermute x2, waiting for transfers between devices, exchanged(): lax.ppermute(array[k - 1], 'red', [(i, (i + k) % parts) for i in range(pa...  1.09 us
    ppermute x1, waiting for transfers between devices, crossed(): lax.ppermute(array, ('blk', 'red'), [(b * parts + r, c * parts + t) for (...  1.03 us
  transfers between devices with their start and end apart: 8, of which 5 were waited for; matrix products, arithmetic and copies ran while one was open for 0% of the time, Pallas kernels for 18%

profile of v22, /device:TPU:0, one launch (start us, length us, event | category | flops | bytes accessed | tf_op | source)
XLA Modules:
  0.0 18.9 jit_solution(8652726229825928552)
XLA Ops:
  0.0 1.4 %shard_map.55.slab_ref.own_ref = f32[200,256]{1,0:T(8,128)S(1)} custom-call(f32[256,768]{1,0:T(8,128)} %amp_ref.1, s32[1,256]{1,0:T(1,128)} %ij_ref.1, s32[1,768]{1,0:T(1,128)} %cd_ref.3), custom_call_target="tpu_custom_call" | custom-call | flops 786432 | tf_op jit(solution)/shard_map/pallas_call | solution.py:245
  1.4 3.0 %collective-permute-start = (f32[200,256]{1,0:T(8,128)S(1)}, f32[200,256]{1,0:T(8,128)S(1)}, u32[]{:S(2)}, u32[]{:S(2)}) collective-permute-start(f32[200,256]{1,0:T(8,128)S(1)} %shard_map.55.slab_ref.own_ref), channel_id=1, source_target_pairs={{0,4},{2,6},{4,8},{6,10},{8,12},{10,14},{12,16},{14,18},{16,20},{1... | collective-permute-start | bytes 614408 | tf_op jit(solution)/shard_map/ppermute | solution.py:265
  4.4 0.0 collective-permute-start.2
  4.4 1.3 %shard_map.57.rows_ref = f32[256,256]{1,0:T(8,128)S(1)} custom-call(f32[256,768]{1,0:T(8,128)} %v_ref, s32[1,256]{1,0:T(1,128)} %ab_ref.1, s32[1,768]{1,0:T(1,128)} %cd_ref.3), custom_call_target="tpu_custom_call" | custom-call | tf_op jit(solution)/shard_map/pallas_call | solution.py:245
  5.7 1.8 %collective-permute-start.1 = (f32[256,256]{1,0:T(8,128)S(1)}, f32[256,256]{1,0:T(8,128)S(1)}, u32[]{:S(2)}, u32[]{:S(2)}) collective-permute-start(f32[256,256]{1,0:T(8,128)S(1)} %shard_map.57.rows_ref), channel_id=1, source_target_pairs={{0,2},{2,0},{4,6},{6,4},{8,10},{10,8},{12,14},{14,12},{16,18},{18,... | collective-permute-start | bytes 786440 | tf_op jit(solution)/shard_map/ppermute | solution.py:265
  7.4 0.3 %shard_map.58 = (f32[128,128]{1,0:T(8,128)S(1)}, f32[1,64,128]{2,1,0:T(8,128)S(1)}) custom-call(f32[256,256]{1,0:T(8,128)S(1)} %shard_map.57.rows_ref, f32[200,256]{1,0:T(8,128)S(1)} %shard_map.55.slab_ref.own_ref), custom_call_target="tpu_custom_call" | custom-call | flops 9663676416 | tf_op jit(solution)/shard_map/pallas_call | solution.py:245
  7.8 0.1 collective-permute-start.4
  7.8 1.6 %collective-permute-start.3 = (f32[64,128]{1,0:T(8,128)S(1)}, f32[64,128]{1,0:T(8,128)S(1)}, u32[]{:S(2)}, u32[]{:S(2)}) collective-permute-start(f32[64,128]{1,0:T(8,128)S(1)} %bitcast.5), channel_id=1, source_target_pairs={{0,1},{1,0},{2,3},{3,2},{4,5},{5,4},{6,7},{7,6},{8,9},{9,8},{10,11... | collective-permute-start | bytes 98312 | tf_op jit(solution)/shard_map/ppermute | solution.py:269
  9.4 1.9 %collective-permute-done.2.slab_ref.mix_ref = f32[200,256]{1,0:T(8,128)S(1)} collective-permute-done((f32[200,256]{1,0:T(8,128)S(1)}, f32[200,256]{1,0:T(8,128)S(1)}, u32[]{:S(2)}, u32[]{:S(2)}) %collective-permute-start.2) | collective-permute-done | bytes 204832 | tf_op jit(solution)/shard_map/ppermute | solution.py:265
  11.4 0.3 %shard_map.59.mix_term = f32[128,128]{1,0:T(8,128)S(1)} custom-call(f32[256,256]{1,0:T(8,128)S(1)} %shard_map.57.rows_ref, f32[200,256]{1,0:T(8,128)S(1)} %collective-permute-done.2.slab_ref.mix_ref), custom_call_target="tpu_custom_call" | custom-call | tf_op jit(solution)/shard_map/pallas_call | solution.py:245
  11.7 0.2 collective-permute-done.3.refs_0_
  11.8 0.7 %collective-permute-done.two_ref = f32[200,256]{1,0:T(8,128)S(1)} collective-permute-done((f32[200,256]{1,0:T(8,128)S(1)}, f32[200,256]{1,0:T(8,128)S(1)}, u32[]{:S(2)}, u32[]{:S(2)}) %collective-permute-start) | collective-permute-done | bytes 204832 | tf_op jit(solution)/shard_map/ppermute | solution.py:265
  12.5 0.0 collective-permute-done.1.twin_ref
  12.5 0.3 %shard_map.60 = f32[1,64,128]{2,1,0:T(8,128)S(1)} custom-call(f32[256,256]{1,0:T(8,128)S(1)} %collective-permute-done.1.twin_ref, f32[200,256]{1,0:T(8,128)S(1)} %collective-permute-done.two_ref), custom_call_target="tpu_custom_call" | custom-call | tf_op jit(solution)/shard_map/pallas_call | solution.py:245
  12.8 0.2 %collective-permute-start.5 = (f32[64,128]{1,0:T(8,128)S(1)}, f32[64,128]{1,0:T(8,128)S(1)}, u32[]{:S(2)}, u32[]{:S(2)}) collective-permute-start(f32[64,128]{1,0:T(8,128)S(1)} %bitcast.4), channel_id=1, source_target_pairs={{0,3},{1,2},{2,1},{3,0},{4,7},{5,6},{6,5},{7,4},{8,11},{9,10},{10,... | collective-permute-start | bytes 98312 | tf_op jit(solution)/shard_map/ppermute | solution.py:288
  13.0 0.3 %shard_map.61 = f32[1,128,128]{2,1,0:T(8,128)S(1)} custom-call(f32[256,256]{1,0:T(8,128)S(1)} %shard_map.57.rows_ref, f32[200,256]{1,0:T(8,128)S(1)} %collective-permute-done.two_ref, f32[200,256]{1,0:T(8,128)S(1)} %collective-permute-done.4.late_ref, f32[128,128]{1,0:T(8,128)S(1)} %shard_map.59.mix_term), custom_call_target="tpu_custom_call" | custom-call | tf_op jit(solution)/shard_map/pallas_call | solution.py:245
  13.3 1.4 %collective-permute-start.7 = (f32[128,128]{1,0:T(8,128)S(1)}, f32[128,128]{1,0:T(8,128)S(1)}, u32[]{:S(2)}, u32[]{:S(2)}) collective-permute-start(f32[128,128]{1,0:T(8,128)S(1)} %bitcast.3), channel_id=1, source_target_pairs={{0,1},{1,0},{2,3},{3,2},{4,5},{5,4},{6,7},{7,6},{8,9},{9,8},{10,11... | collective-permute-start | bytes 196616 | tf_op jit(solution)/shard_map/ppermute | solution.py:269
  14.8 0.3 %shard_map.63 = f32[72,128]{1,0:T(8,128)S(1)} custom-call(f32[256,256]{1,0:T(8,128)S(1)} %collective-permute-done.1.twin_ref, f32[200,256]{1,0:T(8,128)S(1)} %collective-permute-done.two_ref), custom_call_target="tpu_custom_call" | custom-call | tf_op jit(solution)/shard_map/pallas_call | solution.py:245
  15.1 0.4 %collective-permute-start.6 = (f32[72,128]{1,0:T(8,128)S(1)}, f32[72,128]{1,0:T(8,128)S(1)}, u32[]{:S(2)}, u32[]{:S(2)}) collective-permute-start(f32[72,128]{1,0:T(8,128)S(1)} %shard_map.63), channel_id=1, source_target_pairs={{0,2},{2,0},{4,6},{6,4},{8,10},{10,8},{12,14},{14,12},{16,18},{18,... | collective-permute-start | bytes 110600 | tf_op jit(solution)/shard_map/ppermute | solution.py:265
  15.4 1.0 %collective-permute-done.5.refs_0_ = f32[64,128]{1,0:T(8,128)S(1)} collective-permute-done((f32[64,128]{1,0:T(8,128)S(1)}, f32[64,128]{1,0:T(8,128)S(1)}, u32[]{:S(2)}, u32[]{:S(2)}) %collective-permute-start.5) | collective-permute-done | bytes 32800 | tf_op jit(solution)/shard_map/ppermute | solution.py:288
  16.5 0.6 %shard_map.62 = (f32[128,128]{1,0:T(8,128)S(1)}, f32[128,128]{1,0:T(8,128)S(1)}, f32[128,128]{1,0:T(8,128)S(1)}) custom-call(f32[256,256]{1,0:T(8,128)S(1)} %shard_map.57.rows_ref, f32[200,256]{1,0:T(8,128)S(1)} %collective-permute-done.two_ref, f32[200,256]{1,0:T(8,128)S(1)} %collective-permute-done.2.slab_ref.mix_ref, ...), custom_call_target="tpu_custom_call" | custom-call | flops 603979776 | tf_op jit(solution)/shard_map/pallas_call | solution.py:245
  17.0 0.9 %collective-permute-done.7.refs_0_ = f32[128,128]{1,0:T(8,128)S(1)} collective-permute-done((f32[128,128]{1,0:T(8,128)S(1)}, f32[128,128]{1,0:T(8,128)S(1)}, u32[]{:S(2)}, u32[]{:S(2)}) %collective-permute-start.7) | collective-permute-done | bytes 65568 | tf_op jit(solution)/shard_map/ppermute | solution.py:269
  18.0 0.0 collective-permute-done.6.core_ref
  18.0 0.9 %shard_map.65 = f32[4,128,256]{2,1,0:T(8,128)} custom-call(f32[256,256]{1,0:T(8,128)S(1)} %shard_map.57.rows_ref, f32[128,128]{1,0:T(8,128)S(1)} %get-tuple-element.17.own_keep, f32[128,128]{1,0:T(8,128)S(1)} %get-tuple-element.24.two_keep, f32[128,128]{1,0:T(8,128)S(1)} %get-tuple-element.25.third_keep, f32[128,128]{1,0:T(8,128)S(1)} %get-tuple-element.26.crossed_ref, ...), custom_call_target="tpu_custom_call" | custom-call | tf_op jit(solution)/shard_map/pallas_call | solution.py:245
  (3 shorter events, 0.0 us)
Async XLA Ops:
  1.4 11.1 %collective-permute-start = (f32[200,256]{1,0:T(8,128)S(1)}, f32[200,256]{1,0:T(8,128)S(1)}, u32[]{:S(2)}, u32[]{:S(2)}) collective-permute-start(f32[200,256]{1,0:T(8,128)S(1)} %shard_map.55.slab_ref.own_ref), channel_id=1, source_target_pairs={{0,4},{2,6},{4,8},{6,10},{8,12},{10,14},{12,16},{14,18},{16,20},{1... | collective-permute-start | bytes 614408 | tf_op jit(solution)/shard_map/ppermute | solution.py:265
  4.4 7.0 %collective-permute-start.2 = (f32[200,256]{1,0:T(8,128)S(1)}, f32[200,256]{1,0:T(8,128)S(1)}, u32[]{:S(2)}, u32[]{:S(2)}) collective-permute-start(f32[200,256]{1,0:T(8,128)S(1)} %shard_map.55.slab_ref.own_ref), channel_id=1, source_target_pairs={{0,2},{2,8},{4,6},{6,4},{8,10},{10,16},{12,14},{14,12},{16,18},{18... | collective-permute-start | bytes 614408 | tf_op jit(solution)/shard_map/ppermute | solution.py:265
  5.7 6.8 %collective-permute-start.1 = (f32[256,256]{1,0:T(8,128)S(1)}, f32[256,256]{1,0:T(8,128)S(1)}, u32[]{:S(2)}, u32[]{:S(2)}) collective-permute-start(f32[256,256]{1,0:T(8,128)S(1)} %shard_map.57.rows_ref), channel_id=1, source_target_pairs={{0,2},{2,0},{4,6},{6,4},{8,10},{10,8},{12,14},{14,12},{16,18},{18,... | collective-permute-start | bytes 786440 | tf_op jit(solution)/shard_map/ppermute | solution.py:265
  7.8 5.3 %collective-permute-start.4 = (f32[200,256]{1,0:T(8,128)S(1)}, f32[200,256]{1,0:T(8,128)S(1)}, u32[]{:S(2)}, u32[]{:S(2)}) collective-permute-start(f32[200,256]{1,0:T(8,128)S(1)} %shard_map.55.slab_ref.own_ref), channel_id=1, source_target_pairs={{0,2},{2,0},{4,6},{6,12},{8,10},{10,8},{12,14},{14,20},{16,18},{18... | collective-permute-start | bytes 614408 | tf_op jit(solution)/shard_map/ppermute | solution.py:265
  7.8 4.0 %collective-permute-start.3 = (f32[64,128]{1,0:T(8,128)S(1)}, f32[64,128]{1,0:T(8,128)S(1)}, u32[]{:S(2)}, u32[]{:S(2)}) collective-permute-start(f32[64,128]{1,0:T(8,128)S(1)} %bitcast.5), channel_id=1, source_target_pairs={{0,1},{1,0},{2,3},{3,2},{4,5},{5,4},{6,7},{7,6},{8,9},{9,8},{10,11... | collective-permute-start | bytes 98312 | tf_op jit(solution)/shard_map/ppermute | solution.py:269
  12.8 3.7 %collective-permute-start.5 = (f32[64,128]{1,0:T(8,128)S(1)}, f32[64,128]{1,0:T(8,128)S(1)}, u32[]{:S(2)}, u32[]{:S(2)}) collective-permute-start(f32[64,128]{1,0:T(8,128)S(1)} %bitcast.4), channel_id=1, source_target_pairs={{0,3},{1,2},{2,1},{3,0},{4,7},{5,6},{6,5},{7,4},{8,11},{9,10},{10,... | collective-permute-start | bytes 98312 | tf_op jit(solution)/shard_map/ppermute | solution.py:288
  13.3 4.6 %collective-permute-start.7 = (f32[128,128]{1,0:T(8,128)S(1)}, f32[128,128]{1,0:T(8,128)S(1)}, u32[]{:S(2)}, u32[]{:S(2)}) collective-permute-start(f32[128,128]{1,0:T(8,128)S(1)} %bitcast.3), channel_id=1, source_target_pairs={{0,1},{1,0},{2,3},{3,2},{4,5},{5,4},{6,7},{7,6},{8,9},{9,8},{10,11... | collective-permute-start | bytes 196616 | tf_op jit(solution)/shard_map/ppermute | solution.py:269
  15.1 2.9 %collective-permute-start.6 = (f32[72,128]{1,0:T(8,128)S(1)}, f32[72,128]{1,0:T(8,128)S(1)}, u32[]{:S(2)}, u32[]{:S(2)}) collective-permute-start(f32[72,128]{1,0:T(8,128)S(1)} %shard_map.63), channel_id=1, source_target_pairs={{0,2},{2,0},{4,6},{6,4},{8,10},{10,8},{12,14},{14,12},{16,18},{18,... | collective-permute-start | bytes 110600 | tf_op jit(solution)/shard_map/ppermute | solution.py:265

commit v23 on v22

--- a/solution.py
+++ b/solution.py
@@ -152,7 +152,17 @@
     out_ref[...] = narrowed(rows_ref[count:, :], slab_ref)
 
 
-def pair_kernel(rows_ref, two_ref, late_ref, mix_term, send_ref, third):
+def both_kernel(rows_ref, twin_ref, two_ref, out_ref, send_ref):
+    parts, half = send_ref.shape[0] + 1, send_ref.shape[1]
+    sent = out_ref.shape[0]
+    rows = jnp.concatenate([twin_ref[2 * half:, :], rows_ref[2 * half:, :]], axis=0)
+    term = narrowed(rows, two_ref)
+    for k in range(1, parts):
+        send_ref[k - 1] = halved(term[2 * (k - 1) * half:2 * k * half])
+    out_ref[...] = term[sent:]
+
+
+def pair_kernel(rows_ref, late_ref, two_term, mix_term, send_ref, third):
     parts, count = send_ref.shape[0] + 1, send_ref.shape[1]
     third[...] = mix_term[...]
 
@@ -160,16 +170,9 @@
     def _():
         third[...] = narrowed(rows_ref[count:, :], late_ref)
 
-    both = beside(narrowed(rows_ref[count:, :], two_ref), third[...])
+    both = beside(two_term[...], third[...])
     for k in range(1, parts):
         send_ref[k - 1] = both[(k - 1) * count:k * count]
-
-
-def diagonal_kernel(twin_ref, two_ref, send_ref):
-    parts, half = send_ref.shape[0] + 1, send_ref.shape[1]
-    term = narrowed(twin_ref[2 * half:, :], two_ref)
-    for k in range(1, parts):
-        send_ref[k - 1] = halved(term[2 * (k - 1) * half:2 * k * half])
 
 
 def core_kernel(twin_ref, two_ref, send_ref):
@@ -302,10 +305,11 @@
     late = moved(after(own, own_keep), (1, -1, 1, 3))
     rest = whole(row_count - count, LANES)
     mix_term, = call(sent_kernel, [rest], (rows, mix), 0)
-    diagonal_send, = call(diagonal_kernel, [whole(parts - 1, count // 2, LANES)],
-                          (twin, after(two, mix_term, *own_in)), 0)
+    two_term, diagonal_send = call(
+        both_kernel, [rest, whole(parts - 1, count // 2, LANES)],
+        (rows, twin, after(two, mix_term, *own_in)), 0)
     diagonal_in = [crossed(diagonal_send[k - 1], k) for k in range(1, parts)]
-    pair_send, = call(pair_kernel, [whole(parts - 1, count, LANES)], (rows, after(two, diagonal_send), late, mix_term),
+    pair_send, = call(pair_kernel, [whole(parts - 1, count, LANES)], (rows, late, two_term, mix_term),
                       0, 0, [pltpu.VMEM(rest.shape, F32)])
     pair_in = exchanged(pair_send)
     core_send, = call(core_kernel, [whole(count // 2 + 8, LANES)], (twin, after(two, pair_send)), 0)

time: 19.1 us -> 18.9 us (0.990)
  Pallas kernels: 5.63 us -> 5.42 us
    ppermute x2, waiting for transfers between devices: 1.09 us -> 0.81 us  [exchanged(): lax.ppermute(array[k - 1], 'red', [(i, (i + k) % parts) for i in range(pa...]
    ppermute x1, waiting for transfers between devices: 1.03 us -> 1.31 us  [crossed(): lax.ppermute(array, ('blk', 'red'), [(b * parts + r, c * parts + t) for (...]
    pallas_call x11, Pallas kernels: 5.63 us -> 5.42 us  [call(): pl.pallas_call(kernel, out_shape=out_shape, in_specs=[OFFCHIP] * off + [O...]
  transfers between devices with their start and end apart: 8 -> 8, of which waited for: 5 -> 5; matrix products, arithmetic and copies ran while one was open for 0% -> 0% of each run, Pallas kernels for 18% -> 17%
where the time goes in v23:
time: 18.9 us; the launch traced here: 18.7 us
  starting transfers between devices  8.45 us (45%)
  Pallas kernels  5.42 us (29%)
  waiting for transfers between devices  4.74 us (25%)
    pallas_call x11, Pallas kernels, call(): pl.pallas_call(kernel, out_shape=out_shape, in_specs=[OFFCHIP] * off + [O...  5.42 us
    ppermute x5, starting transfers between devices, moved(): lax.ppermute(array, 'blk', [(i, (i + steps[i % 4]) % blocks) for i in ran...  5.19 us
    ppermute x2, starting transfers between devices, exchanged(): lax.ppermute(array[k - 1], 'red', [(i, (i + k) % parts) for i in range(pa...  3.02 us
    ppermute x5, waiting for transfers between devices, moved(): lax.ppermute(array, 'blk', [(i, (i + steps[i % 4]) % blocks) for i in ran...  2.62 us
    ppermute x1, waiting for transfers between devices, crossed(): lax.ppermute(array, ('blk', 'red'), [(b * parts + r, c * parts + t) for (...  1.31 us
    ppermute x2, waiting for transfers between devices, exchanged(): lax.ppermute(array[k - 1], 'red', [(i, (i + k) % parts) for i in range(pa...  0.81 us
  transfers between devices with their start and end apart: 8, of which 5 were waited for; matrix products, arithmetic and copies ran while one was open for 0% of the time, Pallas kernels for 17%

profile of v23, /device:TPU:0, one launch (start us, length us, event | category | flops | bytes accessed | tf_op | source)
XLA Modules:
  0.0 18.7 jit_solution(14805463079708884289)
XLA Ops:
  0.0 1.4 %shard_map.55.slab_ref.own_ref = f32[200,256]{1,0:T(8,128)S(1)} custom-call(f32[256,768]{1,0:T(8,128)} %amp_ref.1, s32[1,256]{1,0:T(1,128)} %ij_ref.1, s32[1,768]{1,0:T(1,128)} %cd_ref.3), custom_call_target="tpu_custom_call" | custom-call | flops 786432 | tf_op jit(solution)/shard_map/pallas_call | solution.py:248
  1.4 3.0 %collective-permute-start = (f32[200,256]{1,0:T(8,128)S(1)}, f32[200,256]{1,0:T(8,128)S(1)}, u32[]{:S(2)}, u32[]{:S(2)}) collective-permute-start(f32[200,256]{1,0:T(8,128)S(1)} %shard_map.55.slab_ref.own_ref), channel_id=1, source_target_pairs={{0,4},{2,6},{4,8},{6,10},{8,12},{10,14},{12,16},{14,18},{16,20},{1... | collective-permute-start | bytes 614408 | tf_op jit(solution)/shard_map/ppermute | solution.py:268
  4.4 0.0 collective-permute-start.3
  4.4 1.3 %shard_map.57.rows_ref = f32[256,256]{1,0:T(8,128)S(1)} custom-call(f32[256,768]{1,0:T(8,128)} %v_ref, s32[1,256]{1,0:T(1,128)} %ab_ref.1, s32[1,768]{1,0:T(1,128)} %cd_ref.3), custom_call_target="tpu_custom_call" | custom-call | tf_op jit(solution)/shard_map/pallas_call | solution.py:248
  5.7 1.8 %collective-permute-start.2 = (f32[256,256]{1,0:T(8,128)S(1)}, f32[256,256]{1,0:T(8,128)S(1)}, u32[]{:S(2)}, u32[]{:S(2)}) collective-permute-start(f32[256,256]{1,0:T(8,128)S(1)} %shard_map.57.rows_ref), channel_id=1, source_target_pairs={{0,2},{2,0},{4,6},{6,4},{8,10},{10,8},{12,14},{14,12},{16,18},{18,... | collective-permute-start | bytes 786440 | tf_op jit(solution)/shard_map/ppermute | solution.py:268
  7.4 0.3 %shard_map.58 = (f32[128,128]{1,0:T(8,128)S(1)}, f32[1,64,128]{2,1,0:T(8,128)S(1)}) custom-call(f32[256,256]{1,0:T(8,128)S(1)} %shard_map.57.rows_ref, f32[200,256]{1,0:T(8,128)S(1)} %shard_map.55.slab_ref.own_ref), custom_call_target="tpu_custom_call" | custom-call | flops 9663676416 | tf_op jit(solution)/shard_map/pallas_call | solution.py:248
  7.8 0.1 collective-permute-start.1
  7.8 1.6 %collective-permute-start.4 = (f32[64,128]{1,0:T(8,128)S(1)}, f32[64,128]{1,0:T(8,128)S(1)}, u32[]{:S(2)}, u32[]{:S(2)}) collective-permute-start(f32[64,128]{1,0:T(8,128)S(1)} %bitcast.5), channel_id=1, source_target_pairs={{0,1},{1,0},{2,3},{3,2},{4,5},{5,4},{6,7},{7,6},{8,9},{9,8},{10,11... | collective-permute-start | bytes 98312 | tf_op jit(solution)/shard_map/ppermute | solution.py:272
  9.4 1.9 %collective-permute-done.3.slab_ref.mix_ref = f32[200,256]{1,0:T(8,128)S(1)} collective-permute-done((f32[200,256]{1,0:T(8,128)S(1)}, f32[200,256]{1,0:T(8,128)S(1)}, u32[]{:S(2)}, u32[]{:S(2)}) %collective-permute-start.3) | collective-permute-done | bytes 204832 | tf_op jit(solution)/shard_map/ppermute | solution.py:268
  11.4 0.3 %shard_map.59.mix_term = f32[128,128]{1,0:T(8,128)S(1)} custom-call(f32[256,256]{1,0:T(8,128)S(1)} %shard_map.57.rows_ref, f32[200,256]{1,0:T(8,128)S(1)} %collective-permute-done.3.slab_ref.mix_ref), custom_call_target="tpu_custom_call" | custom-call | tf_op jit(solution)/shard_map/pallas_call | solution.py:248
  11.7 0.2 collective-permute-done.4.refs_0_
  11.8 0.7 %collective-permute-done.two_ref = f32[200,256]{1,0:T(8,128)S(1)} collective-permute-done((f32[200,256]{1,0:T(8,128)S(1)}, f32[200,256]{1,0:T(8,128)S(1)}, u32[]{:S(2)}, u32[]{:S(2)}) %collective-permute-start) | collective-permute-done | bytes 204832 | tf_op jit(solution)/shard_map/ppermute | solution.py:268
  12.5 0.0 collective-permute-done.2.twin_ref
  12.5 0.3 %shard_map.60 = (f32[128,128]{1,0:T(8,128)S(1)}, f32[1,64,128]{2,1,0:T(8,128)S(1)}) custom-call(f32[256,256]{1,0:T(8,128)S(1)} %shard_map.57.rows_ref, f32[256,256]{1,0:T(8,128)S(1)} %collective-permute-done.2.twin_ref, f32[200,256]{1,0:T(8,128)S(1)} %collective-permute-done.two_ref), custom_call_target="tpu_custom_call" | custom-call | tf_op jit(solution)/shard_map/pallas_call | solution.py:248
  12.9 0.2 %collective-permute-start.5 = (f32[64,128]{1,0:T(8,128)S(1)}, f32[64,128]{1,0:T(8,128)S(1)}, u32[]{:S(2)}, u32[]{:S(2)}) collective-permute-start(f32[64,128]{1,0:T(8,128)S(1)} %bitcast.4), channel_id=1, source_target_pairs={{0,3},{1,2},{2,1},{3,0},{4,7},{5,6},{6,5},{7,4},{8,11},{9,10},{10,... | collective-permute-start | bytes 98312 | tf_op jit(solution)/shard_map/ppermute | solution.py:291
  13.1 0.0 collective-permute-done.1.late_ref
  13.1 1.4 %collective-permute-start.7 = (f32[128,128]{1,0:T(8,128)S(1)}, f32[128,128]{1,0:T(8,128)S(1)}, u32[]{:S(2)}, u32[]{:S(2)}) collective-permute-start(f32[128,128]{1,0:T(8,128)S(1)} %bitcast.3), channel_id=1, source_target_pairs={{0,1},{1,0},{2,3},{3,2},{4,5},{5,4},{6,7},{7,6},{8,9},{9,8},{10,11... | collective-permute-start | bytes 196616 | tf_op jit(solution)/shard_map/ppermute | solution.py:272
  14.6 0.3 %shard_map.63 = f32[72,128]{1,0:T(8,128)S(1)} custom-call(f32[256,256]{1,0:T(8,128)S(1)} %collective-permute-done.2.twin_ref, f32[200,256]{1,0:T(8,128)S(1)} %collective-permute-done.two_ref), custom_call_target="tpu_custom_call" | custom-call | tf_op jit(solution)/shard_map/pallas_call | solution.py:248
  14.8 0.4 %collective-permute-start.6 = (f32[72,128]{1,0:T(8,128)S(1)}, f32[72,128]{1,0:T(8,128)S(1)}, u32[]{:S(2)}, u32[]{:S(2)}) collective-permute-start(f32[72,128]{1,0:T(8,128)S(1)} %shard_map.63), channel_id=1, source_target_pairs={{0,2},{2,0},{4,6},{6,4},{8,10},{10,8},{12,14},{14,12},{16,18},{18,... | collective-permute-start | bytes 110600 | tf_op jit(solution)/shard_map/ppermute | solution.py:268
  15.2 1.3 %collective-permute-done.5.refs_0_ = f32[64,128]{1,0:T(8,128)S(1)} collective-permute-done((f32[64,128]{1,0:T(8,128)S(1)}, f32[64,128]{1,0:T(8,128)S(1)}, u32[]{:S(2)}, u32[]{:S(2)}) %collective-permute-start.5) | collective-permute-done | bytes 32800 | tf_op jit(solution)/shard_map/ppermute | solution.py:291
  16.5 0.6 %shard_map.62 = (f32[128,128]{1,0:T(8,128)S(1)}, f32[128,128]{1,0:T(8,128)S(1)}, f32[128,128]{1,0:T(8,128)S(1)}) custom-call(f32[256,256]{1,0:T(8,128)S(1)} %shard_map.57.rows_ref, f32[200,256]{1,0:T(8,128)S(1)} %collective-permute-done.two_ref, f32[200,256]{1,0:T(8,128)S(1)} %collective-permute-done.3.slab_ref.mix_ref, ...), custom_call_target="tpu_custom_call" | custom-call | flops 603979776 | tf_op jit(solution)/shard_map/pallas_call | solution.py:248
  17.1 0.6 %collective-permute-done.7.refs_0_ = f32[128,128]{1,0:T(8,128)S(1)} collective-permute-done((f32[128,128]{1,0:T(8,128)S(1)}, f32[128,128]{1,0:T(8,128)S(1)}, u32[]{:S(2)}, u32[]{:S(2)}) %collective-permute-start.7) | collective-permute-done | bytes 65568 | tf_op jit(solution)/shard_map/ppermute | solution.py:272
  17.8 0.0 collective-permute-done.6.core_ref
  17.8 0.9 %shard_map.65 = f32[4,128,256]{2,1,0:T(8,128)} custom-call(f32[256,256]{1,0:T(8,128)S(1)} %shard_map.57.rows_ref, f32[128,128]{1,0:T(8,128)S(1)} %get-tuple-element.18.own_keep, f32[128,128]{1,0:T(8,128)S(1)} %get-tuple-element.26.two_keep, f32[128,128]{1,0:T(8,128)S(1)} %get-tuple-element.27.third_keep, f32[128,128]{1,0:T(8,128)S(1)} %get-tuple-element.28.crossed_ref, ...), custom_call_target="tpu_custom_call" | custom-call | tf_op jit(solution)/shard_map/pallas_call | solution.py:248
  (3 shorter events, 0.0 us)
Async XLA Ops:
  1.4 11.1 %collective-permute-start = (f32[200,256]{1,0:T(8,128)S(1)}, f32[200,256]{1,0:T(8,128)S(1)}, u32[]{:S(2)}, u32[]{:S(2)}) collective-permute-start(f32[200,256]{1,0:T(8,128)S(1)} %shard_map.55.slab_ref.own_ref), channel_id=1, source_target_pairs={{0,4},{2,6},{4,8},{6,10},{8,12},{10,14},{12,16},{14,18},{16,20},{1... | collective-permute-start | bytes 614408 | tf_op jit(solution)/shard_map/ppermute | solution.py:268
  4.4 7.0 %collective-permute-start.3 = (f32[200,256]{1,0:T(8,128)S(1)}, f32[200,256]{1,0:T(8,128)S(1)}, u32[]{:S(2)}, u32[]{:S(2)}) collective-permute-start(f32[200,256]{1,0:T(8,128)S(1)} %shard_map.55.slab_ref.own_ref), channel_id=1, source_target_pairs={{0,2},{2,8},{4,6},{6,4},{8,10},{10,16},{12,14},{14,12},{16,18},{18... | collective-permute-start | bytes 614408 | tf_op jit(solution)/shard_map/ppermute | solution.py:268
  5.7 6.8 %collective-permute-start.2 = (f32[256,256]{1,0:T(8,128)S(1)}, f32[256,256]{1,0:T(8,128)S(1)}, u32[]{:S(2)}, u32[]{:S(2)}) collective-permute-start(f32[256,256]{1,0:T(8,128)S(1)} %shard_map.57.rows_ref), channel_id=1, source_target_pairs={{0,2},{2,0},{4,6},{6,4},{8,10},{10,8},{12,14},{14,12},{16,18},{18,... | collective-permute-start | bytes 786440 | tf_op jit(solution)/shard_map/ppermute | solution.py:268
  7.8 5.3 %collective-permute-start.1 = (f32[200,256]{1,0:T(8,128)S(1)}, f32[200,256]{1,0:T(8,128)S(1)}, u32[]{:S(2)}, u32[]{:S(2)}) collective-permute-start(f32[200,256]{1,0:T(8,128)S(1)} %shard_map.55.slab_ref.own_ref), channel_id=1, source_target_pairs={{0,2},{2,0},{4,6},{6,12},{8,10},{10,8},{12,14},{14,20},{16,18},{18... | collective-permute-start | bytes 614408 | tf_op jit(solution)/shard_map/ppermute | solution.py:268
  7.8 4.0 %collective-permute-start.4 = (f32[64,128]{1,0:T(8,128)S(1)}, f32[64,128]{1,0:T(8,128)S(1)}, u32[]{:S(2)}, u32[]{:S(2)}) collective-permute-start(f32[64,128]{1,0:T(8,128)S(1)} %bitcast.5), channel_id=1, source_target_pairs={{0,1},{1,0},{2,3},{3,2},{4,5},{5,4},{6,7},{7,6},{8,9},{9,8},{10,11... | collective-permute-start | bytes 98312 | tf_op jit(solution)/shard_map/ppermute | solution.py:272
  12.9 3.7 %collective-permute-start.5 = (f32[64,128]{1,0:T(8,128)S(1)}, f32[64,128]{1,0:T(8,128)S(1)}, u32[]{:S(2)}, u32[]{:S(2)}) collective-permute-start(f32[64,128]{1,0:T(8,128)S(1)} %bitcast.4), channel_id=1, source_target_pairs={{0,3},{1,2},{2,1},{3,0},{4,7},{5,6},{6,5},{7,4},{8,11},{9,10},{10,... | collective-permute-start | bytes 98312 | tf_op jit(solution)/shard_map/ppermute | solution.py:291
  13.1 4.6 %collective-permute-start.7 = (f32[128,128]{1,0:T(8,128)S(1)}, f32[128,128]{1,0:T(8,128)S(1)}, u32[]{:S(2)}, u32[]{:S(2)}) collective-permute-start(f32[128,128]{1,0:T(8,128)S(1)} %bitcast.3), channel_id=1, source_target_pairs={{0,1},{1,0},{2,3},{3,2},{4,5},{5,4},{6,7},{7,6},{8,9},{9,8},{10,11... | collective-permute-start | bytes 196616 | tf_op jit(solution)/shard_map/ppermute | solution.py:272
  14.8 2.9 %collective-permute-start.6 = (f32[72,128]{1,0:T(8,128)S(1)}, f32[72,128]{1,0:T(8,128)S(1)}, u32[]{:S(2)}, u32[]{:S(2)}) collective-permute-start(f32[72,128]{1,0:T(8,128)S(1)} %shard_map.63), channel_id=1, source_target_pairs={{0,2},{2,0},{4,6},{6,4},{8,10},{10,8},{12,14},{14,12},{16,18},{18,... | collective-permute-start | bytes 110600 | tf_op jit(solution)/shard_map/ppermute | solution.py:268

commit v24 on v23

--- a/solution.py
+++ b/solution.py
@@ -184,11 +184,8 @@
     send_ref[half:, :] = jnp.concatenate((tiles * 8)[:8], axis=0)
 
 
-def keep_kernel(rows_ref, two_ref, mix_ref, late_ref, *refs):
-    diagonal_in, (two_out, third_out, crossed_out) = refs[:-3], refs[-3:]
+def keep_kernel(rows_ref, two_ref, mix_ref, late_ref, two_out, third_out):
     count = two_out.shape[0]
-    terms = [unhalved(ref[...]) for ref in diagonal_in]
-    crossed_out[...] = sum(terms[1:], terms[0])
     two_out[...] = narrowed(rows_ref[:count, :], two_ref)
 
     @pl.when(second())
@@ -200,55 +197,69 @@
         third_out[...] = narrowed(rows_ref[:count, :], mix_ref)
 
 
+def halves_kernel(*refs):
+    terms, out_ref = [unhalved(ref[...]) for ref in refs[:-1]], refs[-1]
+    out_ref[...] = sum(terms[1:], terms[0])
+
+
+def tiles_of(ref, row, tiles):
+    return [ref[row:row + 1, k * LANES:(k + 1) * LANES] for k in range(tiles)]
+
+
+def stored(place, plane, term, rows, labels, out_ref, out, sems):
+    for k, label in enumerate(labels):
+        out[plane, :, k * LANES:(k + 1) * LANES] = jnp.where(rows == label, term, 0.0)
+    copy = pltpu.make_async_copy(out.at[plane], out_ref.at[place], sems.at[plane])
+    copy.start()
+    return copy
+
+
+def early_kernel(rows_ref, own_keep, own_labels, crossed_ref, core_ref, *refs):
+    own_in, (out_ref, out, sems) = refs[:-3], refs[-3:]
+    count = own_keep.shape[0]
+    tiles = out.shape[2] // LANES
+    rows = row_labels(rows_ref[:count, :])
+    own = sum([unhalved(ref[...]) for ref in own_in], own_keep[...])
+    first = stored(0, 0, own, rows, tiles_of(own_labels, 0, tiles), out_ref, out, sems)
+    crossed = crossed_ref[...] + unhalved(core_ref[:count // 2, :])
+    labels = [core_ref[count // 2 + k:count // 2 + k + 1, :] for k in range(tiles)]
+    last = stored(jnp.where(odd(), 3, 1), 1, crossed, rows, labels, out_ref, out, sems)
+    first.wait()
+    last.wait()
+
+
+def finish_kernel(rows_ref, two_keep, third_keep, two_ref, mix_ref, late_ref, pair_ref, begun_ref, out_ref, out, sems):
+    count = two_keep.shape[0]
+    width = two_ref.shape[0] - 8
+    tiles = out.shape[2] // LANES
+    rows = row_labels(rows_ref[:count, :])
+    two, third = apart(pair_ref[...])
+    first = stored(2, 0, two + two_keep[...], rows, tiles_of(two_ref, width, tiles), out_ref, out, sems)
+    labels = [
+        jnp.where(second(), x, y) for x, y in zip(tiles_of(late_ref, width, tiles), tiles_of(mix_ref, width, tiles))
+    ]
+    last = stored(jnp.where(odd(), 1, 3), 1, third + third_keep[...], rows, labels, out_ref, out, sems)
+    first.wait()
+    last.wait()
+
+
 def total_kernel(*refs):
     terms, out_ref = [ref[...] for ref in refs[:-1]], refs[-1]
     out_ref[...] = sum(terms[1:], terms[0])
 
 
-def finish_kernel(parts, rows_ref, own_keep, two_keep, third_keep, crossed_ref, own_labels, two_ref, mix_ref, late_ref, core_ref, *refs):
-    own_in, (pair_ref, out_ref, out, sems) = refs[:parts - 1], refs[parts - 1:]
-    count = own_keep.shape[0]
-    width = two_ref.shape[0] - 8
-    tiles = out.shape[2] // LANES
-    rows = row_labels(rows_ref[:count, :])
-    copies = []
-
-    def store(m, term, labels):
-        for k in range(tiles):
-            out[m, :, k * LANES:(k + 1) * LANES] = jnp.where(rows == labels[k], term, 0.0)
-        copies.append(pltpu.make_async_copy(out.at[m], out_ref.at[m], sems.at[m]))
-        copies[-1].start()
-
-    def of(ref, row=width):
-        return [ref[row:row + 1, k * LANES:(k + 1) * LANES] for k in range(tiles)]
-
-    def pick(here, one, other):
-        return [jnp.where(here, x, y) for x, y in zip(one, other)]
-
-    two, third = apart(pair_ref[...])
-    store(0, sum([unhalved(ref[...]) for ref in own_in], own_keep[...]), of(own_labels, 0))
-    store(2, two + two_keep[...], of(two_ref))
-    third = third + third_keep[...]
-    crossed = crossed_ref[...] + unhalved(core_ref[:count // 2, :])
-    crossed_labels = [core_ref[count // 2 + k:count // 2 + k + 1, :] for k in range(tiles)]
-    third_labels = pick(second(), of(late_ref), of(mix_ref))
-    store(1, jnp.where(odd(), third, crossed), pick(odd(), third_labels, crossed_labels))
-    store(3, jnp.where(odd(), crossed, third), pick(odd(), crossed_labels, third_labels))
-    for copy in copies:
-        copy.wait()
-
-
 def whole(*shape):
     return jax.ShapeDtypeStruct(shape, F32)
 
 
-def call(kernel, out_shape, args, flops, off=0, scratch=(), out_specs=ONCHIP):
+def call(kernel, out_shape, args, flops, off=0, scratch=(), out_specs=ONCHIP, onto=None):
     moved = sum(a.size * 4 for a in list(args) + out_shape)
     args = [pltpu.with_memory_space_constraint(a, pltpu.HBM) for a in args[:off]] + list(args[off:])
     return pl.pallas_call(
         kernel,
         out_shape=out_shape,
-        in_specs=[OFFCHIP] * off + [ONCHIP] * (len(args) - off),
+        in_specs=[OFFCHIP if i < off or i == onto else ONCHIP for i in range(len(args))],
+        input_output_aliases={} if onto is None else {onto: 0},
         out_specs=[out_specs] * len(out_shape),
         scratch_shapes=list(scratch),
         cost_estimate=pl.CostEstimate(flops=flops, bytes_accessed=0, transcendentals=0),
@@ -314,12 +325,14 @@
     pair_in = exchanged(pair_send)
     core_send, = call(core_kernel, [whole(count // 2 + 8, LANES)], (twin, after(two, pair_send)), 0)
     core_in = moved(core_send, (1, -1, 1, -1))
-    two_keep, third_keep, crossed_sum = call(
-        keep_kernel, [whole(count, LANES)] * 3, (rows, after(two, pair_send), mix, late, *diagonal_in), 4 * one_product)
+    two_keep, third_keep = call(keep_kernel, [whole(count, LANES)] * 2, (rows, after(two, pair_send), mix, late), 0)
+    crossed_sum, = call(halves_kernel, [whole(count, LANES)], tuple(diagonal_in), 3 * one_product)
+    stage = [pltpu.VMEM((2, count, pairs), F32), pltpu.SemaphoreType.DMA((2,))]
+    begun, = call(early_kernel, [whole(4, count, pairs)],
+                  (rows, own_keep, own_labels, crossed_sum, core_in, *own_in), 0, 0, stage, OFFCHIP)
     pair_sum, = call(total_kernel, [whole(count, LANES)], tuple(pair_in), 0)
-    out, = call(functools.partial(finish_kernel, parts), [whole(4, count, pairs)],
-                (rows, own_keep, two_keep, third_keep, crossed_sum, own_labels, two, mix, late, core_in, *own_in, pair_sum),
-                0, 0, [pltpu.VMEM((4, count, pairs), F32), pltpu.SemaphoreType.DMA((4,))], OFFCHIP)
+    out, = call(finish_kernel, [whole(4, count, pairs)],
+                (rows, two_keep, third_keep, two, mix, late, pair_sum, begun), 0, 0, stage, OFFCHIP, 7)
     return out
 
 

time: 18.9 us -> 18.8 us (level)
  waiting for transfers between devices: 4.74 us -> 3.84 us
  Pallas kernels: 5.42 us -> 6.21 us
    pallas_call x11 -> x13, Pallas kernels: 5.42 us -> 6.21 us  [call(): pl.pallas_call(kernel, out_shape=out_shape, in_specs=[OFFCHIP if i < off...]
    ppermute x1, waiting for transfers between devices: 1.31 us -> 0.73 us  [crossed(): lax.ppermute(array, ('blk', 'red'), [(b * parts + r, c * parts + t) for (...]
    ppermute x2, waiting for transfers between devices: 0.81 us -> 0.48 us  [exchanged(): lax.ppermute(array[k - 1], 'red', [(i, (i + k) % parts) for i in range(pa...]
  transfers between devices with their start and end apart: 8 -> 8, of which waited for: 5 -> 5; matrix products, arithmetic and copies ran while one was open for 0% -> 0% of each run, Pallas kernels for 17% -> 22%
where the time goes in v24:
time: 18.8 us; the launch traced here: 18.6 us
  starting transfers between devices  8.45 us (45%)
  Pallas kernels  6.21 us (33%)
  waiting for transfers between devices  3.84 us (20%)
    pallas_call x13, Pallas kernels, call(): pl.pallas_call(kernel, out_shape=out_shape, in_specs=[OFFCHIP if i < off...  6.21 us
    ppermute x5, starting transfers between devices, moved(): lax.ppermute(array, 'blk', [(i, (i + steps[i % 4]) % blocks) for i in ran...  5.19 us
    ppermute x2, starting transfers between devices, exchanged(): lax.ppermute(array[k - 1], 'red', [(i, (i + k) % parts) for i in range(pa...  3.02 us
    ppermute x5, waiting for transfers between devices, moved(): lax.ppermute(array, 'blk', [(i, (i + steps[i % 4]) % blocks) for i in ran...  2.63 us
    ppermute x1, waiting for transfers between devices, crossed(): lax.ppermute(array, ('blk', 'red'), [(b * parts + r, c * parts + t) for (...  0.73 us
    ppermute x2, waiting for transfers between devices, exchanged(): lax.ppermute(array[k - 1], 'red', [(i, (i + k) % parts) for i in range(pa...  0.48 us
  transfers between devices with their start and end apart: 8, of which 5 were waited for; matrix products, arithmetic and copies ran while one was open for 0% of the time, Pallas kernels for 22%

profile of v24, /device:TPU:0, one launch (start us, length us, event | category | flops | bytes accessed | tf_op | source)
XLA Modules:
  0.0 18.6 jit_solution(10185692314898137332)
XLA Ops:
  0.0 1.4 %shard_map.55.slab_ref.own_ref = f32[200,256]{1,0:T(8,128)S(1)} custom-call(f32[256,768]{1,0:T(8,128)} %amp_ref.1, s32[1,256]{1,0:T(1,128)} %ij_ref.1, s32[1,768]{1,0:T(1,128)} %cd_ref.3), custom_call_target="tpu_custom_call" | custom-call | flops 786432 | tf_op jit(solution)/shard_map/pallas_call | solution.py:258
  1.4 3.0 %collective-permute-start = (f32[200,256]{1,0:T(8,128)S(1)}, f32[200,256]{1,0:T(8,128)S(1)}, u32[]{:S(2)}, u32[]{:S(2)}) collective-permute-start(f32[200,256]{1,0:T(8,128)S(1)} %shard_map.55.slab_ref.own_ref), channel_id=1, source_target_pairs={{0,4},{2,6},{4,8},{6,10},{8,12},{10,14},{12,16},{14,18},{16,20},{1... | collective-permute-start | bytes 614408 | tf_op jit(solution)/shard_map/ppermute | solution.py:279
  4.4 0.0 collective-permute-start.3
  4.4 1.3 %shard_map.57.rows_ref = f32[256,256]{1,0:T(8,128)S(1)} custom-call(f32[256,768]{1,0:T(8,128)} %v_ref, s32[1,256]{1,0:T(1,128)} %ab_ref.1, s32[1,768]{1,0:T(1,128)} %cd_ref.3), custom_call_target="tpu_custom_call" | custom-call | tf_op jit(solution)/shard_map/pallas_call | solution.py:258
  5.7 1.8 %collective-permute-start.2 = (f32[256,256]{1,0:T(8,128)S(1)}, f32[256,256]{1,0:T(8,128)S(1)}, u32[]{:S(2)}, u32[]{:S(2)}) collective-permute-start(f32[256,256]{1,0:T(8,128)S(1)} %shard_map.57.rows_ref), channel_id=1, source_target_pairs={{0,2},{2,0},{4,6},{6,4},{8,10},{10,8},{12,14},{14,12},{16,18},{18,... | collective-permute-start | bytes 786440 | tf_op jit(solution)/shard_map/ppermute | solution.py:279
  7.4 0.3 %shard_map.58 = (f32[128,128]{1,0:T(8,128)S(1)}, f32[1,64,128]{2,1,0:T(8,128)S(1)}) custom-call(f32[256,256]{1,0:T(8,128)S(1)} %shard_map.57.rows_ref, f32[200,256]{1,0:T(8,128)S(1)} %shard_map.55.slab_ref.own_ref), custom_call_target="tpu_custom_call" | custom-call | flops 9663676416 | tf_op jit(solution)/shard_map/pallas_call | solution.py:258
  7.8 0.1 collective-permute-start.1
  7.8 1.6 %collective-permute-start.4 = (f32[64,128]{1,0:T(8,128)S(1)}, f32[64,128]{1,0:T(8,128)S(1)}, u32[]{:S(2)}, u32[]{:S(2)}) collective-permute-start(f32[64,128]{1,0:T(8,128)S(1)} %bitcast.5), channel_id=1, source_target_pairs={{0,1},{1,0},{2,3},{3,2},{4,5},{5,4},{6,7},{7,6},{8,9},{9,8},{10,11... | collective-permute-start | bytes 98312 | tf_op jit(solution)/shard_map/ppermute | solution.py:283
  9.4 1.9 %collective-permute-done.3.slab_ref.mix_ref = f32[200,256]{1,0:T(8,128)S(1)} collective-permute-done((f32[200,256]{1,0:T(8,128)S(1)}, f32[200,256]{1,0:T(8,128)S(1)}, u32[]{:S(2)}, u32[]{:S(2)}) %collective-permute-start.3) | collective-permute-done | bytes 204832 | tf_op jit(solution)/shard_map/ppermute | solution.py:279
  11.4 0.3 %shard_map.59.mix_term = f32[128,128]{1,0:T(8,128)S(1)} custom-call(f32[256,256]{1,0:T(8,128)S(1)} %shard_map.57.rows_ref, f32[200,256]{1,0:T(8,128)S(1)} %collective-permute-done.3.slab_ref.mix_ref), custom_call_target="tpu_custom_call" | custom-call | tf_op jit(solution)/shard_map/pallas_call | solution.py:258
  11.7 0.2 collective-permute-done.4.refs_0_
  11.8 0.7 %collective-permute-done.two_ref = f32[200,256]{1,0:T(8,128)S(1)} collective-permute-done((f32[200,256]{1,0:T(8,128)S(1)}, f32[200,256]{1,0:T(8,128)S(1)}, u32[]{:S(2)}, u32[]{:S(2)}) %collective-permute-start) | collective-permute-done | bytes 204832 | tf_op jit(solution)/shard_map/ppermute | solution.py:279
  12.5 0.3 %shard_map.60 = (f32[128,128]{1,0:T(8,128)S(1)}, f32[1,64,128]{2,1,0:T(8,128)S(1)}) custom-call(f32[256,256]{1,0:T(8,128)S(1)} %shard_map.57.rows_ref, f32[256,256]{1,0:T(8,128)S(1)} %collective-permute-done.2.twin_ref, f32[200,256]{1,0:T(8,128)S(1)} %collective-permute-done.two_ref), custom_call_target="tpu_custom_call" | custom-call | tf_op jit(solution)/shard_map/pallas_call | solution.py:258
  12.9 0.2 %collective-permute-start.6 = (f32[64,128]{1,0:T(8,128)S(1)}, f32[64,128]{1,0:T(8,128)S(1)}, u32[]{:S(2)}, u32[]{:S(2)}) collective-permute-start(f32[64,128]{1,0:T(8,128)S(1)} %bitcast.4), channel_id=1, source_target_pairs={{0,3},{1,2},{2,1},{3,0},{4,7},{5,6},{6,5},{7,4},{8,11},{9,10},{10,... | collective-permute-start | bytes 98312 | tf_op jit(solution)/shard_map/ppermute | solution.py:302
  13.1 1.4 %collective-permute-start.5 = (f32[128,128]{1,0:T(8,128)S(1)}, f32[128,128]{1,0:T(8,128)S(1)}, u32[]{:S(2)}, u32[]{:S(2)}) collective-permute-start(f32[128,128]{1,0:T(8,128)S(1)} %bitcast.3), channel_id=1, source_target_pairs={{0,1},{1,0},{2,3},{3,2},{4,5},{5,4},{6,7},{7,6},{8,9},{9,8},{10,11... | collective-permute-start | bytes 196616 | tf_op jit(solution)/shard_map/ppermute | solution.py:283
  14.6 0.3 %shard_map.65 = f32[72,128]{1,0:T(8,128)S(1)} custom-call(f32[256,256]{1,0:T(8,128)S(1)} %collective-permute-done.2.twin_ref, f32[200,256]{1,0:T(8,128)S(1)} %collective-permute-done.two_ref), custom_call_target="tpu_custom_call" | custom-call | tf_op jit(solution)/shard_map/pallas_call | solution.py:258
  14.8 0.4 %collective-permute-start.7 = (f32[72,128]{1,0:T(8,128)S(1)}, f32[72,128]{1,0:T(8,128)S(1)}, u32[]{:S(2)}, u32[]{:S(2)}) collective-permute-start(f32[72,128]{1,0:T(8,128)S(1)} %shard_map.65), channel_id=1, source_target_pairs={{0,2},{2,0},{4,6},{6,4},{8,10},{10,8},{12,14},{14,12},{16,18},{18,... | collective-permute-start | bytes 110600 | tf_op jit(solution)/shard_map/ppermute | solution.py:279
  15.2 0.6 %shard_map.62 = (f32[128,128]{1,0:T(8,128)S(1)}, f32[128,128]{1,0:T(8,128)S(1)}) custom-call(f32[256,256]{1,0:T(8,128)S(1)} %shard_map.57.rows_ref, f32[200,256]{1,0:T(8,128)S(1)} %collective-permute-done.two_ref, f32[200,256]{1,0:T(8,128)S(1)} %collective-permute-done.3.slab_ref.mix_ref, f32[200,256]{1,0:T(8,128)S(1)} %collective-permute-done.1.late_ref), custom_call_target="tpu_custom_call" | custom-call | tf_op jit(solution)/shard_map/pallas_call | solution.py:258
  15.8 0.7 %collective-permute-done.6.refs_0_ = f32[64,128]{1,0:T(8,128)S(1)} collective-permute-done((f32[64,128]{1,0:T(8,128)S(1)}, f32[64,128]{1,0:T(8,128)S(1)}, u32[]{:S(2)}, u32[]{:S(2)}) %collective-permute-start.6) | collective-permute-done | bytes 32800 | tf_op jit(solution)/shard_map/ppermute | solution.py:302
  16.5 0.1 shard_map.64.crossed_ref
  16.6 0.0 collective-permute-done.7.core_ref
  16.6 0.8 %shard_map.66.begun_ref = f32[4,128,256]{2,1,0:T(8,128)} custom-call(f32[256,256]{1,0:T(8,128)S(1)} %shard_map.57.rows_ref, f32[128,128]{1,0:T(8,128)S(1)} %get-tuple-element.17.own_keep, f32[8,256]{1,0:T(8,128)S(1)} %shard_map.56.own_labels, f32[128,128]{1,0:T(8,128)S(1)} %shard_map.64.crossed_ref, f32[72,128]{1,0:T(8,128)S(1)} %collective-permute-done.7.core_ref, ...), custom_call_target="tpu_custom_call" | custom-call | tf_op jit(solution)/shard_map/pallas_call | solution.py:258
  17.4 0.3 %collective-permute-done.5.refs_0_ = f32[128,128]{1,0:T(8,128)S(1)} collective-permute-done((f32[128,128]{1,0:T(8,128)S(1)}, f32[128,128]{1,0:T(8,128)S(1)}, u32[]{:S(2)}, u32[]{:S(2)}) %collective-permute-start.5) | collective-permute-done | bytes 65568 | tf_op jit(solution)/shard_map/ppermute | solution.py:283
  17.8 0.8 %shard_map.67 = f32[4,128,256]{2,1,0:T(8,128)} custom-call(f32[256,256]{1,0:T(8,128)S(1)} %shard_map.57.rows_ref, f32[128,128]{1,0:T(8,128)S(1)} %get-tuple-element.24.two_keep, f32[128,128]{1,0:T(8,128)S(1)} %get-tuple-element.25.third_keep, f32[200,256]{1,0:T(8,128)S(1)} %collective-permute-done.two_ref, ...), custom_call_target="tpu_custom_call", output_to_operand_aliasing={{}: (7, {})} | custom-call | tf_op jit(solution)/shard_map/pallas_call | solution.py:258
  (5 shorter events, 0.0 us)
Async XLA Ops:
  1.4 11.1 %collective-permute-start = (f32[200,256]{1,0:T(8,128)S(1)}, f32[200,256]{1,0:T(8,128)S(1)}, u32[]{:S(2)}, u32[]{:S(2)}) collective-permute-start(f32[200,256]{1,0:T(8,128)S(1)} %shard_map.55.slab_ref.own_ref), channel_id=1, source_target_pairs={{0,4},{2,6},{4,8},{6,10},{8,12},{10,14},{12,16},{14,18},{16,20},{1... | collective-permute-start | bytes 614408 | tf_op jit(solution)/shard_map/ppermute | solution.py:279
  4.4 7.0 %collective-permute-start.3 = (f32[200,256]{1,0:T(8,128)S(1)}, f32[200,256]{1,0:T(8,128)S(1)}, u32[]{:S(2)}, u32[]{:S(2)}) collective-permute-start(f32[200,256]{1,0:T(8,128)S(1)} %shard_map.55.slab_ref.own_ref), channel_id=1, source_target_pairs={{0,2},{2,8},{4,6},{6,4},{8,10},{10,16},{12,14},{14,12},{16,18},{18... | collective-permute-start | bytes 614408 | tf_op jit(solution)/shard_map/ppermute | solution.py:279
  5.7 6.8 %collective-permute-start.2 = (f32[256,256]{1,0:T(8,128)S(1)}, f32[256,256]{1,0:T(8,128)S(1)}, u32[]{:S(2)}, u32[]{:S(2)}) collective-permute-start(f32[256,256]{1,0:T(8,128)S(1)} %shard_map.57.rows_ref), channel_id=1, source_target_pairs={{0,2},{2,0},{4,6},{6,4},{8,10},{10,8},{12,14},{14,12},{16,18},{18,... | collective-permute-start | bytes 786440 | tf_op jit(solution)/shard_map/ppermute | solution.py:279
  7.8 5.3 %collective-permute-start.1 = (f32[200,256]{1,0:T(8,128)S(1)}, f32[200,256]{1,0:T(8,128)S(1)}, u32[]{:S(2)}, u32[]{:S(2)}) collective-permute-start(f32[200,256]{1,0:T(8,128)S(1)} %shard_map.55.slab_ref.own_ref), channel_id=1, source_target_pairs={{0,2},{2,0},{4,6},{6,12},{8,10},{10,8},{12,14},{14,20},{16,18},{18... | collective-permute-start | bytes 614408 | tf_op jit(solution)/shard_map/ppermute | solution.py:279
  7.8 4.0 %collective-permute-start.4 = (f32[64,128]{1,0:T(8,128)S(1)}, f32[64,128]{1,0:T(8,128)S(1)}, u32[]{:S(2)}, u32[]{:S(2)}) collective-permute-start(f32[64,128]{1,0:T(8,128)S(1)} %bitcast.5), channel_id=1, source_target_pairs={{0,1},{1,0},{2,3},{3,2},{4,5},{5,4},{6,7},{7,6},{8,9},{9,8},{10,11... | collective-permute-start | bytes 98312 | tf_op jit(solution)/shard_map/ppermute | solution.py:283
  12.9 3.7 %collective-permute-start.6 = (f32[64,128]{1,0:T(8,128)S(1)}, f32[64,128]{1,0:T(8,128)S(1)}, u32[]{:S(2)}, u32[]{:S(2)}) collective-permute-start(f32[64,128]{1,0:T(8,128)S(1)} %bitcast.4), channel_id=1, source_target_pairs={{0,3},{1,2},{2,1},{3,0},{4,7},{5,6},{6,5},{7,4},{8,11},{9,10},{10,... | collective-permute-start | bytes 98312 | tf_op jit(solution)/shard_map/ppermute | solution.py:302
  13.1 4.6 %collective-permute-start.5 = (f32[128,128]{1,0:T(8,128)S(1)}, f32[128,128]{1,0:T(8,128)S(1)}, u32[]{:S(2)}, u32[]{:S(2)}) collective-permute-start(f32[128,128]{1,0:T(8,128)S(1)} %bitcast.3), channel_id=1, source_target_pairs={{0,1},{1,0},{2,3},{3,2},{4,5},{5,4},{6,7},{7,6},{8,9},{9,8},{10,11... | collective-permute-start | bytes 196616 | tf_op jit(solution)/shard_map/ppermute | solution.py:283
  14.8 1.8 %collective-permute-start.7 = (f32[72,128]{1,0:T(8,128)S(1)}, f32[72,128]{1,0:T(8,128)S(1)}, u32[]{:S(2)}, u32[]{:S(2)}) collective-permute-start(f32[72,128]{1,0:T(8,128)S(1)} %shard_map.65), channel_id=1, source_target_pairs={{0,2},{2,0},{4,6},{6,4},{8,10},{10,8},{12,14},{14,12},{16,18},{18,... | collective-permute-start | bytes 110600 | tf_op jit(solution)/shard_map/ppermute | solution.py:279

commit v25 on v24

--- a/solution.py
+++ b/solution.py
@@ -315,7 +315,7 @@
     own_in = exchanged(own_send)
     late = moved(after(own, own_keep), (1, -1, 1, 3))
     rest = whole(row_count - count, LANES)
-    mix_term, = call(sent_kernel, [rest], (rows, mix), 0)
+    mix_term, = call(sent_kernel, [rest], (rows, mix), 64 * one_product)
     two_term, diagonal_send = call(
         both_kernel, [rest, whole(parts - 1, count // 2, LANES)],
         (rows, twin, after(two, mix_term, *own_in)), 0)

time: 18.8 us -> 19.4 us (1.032)
  the two profiles are of different devices: /device:TPU:0 before, /device:TPU:2 now
where the time goes in v25:
time: 19.4 us; the launch traced here: 19.2 us
  waiting for transfers between devices  7.91 us (41%)
  Pallas kernels  6.48 us (33%)
  starting transfers between devices  4.76 us (25%)
    pallas_call x13, Pallas kernels, call(): pl.pallas_call(kernel, out_shape=out_shape, in_specs=[OFFCHIP if i < off...  6.48 us
    ppermute x5, waiting for transfers between devices, moved(): lax.ppermute(array, 'blk', [(i, (i + steps[i % 4]) % blocks) for i in ran...  4.43 us
    ppermute x2, waiting for transfers between devices, exchanged(): lax.ppermute(array[k - 1], 'red', [(i, (i + k) % parts) for i in range(pa...  3.48 us
    ppermute x5, starting transfers between devices, moved(): lax.ppermute(array, 'blk', [(i, (i + steps[i % 4]) % blocks) for i in ran...  2.25 us
    ppermute x2, starting transfers between devices, exchanged(): lax.ppermute(array[k - 1], 'red', [(i, (i + k) % parts) for i in range(pa...  2.16 us
  transfers between devices with their start and end apart: 8, of which 4 were waited for; matrix products, arithmetic and copies ran while one was open for 0% of the time, Pallas kernels for 22%

profile of v25, /device:TPU:2, one launch (start us, length us, event | category | flops | bytes accessed | tf_op | source)
XLA Modules:
  0.0 19.2 jit_solution(2488795238830252812)
XLA Ops:
  0.0 1.4 %shard_map.55.slab_ref.own_ref = f32[200,256]{1,0:T(8,128)S(1)} custom-call(f32[256,768]{1,0:T(8,128)} %amp_ref.1, s32[1,256]{1,0:T(1,128)} %ij_ref.1, s32[1,768]{1,0:T(1,128)} %cd_ref.3), custom_call_target="tpu_custom_call" | custom-call | flops 786432 | tf_op jit(solution)/shard_map/pallas_call | solution.py:258
  1.4 1.6 %collective-permute-start = (f32[200,256]{1,0:T(8,128)S(1)}, f32[200,256]{1,0:T(8,128)S(1)}, u32[]{:S(2)}, u32[]{:S(2)}) collective-permute-start(f32[200,256]{1,0:T(8,128)S(1)} %shard_map.55.slab_ref.own_ref), channel_id=1, source_target_pairs={{0,4},{2,6},{4,8},{6,10},{8,12},{10,14},{12,16},{14,18},{16,20},{1... | collective-permute-start | bytes 614408 | tf_op jit(solution)/shard_map/ppermute | solution.py:279
  3.0 1.3 %shard_map.57.rows_ref = f32[256,256]{1,0:T(8,128)S(1)} custom-call(f32[256,768]{1,0:T(8,128)} %v_ref, s32[1,256]{1,0:T(1,128)} %ab_ref.1, s32[1,768]{1,0:T(1,128)} %cd_ref.3), custom_call_target="tpu_custom_call" | custom-call | tf_op jit(solution)/shard_map/pallas_call | solution.py:258
  4.3 0.6 %collective-permute-start.2 = (f32[256,256]{1,0:T(8,128)S(1)}, f32[256,256]{1,0:T(8,128)S(1)}, u32[]{:S(2)}, u32[]{:S(2)}) collective-permute-start(f32[256,256]{1,0:T(8,128)S(1)} %shard_map.57.rows_ref), channel_id=1, source_target_pairs={{0,2},{2,0},{4,6},{6,4},{8,10},{10,8},{12,14},{14,12},{16,18},{18,... | collective-permute-start | bytes 786440 | tf_op jit(solution)/shard_map/ppermute | solution.py:279
  4.9 0.3 %shard_map.58 = (f32[128,128]{1,0:T(8,128)S(1)}, f32[1,64,128]{2,1,0:T(8,128)S(1)}) custom-call(f32[256,256]{1,0:T(8,128)S(1)} %shard_map.57.rows_ref, f32[200,256]{1,0:T(8,128)S(1)} %shard_map.55.slab_ref.own_ref), custom_call_target="tpu_custom_call" | custom-call | flops 9663676416 | tf_op jit(solution)/shard_map/pallas_call | solution.py:258
  5.2 1.6 %collective-permute-start.4 = (f32[64,128]{1,0:T(8,128)S(1)}, f32[64,128]{1,0:T(8,128)S(1)}, u32[]{:S(2)}, u32[]{:S(2)}) collective-permute-start(f32[64,128]{1,0:T(8,128)S(1)} %bitcast.5), channel_id=1, source_target_pairs={{0,1},{1,0},{2,3},{3,2},{4,5},{5,4},{6,7},{7,6},{8,9},{9,8},{10,11... | collective-permute-start | bytes 98312 | tf_op jit(solution)/shard_map/ppermute | solution.py:283
  6.8 0.0 collective-permute-done.3.slab_ref.mix_ref
  6.8 0.3 %shard_map.59.mix_term = f32[128,128]{1,0:T(8,128)S(1)} custom-call(f32[256,256]{1,0:T(8,128)S(1)} %shard_map.57.rows_ref, f32[200,256]{1,0:T(8,128)S(1)} %collective-permute-done.3.slab_ref.mix_ref), custom_call_target="tpu_custom_call" | custom-call | flops 9663676416 | tf_op jit(solution)/shard_map/pallas_call | solution.py:258
  7.1 2.1 %collective-permute-done.4.refs_0_ = f32[64,128]{1,0:T(8,128)S(1)} collective-permute-done((f32[64,128]{1,0:T(8,128)S(1)}, f32[64,128]{1,0:T(8,128)S(1)}, u32[]{:S(2)}, u32[]{:S(2)}) %collective-permute-start.4) | collective-permute-done | bytes 32800 | tf_op jit(solution)/shard_map/ppermute | solution.py:283
  9.2 0.0 collective-permute-done.two_ref
  9.2 0.0 collective-permute-done.2.twin_ref
  9.2 0.3 %shard_map.60 = (f32[128,128]{1,0:T(8,128)S(1)}, f32[1,64,128]{2,1,0:T(8,128)S(1)}) custom-call(f32[256,256]{1,0:T(8,128)S(1)} %shard_map.57.rows_ref, f32[256,256]{1,0:T(8,128)S(1)} %collective-permute-done.2.twin_ref, f32[200,256]{1,0:T(8,128)S(1)} %collective-permute-done.two_ref), custom_call_target="tpu_custom_call" | custom-call | tf_op jit(solution)/shard_map/pallas_call | solution.py:258
  9.5 0.4 %collective-permute-start.6 = (f32[64,128]{1,0:T(8,128)S(1)}, f32[64,128]{1,0:T(8,128)S(1)}, u32[]{:S(2)}, u32[]{:S(2)}) collective-permute-start(f32[64,128]{1,0:T(8,128)S(1)} %bitcast.4), channel_id=1, source_target_pairs={{0,3},{1,2},{2,1},{3,0},{4,7},{5,6},{6,5},{7,4},{8,11},{9,10},{10,... | collective-permute-start | bytes 98312 | tf_op jit(solution)/shard_map/ppermute | solution.py:302
  9.9 3.9 %collective-permute-done.1.late_ref = f32[200,256]{1,0:T(8,128)S(1)} collective-permute-done((f32[200,256]{1,0:T(8,128)S(1)}, f32[200,256]{1,0:T(8,128)S(1)}, u32[]{:S(2)}, u32[]{:S(2)}) %collective-permute-start.1) | collective-permute-done | bytes 204832 | tf_op jit(solution)/shard_map/ppermute | solution.py:279
  13.8 0.3 %shard_map.61 = f32[1,128,128]{2,1,0:T(8,128)S(1)} custom-call(f32[256,256]{1,0:T(8,128)S(1)} %shard_map.57.rows_ref, f32[200,256]{1,0:T(8,128)S(1)} %collective-permute-done.1.late_ref, f32[128,128]{1,0:T(8,128)S(1)} %get-tuple-element.22.two_term, f32[128,128]{1,0:T(8,128)S(1)} %shard_map.59.mix_term), custom_call_target="tpu_custom_call" | custom-call | tf_op jit(solution)/shard_map/pallas_call | solution.py:258
  14.1 0.6 %collective-permute-start.5 = (f32[128,128]{1,0:T(8,128)S(1)}, f32[128,128]{1,0:T(8,128)S(1)}, u32[]{:S(2)}, u32[]{:S(2)}) collective-permute-start(f32[128,128]{1,0:T(8,128)S(1)} %bitcast.3), channel_id=1, source_target_pairs={{0,1},{1,0},{2,3},{3,2},{4,5},{5,4},{6,7},{7,6},{8,9},{9,8},{10,11... | collective-permute-start | bytes 196616 | tf_op jit(solution)/shard_map/ppermute | solution.py:283
  14.6 0.3 %shard_map.65 = f32[72,128]{1,0:T(8,128)S(1)} custom-call(f32[256,256]{1,0:T(8,128)S(1)} %collective-permute-done.2.twin_ref, f32[200,256]{1,0:T(8,128)S(1)} %collective-permute-done.two_ref), custom_call_target="tpu_custom_call" | custom-call | tf_op jit(solution)/shard_map/pallas_call | solution.py:258
  14.9 0.1 collective-permute-start.7
  15.0 0.6 %shard_map.62 = (f32[128,128]{1,0:T(8,128)S(1)}, f32[128,128]{1,0:T(8,128)S(1)}) custom-call(f32[256,256]{1,0:T(8,128)S(1)} %shard_map.57.rows_ref, f32[200,256]{1,0:T(8,128)S(1)} %collective-permute-done.two_ref, f32[200,256]{1,0:T(8,128)S(1)} %collective-permute-done.3.slab_ref.mix_ref, f32[200,256]{1,0:T(8,128)S(1)} %collective-permute-done.1.late_ref), custom_call_target="tpu_custom_call" | custom-call | tf_op jit(solution)/shard_map/pallas_call | solution.py:258
  15.6 0.1 shard_map.64.crossed_ref
  15.7 0.5 %collective-permute-done.7.core_ref = f32[72,128]{1,0:T(8,128)S(1)} collective-permute-done((f32[72,128]{1,0:T(8,128)S(1)}, f32[72,128]{1,0:T(8,128)S(1)}, u32[]{:S(2)}, u32[]{:S(2)}) %collective-permute-start.7) | collective-permute-done | bytes 36896 | tf_op jit(solution)/shard_map/ppermute | solution.py:279
  16.2 0.8 %shard_map.66.begun_ref = f32[4,128,256]{2,1,0:T(8,128)} custom-call(f32[256,256]{1,0:T(8,128)S(1)} %shard_map.57.rows_ref, f32[128,128]{1,0:T(8,128)S(1)} %get-tuple-element.17.own_keep, f32[8,256]{1,0:T(8,128)S(1)} %shard_map.56.own_labels, f32[128,128]{1,0:T(8,128)S(1)} %shard_map.64.crossed_ref, f32[72,128]{1,0:T(8,128)S(1)} %collective-permute-done.7.core_ref, ...), custom_call_target="tpu_custom_call" | custom-call | tf_op jit(solution)/shard_map/pallas_call | solution.py:258
  17.0 1.4 %collective-permute-done.5.refs_0_ = f32[128,128]{1,0:T(8,128)S(1)} collective-permute-done((f32[128,128]{1,0:T(8,128)S(1)}, f32[128,128]{1,0:T(8,128)S(1)}, u32[]{:S(2)}, u32[]{:S(2)}) %collective-permute-start.5) | collective-permute-done | bytes 65568 | tf_op jit(solution)/shard_map/ppermute | solution.py:283
  18.4 0.8 %shard_map.67 = f32[4,128,256]{2,1,0:T(8,128)} custom-call(f32[256,256]{1,0:T(8,128)S(1)} %shard_map.57.rows_ref, f32[128,128]{1,0:T(8,128)S(1)} %get-tuple-element.24.two_keep, f32[128,128]{1,0:T(8,128)S(1)} %get-tuple-element.25.third_keep, f32[200,256]{1,0:T(8,128)S(1)} %collective-permute-done.two_ref, ...), custom_call_target="tpu_custom_call", output_to_operand_aliasing={{}: (7, {})} | custom-call | tf_op jit(solution)/shard_map/pallas_call | solution.py:258
  (5 shorter events, 0.0 us)
Async XLA Ops:
  1.4 7.8 %collective-permute-start = (f32[200,256]{1,0:T(8,128)S(1)}, f32[200,256]{1,0:T(8,128)S(1)}, u32[]{:S(2)}, u32[]{:S(2)}) collective-permute-start(f32[200,256]{1,0:T(8,128)S(1)} %shard_map.55.slab_ref.own_ref), channel_id=1, source_target_pairs={{0,4},{2,6},{4,8},{6,10},{8,12},{10,14},{12,16},{14,18},{16,20},{1... | collective-permute-start | bytes 614408 | tf_op jit(solution)/shard_map/ppermute | solution.py:279
  3.0 3.8 %collective-permute-start.3 = (f32[200,256]{1,0:T(8,128)S(1)}, f32[200,256]{1,0:T(8,128)S(1)}, u32[]{:S(2)}, u32[]{:S(2)}) collective-permute-start(f32[200,256]{1,0:T(8,128)S(1)} %shard_map.55.slab_ref.own_ref), channel_id=1, source_target_pairs={{0,2},{2,8},{4,6},{6,4},{8,10},{10,16},{12,14},{14,12},{16,18},{18... | collective-permute-start | bytes 614408 | tf_op jit(solution)/shard_map/ppermute | solution.py:279
  4.3 4.9 %collective-permute-start.2 = (f32[256,256]{1,0:T(8,128)S(1)}, f32[256,256]{1,0:T(8,128)S(1)}, u32[]{:S(2)}, u32[]{:S(2)}) collective-permute-start(f32[256,256]{1,0:T(8,128)S(1)} %shard_map.57.rows_ref), channel_id=1, source_target_pairs={{0,2},{2,0},{4,6},{6,4},{8,10},{10,8},{12,14},{14,12},{16,18},{18,... | collective-permute-start | bytes 786440 | tf_op jit(solution)/shard_map/ppermute | solution.py:279
  5.2 4.0 %collective-permute-start.4 = (f32[64,128]{1,0:T(8,128)S(1)}, f32[64,128]{1,0:T(8,128)S(1)}, u32[]{:S(2)}, u32[]{:S(2)}) collective-permute-start(f32[64,128]{1,0:T(8,128)S(1)} %bitcast.5), channel_id=1, source_target_pairs={{0,1},{1,0},{2,3},{3,2},{4,5},{5,4},{6,7},{7,6},{8,9},{9,8},{10,11... | collective-permute-start | bytes 98312 | tf_op jit(solution)/shard_map/ppermute | solution.py:283
  6.8 7.0 %collective-permute-start.1 = (f32[200,256]{1,0:T(8,128)S(1)}, f32[200,256]{1,0:T(8,128)S(1)}, u32[]{:S(2)}, u32[]{:S(2)}) collective-permute-start(f32[200,256]{1,0:T(8,128)S(1)} %shard_map.55.slab_ref.own_ref), channel_id=1, source_target_pairs={{0,2},{2,0},{4,6},{6,12},{8,10},{10,8},{12,14},{14,20},{16,18},{18... | collective-permute-start | bytes 614408 | tf_op jit(solution)/shard_map/ppermute | solution.py:279
  9.5 6.1 %collective-permute-start.6 = (f32[64,128]{1,0:T(8,128)S(1)}, f32[64,128]{1,0:T(8,128)S(1)}, u32[]{:S(2)}, u32[]{:S(2)}) collective-permute-start(f32[64,128]{1,0:T(8,128)S(1)} %bitcast.4), channel_id=1, source_target_pairs={{0,3},{1,2},{2,1},{3,0},{4,7},{5,6},{6,5},{7,4},{8,11},{9,10},{10,... | collective-permute-start | bytes 98312 | tf_op jit(solution)/shard_map/ppermute | solution.py:302
  14.1 4.3 %collective-permute-start.5 = (f32[128,128]{1,0:T(8,128)S(1)}, f32[128,128]{1,0:T(8,128)S(1)}, u32[]{:S(2)}, u32[]{:S(2)}) collective-permute-start(f32[128,128]{1,0:T(8,128)S(1)} %bitcast.3), channel_id=1, source_target_pairs={{0,1},{1,0},{2,3},{3,2},{4,5},{5,4},{6,7},{7,6},{8,9},{9,8},{10,11... | collective-permute-start | bytes 196616 | tf_op jit(solution)/shard_map/ppermute | solution.py:283
  14.9 1.3 %collective-permute-start.7 = (f32[72,128]{1,0:T(8,128)S(1)}, f32[72,128]{1,0:T(8,128)S(1)}, u32[]{:S(2)}, u32[]{:S(2)}) collective-permute-start(f32[72,128]{1,0:T(8,128)S(1)} %shard_map.65), channel_id=1, source_target_pairs={{0,2},{2,0},{4,6},{6,4},{8,10},{10,8},{12,14},{14,12},{16,18},{18,... | collective-permute-start | bytes 110600 | tf_op jit(solution)/shard_map/ppermute | solution.py:279

commit v26 on v24

--- a/solution.py
+++ b/solution.py
@@ -71,7 +71,7 @@
 
 
 def product(one, other):
-    (one_high, one_low), (other_high, other_low) = split(one), split(other)
+    (one_high, one_low), (other_high, other_low) = one, other
 
     def dot(left, right):
         return jnp.dot(left, right, preferred_element_type=F32)
@@ -81,8 +81,13 @@
 
 def narrowed(rows, slab_ref):
     width = slab_ref.shape[0] - 8
-    full = product(rows[:, :width], slab_ref[:width, :])
-    slab_labels, own_labels = slab_ref[width:width + 1, :], row_labels(rows)
+    return residual(split(rows[:, :width]), row_labels(rows), slab_ref)
+
+
+def residual(rows, own_labels, slab_ref):
+    width = slab_ref.shape[0] - 8
+    full = product(rows, split(slab_ref[:width, :]))
+    slab_labels = slab_ref[width:width + 1, :]
     total = None
     for start in range(0, full.shape[1], LANES):
         part = slice(start, start + LANES)
@@ -152,11 +157,17 @@
     out_ref[...] = narrowed(rows_ref[count:, :], slab_ref)
 
 
-def both_kernel(rows_ref, twin_ref, two_ref, out_ref, send_ref):
+def ready_kernel(count, rows_ref, twin_ref, high_ref, low_ref, labels_ref):
+    width = high_ref.shape[1]
+    rows = jnp.concatenate([twin_ref[count:, :], rows_ref[count:, :]], axis=0)
+    high_ref[...], low_ref[...] = split(rows[:, :width])
+    labels_ref[...] = row_labels(rows)
+
+
+def both_kernel(high_ref, low_ref, labels_ref, two_ref, out_ref, send_ref):
     parts, half = send_ref.shape[0] + 1, send_ref.shape[1]
     sent = out_ref.shape[0]
-    rows = jnp.concatenate([twin_ref[2 * half:, :], rows_ref[2 * half:, :]], axis=0)
-    term = narrowed(rows, two_ref)
+    term = residual((high_ref[...], low_ref[...]), labels_ref[...], two_ref)
     for k in range(1, parts):
         send_ref[k - 1] = halved(term[2 * (k - 1) * half:2 * k * half])
     out_ref[...] = term[sent:]
@@ -234,13 +245,18 @@
     tiles = out.shape[2] // LANES
     rows = row_labels(rows_ref[:count, :])
     two, third = apart(pair_ref[...])
-    first = stored(2, 0, two + two_keep[...], rows, tiles_of(two_ref, width, tiles), out_ref, out, sems)
     labels = [
         jnp.where(second(), x, y) for x, y in zip(tiles_of(late_ref, width, tiles), tiles_of(mix_ref, width, tiles))
     ]
-    last = stored(jnp.where(odd(), 1, 3), 1, third + third_keep[...], rows, labels, out_ref, out, sems)
-    first.wait()
-    last.wait()
+    place = jnp.where(odd(), 1, 0)
+    for plane, term, plane_labels in (
+        (place, two + two_keep[...], tiles_of(two_ref, width, tiles)), (1 - place, third + third_keep[...], labels)
+    ):
+        for k, label in enumerate(plane_labels):
+            out[plane, :, k * LANES:(k + 1) * LANES] = jnp.where(rows == label, term, 0.0)
+    copy = pltpu.make_async_copy(out, out_ref.at[pl.ds(2 - place, 2)], sems.at[0])
+    copy.start()
+    copy.wait()
 
 
 def total_kernel(*refs):
@@ -316,9 +332,12 @@
     late = moved(after(own, own_keep), (1, -1, 1, 3))
     rest = whole(row_count - count, LANES)
     mix_term, = call(sent_kernel, [rest], (rows, mix), 0)
+    sent = 2 * (row_count - count)
+    ready = call(functools.partial(ready_kernel, count),
+                 [jax.ShapeDtypeStruct((sent, width), jnp.bfloat16)] * 2 + [whole(sent, LANES)], (rows, twin), 0)
     two_term, diagonal_send = call(
         both_kernel, [rest, whole(parts - 1, count // 2, LANES)],
-        (rows, twin, after(two, mix_term, *own_in)), 0)
+        (*ready, after(two, mix_term, *ready, *own_in)), 0)
     diagonal_in = [crossed(diagonal_send[k - 1], k) for k in range(1, parts)]
     pair_send, = call(pair_kernel, [whole(parts - 1, count, LANES)], (rows, late, two_term, mix_term),
                       0, 0, [pltpu.VMEM(rest.shape, F32)])

time: 18.8 us -> 18.7 us (level)
    pallas_call x13 -> x14, Pallas kernels: 6.21 us -> 6.31 us  [call(): pl.pallas_call(kernel, out_shape=out_shape, in_specs=[OFFCHIP if i < off...]
where the time goes in v26:
time: 18.7 us; the launch traced here: 18.6 us
  starting transfers between devices  8.45 us (45%)
  Pallas kernels  6.31 us (34%)
  waiting for transfers between devices  3.71 us (20%)
    pallas_call x14, Pallas kernels, call(): pl.pallas_call(kernel, out_shape=out_shape, in_specs=[OFFCHIP if i < off...  6.31 us
    ppermute x5, starting transfers between devices, moved(): lax.ppermute(array, 'blk', [(i, (i + steps[i % 4]) % blocks) for i in ran...  5.19 us
    ppermute x2, starting transfers between devices, exchanged(): lax.ppermute(array[k - 1], 'red', [(i, (i + k) % parts) for i in range(pa...  3.02 us
    ppermute x5, waiting for transfers between devices, moved(): lax.ppermute(array, 'blk', [(i, (i + steps[i % 4]) % blocks) for i in ran...  2.63 us
    ppermute x1, waiting for transfers between devices, crossed(): lax.ppermute(array, ('blk', 'red'), [(b * parts + r, c * parts + t) for (...  0.73 us
  transfers between devices with their start and end apart: 8, of which 5 were waited for; matrix products, arithmetic and copies ran while one was open for 0% of the time, Pallas kernels for 22%

profile of v26, /device:TPU:0, one launch (start us, length us, event | category | flops | bytes accessed | tf_op | source)
XLA Modules:
  0.0 18.6 jit_solution(17128229689673295965)
XLA Ops:
  0.0 1.4 %shard_map.55.slab_ref.own_ref = f32[200,256]{1,0:T(8,128)S(1)} custom-call(f32[256,768]{1,0:T(8,128)} %amp_ref.1, s32[1,256]{1,0:T(1,128)} %ij_ref.1, s32[1,768]{1,0:T(1,128)} %cd_ref.3), custom_call_target="tpu_custom_call" | custom-call | flops 786432 | tf_op jit(solution)/shard_map/pallas_call | solution.py:274
  1.4 3.0 %collective-permute-start = (f32[200,256]{1,0:T(8,128)S(1)}, f32[200,256]{1,0:T(8,128)S(1)}, u32[]{:S(2)}, u32[]{:S(2)}) collective-permute-start(f32[200,256]{1,0:T(8,128)S(1)} %shard_map.55.slab_ref.own_ref), channel_id=1, source_target_pairs={{0,4},{2,6},{4,8},{6,10},{8,12},{10,14},{12,16},{14,18},{16,20},{1... | collective-permute-start | bytes 614408 | tf_op jit(solution)/shard_map/ppermute | solution.py:295
  4.4 0.0 collective-permute-start.3
  4.4 1.3 %shard_map.57.rows_ref = f32[256,256]{1,0:T(8,128)S(1)} custom-call(f32[256,768]{1,0:T(8,128)} %v_ref, s32[1,256]{1,0:T(1,128)} %ab_ref.1, s32[1,768]{1,0:T(1,128)} %cd_ref.3), custom_call_target="tpu_custom_call" | custom-call | tf_op jit(solution)/shard_map/pallas_call | solution.py:274
  5.7 1.8 %collective-permute-start.2 = (f32[256,256]{1,0:T(8,128)S(1)}, f32[256,256]{1,0:T(8,128)S(1)}, u32[]{:S(2)}, u32[]{:S(2)}) collective-permute-start(f32[256,256]{1,0:T(8,128)S(1)} %shard_map.57.rows_ref), channel_id=1, source_target_pairs={{0,2},{2,0},{4,6},{6,4},{8,10},{10,8},{12,14},{14,12},{16,18},{18,... | collective-permute-start | bytes 786440 | tf_op jit(solution)/shard_map/ppermute | solution.py:295
  7.4 0.3 %shard_map.58 = (f32[128,128]{1,0:T(8,128)S(1)}, f32[1,64,128]{2,1,0:T(8,128)S(1)}) custom-call(f32[256,256]{1,0:T(8,128)S(1)} %shard_map.57.rows_ref, f32[200,256]{1,0:T(8,128)S(1)} %shard_map.55.slab_ref.own_ref), custom_call_target="tpu_custom_call" | custom-call | flops 9663676416 | tf_op jit(solution)/shard_map/pallas_call | solution.py:274
  7.8 0.1 collective-permute-start.1
  7.8 1.6 %collective-permute-start.4 = (f32[64,128]{1,0:T(8,128)S(1)}, f32[64,128]{1,0:T(8,128)S(1)}, u32[]{:S(2)}, u32[]{:S(2)}) collective-permute-start(f32[64,128]{1,0:T(8,128)S(1)} %bitcast.5), channel_id=1, source_target_pairs={{0,1},{1,0},{2,3},{3,2},{4,5},{5,4},{6,7},{7,6},{8,9},{9,8},{10,11... | collective-permute-start | bytes 98312 | tf_op jit(solution)/shard_map/ppermute | solution.py:299
  9.4 1.9 %collective-permute-done.3.slab_ref.mix_ref = f32[200,256]{1,0:T(8,128)S(1)} collective-permute-done((f32[200,256]{1,0:T(8,128)S(1)}, f32[200,256]{1,0:T(8,128)S(1)}, u32[]{:S(2)}, u32[]{:S(2)}) %collective-permute-start.3) | collective-permute-done | bytes 204832 | tf_op jit(solution)/shard_map/ppermute | solution.py:295
  11.4 0.3 %shard_map.60.mix_term = f32[128,128]{1,0:T(8,128)S(1)} custom-call(f32[256,256]{1,0:T(8,128)S(1)} %shard_map.57.rows_ref, f32[200,256]{1,0:T(8,128)S(1)} %collective-permute-done.3.slab_ref.mix_ref), custom_call_target="tpu_custom_call" | custom-call | tf_op jit(solution)/shard_map/pallas_call | solution.py:274
  11.7 0.1 shard_map.59
  11.8 0.1 collective-permute-done.4.refs_0_
  11.8 0.7 %collective-permute-done.two_ref = f32[200,256]{1,0:T(8,128)S(1)} collective-permute-done((f32[200,256]{1,0:T(8,128)S(1)}, f32[200,256]{1,0:T(8,128)S(1)}, u32[]{:S(2)}, u32[]{:S(2)}) %collective-permute-start) | collective-permute-done | bytes 204832 | tf_op jit(solution)/shard_map/ppermute | solution.py:295
  12.5 0.3 %shard_map.61 = (f32[128,128]{1,0:T(8,128)S(1)}, f32[1,64,128]{2,1,0:T(8,128)S(1)}) custom-call(bf16[256,192]{1,0:T(8,128)(2,1)S(1)} %get-tuple-element.22.high_ref, bf16[256,192]{1,0:T(8,128)(2,1)S(1)} %get-tuple-element.23.low_ref, f32[256,128]{1,0:T(8,128)S(1)} %get-tuple-element.24.labels_ref, f32[200,256]{1,0:T(8,128)S(1)} %collective-permute-done.two_ref), custom_call_target="tpu_custom_call" | custom-call | tf_op jit(solution)/shard_map/pallas_call | solution.py:274
  12.8 0.2 %collective-permute-start.6 = (f32[64,128]{1,0:T(8,128)S(1)}, f32[64,128]{1,0:T(8,128)S(1)}, u32[]{:S(2)}, u32[]{:S(2)}) collective-permute-start(f32[64,128]{1,0:T(8,128)S(1)} %bitcast.4), channel_id=1, source_target_pairs={{0,3},{1,2},{2,1},{3,0},{4,7},{5,6},{6,5},{7,4},{8,11},{9,10},{10,... | collective-permute-start | bytes 98312 | tf_op jit(solution)/shard_map/ppermute | solution.py:318
  13.1 1.4 %collective-permute-start.5 = (f32[128,128]{1,0:T(8,128)S(1)}, f32[128,128]{1,0:T(8,128)S(1)}, u32[]{:S(2)}, u32[]{:S(2)}) collective-permute-start(f32[128,128]{1,0:T(8,128)S(1)} %bitcast.3), channel_id=1, source_target_pairs={{0,1},{1,0},{2,3},{3,2},{4,5},{5,4},{6,7},{7,6},{8,9},{9,8},{10,11... | collective-permute-start | bytes 196616 | tf_op jit(solution)/shard_map/ppermute | solution.py:299
  14.6 0.3 %shard_map.66 = f32[72,128]{1,0:T(8,128)S(1)} custom-call(f32[256,256]{1,0:T(8,128)S(1)} %collective-permute-done.2.twin_ref, f32[200,256]{1,0:T(8,128)S(1)} %collective-permute-done.two_ref), custom_call_target="tpu_custom_call" | custom-call | tf_op jit(solution)/shard_map/pallas_call | solution.py:274
  14.8 0.4 %collective-permute-start.7 = (f32[72,128]{1,0:T(8,128)S(1)}, f32[72,128]{1,0:T(8,128)S(1)}, u32[]{:S(2)}, u32[]{:S(2)}) collective-permute-start(f32[72,128]{1,0:T(8,128)S(1)} %shard_map.66), channel_id=1, source_target_pairs={{0,2},{2,0},{4,6},{6,4},{8,10},{10,8},{12,14},{14,12},{16,18},{18,... | collective-permute-start | bytes 110600 | tf_op jit(solution)/shard_map/ppermute | solution.py:295
  15.2 0.6 %shard_map.63 = (f32[128,128]{1,0:T(8,128)S(1)}, f32[128,128]{1,0:T(8,128)S(1)}) custom-call(f32[256,256]{1,0:T(8,128)S(1)} %shard_map.57.rows_ref, f32[200,256]{1,0:T(8,128)S(1)} %collective-permute-done.two_ref, f32[200,256]{1,0:T(8,128)S(1)} %collective-permute-done.3.slab_ref.mix_ref, f32[200,256]{1,0:T(8,128)S(1)} %collective-permute-done.1.late_ref), custom_call_target="tpu_custom_call" | custom-call | tf_op jit(solution)/shard_map/pallas_call | solution.py:274
  15.8 0.7 %collective-permute-done.6.refs_0_ = f32[64,128]{1,0:T(8,128)S(1)} collective-permute-done((f32[64,128]{1,0:T(8,128)S(1)}, f32[64,128]{1,0:T(8,128)S(1)}, u32[]{:S(2)}, u32[]{:S(2)}) %collective-permute-start.6) | collective-permute-done | bytes 32800 | tf_op jit(solution)/shard_map/ppermute | solution.py:318
  16.5 0.1 shard_map.65.crossed_ref
  16.6 0.8 %shard_map.67.begun_ref = f32[4,128,256]{2,1,0:T(8,128)} custom-call(f32[256,256]{1,0:T(8,128)S(1)} %shard_map.57.rows_ref, f32[128,128]{1,0:T(8,128)S(1)} %get-tuple-element.20.own_keep, f32[8,256]{1,0:T(8,128)S(1)} %shard_map.56.own_labels, f32[128,128]{1,0:T(8,128)S(1)} %shard_map.65.crossed_ref, f32[72,128]{1,0:T(8,128)S(1)} %collective-permute-done.7.core_ref, ...), custom_call_target="tpu_custom_call" | custom-call | tf_op jit(solution)/shard_map/pallas_call | solution.py:274
  17.4 0.3 %collective-permute-done.5.refs_0_ = f32[128,128]{1,0:T(8,128)S(1)} collective-permute-done((f32[128,128]{1,0:T(8,128)S(1)}, f32[128,128]{1,0:T(8,128)S(1)}, u32[]{:S(2)}, u32[]{:S(2)}) %collective-permute-start.5) | collective-permute-done | bytes 65568 | tf_op jit(solution)/shard_map/ppermute | solution.py:299
  17.7 0.8 %shard_map.68 = f32[4,128,256]{2,1,0:T(8,128)} custom-call(f32[256,256]{1,0:T(8,128)S(1)} %shard_map.57.rows_ref, f32[128,128]{1,0:T(8,128)S(1)} %get-tuple-element.30.two_keep, f32[128,128]{1,0:T(8,128)S(1)} %get-tuple-element.31.third_keep, f32[200,256]{1,0:T(8,128)S(1)} %collective-permute-done.two_ref, ...), custom_call_target="tpu_custom_call", output_to_operand_aliasing={{}: (7, {})} | custom-call | tf_op jit(solution)/shard_map/pallas_call | solution.py:274
  (6 shorter events, 0.0 us)
Async XLA Ops:
  1.4 11.1 %collective-permute-start = (f32[200,256]{1,0:T(8,128)S(1)}, f32[200,256]{1,0:T(8,128)S(1)}, u32[]{:S(2)}, u32[]{:S(2)}) collective-permute-start(f32[200,256]{1,0:T(8,128)S(1)} %shard_map.55.slab_ref.own_ref), channel_id=1, source_target_pairs={{0,4},{2,6},{4,8},{6,10},{8,12},{10,14},{12,16},{14,18},{16,20},{1... | collective-permute-start | bytes 614408 | tf_op jit(solution)/shard_map/ppermute | solution.py:295
  4.4 7.0 %collective-permute-start.3 = (f32[200,256]{1,0:T(8,128)S(1)}, f32[200,256]{1,0:T(8,128)S(1)}, u32[]{:S(2)}, u32[]{:S(2)}) collective-permute-start(f32[200,256]{1,0:T(8,128)S(1)} %shard_map.55.slab_ref.own_ref), channel_id=1, source_target_pairs={{0,2},{2,8},{4,6},{6,4},{8,10},{10,16},{12,14},{14,12},{16,18},{18... | collective-permute-start | bytes 614408 | tf_op jit(solution)/shard_map/ppermute | solution.py:295
  5.7 6.0 %collective-permute-start.2 = (f32[256,256]{1,0:T(8,128)S(1)}, f32[256,256]{1,0:T(8,128)S(1)}, u32[]{:S(2)}, u32[]{:S(2)}) collective-permute-start(f32[256,256]{1,0:T(8,128)S(1)} %shard_map.57.rows_ref), channel_id=1, source_target_pairs={{0,2},{2,0},{4,6},{6,4},{8,10},{10,8},{12,14},{14,12},{16,18},{18,... | collective-permute-start | bytes 786440 | tf_op jit(solution)/shard_map/ppermute | solution.py:295
  7.8 5.3 %collective-permute-start.1 = (f32[200,256]{1,0:T(8,128)S(1)}, f32[200,256]{1,0:T(8,128)S(1)}, u32[]{:S(2)}, u32[]{:S(2)}) collective-permute-start(f32[200,256]{1,0:T(8,128)S(1)} %shard_map.55.slab_ref.own_ref), channel_id=1, source_target_pairs={{0,2},{2,0},{4,6},{6,12},{8,10},{10,8},{12,14},{14,20},{16,18},{18... | collective-permute-start | bytes 614408 | tf_op jit(solution)/shard_map/ppermute | solution.py:295
  7.8 4.0 %collective-permute-start.4 = (f32[64,128]{1,0:T(8,128)S(1)}, f32[64,128]{1,0:T(8,128)S(1)}, u32[]{:S(2)}, u32[]{:S(2)}) collective-permute-start(f32[64,128]{1,0:T(8,128)S(1)} %bitcast.5), channel_id=1, source_target_pairs={{0,1},{1,0},{2,3},{3,2},{4,5},{5,4},{6,7},{7,6},{8,9},{9,8},{10,11... | collective-permute-start | bytes 98312 | tf_op jit(solution)/shard_map/ppermute | solution.py:299
  12.8 3.7 %collective-permute-start.6 = (f32[64,128]{1,0:T(8,128)S(1)}, f32[64,128]{1,0:T(8,128)S(1)}, u32[]{:S(2)}, u32[]{:S(2)}) collective-permute-start(f32[64,128]{1,0:T(8,128)S(1)} %bitcast.4), channel_id=1, source_target_pairs={{0,3},{1,2},{2,1},{3,0},{4,7},{5,6},{6,5},{7,4},{8,11},{9,10},{10,... | collective-permute-start | bytes 98312 | tf_op jit(solution)/shard_map/ppermute | solution.py:318
  13.1 4.6 %collective-permute-start.5 = (f32[128,128]{1,0:T(8,128)S(1)}, f32[128,128]{1,0:T(8,128)S(1)}, u32[]{:S(2)}, u32[]{:S(2)}) collective-permute-start(f32[128,128]{1,0:T(8,128)S(1)} %bitcast.3), channel_id=1, source_target_pairs={{0,1},{1,0},{2,3},{3,2},{4,5},{5,4},{6,7},{7,6},{8,9},{9,8},{10,11... | collective-permute-start | bytes 196616 | tf_op jit(solution)/shard_map/ppermute | solution.py:299
  14.8 1.8 %collective-permute-start.7 = (f32[72,128]{1,0:T(8,128)S(1)}, f32[72,128]{1,0:T(8,128)S(1)}, u32[]{:S(2)}, u32[]{:S(2)}) collective-permute-start(f32[72,128]{1,0:T(8,128)S(1)} %shard_map.66), channel_id=1, source_target_pairs={{0,2},{2,0},{4,6},{6,4},{8,10},{10,8},{12,14},{14,12},{16,18},{18,... | collective-permute-start | bytes 110600 | tf_op jit(solution)/shard_map/ppermute | solution.py:295

commit v27 on v26

--- a/solution.py
+++ b/solution.py
@@ -329,7 +329,7 @@
     own_keep, own_send = call(
         own_kernel, [whole(count, LANES), whole(parts - 1, count // 2, LANES)], (rows, own), 64 * one_product)
     own_in = exchanged(own_send)
-    late = moved(after(own, own_keep), (1, -1, 1, 3))
+    late = moved(after(own, own_keep, twin), (1, -1, 1, 3))
     rest = whole(row_count - count, LANES)
     mix_term, = call(sent_kernel, [rest], (rows, mix), 0)
     sent = 2 * (row_count - count)

time: 18.7 us -> 19.5 us (1.043)
  waiting for transfers between devices: 3.71 us -> 4.23 us
  starting transfers between devices: 8.45 us -> 8.7 us
    ppermute x5, waiting for transfers between devices: 2.63 us -> 1.7 us  [moved(): lax.ppermute(array, 'blk', [(i, (i + steps[i % 4]) % blocks) for i in ran...]
    ppermute x2, waiting for transfers between devices: 0.35 us -> 1.24 us  [exchanged(): lax.ppermute(array[k - 1], 'red', [(i, (i + k) % parts) for i in range(pa...]
    ppermute x1, waiting for transfers between devices: 0.73 us -> 1.3 us  [crossed(): lax.ppermute(array, ('blk', 'red'), [(b * parts + r, c * parts + t) for (...]
    ppermute x5, starting transfers between devices: 5.19 us -> 5.5 us  [moved(): lax.ppermute(array, 'blk', [(i, (i + steps[i % 4]) % blocks) for i in ran...]
    ppermute x2, starting transfers between devices: 3.02 us -> 2.73 us  [exchanged(): lax.ppermute(array[k - 1], 'red', [(i, (i + k) % parts) for i in range(pa...]
    ppermute x1, starting transfers between devices: 0.24 us -> 0.47 us  [crossed(): lax.ppermute(array, ('blk', 'red'), [(b * parts + r, c * parts + t) for (...]
  transfers between devices with their start and end apart: 8 -> 8, of which waited for: 5 -> 5; matrix products, arithmetic and copies ran while one was open for 0% -> 0% of each run, Pallas kernels for 22% -> 21%
where the time goes in v27:
time: 19.5 us; the launch traced here: 19.3 us
  starting transfers between devices  8.7 us (45%)
  Pallas kernels  6.31 us (32%)
  waiting for transfers between devices  4.23 us (22%)
    pallas_call x14, Pallas kernels, call(): pl.pallas_call(kernel, out_shape=out_shape, in_specs=[OFFCHIP if i < off...  6.31 us
    ppermute x5, starting transfers between devices, moved(): lax.ppermute(array, 'blk', [(i, (i + steps[i % 4]) % blocks) for i in ran...  5.5 us
    ppermute x2, starting transfers between devices, exchanged(): lax.ppermute(array[k - 1], 'red', [(i, (i + k) % parts) for i in range(pa...  2.73 us
    ppermute x5, waiting for transfers between devices, moved(): lax.ppermute(array, 'blk', [(i, (i + steps[i % 4]) % blocks) for i in ran...  1.7 us
    ppermute x1, waiting for transfers between devices, crossed(): lax.ppermute(array, ('blk', 'red'), [(b * parts + r, c * parts + t) for (...  1.3 us
    ppermute x2, waiting for transfers between devices, exchanged(): lax.ppermute(array[k - 1], 'red', [(i, (i + k) % parts) for i in range(pa...  1.24 us
    ppermute x1, starting transfers between devices, crossed(): lax.ppermute(array, ('blk', 'red'), [(b * parts + r, c * parts + t) for (...  0.47 us
  transfers between devices with their start and end apart: 8, of which 5 were waited for; matrix products, arithmetic and copies ran while one was open for 0% of the time, Pallas kernels for 21%

profile of v27, /device:TPU:0, one launch (start us, length us, event | category | flops | bytes accessed | tf_op | source)
XLA Modules:
  0.0 19.3 jit_solution(8732289544511434189)
XLA Ops:
  0.0 1.4 %shard_map.55.slab_ref.own_ref = f32[200,256]{1,0:T(8,128)S(1)} custom-call(f32[256,768]{1,0:T(8,128)} %amp_ref.1, s32[1,256]{1,0:T(1,128)} %ij_ref.1, s32[1,768]{1,0:T(1,128)} %cd_ref.3), custom_call_target="tpu_custom_call" | custom-call | flops 786432 | tf_op jit(solution)/shard_map/pallas_call | solution.py:274
  1.4 3.0 %collective-permute-start = (f32[200,256]{1,0:T(8,128)S(1)}, f32[200,256]{1,0:T(8,128)S(1)}, u32[]{:S(2)}, u32[]{:S(2)}) collective-permute-start(f32[200,256]{1,0:T(8,128)S(1)} %shard_map.55.slab_ref.own_ref), channel_id=1, source_target_pairs={{0,4},{2,6},{4,8},{6,10},{8,12},{10,14},{12,16},{14,18},{16,20},{1... | collective-permute-start | bytes 614408 | tf_op jit(solution)/shard_map/ppermute | solution.py:295
  4.4 0.0 collective-permute-start.3
  4.4 1.3 %shard_map.57.rows_ref = f32[256,256]{1,0:T(8,128)S(1)} custom-call(f32[256,768]{1,0:T(8,128)} %v_ref, s32[1,256]{1,0:T(1,128)} %ab_ref.1, s32[1,768]{1,0:T(1,128)} %cd_ref.3), custom_call_target="tpu_custom_call" | custom-call | tf_op jit(solution)/shard_map/pallas_call | solution.py:274
  5.7 1.8 %collective-permute-start.1 = (f32[256,256]{1,0:T(8,128)S(1)}, f32[256,256]{1,0:T(8,128)S(1)}, u32[]{:S(2)}, u32[]{:S(2)}) collective-permute-start(f32[256,256]{1,0:T(8,128)S(1)} %shard_map.57.rows_ref), channel_id=1, source_target_pairs={{0,2},{2,0},{4,6},{6,4},{8,10},{10,8},{12,14},{14,12},{16,18},{18,... | collective-permute-start | bytes 786440 | tf_op jit(solution)/shard_map/ppermute | solution.py:295
  7.4 0.3 %shard_map.58 = (f32[128,128]{1,0:T(8,128)S(1)}, f32[1,64,128]{2,1,0:T(8,128)S(1)}) custom-call(f32[256,256]{1,0:T(8,128)S(1)} %shard_map.57.rows_ref, f32[200,256]{1,0:T(8,128)S(1)} %shard_map.55.slab_ref.own_ref), custom_call_target="tpu_custom_call" | custom-call | flops 9663676416 | tf_op jit(solution)/shard_map/pallas_call | solution.py:274
  7.8 0.8 %collective-permute-done.1.twin_ref = f32[256,256]{1,0:T(8,128)S(1)} collective-permute-done((f32[256,256]{1,0:T(8,128)S(1)}, f32[256,256]{1,0:T(8,128)S(1)}, u32[]{:S(2)}, u32[]{:S(2)}) %collective-permute-start.1) | collective-permute-done | bytes 262176 | tf_op jit(solution)/shard_map/ppermute | solution.py:295
  8.6 0.4 %collective-permute-start.2 = (f32[200,256]{1,0:T(8,128)S(1)}, f32[200,256]{1,0:T(8,128)S(1)}, u32[]{:S(2)}, u32[]{:S(2)}) collective-permute-start(f32[200,256]{1,0:T(8,128)S(1)} %shard_map.55.slab_ref.own_ref), channel_id=1, source_target_pairs={{0,2},{2,0},{4,6},{6,12},{8,10},{10,8},{12,14},{14,20},{16,18},{18... | collective-permute-start | bytes 614408 | tf_op jit(solution)/shard_map/ppermute | solution.py:295
  9.0 1.5 %collective-permute-start.4 = (f32[64,128]{1,0:T(8,128)S(1)}, f32[64,128]{1,0:T(8,128)S(1)}, u32[]{:S(2)}, u32[]{:S(2)}) collective-permute-start(f32[64,128]{1,0:T(8,128)S(1)} %bitcast.5), channel_id=1, source_target_pairs={{0,1},{1,0},{2,3},{3,2},{4,5},{5,4},{6,7},{7,6},{8,9},{9,8},{10,11... | collective-permute-start | bytes 98312 | tf_op jit(solution)/shard_map/ppermute | solution.py:299
  10.5 0.9 %collective-permute-done.3.slab_ref.mix_ref = f32[200,256]{1,0:T(8,128)S(1)} collective-permute-done((f32[200,256]{1,0:T(8,128)S(1)}, f32[200,256]{1,0:T(8,128)S(1)}, u32[]{:S(2)}, u32[]{:S(2)}) %collective-permute-start.3) | collective-permute-done | bytes 204832 | tf_op jit(solution)/shard_map/ppermute | solution.py:295
  11.4 0.3 %shard_map.60.mix_term = f32[128,128]{1,0:T(8,128)S(1)} custom-call(f32[256,256]{1,0:T(8,128)S(1)} %shard_map.57.rows_ref, f32[200,256]{1,0:T(8,128)S(1)} %collective-permute-done.3.slab_ref.mix_ref), custom_call_target="tpu_custom_call" | custom-call | tf_op jit(solution)/shard_map/pallas_call | solution.py:274
  11.7 0.1 shard_map.59
  11.8 1.1 %collective-permute-done.4.refs_0_ = f32[64,128]{1,0:T(8,128)S(1)} collective-permute-done((f32[64,128]{1,0:T(8,128)S(1)}, f32[64,128]{1,0:T(8,128)S(1)}, u32[]{:S(2)}, u32[]{:S(2)}) %collective-permute-start.4) | collective-permute-done | bytes 32800 | tf_op jit(solution)/shard_map/ppermute | solution.py:299
  12.9 0.3 %shard_map.61 = (f32[128,128]{1,0:T(8,128)S(1)}, f32[1,64,128]{2,1,0:T(8,128)S(1)}) custom-call(bf16[256,192]{1,0:T(8,128)(2,1)S(1)} %get-tuple-element.22.high_ref, bf16[256,192]{1,0:T(8,128)(2,1)S(1)} %get-tuple-element.23.low_ref, f32[256,128]{1,0:T(8,128)S(1)} %get-tuple-element.24.labels_ref, f32[200,256]{1,0:T(8,128)S(1)} %collective-permute-done.two_ref), custom_call_target="tpu_custom_call" | custom-call | tf_op jit(solution)/shard_map/pallas_call | solution.py:274
  13.2 0.5 %collective-permute-start.6 = (f32[64,128]{1,0:T(8,128)S(1)}, f32[64,128]{1,0:T(8,128)S(1)}, u32[]{:S(2)}, u32[]{:S(2)}) collective-permute-start(f32[64,128]{1,0:T(8,128)S(1)} %bitcast.4), channel_id=1, source_target_pairs={{0,3},{1,2},{2,1},{3,0},{4,7},{5,6},{6,5},{7,4},{8,11},{9,10},{10,... | collective-permute-start | bytes 98312 | tf_op jit(solution)/shard_map/ppermute | solution.py:318
  13.7 1.2 %collective-permute-start.5 = (f32[128,128]{1,0:T(8,128)S(1)}, f32[128,128]{1,0:T(8,128)S(1)}, u32[]{:S(2)}, u32[]{:S(2)}) collective-permute-start(f32[128,128]{1,0:T(8,128)S(1)} %bitcast.3), channel_id=1, source_target_pairs={{0,1},{1,0},{2,3},{3,2},{4,5},{5,4},{6,7},{7,6},{8,9},{9,8},{10,11... | collective-permute-start | bytes 196616 | tf_op jit(solution)/shard_map/ppermute | solution.py:299
  14.9 0.3 %shard_map.66 = f32[72,128]{1,0:T(8,128)S(1)} custom-call(f32[256,256]{1,0:T(8,128)S(1)} %collective-permute-done.1.twin_ref, f32[200,256]{1,0:T(8,128)S(1)} %collective-permute-done.two_ref), custom_call_target="tpu_custom_call" | custom-call | tf_op jit(solution)/shard_map/pallas_call | solution.py:274
  15.2 0.4 %collective-permute-start.7 = (f32[72,128]{1,0:T(8,128)S(1)}, f32[72,128]{1,0:T(8,128)S(1)}, u32[]{:S(2)}, u32[]{:S(2)}) collective-permute-start(f32[72,128]{1,0:T(8,128)S(1)} %shard_map.66), channel_id=1, source_target_pairs={{0,2},{2,0},{4,6},{6,4},{8,10},{10,8},{12,14},{14,12},{16,18},{18,... | collective-permute-start | bytes 110600 | tf_op jit(solution)/shard_map/ppermute | solution.py:295
  15.6 1.3 %collective-permute-done.6.refs_0_ = f32[64,128]{1,0:T(8,128)S(1)} collective-permute-done((f32[64,128]{1,0:T(8,128)S(1)}, f32[64,128]{1,0:T(8,128)S(1)}, u32[]{:S(2)}, u32[]{:S(2)}) %collective-permute-start.6) | collective-permute-done | bytes 32800 | tf_op jit(solution)/shard_map/ppermute | solution.py:318
  16.9 0.1 shard_map.65.crossed_ref
  17.0 0.6 %shard_map.63 = (f32[128,128]{1,0:T(8,128)S(1)}, f32[128,128]{1,0:T(8,128)S(1)}) custom-call(f32[256,256]{1,0:T(8,128)S(1)} %shard_map.57.rows_ref, f32[200,256]{1,0:T(8,128)S(1)} %collective-permute-done.two_ref, f32[200,256]{1,0:T(8,128)S(1)} %collective-permute-done.3.slab_ref.mix_ref, f32[200,256]{1,0:T(8,128)S(1)} %collective-permute-done.2.late_ref), custom_call_target="tpu_custom_call" | custom-call | tf_op jit(solution)/shard_map/pallas_call | solution.py:274
  17.6 0.8 %shard_map.67.begun_ref = f32[4,128,256]{2,1,0:T(8,128)} custom-call(f32[256,256]{1,0:T(8,128)S(1)} %shard_map.57.rows_ref, f32[128,128]{1,0:T(8,128)S(1)} %get-tuple-element.20.own_keep, f32[8,256]{1,0:T(8,128)S(1)} %shard_map.56.own_labels, f32[128,128]{1,0:T(8,128)S(1)} %shard_map.65.crossed_ref, f32[72,128]{1,0:T(8,128)S(1)} %collective-permute-done.7.core_ref, ...), custom_call_target="tpu_custom_call" | custom-call | tf_op jit(solution)/shard_map/pallas_call | solution.py:274
  18.4 0.1 collective-permute-done.5.refs_0_
  18.5 0.8 %shard_map.68 = f32[4,128,256]{2,1,0:T(8,128)} custom-call(f32[256,256]{1,0:T(8,128)S(1)} %shard_map.57.rows_ref, f32[128,128]{1,0:T(8,128)S(1)} %get-tuple-element.30.two_keep, f32[128,128]{1,0:T(8,128)S(1)} %get-tuple-element.31.third_keep, f32[200,256]{1,0:T(8,128)S(1)} %collective-permute-done.two_ref, ...), custom_call_target="tpu_custom_call", output_to_operand_aliasing={{}: (7, {})} | custom-call | tf_op jit(solution)/shard_map/pallas_call | solution.py:274
  (6 shorter events, 0.0 us)
Async XLA Ops:
  1.4 11.5 %collective-permute-start = (f32[200,256]{1,0:T(8,128)S(1)}, f32[200,256]{1,0:T(8,128)S(1)}, u32[]{:S(2)}, u32[]{:S(2)}) collective-permute-start(f32[200,256]{1,0:T(8,128)S(1)} %shard_map.55.slab_ref.own_ref), channel_id=1, source_target_pairs={{0,4},{2,6},{4,8},{6,10},{8,12},{10,14},{12,16},{14,18},{16,20},{1... | collective-permute-start | bytes 614408 | tf_op jit(solution)/shard_map/ppermute | solution.py:295
  4.4 7.0 %collective-permute-start.3 = (f32[200,256]{1,0:T(8,128)S(1)}, f32[200,256]{1,0:T(8,128)S(1)}, u32[]{:S(2)}, u32[]{:S(2)}) collective-permute-start(f32[200,256]{1,0:T(8,128)S(1)} %shard_map.55.slab_ref.own_ref), channel_id=1, source_target_pairs={{0,2},{2,8},{4,6},{6,4},{8,10},{10,16},{12,14},{14,12},{16,18},{18... | collective-permute-start | bytes 614408 | tf_op jit(solution)/shard_map/ppermute | solution.py:295
  5.7 2.9 %collective-permute-start.1 = (f32[256,256]{1,0:T(8,128)S(1)}, f32[256,256]{1,0:T(8,128)S(1)}, u32[]{:S(2)}, u32[]{:S(2)}) collective-permute-start(f32[256,256]{1,0:T(8,128)S(1)} %shard_map.57.rows_ref), channel_id=1, source_target_pairs={{0,2},{2,0},{4,6},{6,4},{8,10},{10,8},{12,14},{14,12},{16,18},{18,... | collective-permute-start | bytes 786440 | tf_op jit(solution)/shard_map/ppermute | solution.py:295
  8.6 5.1 %collective-permute-start.2 = (f32[200,256]{1,0:T(8,128)S(1)}, f32[200,256]{1,0:T(8,128)S(1)}, u32[]{:S(2)}, u32[]{:S(2)}) collective-permute-start(f32[200,256]{1,0:T(8,128)S(1)} %shard_map.55.slab_ref.own_ref), channel_id=1, source_target_pairs={{0,2},{2,0},{4,6},{6,12},{8,10},{10,8},{12,14},{14,20},{16,18},{18... | collective-permute-start | bytes 614408 | tf_op jit(solution)/shard_map/ppermute | solution.py:295
  9.0 3.9 %collective-permute-start.4 = (f32[64,128]{1,0:T(8,128)S(1)}, f32[64,128]{1,0:T(8,128)S(1)}, u32[]{:S(2)}, u32[]{:S(2)}) collective-permute-start(f32[64,128]{1,0:T(8,128)S(1)} %bitcast.5), channel_id=1, source_target_pairs={{0,1},{1,0},{2,3},{3,2},{4,5},{5,4},{6,7},{7,6},{8,9},{9,8},{10,11... | collective-permute-start | bytes 98312 | tf_op jit(solution)/shard_map/ppermute | solution.py:299
  13.2 3.7 %collective-permute-start.6 = (f32[64,128]{1,0:T(8,128)S(1)}, f32[64,128]{1,0:T(8,128)S(1)}, u32[]{:S(2)}, u32[]{:S(2)}) collective-permute-start(f32[64,128]{1,0:T(8,128)S(1)} %bitcast.4), channel_id=1, source_target_pairs={{0,3},{1,2},{2,1},{3,0},{4,7},{5,6},{6,5},{7,4},{8,11},{9,10},{10,... | collective-permute-start | bytes 98312 | tf_op jit(solution)/shard_map/ppermute | solution.py:318
  13.7 4.8 %collective-permute-start.5 = (f32[128,128]{1,0:T(8,128)S(1)}, f32[128,128]{1,0:T(8,128)S(1)}, u32[]{:S(2)}, u32[]{:S(2)}) collective-permute-start(f32[128,128]{1,0:T(8,128)S(1)} %bitcast.3), channel_id=1, source_target_pairs={{0,1},{1,0},{2,3},{3,2},{4,5},{5,4},{6,7},{7,6},{8,9},{9,8},{10,11... | collective-permute-start | bytes 196616 | tf_op jit(solution)/shard_map/ppermute | solution.py:299
  15.2 2.3 %collective-permute-start.7 = (f32[72,128]{1,0:T(8,128)S(1)}, f32[72,128]{1,0:T(8,128)S(1)}, u32[]{:S(2)}, u32[]{:S(2)}) collective-permute-start(f32[72,128]{1,0:T(8,128)S(1)} %shard_map.66), channel_id=1, source_target_pairs={{0,2},{2,0},{4,6},{6,4},{8,10},{10,8},{12,14},{14,12},{16,18},{18,... | collective-permute-start | bytes 110600 | tf_op jit(solution)/shard_map/ppermute | solution.py:295

commit v28 on v27

--- a/solution.py
+++ b/solution.py
@@ -329,7 +329,7 @@
     own_keep, own_send = call(
         own_kernel, [whole(count, LANES), whole(parts - 1, count // 2, LANES)], (rows, own), 64 * one_product)
     own_in = exchanged(own_send)
-    late = moved(after(own, own_keep, twin), (1, -1, 1, 3))
+    late = moved(after(own, rows), (1, -1, 1, 3))
     rest = whole(row_count - count, LANES)
     mix_term, = call(sent_kernel, [rest], (rows, mix), 0)
     sent = 2 * (row_count - count)

time: 19.5 us -> 18.9 us (0.969)
  waiting for transfers between devices: 4.23 us -> 3.8 us
  starting transfers between devices: 8.7 us -> 8.43 us
    ppermute x5, waiting for transfers between devices: 1.7 us -> 3.03 us  [moved(): lax.ppermute(array, 'blk', [(i, (i + steps[i % 4]) % blocks) for i in ran...]
    ppermute x2, waiting for transfers between devices: 1.24 us -> 0.05 us  [exchanged(): lax.ppermute(array[k - 1], 'red', [(i, (i + k) % parts) for i in range(pa...]
    ppermute x1, waiting for transfers between devices: 1.3 us -> 0.72 us  [crossed(): lax.ppermute(array, ('blk', 'red'), [(b * parts + r, c * parts + t) for (...]
    ppermute x2, starting transfers between devices: 2.73 us -> 3.17 us  [exchanged(): lax.ppermute(array[k - 1], 'red', [(i, (i + k) % parts) for i in range(pa...]
    ppermute x1, starting transfers between devices: 0.47 us -> 0.07 us  [crossed(): lax.ppermute(array, ('blk', 'red'), [(b * parts + r, c * parts + t) for (...]
    ppermute x5, starting transfers between devices: 5.5 us -> 5.19 us  [moved(): lax.ppermute(array, 'blk', [(i, (i + steps[i % 4]) % blocks) for i in ran...]
  transfers between devices with their start and end apart: 8 -> 8, of which waited for: 5 -> 3; matrix products, arithmetic and copies ran while one was open for 0% -> 0% of each run, Pallas kernels for 21% -> 22%
where the time goes in v28:
time: 18.9 us; the launch traced here: 18.7 us
  starting transfers between devices  8.43 us (45%)
  Pallas kernels  6.31 us (33%)
  waiting for transfers between devices  3.8 us (20%)
    pallas_call x14, Pallas kernels, call(): pl.pallas_call(kernel, out_shape=out_shape, in_specs=[OFFCHIP if i < off...  6.31 us
    ppermute x5, starting transfers between devices, moved(): lax.ppermute(array, 'blk', [(i, (i + steps[i % 4]) % blocks) for i in ran...  5.19 us
    ppermute x2, starting transfers between devices, exchanged(): lax.ppermute(array[k - 1], 'red', [(i, (i + k) % parts) for i in range(pa...  3.17 us
    ppermute x5, waiting for transfers between devices, moved(): lax.ppermute(array, 'blk', [(i, (i + steps[i % 4]) % blocks) for i in ran...  3.03 us
    ppermute x1, waiting for transfers between devices, crossed(): lax.ppermute(array, ('blk', 'red'), [(b * parts + r, c * parts + t) for (...  0.72 us
  transfers between devices with their start and end apart: 8, of which 3 were waited for; matrix products, arithmetic and copies ran while one was open for 0% of the time, Pallas kernels for 22%

profile of v28, /device:TPU:0, one launch (start us, length us, event | category | flops | bytes accessed | tf_op | source)
XLA Modules:
  0.0 18.7 jit_solution(17855571114937932672)
XLA Ops:
  0.0 1.4 %shard_map.55.slab_ref.own_ref = f32[200,256]{1,0:T(8,128)S(1)} custom-call(f32[256,768]{1,0:T(8,128)} %amp_ref.1, s32[1,256]{1,0:T(1,128)} %ij_ref.1, s32[1,768]{1,0:T(1,128)} %cd_ref.3), custom_call_target="tpu_custom_call" | custom-call | flops 786432 | tf_op jit(solution)/shard_map/pallas_call | solution.py:274
  1.4 3.0 %collective-permute-start = (f32[200,256]{1,0:T(8,128)S(1)}, f32[200,256]{1,0:T(8,128)S(1)}, u32[]{:S(2)}, u32[]{:S(2)}) collective-permute-start(f32[200,256]{1,0:T(8,128)S(1)} %shard_map.55.slab_ref.own_ref), channel_id=1, source_target_pairs={{0,4},{2,6},{4,8},{6,10},{8,12},{10,14},{12,16},{14,18},{16,20},{1... | collective-permute-start | bytes 614408 | tf_op jit(solution)/shard_map/ppermute | solution.py:295
  4.4 1.3 %shard_map.57.rows_ref = f32[256,256]{1,0:T(8,128)S(1)} custom-call(f32[256,768]{1,0:T(8,128)} %v_ref, s32[1,256]{1,0:T(1,128)} %ab_ref.1, s32[1,768]{1,0:T(1,128)} %cd_ref.3), custom_call_target="tpu_custom_call" | custom-call | tf_op jit(solution)/shard_map/pallas_call | solution.py:274
  5.7 1.8 %collective-permute-start.2 = (f32[256,256]{1,0:T(8,128)S(1)}, f32[256,256]{1,0:T(8,128)S(1)}, u32[]{:S(2)}, u32[]{:S(2)}) collective-permute-start(f32[256,256]{1,0:T(8,128)S(1)} %shard_map.57.rows_ref), channel_id=1, source_target_pairs={{0,2},{2,0},{4,6},{6,4},{8,10},{10,8},{12,14},{14,12},{16,18},{18,... | collective-permute-start | bytes 786440 | tf_op jit(solution)/shard_map/ppermute | solution.py:295
  7.4 0.1 collective-permute-start.1
  7.5 0.3 %shard_map.60 = (f32[128,128]{1,0:T(8,128)S(1)}, f32[1,64,128]{2,1,0:T(8,128)S(1)}) custom-call(f32[256,256]{1,0:T(8,128)S(1)} %shard_map.57.rows_ref, f32[200,256]{1,0:T(8,128)S(1)} %shard_map.55.slab_ref.own_ref), custom_call_target="tpu_custom_call" | custom-call | flops 9663676416 | tf_op jit(solution)/shard_map/pallas_call | solution.py:274
  7.8 1.6 %collective-permute-start.4 = (f32[64,128]{1,0:T(8,128)S(1)}, f32[64,128]{1,0:T(8,128)S(1)}, u32[]{:S(2)}, u32[]{:S(2)}) collective-permute-start(f32[64,128]{1,0:T(8,128)S(1)} %bitcast.5), channel_id=1, source_target_pairs={{0,1},{1,0},{2,3},{3,2},{4,5},{5,4},{6,7},{7,6},{8,9},{9,8},{10,11... | collective-permute-start | bytes 98312 | tf_op jit(solution)/shard_map/ppermute | solution.py:299
  9.4 1.9 %collective-permute-done.3.slab_ref.mix_ref = f32[200,256]{1,0:T(8,128)S(1)} collective-permute-done((f32[200,256]{1,0:T(8,128)S(1)}, f32[200,256]{1,0:T(8,128)S(1)}, u32[]{:S(2)}, u32[]{:S(2)}) %collective-permute-start.3) | collective-permute-done | bytes 204832 | tf_op jit(solution)/shard_map/ppermute | solution.py:295
  11.4 0.3 %shard_map.59.mix_term = f32[128,128]{1,0:T(8,128)S(1)} custom-call(f32[256,256]{1,0:T(8,128)S(1)} %shard_map.57.rows_ref, f32[200,256]{1,0:T(8,128)S(1)} %collective-permute-done.3.slab_ref.mix_ref), custom_call_target="tpu_custom_call" | custom-call | tf_op jit(solution)/shard_map/pallas_call | solution.py:274
  11.7 0.0 collective-permute-done.2.twin_ref
  11.7 0.1 shard_map.58
  11.8 0.1 collective-permute-done.4.refs_0_
  11.8 1.1 %collective-permute-done.two_ref = f32[200,256]{1,0:T(8,128)S(1)} collective-permute-done((f32[200,256]{1,0:T(8,128)S(1)}, f32[200,256]{1,0:T(8,128)S(1)}, u32[]{:S(2)}, u32[]{:S(2)}) %collective-permute-start) | collective-permute-done | bytes 204832 | tf_op jit(solution)/shard_map/ppermute | solution.py:295
  12.9 0.3 %shard_map.61 = (f32[128,128]{1,0:T(8,128)S(1)}, f32[1,64,128]{2,1,0:T(8,128)S(1)}) custom-call(bf16[256,192]{1,0:T(8,128)(2,1)S(1)} %get-tuple-element.21.high_ref, bf16[256,192]{1,0:T(8,128)(2,1)S(1)} %get-tuple-element.22.low_ref, f32[256,128]{1,0:T(8,128)S(1)} %get-tuple-element.23.labels_ref, f32[200,256]{1,0:T(8,128)S(1)} %collective-permute-done.two_ref), custom_call_target="tpu_custom_call" | custom-call | tf_op jit(solution)/shard_map/pallas_call | solution.py:274
  13.2 0.1 collective-permute-start.6
  13.4 1.6 %collective-permute-start.5 = (f32[128,128]{1,0:T(8,128)S(1)}, f32[128,128]{1,0:T(8,128)S(1)}, u32[]{:S(2)}, u32[]{:S(2)}) collective-permute-start(f32[128,128]{1,0:T(8,128)S(1)} %bitcast.3), channel_id=1, source_target_pairs={{0,1},{1,0},{2,3},{3,2},{4,5},{5,4},{6,7},{7,6},{8,9},{9,8},{10,11... | collective-permute-start | bytes 196616 | tf_op jit(solution)/shard_map/ppermute | solution.py:299
  14.9 0.3 %shard_map.66 = f32[72,128]{1,0:T(8,128)S(1)} custom-call(f32[256,256]{1,0:T(8,128)S(1)} %collective-permute-done.2.twin_ref, f32[200,256]{1,0:T(8,128)S(1)} %collective-permute-done.two_ref), custom_call_target="tpu_custom_call" | custom-call | tf_op jit(solution)/shard_map/pallas_call | solution.py:274
  15.2 0.4 %collective-permute-start.7 = (f32[72,128]{1,0:T(8,128)S(1)}, f32[72,128]{1,0:T(8,128)S(1)}, u32[]{:S(2)}, u32[]{:S(2)}) collective-permute-start(f32[72,128]{1,0:T(8,128)S(1)} %shard_map.66), channel_id=1, source_target_pairs={{0,2},{2,0},{4,6},{6,4},{8,10},{10,8},{12,14},{14,12},{16,18},{18,... | collective-permute-start | bytes 110600 | tf_op jit(solution)/shard_map/ppermute | solution.py:295
  15.6 0.6 %shard_map.63 = (f32[128,128]{1,0:T(8,128)S(1)}, f32[128,128]{1,0:T(8,128)S(1)}) custom-call(f32[256,256]{1,0:T(8,128)S(1)} %shard_map.57.rows_ref, f32[200,256]{1,0:T(8,128)S(1)} %collective-permute-done.two_ref, f32[200,256]{1,0:T(8,128)S(1)} %collective-permute-done.3.slab_ref.mix_ref, f32[200,256]{1,0:T(8,128)S(1)} %collective-permute-done.1.late_ref), custom_call_target="tpu_custom_call" | custom-call | tf_op jit(solution)/shard_map/pallas_call | solution.py:274
  16.2 0.7 %collective-permute-done.6.refs_0_ = f32[64,128]{1,0:T(8,128)S(1)} collective-permute-done((f32[64,128]{1,0:T(8,128)S(1)}, f32[64,128]{1,0:T(8,128)S(1)}, u32[]{:S(2)}, u32[]{:S(2)}) %collective-permute-start.6) | collective-permute-done | bytes 32800 | tf_op jit(solution)/shard_map/ppermute | solution.py:318
  16.9 0.1 shard_map.65.crossed_ref
  17.0 0.8 %shard_map.67.begun_ref = f32[4,128,256]{2,1,0:T(8,128)} custom-call(f32[256,256]{1,0:T(8,128)S(1)} %shard_map.57.rows_ref, f32[128,128]{1,0:T(8,128)S(1)} %get-tuple-element.31.own_keep, f32[8,256]{1,0:T(8,128)S(1)} %shard_map.56.own_labels, f32[128,128]{1,0:T(8,128)S(1)} %shard_map.65.crossed_ref, f32[72,128]{1,0:T(8,128)S(1)} %collective-permute-done.7.core_ref, ...), custom_call_target="tpu_custom_call" | custom-call | tf_op jit(solution)/shard_map/pallas_call | solution.py:274
  17.8 0.0 collective-permute-done.5.refs_0_
  17.8 0.8 %shard_map.68 = f32[4,128,256]{2,1,0:T(8,128)} custom-call(f32[256,256]{1,0:T(8,128)S(1)} %shard_map.57.rows_ref, f32[128,128]{1,0:T(8,128)S(1)} %get-tuple-element.29.two_keep, f32[128,128]{1,0:T(8,128)S(1)} %get-tuple-element.30.third_keep, f32[200,256]{1,0:T(8,128)S(1)} %collective-permute-done.two_ref, ...), custom_call_target="tpu_custom_call", output_to_operand_aliasing={{}: (7, {})} | custom-call | tf_op jit(solution)/shard_map/pallas_call | solution.py:274
  (6 shorter events, 0.0 us)
Async XLA Ops:
  1.4 11.5 %collective-permute-start = (f32[200,256]{1,0:T(8,128)S(1)}, f32[200,256]{1,0:T(8,128)S(1)}, u32[]{:S(2)}, u32[]{:S(2)}) collective-permute-start(f32[200,256]{1,0:T(8,128)S(1)} %shard_map.55.slab_ref.own_ref), channel_id=1, source_target_pairs={{0,4},{2,6},{4,8},{6,10},{8,12},{10,14},{12,16},{14,18},{16,20},{1... | collective-permute-start | bytes 614408 | tf_op jit(solution)/shard_map/ppermute | solution.py:295
  4.4 7.0 %collective-permute-start.3 = (f32[200,256]{1,0:T(8,128)S(1)}, f32[200,256]{1,0:T(8,128)S(1)}, u32[]{:S(2)}, u32[]{:S(2)}) collective-permute-start(f32[200,256]{1,0:T(8,128)S(1)} %shard_map.55.slab_ref.own_ref), channel_id=1, source_target_pairs={{0,2},{2,8},{4,6},{6,4},{8,10},{10,16},{12,14},{14,12},{16,18},{18... | collective-permute-start | bytes 614408 | tf_op jit(solution)/shard_map/ppermute | solution.py:295
  5.7 6.0 %collective-permute-start.2 = (f32[256,256]{1,0:T(8,128)S(1)}, f32[256,256]{1,0:T(8,128)S(1)}, u32[]{:S(2)}, u32[]{:S(2)}) collective-permute-start(f32[256,256]{1,0:T(8,128)S(1)} %shard_map.57.rows_ref), channel_id=1, source_target_pairs={{0,2},{2,0},{4,6},{6,4},{8,10},{10,8},{12,14},{14,12},{16,18},{18,... | collective-permute-start | bytes 786440 | tf_op jit(solution)/shard_map/ppermute | solution.py:295
  7.4 5.9 %collective-permute-start.1 = (f32[200,256]{1,0:T(8,128)S(1)}, f32[200,256]{1,0:T(8,128)S(1)}, u32[]{:S(2)}, u32[]{:S(2)}) collective-permute-start(f32[200,256]{1,0:T(8,128)S(1)} %shard_map.55.slab_ref.own_ref), channel_id=1, source_target_pairs={{0,2},{2,0},{4,6},{6,12},{8,10},{10,8},{12,14},{14,20},{16,18},{18... | collective-permute-start | bytes 614408 | tf_op jit(solution)/shard_map/ppermute | solution.py:295
  7.8 4.0 %collective-permute-start.4 = (f32[64,128]{1,0:T(8,128)S(1)}, f32[64,128]{1,0:T(8,128)S(1)}, u32[]{:S(2)}, u32[]{:S(2)}) collective-permute-start(f32[64,128]{1,0:T(8,128)S(1)} %bitcast.5), channel_id=1, source_target_pairs={{0,1},{1,0},{2,3},{3,2},{4,5},{5,4},{6,7},{7,6},{8,9},{9,8},{10,11... | collective-permute-start | bytes 98312 | tf_op jit(solution)/shard_map/ppermute | solution.py:299
  13.2 3.7 %collective-permute-start.6 = (f32[64,128]{1,0:T(8,128)S(1)}, f32[64,128]{1,0:T(8,128)S(1)}, u32[]{:S(2)}, u32[]{:S(2)}) collective-permute-start(f32[64,128]{1,0:T(8,128)S(1)} %bitcast.4), channel_id=1, source_target_pairs={{0,3},{1,2},{2,1},{3,0},{4,7},{5,6},{6,5},{7,4},{8,11},{9,10},{10,... | collective-permute-start | bytes 98312 | tf_op jit(solution)/shard_map/ppermute | solution.py:318
  13.4 4.5 %collective-permute-start.5 = (f32[128,128]{1,0:T(8,128)S(1)}, f32[128,128]{1,0:T(8,128)S(1)}, u32[]{:S(2)}, u32[]{:S(2)}) collective-permute-start(f32[128,128]{1,0:T(8,128)S(1)} %bitcast.3), channel_id=1, source_target_pairs={{0,1},{1,0},{2,3},{3,2},{4,5},{5,4},{6,7},{7,6},{8,9},{9,8},{10,11... | collective-permute-start | bytes 196616 | tf_op jit(solution)/shard_map/ppermute | solution.py:299
  15.2 1.7 %collective-permute-start.7 = (f32[72,128]{1,0:T(8,128)S(1)}, f32[72,128]{1,0:T(8,128)S(1)}, u32[]{:S(2)}, u32[]{:S(2)}) collective-permute-start(f32[72,128]{1,0:T(8,128)S(1)} %shard_map.66), channel_id=1, source_target_pairs={{0,2},{2,0},{4,6},{6,4},{8,10},{10,8},{12,14},{14,12},{16,18},{18,... | collective-permute-start | bytes 110600 | tf_op jit(solution)/shard_map/ppermute | solution.py:295

commit v29 on v26

--- a/solution.py
+++ b/solution.py
@@ -225,8 +225,8 @@
     return copy
 
 
-def early_kernel(rows_ref, own_keep, own_labels, crossed_ref, core_ref, *refs):
-    own_in, (out_ref, out, sems) = refs[:-3], refs[-3:]
+def early_kernel(rows_ref, own_keep, own_labels, crossed_ref, core_ref, mix_ref, late_ref, *refs):
+    own_in, (out_ref, column_ref, third_ref, out, sems) = refs[:-5], refs[-5:]
     count = own_keep.shape[0]
     tiles = out.shape[2] // LANES
     rows = row_labels(rows_ref[:count, :])
@@ -235,19 +235,20 @@
     crossed = crossed_ref[...] + unhalved(core_ref[:count // 2, :])
     labels = [core_ref[count // 2 + k:count // 2 + k + 1, :] for k in range(tiles)]
     last = stored(jnp.where(odd(), 3, 1), 1, crossed, rows, labels, out_ref, out, sems)
+    width = mix_ref.shape[0] - 8
+    column_ref[...] = rows
+    third_ref[...] = jnp.where(second(), late_ref[width:, :], mix_ref[width:, :])
     first.wait()
     last.wait()
 
 
-def finish_kernel(rows_ref, two_keep, third_keep, two_ref, mix_ref, late_ref, pair_ref, begun_ref, out_ref, out, sems):
+def finish_kernel(column_ref, two_keep, third_keep, two_ref, third_ref, pair_ref, begun_ref, out_ref, out, sems):
     count = two_keep.shape[0]
     width = two_ref.shape[0] - 8
     tiles = out.shape[2] // LANES
-    rows = row_labels(rows_ref[:count, :])
+    rows = column_ref[...]
     two, third = apart(pair_ref[...])
-    labels = [
-        jnp.where(second(), x, y) for x, y in zip(tiles_of(late_ref, width, tiles), tiles_of(mix_ref, width, tiles))
-    ]
+    labels = tiles_of(third_ref, 0, tiles)
     place = jnp.where(odd(), 1, 0)
     for plane, term, plane_labels in (
         (place, two + two_keep[...], tiles_of(two_ref, width, tiles)), (1 - place, third + third_keep[...], labels)
@@ -276,7 +277,7 @@
         out_shape=out_shape,
         in_specs=[OFFCHIP if i < off or i == onto else ONCHIP for i in range(len(args))],
         input_output_aliases={} if onto is None else {onto: 0},
-        out_specs=[out_specs] * len(out_shape),
+        out_specs=[out_specs] + [ONCHIP] * (len(out_shape) - 1),
         scratch_shapes=list(scratch),
         cost_estimate=pl.CostEstimate(flops=flops, bytes_accessed=0, transcendentals=0),
         compiler_params=pltpu.CompilerParams(vmem_limit_bytes=32 * 1024 * 1024),
@@ -347,11 +348,12 @@
     two_keep, third_keep = call(keep_kernel, [whole(count, LANES)] * 2, (rows, after(two, pair_send), mix, late), 0)
     crossed_sum, = call(halves_kernel, [whole(count, LANES)], tuple(diagonal_in), 3 * one_product)
     stage = [pltpu.VMEM((2, count, pairs), F32), pltpu.SemaphoreType.DMA((2,))]
-    begun, = call(early_kernel, [whole(4, count, pairs)],
-                  (rows, own_keep, own_labels, crossed_sum, core_in, *own_in), 0, 0, stage, OFFCHIP)
+    begun, column_kept, third_labels = call(
+                  early_kernel, [whole(4, count, pairs), whole(count, LANES), whole(8, pairs)],
+                  (rows, own_keep, own_labels, crossed_sum, core_in, mix, late, *own_in), 0, 0, stage, OFFCHIP)
     pair_sum, = call(total_kernel, [whole(count, LANES)], tuple(pair_in), 0)
     out, = call(finish_kernel, [whole(4, count, pairs)],
-                (rows, two_keep, third_keep, two, mix, late, pair_sum, begun), 0, 0, stage, OFFCHIP, 7)
+                (column_kept, two_keep, third_keep, two, third_labels, pair_sum, begun), 0, 0, stage, OFFCHIP, 6)
     return out
 
 

time: 18.7 us -> 19.3 us (1.032)
  waiting for transfers between devices: 3.71 us -> 4.23 us
    ppermute x5, waiting for transfers between devices: 2.63 us -> 3.49 us  [moved(): lax.ppermute(array, 'blk', [(i, (i + steps[i % 4]) % blocks) for i in ran...]
    ppermute x2, waiting for transfers between devices: 0.35 us -> 0.01 us  [exchanged(): lax.ppermute(array[k - 1], 'red', [(i, (i + k) % parts) for i in range(pa...]
  transfers between devices with their start and end apart: 8 -> 8, of which waited for: 5 -> 2; matrix products, arithmetic and copies ran while one was open for 0% -> 0% of each run, Pallas kernels for 22% -> 21%
where the time goes in v29:
time: 19.3 us; the launch traced here: 19.1 us
  starting transfers between devices  8.41 us (44%)
  Pallas kernels  6.31 us (33%)
  waiting for transfers between devices  4.23 us (22%)
    pallas_call x14, Pallas kernels, call(): pl.pallas_call(kernel, out_shape=out_shape, in_specs=[OFFCHIP if i < off...  6.31 us
    ppermute x5, starting transfers between devices, moved(): lax.ppermute(array, 'blk', [(i, (i + steps[i % 4]) % blocks) for i in ran...  5.24 us
    ppermute x5, waiting for transfers between devices, moved(): lax.ppermute(array, 'blk', [(i, (i + steps[i % 4]) % blocks) for i in ran...  3.49 us
    ppermute x2, starting transfers between devices, exchanged(): lax.ppermute(array[k - 1], 'red', [(i, (i + k) % parts) for i in range(pa...  3.1 us
    ppermute x1, waiting for transfers between devices, crossed(): lax.ppermute(array, ('blk', 'red'), [(b * parts + r, c * parts + t) for (...  0.73 us
  transfers between devices with their start and end apart: 8, of which 2 were waited for; matrix products, arithmetic and copies ran while one was open for 0% of the time, Pallas kernels for 21%

profile of v29, /device:TPU:0, one launch (start us, length us, event | category | flops | bytes accessed | tf_op | source)
XLA Modules:
  0.0 19.1 jit_solution(3063852742588622166)
XLA Ops:
  0.0 1.4 %shard_map.55.slab_ref.own_ref = f32[200,256]{1,0:T(8,128)S(1)} custom-call(f32[256,768]{1,0:T(8,128)} %amp_ref.1, s32[1,256]{1,0:T(1,128)} %ij_ref.1, s32[1,768]{1,0:T(1,128)} %cd_ref.3), custom_call_target="tpu_custom_call" | custom-call | flops 786432 | tf_op jit(solution)/shard_map/pallas_call | solution.py:275
  1.4 3.0 %collective-permute-start.1 = (f32[200,256]{1,0:T(8,128)S(1)}, f32[200,256]{1,0:T(8,128)S(1)}, u32[]{:S(2)}, u32[]{:S(2)}) collective-permute-start(f32[200,256]{1,0:T(8,128)S(1)} %shard_map.55.slab_ref.own_ref), channel_id=1, source_target_pairs={{0,4},{2,6},{4,8},{6,10},{8,12},{10,14},{12,16},{14,18},{16,20},{1... | collective-permute-start | bytes 614408 | tf_op jit(solution)/shard_map/ppermute | solution.py:296
  4.4 1.3 %shard_map.57.rows_ref = f32[256,256]{1,0:T(8,128)S(1)} custom-call(f32[256,768]{1,0:T(8,128)} %v_ref, s32[1,256]{1,0:T(1,128)} %ab_ref.1, s32[1,768]{1,0:T(1,128)} %cd_ref.3), custom_call_target="tpu_custom_call" | custom-call | tf_op jit(solution)/shard_map/pallas_call | solution.py:275
  5.7 0.1 collective-permute-start
  5.8 0.5 %collective-permute-start.2 = (f32[200,256]{1,0:T(8,128)S(1)}, f32[200,256]{1,0:T(8,128)S(1)}, u32[]{:S(2)}, u32[]{:S(2)}) collective-permute-start(f32[200,256]{1,0:T(8,128)S(1)} %shard_map.55.slab_ref.own_ref), channel_id=1, source_target_pairs={{0,2},{2,8},{4,6},{6,4},{8,10},{10,16},{12,14},{14,12},{16,18},{18... | collective-permute-start | bytes 614408 | tf_op jit(solution)/shard_map/ppermute | solution.py:296
  6.3 0.3 %shard_map.58 = (f32[128,128]{1,0:T(8,128)S(1)}, f32[1,64,128]{2,1,0:T(8,128)S(1)}) custom-call(f32[256,256]{1,0:T(8,128)S(1)} %shard_map.57.rows_ref, f32[200,256]{1,0:T(8,128)S(1)} %shard_map.55.slab_ref.own_ref), custom_call_target="tpu_custom_call" | custom-call | flops 9663676416 | tf_op jit(solution)/shard_map/pallas_call | solution.py:275
  6.6 1.3 %collective-permute-start.5 = (f32[200,256]{1,0:T(8,128)S(1)}, f32[200,256]{1,0:T(8,128)S(1)}, u32[]{:S(2)}, u32[]{:S(2)}) collective-permute-start(f32[200,256]{1,0:T(8,128)S(1)} %shard_map.55.slab_ref.own_ref), channel_id=1, source_target_pairs={{0,2},{2,0},{4,6},{6,12},{8,10},{10,8},{12,14},{14,20},{16,18},{18... | collective-permute-start | bytes 614408 | tf_op jit(solution)/shard_map/ppermute | solution.py:296
  7.9 1.5 %collective-permute-start.3 = (f32[64,128]{1,0:T(8,128)S(1)}, f32[64,128]{1,0:T(8,128)S(1)}, u32[]{:S(2)}, u32[]{:S(2)}) collective-permute-start(f32[64,128]{1,0:T(8,128)S(1)} %bitcast.5), channel_id=1, source_target_pairs={{0,1},{1,0},{2,3},{3,2},{4,5},{5,4},{6,7},{7,6},{8,9},{9,8},{10,11... | collective-permute-start | bytes 98312 | tf_op jit(solution)/shard_map/ppermute | solution.py:300
  9.4 3.5 %collective-permute-done.2.slab_ref.mix_ref = f32[200,256]{1,0:T(8,128)S(1)} collective-permute-done((f32[200,256]{1,0:T(8,128)S(1)}, f32[200,256]{1,0:T(8,128)S(1)}, u32[]{:S(2)}, u32[]{:S(2)}) %collective-permute-start.2) | collective-permute-done | bytes 204832 | tf_op jit(solution)/shard_map/ppermute | solution.py:296
  12.9 0.3 %shard_map.60.mix_term = f32[128,128]{1,0:T(8,128)S(1)} custom-call(f32[256,256]{1,0:T(8,128)S(1)} %shard_map.57.rows_ref, f32[200,256]{1,0:T(8,128)S(1)} %collective-permute-done.2.slab_ref.mix_ref), custom_call_target="tpu_custom_call" | custom-call | tf_op jit(solution)/shard_map/pallas_call | solution.py:275
  13.2 0.0 collective-permute-done.twin_ref
  13.2 0.1 shard_map.59
  13.3 0.0 collective-permute-done.3.refs_0_
  13.3 0.0 collective-permute-done.1.two_ref
  13.3 0.3 %shard_map.61 = (f32[128,128]{1,0:T(8,128)S(1)}, f32[1,64,128]{2,1,0:T(8,128)S(1)}) custom-call(bf16[256,192]{1,0:T(8,128)(2,1)S(1)} %get-tuple-element.24.high_ref, bf16[256,192]{1,0:T(8,128)(2,1)S(1)} %get-tuple-element.25.low_ref, f32[256,128]{1,0:T(8,128)S(1)} %get-tuple-element.26.labels_ref, f32[200,256]{1,0:T(8,128)S(1)} %collective-permute-done.1.two_ref), custom_call_target="tpu_custom_call" | custom-call | tf_op jit(solution)/shard_map/pallas_call | solution.py:275
  13.7 0.1 collective-permute-start.4
  13.8 1.6 %collective-permute-start.7 = (f32[128,128]{1,0:T(8,128)S(1)}, f32[128,128]{1,0:T(8,128)S(1)}, u32[]{:S(2)}, u32[]{:S(2)}) collective-permute-start(f32[128,128]{1,0:T(8,128)S(1)} %bitcast.3), channel_id=1, source_target_pairs={{0,1},{1,0},{2,3},{3,2},{4,5},{5,4},{6,7},{7,6},{8,9},{9,8},{10,11... | collective-permute-start | bytes 196616 | tf_op jit(solution)/shard_map/ppermute | solution.py:300
  15.4 0.3 %shard_map.64 = f32[72,128]{1,0:T(8,128)S(1)} custom-call(f32[256,256]{1,0:T(8,128)S(1)} %collective-permute-done.twin_ref, f32[200,256]{1,0:T(8,128)S(1)} %collective-permute-done.1.two_ref), custom_call_target="tpu_custom_call" | custom-call | tf_op jit(solution)/shard_map/pallas_call | solution.py:275
  15.7 0.4 %collective-permute-start.6 = (f32[72,128]{1,0:T(8,128)S(1)}, f32[72,128]{1,0:T(8,128)S(1)}, u32[]{:S(2)}, u32[]{:S(2)}) collective-permute-start(f32[72,128]{1,0:T(8,128)S(1)} %shard_map.64), channel_id=1, source_target_pairs={{0,2},{2,0},{4,6},{6,4},{8,10},{10,8},{12,14},{14,12},{16,18},{18,... | collective-permute-start | bytes 110600 | tf_op jit(solution)/shard_map/ppermute | solution.py:296
  16.0 0.6 %shard_map.66 = (f32[128,128]{1,0:T(8,128)S(1)}, f32[128,128]{1,0:T(8,128)S(1)}) custom-call(f32[256,256]{1,0:T(8,128)S(1)} %shard_map.57.rows_ref, f32[200,256]{1,0:T(8,128)S(1)} %collective-permute-done.1.two_ref, f32[200,256]{1,0:T(8,128)S(1)} %collective-permute-done.2.slab_ref.mix_ref, f32[200,256]{1,0:T(8,128)S(1)} %collective-permute-done.5.late_ref), custom_call_target="tpu_custom_call" | custom-call | tf_op jit(solution)/shard_map/pallas_call | solution.py:275
  16.6 0.7 %collective-permute-done.4.refs_0_ = f32[64,128]{1,0:T(8,128)S(1)} collective-permute-done((f32[64,128]{1,0:T(8,128)S(1)}, f32[64,128]{1,0:T(8,128)S(1)}, u32[]{:S(2)}, u32[]{:S(2)}) %collective-permute-start.4) | collective-permute-done | bytes 32800 | tf_op jit(solution)/shard_map/ppermute | solution.py:319
  17.3 0.1 shard_map.62.crossed_ref
  17.4 0.8 %shard_map.65 = (f32[4,128,256]{2,1,0:T(8,128)}, f32[128,128]{1,0:T(8,128)S(1)}, f32[8,256]{1,0:T(8,128)S(1)}) custom-call(f32[256,256]{1,0:T(8,128)S(1)} %shard_map.57.rows_ref, f32[128,128]{1,0:T(8,128)S(1)} %get-tuple-element.23.own_keep, f32[8,256]{1,0:T(8,128)S(1)} %shard_map.56.own_labels, f32[128,128]{1,0:T(8,128)S(1)} %shard_map.62.crossed_ref, ...), custom_call_target="tpu_custom_call" | custom-call | tf_op jit(solution)/shard_map/pallas_call | solution.py:275
  18.3 0.8 %shard_map.68 = f32[4,128,256]{2,1,0:T(8,128)} custom-call(f32[128,128]{1,0:T(8,128)S(1)} %get-tuple-element.34.column_ref, f32[128,128]{1,0:T(8,128)S(1)} %get-tuple-element.35.two_keep, f32[128,128]{1,0:T(8,128)S(1)} %get-tuple-element.36.third_keep, f32[200,256]{1,0:T(8,128)S(1)} %collective-permute-done.1.two_ref, ...), custom_call_target="tpu_custom_call", output_to_operand_aliasing={{}: (6, {})} | custom-call | tf_op jit(solution)/shard_map/pallas_call | solution.py:275
  (6 shorter events, 0.0 us)
Async XLA Ops:
  1.4 11.9 %collective-permute-start.1 = (f32[200,256]{1,0:T(8,128)S(1)}, f32[200,256]{1,0:T(8,128)S(1)}, u32[]{:S(2)}, u32[]{:S(2)}) collective-permute-start(f32[200,256]{1,0:T(8,128)S(1)} %shard_map.55.slab_ref.own_ref), channel_id=1, source_target_pairs={{0,4},{2,6},{4,8},{6,10},{8,12},{10,14},{12,16},{14,18},{16,20},{1... | collective-permute-start | bytes 614408 | tf_op jit(solution)/shard_map/ppermute | solution.py:296
  5.7 7.5 %collective-permute-start = (f32[256,256]{1,0:T(8,128)S(1)}, f32[256,256]{1,0:T(8,128)S(1)}, u32[]{:S(2)}, u32[]{:S(2)}) collective-permute-start(f32[256,256]{1,0:T(8,128)S(1)} %shard_map.57.rows_ref), channel_id=1, source_target_pairs={{0,2},{2,0},{4,6},{6,4},{8,10},{10,8},{12,14},{14,12},{16,18},{18,... | collective-permute-start | bytes 786440 | tf_op jit(solution)/shard_map/ppermute | solution.py:296
  5.8 7.1 %collective-permute-start.2 = (f32[200,256]{1,0:T(8,128)S(1)}, f32[200,256]{1,0:T(8,128)S(1)}, u32[]{:S(2)}, u32[]{:S(2)}) collective-permute-start(f32[200,256]{1,0:T(8,128)S(1)} %shard_map.55.slab_ref.own_ref), channel_id=1, source_target_pairs={{0,2},{2,8},{4,6},{6,4},{8,10},{10,16},{12,14},{14,12},{16,18},{18... | collective-permute-start | bytes 614408 | tf_op jit(solution)/shard_map/ppermute | solution.py:296
  6.6 7.1 %collective-permute-start.5 = (f32[200,256]{1,0:T(8,128)S(1)}, f32[200,256]{1,0:T(8,128)S(1)}, u32[]{:S(2)}, u32[]{:S(2)}) collective-permute-start(f32[200,256]{1,0:T(8,128)S(1)} %shard_map.55.slab_ref.own_ref), channel_id=1, source_target_pairs={{0,2},{2,0},{4,6},{6,12},{8,10},{10,8},{12,14},{14,20},{16,18},{18... | collective-permute-start | bytes 614408 | tf_op jit(solution)/shard_map/ppermute | solution.py:296
  7.9 5.4 %collective-permute-start.3 = (f32[64,128]{1,0:T(8,128)S(1)}, f32[64,128]{1,0:T(8,128)S(1)}, u32[]{:S(2)}, u32[]{:S(2)}) collective-permute-start(f32[64,128]{1,0:T(8,128)S(1)} %bitcast.5), channel_id=1, source_target_pairs={{0,1},{1,0},{2,3},{3,2},{4,5},{5,4},{6,7},{7,6},{8,9},{9,8},{10,11... | collective-permute-start | bytes 98312 | tf_op jit(solution)/shard_map/ppermute | solution.py:300
  13.7 3.7 %collective-permute-start.4 = (f32[64,128]{1,0:T(8,128)S(1)}, f32[64,128]{1,0:T(8,128)S(1)}, u32[]{:S(2)}, u32[]{:S(2)}) collective-permute-start(f32[64,128]{1,0:T(8,128)S(1)} %bitcast.4), channel_id=1, source_target_pairs={{0,3},{1,2},{2,1},{3,0},{4,7},{5,6},{6,5},{7,4},{8,11},{9,10},{10,... | collective-permute-start | bytes 98312 | tf_op jit(solution)/shard_map/ppermute | solution.py:319
  13.8 4.5 %collective-permute-start.7 = (f32[128,128]{1,0:T(8,128)S(1)}, f32[128,128]{1,0:T(8,128)S(1)}, u32[]{:S(2)}, u32[]{:S(2)}) collective-permute-start(f32[128,128]{1,0:T(8,128)S(1)} %bitcast.3), channel_id=1, source_target_pairs={{0,1},{1,0},{2,3},{3,2},{4,5},{5,4},{6,7},{7,6},{8,9},{9,8},{10,11... | collective-permute-start | bytes 196616 | tf_op jit(solution)/shard_map/ppermute | solution.py:300
  15.7 1.8 %collective-permute-start.6 = (f32[72,128]{1,0:T(8,128)S(1)}, f32[72,128]{1,0:T(8,128)S(1)}, u32[]{:S(2)}, u32[]{:S(2)}) collective-permute-start(f32[72,128]{1,0:T(8,128)S(1)} %shard_map.64), channel_id=1, source_target_pairs={{0,2},{2,0},{4,6},{6,4},{8,10},{10,8},{12,14},{14,12},{16,18},{18,... | collective-permute-start | bytes 110600 | tf_op jit(solution)/shard_map/ppermute | solution.py:296

commit v30 on v26

--- a/solution.py
+++ b/solution.py
@@ -349,7 +349,7 @@
     stage = [pltpu.VMEM((2, count, pairs), F32), pltpu.SemaphoreType.DMA((2,))]
     begun, = call(early_kernel, [whole(4, count, pairs)],
                   (rows, own_keep, own_labels, crossed_sum, core_in, *own_in), 0, 0, stage, OFFCHIP)
-    pair_sum, = call(total_kernel, [whole(count, LANES)], tuple(pair_in), 0)
+    pair_sum = pair_in[0] if parts == 2 else call(total_kernel, [whole(count, LANES)], tuple(pair_in), 0)[0]
     out, = call(finish_kernel, [whole(4, count, pairs)],
                 (rows, two_keep, third_keep, two, mix, late, pair_sum, begun), 0, 0, stage, OFFCHIP, 7)
     return out

time: 18.7 us -> 18.7 us (level)
    pallas_call x14 -> x13, Pallas kernels: 6.31 us -> 6.3 us  [call(): pl.pallas_call(kernel, out_shape=out_shape, in_specs=[OFFCHIP if i < off...]
where the time goes in v30:
time: 18.7 us; the launch traced here: 18.5 us
  starting transfers between devices  8.45 us (45%)
  Pallas kernels  6.3 us (34%)
  waiting for transfers between devices  3.71 us (20%)
    pallas_call x13, Pallas kernels, call(): pl.pallas_call(kernel, out_shape=out_shape, in_specs=[OFFCHIP if i < off...  6.3 us
    ppermute x5, starting transfers between devices, moved(): lax.ppermute(array, 'blk', [(i, (i + steps[i % 4]) % blocks) for i in ran...  5.19 us
    ppermute x2, starting transfers between devices, exchanged(): lax.ppermute(array[k - 1], 'red', [(i, (i + k) % parts) for i in range(pa...  3.02 us
    ppermute x5, waiting for transfers between devices, moved(): lax.ppermute(array, 'blk', [(i, (i + steps[i % 4]) % blocks) for i in ran...  2.63 us
    ppermute x1, waiting for transfers between devices, crossed(): lax.ppermute(array, ('blk', 'red'), [(b * parts + r, c * parts + t) for (...  0.73 us
  transfers between devices with their start and end apart: 8, of which 5 were waited for; matrix products, arithmetic and copies ran while one was open for 0% of the time, Pallas kernels for 22%

profile of v30, /device:TPU:0, one launch (start us, length us, event | category | flops | bytes accessed | tf_op | source)
XLA Modules:
  0.0 18.5 jit_solution(5373119808046389668)
XLA Ops:
  0.0 1.4 %shard_map.55.slab_ref.own_ref = f32[200,256]{1,0:T(8,128)S(1)} custom-call(f32[256,768]{1,0:T(8,128)} %amp_ref.1, s32[1,256]{1,0:T(1,128)} %ij_ref.1, s32[1,768]{1,0:T(1,128)} %cd_ref.3), custom_call_target="tpu_custom_call" | custom-call | flops 786432 | tf_op jit(solution)/shard_map/pallas_call | solution.py:274
  1.4 3.0 %collective-permute-start = (f32[200,256]{1,0:T(8,128)S(1)}, f32[200,256]{1,0:T(8,128)S(1)}, u32[]{:S(2)}, u32[]{:S(2)}) collective-permute-start(f32[200,256]{1,0:T(8,128)S(1)} %shard_map.55.slab_ref.own_ref), channel_id=1, source_target_pairs={{0,4},{2,6},{4,8},{6,10},{8,12},{10,14},{12,16},{14,18},{16,20},{1... | collective-permute-start | bytes 614408 | tf_op jit(solution)/shard_map/ppermute | solution.py:295
  4.4 0.0 collective-permute-start.3
  4.4 1.3 %shard_map.57.rows_ref = f32[256,256]{1,0:T(8,128)S(1)} custom-call(f32[256,768]{1,0:T(8,128)} %v_ref, s32[1,256]{1,0:T(1,128)} %ab_ref.1, s32[1,768]{1,0:T(1,128)} %cd_ref.3), custom_call_target="tpu_custom_call" | custom-call | tf_op jit(solution)/shard_map/pallas_call | solution.py:274
  5.7 1.8 %collective-permute-start.2 = (f32[256,256]{1,0:T(8,128)S(1)}, f32[256,256]{1,0:T(8,128)S(1)}, u32[]{:S(2)}, u32[]{:S(2)}) collective-permute-start(f32[256,256]{1,0:T(8,128)S(1)} %shard_map.57.rows_ref), channel_id=1, source_target_pairs={{0,2},{2,0},{4,6},{6,4},{8,10},{10,8},{12,14},{14,12},{16,18},{18,... | collective-permute-start | bytes 786440 | tf_op jit(solution)/shard_map/ppermute | solution.py:295
  7.4 0.3 %shard_map.58 = (f32[128,128]{1,0:T(8,128)S(1)}, f32[1,64,128]{2,1,0:T(8,128)S(1)}) custom-call(f32[256,256]{1,0:T(8,128)S(1)} %shard_map.57.rows_ref, f32[200,256]{1,0:T(8,128)S(1)} %shard_map.55.slab_ref.own_ref), custom_call_target="tpu_custom_call" | custom-call | flops 9663676416 | tf_op jit(solution)/shard_map/pallas_call | solution.py:274
  7.8 0.1 collective-permute-start.1
  7.8 1.6 %collective-permute-start.4 = (f32[64,128]{1,0:T(8,128)S(1)}, f32[64,128]{1,0:T(8,128)S(1)}, u32[]{:S(2)}, u32[]{:S(2)}) collective-permute-start(f32[64,128]{1,0:T(8,128)S(1)} %bitcast.5), channel_id=1, source_target_pairs={{0,1},{1,0},{2,3},{3,2},{4,5},{5,4},{6,7},{7,6},{8,9},{9,8},{10,11... | collective-permute-start | bytes 98312 | tf_op jit(solution)/shard_map/ppermute | solution.py:299
  9.4 1.9 %collective-permute-done.3.slab_ref.mix_ref = f32[200,256]{1,0:T(8,128)S(1)} collective-permute-done((f32[200,256]{1,0:T(8,128)S(1)}, f32[200,256]{1,0:T(8,128)S(1)}, u32[]{:S(2)}, u32[]{:S(2)}) %collective-permute-start.3) | collective-permute-done | bytes 204832 | tf_op jit(solution)/shard_map/ppermute | solution.py:295
  11.4 0.3 %shard_map.60.mix_term = f32[128,128]{1,0:T(8,128)S(1)} custom-call(f32[256,256]{1,0:T(8,128)S(1)} %shard_map.57.rows_ref, f32[200,256]{1,0:T(8,128)S(1)} %collective-permute-done.3.slab_ref.mix_ref), custom_call_target="tpu_custom_call" | custom-call | tf_op jit(solution)/shard_map/pallas_call | solution.py:274
  11.7 0.1 shard_map.59
  11.8 0.1 collective-permute-done.4.refs_0_
  11.8 0.7 %collective-permute-done.two_ref = f32[200,256]{1,0:T(8,128)S(1)} collective-permute-done((f32[200,256]{1,0:T(8,128)S(1)}, f32[200,256]{1,0:T(8,128)S(1)}, u32[]{:S(2)}, u32[]{:S(2)}) %collective-permute-start) | collective-permute-done | bytes 204832 | tf_op jit(solution)/shard_map/ppermute | solution.py:295
  12.5 0.3 %shard_map.61 = (f32[128,128]{1,0:T(8,128)S(1)}, f32[1,64,128]{2,1,0:T(8,128)S(1)}) custom-call(bf16[256,192]{1,0:T(8,128)(2,1)S(1)} %get-tuple-element.22.high_ref, bf16[256,192]{1,0:T(8,128)(2,1)S(1)} %get-tuple-element.23.low_ref, f32[256,128]{1,0:T(8,128)S(1)} %get-tuple-element.24.labels_ref, f32[200,256]{1,0:T(8,128)S(1)} %collective-permute-done.two_ref), custom_call_target="tpu_custom_call" | custom-call | tf_op jit(solution)/shard_map/pallas_call | solution.py:274
  12.8 0.2 %collective-permute-start.6 = (f32[64,128]{1,0:T(8,128)S(1)}, f32[64,128]{1,0:T(8,128)S(1)}, u32[]{:S(2)}, u32[]{:S(2)}) collective-permute-start(f32[64,128]{1,0:T(8,128)S(1)} %bitcast.4), channel_id=1, source_target_pairs={{0,3},{1,2},{2,1},{3,0},{4,7},{5,6},{6,5},{7,4},{8,11},{9,10},{10,... | collective-permute-start | bytes 98312 | tf_op jit(solution)/shard_map/ppermute | solution.py:318
  13.1 1.4 %collective-permute-start.5 = (f32[128,128]{1,0:T(8,128)S(1)}, f32[128,128]{1,0:T(8,128)S(1)}, u32[]{:S(2)}, u32[]{:S(2)}) collective-permute-start(f32[128,128]{1,0:T(8,128)S(1)} %bitcast.3), channel_id=1, source_target_pairs={{0,1},{1,0},{2,3},{3,2},{4,5},{5,4},{6,7},{7,6},{8,9},{9,8},{10,11... | collective-permute-start | bytes 196616 | tf_op jit(solution)/shard_map/ppermute | solution.py:299
  14.6 0.3 %shard_map.65 = f32[72,128]{1,0:T(8,128)S(1)} custom-call(f32[256,256]{1,0:T(8,128)S(1)} %collective-permute-done.2.twin_ref, f32[200,256]{1,0:T(8,128)S(1)} %collective-permute-done.two_ref), custom_call_target="tpu_custom_call" | custom-call | tf_op jit(solution)/shard_map/pallas_call | solution.py:274
  14.8 0.4 %collective-permute-start.7 = (f32[72,128]{1,0:T(8,128)S(1)}, f32[72,128]{1,0:T(8,128)S(1)}, u32[]{:S(2)}, u32[]{:S(2)}) collective-permute-start(f32[72,128]{1,0:T(8,128)S(1)} %shard_map.65), channel_id=1, source_target_pairs={{0,2},{2,0},{4,6},{6,4},{8,10},{10,8},{12,14},{14,12},{16,18},{18,... | collective-permute-start | bytes 110600 | tf_op jit(solution)/shard_map/ppermute | solution.py:295
  15.2 0.6 %shard_map.63 = (f32[128,128]{1,0:T(8,128)S(1)}, f32[128,128]{1,0:T(8,128)S(1)}) custom-call(f32[256,256]{1,0:T(8,128)S(1)} %shard_map.57.rows_ref, f32[200,256]{1,0:T(8,128)S(1)} %collective-permute-done.two_ref, f32[200,256]{1,0:T(8,128)S(1)} %collective-permute-done.3.slab_ref.mix_ref, f32[200,256]{1,0:T(8,128)S(1)} %collective-permute-done.1.late_ref), custom_call_target="tpu_custom_call" | custom-call | tf_op jit(solution)/shard_map/pallas_call | solution.py:274
  15.8 0.7 %collective-permute-done.6.refs_0_ = f32[64,128]{1,0:T(8,128)S(1)} collective-permute-done((f32[64,128]{1,0:T(8,128)S(1)}, f32[64,128]{1,0:T(8,128)S(1)}, u32[]{:S(2)}, u32[]{:S(2)}) %collective-permute-start.6) | collective-permute-done | bytes 32800 | tf_op jit(solution)/shard_map/ppermute | solution.py:318
  16.5 0.1 shard_map.64.crossed_ref
  16.6 0.8 %shard_map.66.begun_ref = f32[4,128,256]{2,1,0:T(8,128)} custom-call(f32[256,256]{1,0:T(8,128)S(1)} %shard_map.57.rows_ref, f32[128,128]{1,0:T(8,128)S(1)} %get-tuple-element.20.own_keep, f32[8,256]{1,0:T(8,128)S(1)} %shard_map.56.own_labels, f32[128,128]{1,0:T(8,128)S(1)} %shard_map.64.crossed_ref, f32[72,128]{1,0:T(8,128)S(1)} %collective-permute-done.7.core_ref, ...), custom_call_target="tpu_custom_call" | custom-call | tf_op jit(solution)/shard_map/pallas_call | solution.py:274
  17.4 0.3 %collective-permute-done.5.pair_ref = f32[128,128]{1,0:T(8,128)S(1)} collective-permute-done((f32[128,128]{1,0:T(8,128)S(1)}, f32[128,128]{1,0:T(8,128)S(1)}, u32[]{:S(2)}, u32[]{:S(2)}) %collective-permute-start.5) | collective-permute-done | bytes 65568 | tf_op jit(solution)/shard_map/ppermute | solution.py:299
  17.7 0.8 %shard_map.67 = f32[4,128,256]{2,1,0:T(8,128)} custom-call(f32[256,256]{1,0:T(8,128)S(1)} %shard_map.57.rows_ref, f32[128,128]{1,0:T(8,128)S(1)} %get-tuple-element.30.two_keep, f32[128,128]{1,0:T(8,128)S(1)} %get-tuple-element.31.third_keep, f32[200,256]{1,0:T(8,128)S(1)} %collective-permute-done.two_ref, ...), custom_call_target="tpu_custom_call", output_to_operand_aliasing={{}: (7, {})} | custom-call | tf_op jit(solution)/shard_map/pallas_call | solution.py:274
  (5 shorter events, 0.0 us)
Async XLA Ops:
  1.4 11.1 %collective-permute-start = (f32[200,256]{1,0:T(8,128)S(1)}, f32[200,256]{1,0:T(8,128)S(1)}, u32[]{:S(2)}, u32[]{:S(2)}) collective-permute-start(f32[200,256]{1,0:T(8,128)S(1)} %shard_map.55.slab_ref.own_ref), channel_id=1, source_target_pairs={{0,4},{2,6},{4,8},{6,10},{8,12},{10,14},{12,16},{14,18},{16,20},{1... | collective-permute-start | bytes 614408 | tf_op jit(solution)/shard_map/ppermute | solution.py:295
  4.4 7.0 %collective-permute-start.3 = (f32[200,256]{1,0:T(8,128)S(1)}, f32[200,256]{1,0:T(8,128)S(1)}, u32[]{:S(2)}, u32[]{:S(2)}) collective-permute-start(f32[200,256]{1,0:T(8,128)S(1)} %shard_map.55.slab_ref.own_ref), channel_id=1, source_target_pairs={{0,2},{2,8},{4,6},{6,4},{8,10},{10,16},{12,14},{14,12},{16,18},{18... | collective-permute-start | bytes 614408 | tf_op jit(solution)/shard_map/ppermute | solution.py:295
  5.7 6.0 %collective-permute-start.2 = (f32[256,256]{1,0:T(8,128)S(1)}, f32[256,256]{1,0:T(8,128)S(1)}, u32[]{:S(2)}, u32[]{:S(2)}) collective-permute-start(f32[256,256]{1,0:T(8,128)S(1)} %shard_map.57.rows_ref), channel_id=1, source_target_pairs={{0,2},{2,0},{4,6},{6,4},{8,10},{10,8},{12,14},{14,12},{16,18},{18,... | collective-permute-start | bytes 786440 | tf_op jit(solution)/shard_map/ppermute | solution.py:295
  7.8 5.3 %collective-permute-start.1 = (f32[200,256]{1,0:T(8,128)S(1)}, f32[200,256]{1,0:T(8,128)S(1)}, u32[]{:S(2)}, u32[]{:S(2)}) collective-permute-start(f32[200,256]{1,0:T(8,128)S(1)} %shard_map.55.slab_ref.own_ref), channel_id=1, source_target_pairs={{0,2},{2,0},{4,6},{6,12},{8,10},{10,8},{12,14},{14,20},{16,18},{18... | collective-permute-start | bytes 614408 | tf_op jit(solution)/shard_map/ppermute | solution.py:295
  7.8 4.0 %collective-permute-start.4 = (f32[64,128]{1,0:T(8,128)S(1)}, f32[64,128]{1,0:T(8,128)S(1)}, u32[]{:S(2)}, u32[]{:S(2)}) collective-permute-start(f32[64,128]{1,0:T(8,128)S(1)} %bitcast.5), channel_id=1, source_target_pairs={{0,1},{1,0},{2,3},{3,2},{4,5},{5,4},{6,7},{7,6},{8,9},{9,8},{10,11... | collective-permute-start | bytes 98312 | tf_op jit(solution)/shard_map/ppermute | solution.py:299
  12.8 3.7 %collective-permute-start.6 = (f32[64,128]{1,0:T(8,128)S(1)}, f32[64,128]{1,0:T(8,128)S(1)}, u32[]{:S(2)}, u32[]{:S(2)}) collective-permute-start(f32[64,128]{1,0:T(8,128)S(1)} %bitcast.4), channel_id=1, source_target_pairs={{0,3},{1,2},{2,1},{3,0},{4,7},{5,6},{6,5},{7,4},{8,11},{9,10},{10,... | collective-permute-start | bytes 98312 | tf_op jit(solution)/shard_map/ppermute | solution.py:318
  13.1 4.6 %collective-permute-start.5 = (f32[128,128]{1,0:T(8,128)S(1)}, f32[128,128]{1,0:T(8,128)S(1)}, u32[]{:S(2)}, u32[]{:S(2)}) collective-permute-start(f32[128,128]{1,0:T(8,128)S(1)} %bitcast.3), channel_id=1, source_target_pairs={{0,1},{1,0},{2,3},{3,2},{4,5},{5,4},{6,7},{7,6},{8,9},{9,8},{10,11... | collective-permute-start | bytes 196616 | tf_op jit(solution)/shard_map/ppermute | solution.py:299
  14.8 1.8 %collective-permute-start.7 = (f32[72,128]{1,0:T(8,128)S(1)}, f32[72,128]{1,0:T(8,128)S(1)}, u32[]{:S(2)}, u32[]{:S(2)}) collective-permute-start(f32[72,128]{1,0:T(8,128)S(1)} %shard_map.65), channel_id=1, source_target_pairs={{0,2},{2,0},{4,6},{6,4},{8,10},{10,8},{12,14},{14,12},{16,18},{18,... | collective-permute-start | bytes 110600 | tf_op jit(solution)/shard_map/ppermute | solution.py:295
